TPU v7x, 32 devices: a whole 2x2x4 slice. The times are simulated.
32 devices in a mesh: group: 2 (over x), attn: 8 (over z, y), expert: 2 (over core).
Axes of the slice: x: 2, y: 2, z: 4, core: 2. Of those that a mesh axis runs over, the one named last changes fastest.
Arguments:
- queries: bfloat16 [64, 6144], P(('group', 'attn'), 'expert'), parts along dimension 0, may hold values from -5 to 5
- key_cache: bfloat16 [64, 512, 1024], P(('group', 'attn'), None, 'expert'), parts along dimension 0, may hold values from -5 to 5
- value_cache: bfloat16 [64, 512, 1024], P(('group', 'attn'), None, 'expert'), parts along dimension 0, may hold values from -6 to 6
- new_key: bfloat16 [64, 1024], P(('group', 'attn'), 'expert'), parts along dimension 0, may hold values from -6 to 6
- new_value: bfloat16 [64, 1024], P(('group', 'attn'), 'expert'), parts along dimension 0, may hold values from -6 to 6
- cache_length: int32 [64], P(('group', 'attn')), parts along dimension 0, may hold values from 2 to 512, as said below
- residual: bfloat16 [64, 6144], P('group', 'attn'), parts along dimension 0, may hold values from -3 to 3
- out_weight: bfloat16 [6144, 6144], P('expert', 'attn'), may hold values from -0.5 to 0.5
- ln_gain: float32 [6144], P('attn'), may hold values from 0.1 to 1.9
- gate_weight: bfloat16 [6144, 2688], P(None, ('attn', 'expert')), may hold values from -0.078125 to 0.078125
- up_weight: bfloat16 [6144, 2688], P(None, ('attn', 'expert')), may hold values from -0.078125 to 0.078125
- down_weight: bfloat16 [2688, 6144], P(('attn', 'expert')), may hold values from -0.15625 to 0.15625
- routes: int32 [64, 4], P('group'), parts along dimension 0, may hold values from 0 to 15, as said below
- route_weight: float32 [64, 4], P('group'), parts along dimension 0, may hold values from 0.05 to 0.6
Outputs:
- attn_stream: bfloat16 [64, 6144], P('group', 'attn'), parts along dimension 0
- expert_out: bfloat16 [64, 6144], P('group', 'attn'), parts along dimension 0
There are 2 independent parts, one for each index of `group`. A program takes and returns all parts, laid end to end along the dimension named above; an argument that names none is the same for every part. Nothing has to cross between parts.
Inputs may be any that keep to these rules, and one draw needn't show every extreme that they name: `routes`: each row names 4 different experts; of the held experts none is named by more than 16 rows, and one of them by exactly 16. `cache_length`: some request has all 512 positions filled.
All inputs are finite; a program needn't handle non-finite values.
Results may differ from a plain program's by a relative error of at most 0.015.
Values may be sent and summed in bfloat16 or wider, within the bound.
No kernel may reach another device: no remote copies, remote signals or barrier semaphores. Data moves between devices by JAX's collectives and lax.ppermute only.
A program may use at most 128 MiB of HBM per device.

v0:
```python
import math

import jax
import jax.numpy as jnp
from jax import lax
from jax.sharding import PartitionSpec as P

D = 6144
HEADS = 48
KV_HEADS = 8
HEAD_DIM = 128
EXPERTS = 16
TOP = 4
HELD = 2


NEG_FILL = -1e30
EPSILON = 1e-05


def slot_table(routes, capacity, row_count):
    flat = routes.reshape(-1)
    onehot = (flat[:, None] == jnp.arange(EXPERTS, dtype=jnp.int32)[None, :]).astype(jnp.int32)
    before = jnp.cumsum(onehot, axis=0) - onehot
    slots = jnp.sum(before * onehot, axis=1)
    owners = jnp.arange(flat.shape[0], dtype=jnp.int32) // TOP
    table = (
        jnp.full((HELD, capacity), row_count, jnp.int32).at[flat, slots].set(owners, mode="drop")
    )
    return (slots.reshape(routes.shape), table)


def attend_local(queries, key_cache, value_cache, new_key, new_value, cache_length):
    row_count = queries.shape[0]
    kv_local = new_key.shape[1] // HEAD_DIM
    group = HEADS // KV_HEADS
    length_max = key_cache.shape[1]
    query_heads = queries.reshape(row_count, kv_local, group, HEAD_DIM)
    key_heads = key_cache.reshape(row_count, length_max, kv_local, HEAD_DIM)
    value_heads = value_cache.reshape(row_count, length_max, kv_local, HEAD_DIM)
    own_keys = new_key.reshape(row_count, kv_local, HEAD_DIM)
    own_values = new_value.reshape(row_count, kv_local, HEAD_DIM)
    scale = 1.0 / math.sqrt(HEAD_DIM)
    past = (
        jnp.einsum("rkgd,rlkd->rkgl", query_heads, key_heads, preferred_element_type=jnp.float32)
        * scale
    )
    valid = jnp.arange(length_max, dtype=jnp.int32)[None, :] < cache_length[:, None]
    past = jnp.where(valid[:, None, None, :], past, NEG_FILL)
    own = (
        jnp.einsum("rkgd,rkd->rkg", query_heads, own_keys, preferred_element_type=jnp.float32)
        * scale
    )
    largest = jnp.maximum(jnp.max(past, axis=3), own)
    past_weight = jnp.exp(past - largest[..., None])
    own_weight = jnp.exp(own - largest)
    total = jnp.sum(past_weight, axis=3) + own_weight
    past_prob = (past_weight / total[..., None]).astype(jnp.bfloat16)
    own_prob = (own_weight / total).astype(jnp.bfloat16)
    result = jnp.einsum(
        "rkgl,rlkd->rkgd", past_prob, value_heads, preferred_element_type=jnp.float32
    )
    result = (
        result
        + own_prob.astype(jnp.float32)[..., None] * own_values.astype(jnp.float32)[:, :, None, :]
    )
    return result.reshape(row_count, kv_local * group * HEAD_DIM).astype(jnp.bfloat16)


def shards(
    queries,
    key_cache,
    value_cache,
    new_key,
    new_value,
    cache_length,
    residual,
    out_weight,
    ln_gain,
    gate_weight,
    up_weight,
    down_weight,
    routes,
    route_weight,
):
    attended = attend_local(queries, key_cache, value_cache, new_key, new_value, cache_length)
    partial_proj = jnp.dot(
        lax.all_gather(attended, "attn", axis=0, tiled=True),
        out_weight,
        preferred_element_type=jnp.float32,
    )
    head_total = lax.psum(partial_proj, "expert")
    attn_stream = (residual.astype(jnp.float32) + head_total).astype(jnp.bfloat16)
    stream_wide = attn_stream.astype(jnp.float32)
    feature_sum, square_sum = lax.psum(
        (jnp.sum(stream_wide, axis=1), jnp.sum(stream_wide * stream_wide, axis=1)), "attn"
    )
    row_mean = feature_sum[:, None] / D
    row_var = square_sum[:, None] / D - row_mean * row_mean
    normed = ((stream_wide - row_mean) * lax.rsqrt(row_var + EPSILON) * ln_gain[None, :]).astype(
        jnp.bfloat16
    )
    row_count = routes.shape[0]
    capacity = row_count * TOP // EXPERTS * 2
    slots, table = slot_table(routes, capacity, row_count)
    attn_count = lax.axis_size("attn")
    core_count = lax.axis_size("expert")
    core_index = lax.axis_index("expert")
    sharers = attn_count * core_count // HELD
    my_expert = (lax.axis_index("attn") * core_count + core_index) // sharers
    feature_cols = normed.shape[1]
    whole_rows = lax.all_gather(normed, "attn", axis=1, tiled=True)
    rows_in = jnp.take(whole_rows, table[my_expert], axis=0, mode="fill", fill_value=0)
    gate_val = jnp.dot(rows_in, gate_weight, preferred_element_type=jnp.float32)
    up_val = jnp.dot(rows_in, up_weight, preferred_element_type=jnp.float32)
    hidden = (jax.nn.silu(gate_val) * up_val).astype(jnp.bfloat16)
    piece_out = jnp.dot(hidden, down_weight, preferred_element_type=jnp.float32).astype(
        jnp.bfloat16
    )
    returned = lax.all_to_all(piece_out, "attn", split_axis=1, concat_axis=0, tiled=True)
    held = routes < HELD
    combined = jnp.zeros((row_count, feature_cols), jnp.float32)
    for block_index in range(sharers):
        holder = routes * sharers + block_index
        keeper = jnp.logical_and(held, holder % core_count == core_index)
        source_rows = jnp.where(keeper, holder // core_count * capacity + slots, 0)
        picked = jnp.take(returned, source_rows.reshape(-1), axis=0).reshape(
            row_count, TOP, feature_cols
        )
        weights = jnp.where(keeper, route_weight, 0.0)
        combined = combined + jnp.sum(weights[:, :, None] * picked.astype(jnp.float32), axis=1)
    expert_out = lax.psum(combined, "expert").astype(jnp.bfloat16)
    return (attn_stream, expert_out)


def solution(mesh):
    return jax.shard_map(
        shards,
        mesh=mesh,
        in_specs=(
            P(("group", "attn"), "expert"),
            P(("group", "attn"), None, "expert"),
            P(("group", "attn"), None, "expert"),
            P(("group", "attn"), "expert"),
            P(("group", "attn"), "expert"),
            P(("group", "attn")),
            P("group", "attn"),
            P("expert", "attn"),
            P("attn"),
            P(None, ("attn", "expert")),
            P(None, ("attn", "expert")),
            P(("attn", "expert"), None),
            P("group", None),
            P("group", None),
        ),
        out_specs=(P("group", "attn"), P("group", "attn")),
        check_vma=False,
    )
```

profile of v0, /device:TPU:0, one launch (start us, length us, event | category | flops | bytes accessed | tf_op | source)
XLA Modules:
  0.0 188.7 jit_solution(780871194803359822)
XLA Ops:
  7.2 0.9 reshape.201
  8.1 0.7 iota_compare_fusion.1
  8.9 0.7 reshape.332
  9.7 0.7 fusion.99
  10.7 2.0 %fusion.15 = bf16[4,4,6,128]{3,2,1,0:T(8,128)(2,1)S(1)} fusion(f32[4,4,6,512]{3,2,1,0:T(8,128)S(1)} %get-tuple-element.29, f32[4,4,6]{2,1,0:T(4,128)S(1)} %get-tuple-element.25, f32[4,4,6]{2,1,0:T(4,128)S(1)} %multiply_maximum_fusion, f32[4,4,128]{2,1,0:T(4,128)S(1)} %reshape.215, f32[4,4,6]{2,1,0:T(4,128)S(1)} %get-tuple-element.24, ...), kind=kOutput, calls=%fused_computation.20 | convolution fusion | flops 12767232 | bytes 2327680 | tf_op jit(solution)/shard_map/rkgl,rlkd->rkgd/dot_general | solution.py:60
  12.8 32.4 %all-gather = bf16[8,4,3072]{2,1,0:T(4,128)(2,1)S(1)} all-gather(bf16[1,4,3072]{2,1,0:T(4,128)(2,1)S(1)} %reshape.310), channel_id=1, replica_groups=mesh['group'=2,'attn'=8,'expert'=2] {'attn'}, dimensions={0}, use_global_device_ids=true | all-gather | bytes 221184 | tf_op jit(solution)/shard_map/all_gather | solution.py:88
  45.3 3.9 %fusion.101 = f32[32,768]{1,0:T(8,128)} fusion(bf16[32,3072]{1,0:T(8,128)(2,1)S(1)} %reshape.311, bf16[3072,768]{1,0:T(8,128)(2,1)} %param.23), kind=kOutput, calls=%fused_computation.240 | convolution fusion | flops 150994944 | bytes 5013504 | tf_op jit(solution)/shard_map/dot_general | solution.py:87
  53.6 0.6 compare_and_fusion.1
  54.4 0.6 compare_and_fusion
  55.0 6.4 %scatter_fusion = s32[2,16]{1,0:T(2,128)S(1)} fusion(s32[2,16]{1,0:T(2,128)S(1)} %broadcast_in_dim.78, s32[128]{0:T(128)S(1)} %fusion.94, s32[128]{0:T(128)S(1)} %and_select_fusion), kind=kCustom, calls=%fused_computation.9 | custom fusion | bytes 2560 | tf_op jit(solution)/shard_map/scatter | solution.py:28
  62.0 0.6 pad_clamp_fusion.6
  62.6 0.6 pad_clamp_fusion.3
  63.8 4.3 %all-reduce.3.cloned.1.call-done = f32[32,768]{1,0:T(8,128)} async-done(((f32[32,768]{1,0:T(8,128)}), f32[32,768]{1,0:T(8,128)}) %all-reduce.3.cloned.1.call-update) | async-done | bytes 98320 | tf_op jit(solution)/shard_map/psum | solution.py:92
  68.1 1.0 convert_reduce_fusion
  69.1 21.7 %all-reduce = (f32[32]{0:T(128)S(1)}, f32[32]{0:T(128)S(1)}) all-reduce(f32[32]{0:T(128)S(1)} %get-tuple-element.4, f32[32]{0:T(128)S(1)} %get-tuple-element.3), channel_id=1, replica_groups=mesh['group'=2,'attn'=8,'expert'=2] {'attn'}, use_global_device_ids=true, to_apply=%region_9.10 | all-reduce | flops 64 | bytes 512 | tf_op jit(solution)/shard_map/psum | solution.py:95
  91.0 31.2 %all_gather.7 = bf16[32,6144]{1,0:T(8,128)(2,1)S(1)} all-gather(bf16[32,768]{1,0:T(8,128)(2,1)S(1)} %fusion.24), channel_id=1, replica_groups=mesh['group'=2,'attn'=8,'expert'=2] {'attn'}, dimensions={1}, use_global_device_ids=true | all-gather | bytes 442368 | tf_op jit(solution)/shard_map/all_gather | solution.py:112
  122.2 0.7 gather_fusion
  122.8 2.2 %fusion.26 = f32[16,168]{1,0:T(8,128)S(1)} fusion(bf16[6144,168]{0,1:T(8,128)(2,1)} %param.25, bf16[16,6144]{1,0:T(8,128)(2,1)S(1)} %gather_fusion, pred[16]{0:T(512)(128)(4,1)S(1)} %compare_and_fusion.8), kind=kOutput, calls=%fused_computation.55 | convolution fusion | flops 33128448 | bytes 2271760 | tf_op jit(solution)/shard_map/dot_general | solution.py:114
  125.1 3.8 %convolution_convert_fusion = bf16[16,6144]{1,0:T(8,128)(2,1)S(1)} fusion(bf16[168,6144]{1,0:T(8,128)(2,1)} %param.27, bf16[6144,168]{0,1:T(8,128)(2,1)} %param.26, bf16[16,6144]{1,0:T(8,128)(2,1)S(1)} %gather_fusion, pred[16]{0:T(512)(128)(4,1)S(1)} %compare_and_fusion.8, f32[16,168]{1,0:T(8,128)S(1)} %fusion.26), kind=kOutput, calls=%fused_computation.10 | convolution fusion | flops 66273024 | bytes 4532752 | tf_op jit(solution)/shard_map/dot_general | solution.py:117
  128.9 0.7 copy.85
  129.6 3.6 %all-to-all-start = ((bf16[16,8,768]{2,0,1:T(8,128)(2,1)}), bf16[16,8,768]{2,0,1:T(8,128)(2,1)S(1)}, u32[]{:S(2)}, u32[]{:S(2)}) async-start(bf16[16,8,768]{2,0,1:T(8,128)(2,1)} %bitcast.52), calls=%async_computation | async-start | bytes 393216 | tf_op jit(solution)/shard_map/all_to_all | solution.py:120
  133.8 0.6 pad_clamp_fusion
  134.4 0.7 broadcast_select_fusion.10
  135.1 5.6 %all-to-all-done = bf16[16,8,768]{2,0,1:T(8,128)(2,1)S(1)} async-done(((bf16[16,8,768]{2,0,1:T(8,128)(2,1)}), bf16[16,8,768]{2,0,1:T(8,128)(2,1)S(1)}, u32[]{:S(2)}, u32[]{:S(2)}) %all-to-all-start) | async-done | bytes 196640 | tf_op jit(solution)/shard_map/all_to_all | solution.py:120
  140.7 0.9 gather_fusion.3
  141.8 0.9 gather_fusion.4
  142.7 0.7 select_convert_fusion.4
  143.4 1.0 gather_fusion.1
  144.4 1.4 select_convert_fusion.7
  145.9 1.1 reshape.216
  147.0 1.7 gather_fusion.2
  148.7 1.8 select_convert_fusion.6
  150.4 1.8 reshape.217
  152.3 1.7 gather_fusion.5
  153.9 1.8 select_convert_fusion.3
  155.7 1.9 reshape.220
  157.6 1.7 gather_fusion.6
  159.2 1.8 select_convert_fusion.2
  161.0 1.8 reshape.221
  162.9 1.7 gather_fusion.7
  164.5 1.8 select_convert_fusion.1
  166.3 1.9 reshape.222
  168.2 1.7 gather_fusion.8
  169.8 1.8 select_convert_fusion
  171.6 1.8 reshape.223
  173.5 1.4 multiply_reduce_fusion.4
  174.9 1.5 multiply_reduce_fusion.6
  177.6 4.2 %psum.31 = bf16[32,768]{1,0:T(8,128)(2,1)} all-reduce(f32[32,768]{1,0:T(8,128)S(1)} %add_add_fusion), channel_id=1, replica_groups=mesh['group'=2,'attn'=8,'expert'=2] {'expert'}, use_global_device_ids=true, to_apply=%region_18.20 | all-reduce | flops 24576 | bytes 147456 | tf_op jit(solution)/shard_map/psum | solution.py:132
  (83 shorter events, 8.4 us)
Async XLA Ops:
  7.2 2.5 %copy-start = (bf16[4,512,512]{2,1,0:T(8,128)(2,1)S(1)}, bf16[4,512,512]{2,1,0:T(8,128)(2,1)}, u32[]{:S(2)}) copy-start(bf16[4,512,512]{2,1,0:T(8,128)(2,1)} %param.17) | copy-start | bytes 6291460
  7.2 3.5 %copy-start.8 = (bf16[4,512]{1,0:T(4,128)(2,1)S(1)}, bf16[4,512]{1,0:T(4,128)(2,1)}, u32[]{:S(2)}) copy-start(bf16[4,512]{1,0:T(4,128)(2,1)} %param.20) | copy-start | bytes 12292
  7.2 60.9 %all-reduce.3.cloned.1.call-start = ((), (), s32[]{:S(2)}) async-start(), calls=%async_computation.1 | async-start | bytes 196608 | tf_op jit(solution)/shard_map/psum | solution.py:92
  45.3 3.9 %copy-start.10 = (s32[32,4]{0,1:T(4,128)S(1)}, s32[32,4]{0,1:T(4,128)}, u32[]{:S(2)}) copy-start(s32[32,4]{0,1:T(4,128)} %param.28) | copy-start | bytes 1540
  45.3 22.8 %copy-start.7 = (bf16[32,768]{1,0:T(8,128)(2,1)S(1)}, bf16[32,768]{1,0:T(8,128)(2,1)}, u32[]{:S(2)}) copy-start(bf16[32,768]{1,0:T(8,128)(2,1)} %param.22) | copy-start | bytes 147460
  49.1 41.7 %copy-start.9 = (f32[768]{0:T(1024)S(1)}, f32[768]{0:T(1024)}, u32[]{:S(2)}) copy-start(f32[768]{0:T(1024)} %param.24) | copy-start | bytes 9220
  69.1 55.9 %copy-start.5 = (bf16[32,768]{1,0:T(8,128)(2,1)}, bf16[32,768]{1,0:T(8,128)(2,1)S(1)}, u32[]{:S(2)}) copy-start(bf16[32,768]{1,0:T(8,128)(2,1)S(1)} %get-tuple-element.7) | copy-start | bytes 147460
  125.1 8.7 %copy-start.11 = (f32[32,4]{0,1:T(4,128)S(1)}, f32[32,4]{0,1:T(4,128)}, u32[]{:S(2)}) copy-start(f32[32,4]{0,1:T(4,128)} %param.29) | copy-start | bytes 1540
  129.6 11.1 %all-to-all-start = ((bf16[16,8,768]{2,0,1:T(8,128)(2,1)}), bf16[16,8,768]{2,0,1:T(8,128)(2,1)S(1)}, u32[]{:S(2)}, u32[]{:S(2)}) async-start(bf16[16,8,768]{2,0,1:T(8,128)(2,1)} %bitcast.52), calls=%async_computation | async-start | bytes 393216 | tf_op jit(solution)/shard_map/all_to_all | solution.py:120
  169.8 5.1 %copy-start.6 = (f32[32,4]{1,0:T(8,128)S(1)}, f32[32,4]{1,0:T(8,128)}, u32[]{:S(2)}) copy-start(f32[32,4]{1,0:T(8,128)} %get-tuple-element.15) | copy-start | bytes 1540
  173.5 3.0 %copy-start.1 = (f32[32,4,768]{2,1,0:T(4,128)S(1)}, f32[32,4,768]{2,1,0:T(4,128)}, u32[]{:S(2)}) copy-start(f32[32,4,768]{2,1,0:T(4,128)} %reshape.220) | copy-start | bytes 1179652
  173.5 3.0 %copy-start.2 = (f32[32,4,768]{2,1,0:T(4,128)S(1)}, f32[32,4,768]{2,1,0:T(4,128)}, u32[]{:S(2)}) copy-start(f32[32,4,768]{2,1,0:T(4,128)} %reshape.221) | copy-start | bytes 1179652
  173.5 3.5 %copy-start.3 = (f32[32,4,768]{2,1,0:T(4,128)S(1)}, f32[32,4,768]{2,1,0:T(4,128)}, u32[]{:S(2)}) copy-start(f32[32,4,768]{2,1,0:T(4,128)} %reshape.222) | copy-start | bytes 1179652
  173.5 3.5 %copy-start.4 = (f32[32,4,768]{2,1,0:T(4,128)S(1)}, f32[32,4,768]{2,1,0:T(4,128)}, u32[]{:S(2)}) copy-start(f32[32,4,768]{2,1,0:T(4,128)} %reshape.223) | copy-start | bytes 1179652
Sparse Core Ops, SparseCore 0:
  49.3 18.7 all-reduce.2
where the time goes:
time: 190 us; the launch traced here: 189 us
  blocking collectives  89.6 us (47%)
  local copies, waits for them, and re-layouts  32.4 us (17%)
  other arithmetic  25.9 us (14%)
  between operations  14.5 us (8%)
  matrix products  12.8 us (7%)
  waiting for transfers between devices  9.9 us (5%)
  starting transfers between devices  3.61 us (2%)
    all_gather x1, blocking collectives, shards(): lax.all_gather(attended, 'attn', axis=0, tiled=True)  32.4 us
    all_gather x1, blocking collectives, shards(): whole_rows = lax.all_gather(normed, 'attn', axis=1, tiled=True)  31.2 us
    psum x1, blocking collectives, shards(): lax.psum((jnp.sum(stream_wide, axis=1), jnp.sum(stream_wide * stream_wide...  21.7 us
    convert_element_type x8, other arithmetic, shards(): picked.astype(jnp.float32)  11.1 us
    gather x8, local copies, waits for them, and re-layouts, shards(): jnp.take(returned, source_rows.reshape(-1), axis=0)  11 us
    convert_element_type x8, local copies, waits for them, and re-layouts, shards(): picked.astype(jnp.float32)  10.6 us
    scatter x1, local copies, waits for them, and re-layouts, slot_table(): jnp.full((HELD, capacity), row_count, jnp.int32).at[flat, slots]  6.4 us
    all_to_all x1, waiting for transfers between devices, shards(): lax.all_to_all(piece_out, 'attn', split_axis=1, concat_axis=0, tiled=True)  5.58 us
  transfers between devices with their start and end apart: 2, of which 2 were waited for; matrix products, arithmetic and copies ran while one was open for 9% of the time, Pallas kernels for 0%

commit v1 on v0

v1 whole, which is shorter than its diff:
```python
import math

import jax
import jax.numpy as jnp
from jax import lax
from jax.sharding import PartitionSpec as P

D = 6144
HEADS = 48
KV_HEADS = 8
HEAD_DIM = 128
EXPERTS = 16
TOP = 4
HELD = 2


NEG_FILL = -1e30
EPSILON = 1e-05


def attend_local(queries, key_cache, value_cache, new_key, new_value, cache_length):
    row_count = queries.shape[0]
    kv_local = new_key.shape[1] // HEAD_DIM
    group = HEADS // KV_HEADS
    length_max = key_cache.shape[1]
    query_heads = queries.reshape(row_count, kv_local, group, HEAD_DIM)
    key_heads = key_cache.reshape(row_count, length_max, kv_local, HEAD_DIM)
    value_heads = value_cache.reshape(row_count, length_max, kv_local, HEAD_DIM)
    own_keys = new_key.reshape(row_count, kv_local, HEAD_DIM)
    own_values = new_value.reshape(row_count, kv_local, HEAD_DIM)
    scale = 1.0 / math.sqrt(HEAD_DIM)
    past = (
        jnp.einsum("rkgd,rlkd->rkgl", query_heads, key_heads, preferred_element_type=jnp.float32)
        * scale
    )
    valid = jnp.arange(length_max, dtype=jnp.int32)[None, :] < cache_length[:, None]
    past = jnp.where(valid[:, None, None, :], past, NEG_FILL)
    own = (
        jnp.einsum("rkgd,rkd->rkg", query_heads, own_keys, preferred_element_type=jnp.float32)
        * scale
    )
    largest = jnp.maximum(jnp.max(past, axis=3), own)
    past_weight = jnp.exp(past - largest[..., None])
    own_weight = jnp.exp(own - largest)
    total = jnp.sum(past_weight, axis=3) + own_weight
    past_prob = (past_weight / total[..., None]).astype(jnp.bfloat16)
    own_prob = (own_weight / total).astype(jnp.bfloat16)
    result = jnp.einsum(
        "rkgl,rlkd->rkgd", past_prob, value_heads, preferred_element_type=jnp.float32
    )
    result = (
        result
        + own_prob.astype(jnp.float32)[..., None] * own_values.astype(jnp.float32)[:, :, None, :]
    )
    return result.reshape(row_count, kv_local * group * HEAD_DIM).astype(jnp.bfloat16)


def selection(routes, route_weight, capacity):
    row_count = routes.shape[0]
    experts = jnp.arange(HELD, dtype=jnp.int32)
    match = routes[None, :, :] == experts[:, None, None]
    hit = jnp.any(match, axis=2)
    row_weight = jnp.sum(jnp.where(match, route_weight[None], 0.0), axis=2)
    earlier = jnp.arange(row_count)[:, None] < jnp.arange(row_count)[None, :]
    slot = jnp.sum(jnp.where(earlier[None] & hit[:, :, None], 1, 0), axis=1)
    taken = hit[:, None, :] & (slot[:, None, :] == jnp.arange(capacity, dtype=jnp.int32)[None, :, None])
    slot_weight = jnp.sum(jnp.where(taken, row_weight[:, None, :], 0.0), axis=2)
    return taken, slot_weight


def gather_attn(block):
    count = lax.axis_size("attn")
    copies = jnp.broadcast_to(block[None], (count,) + block.shape)
    return lax.all_to_all(copies, "attn", split_axis=0, concat_axis=0, tiled=True)


def pair_sum(block):
    return block + lax.ppermute(block, "expert", [(0, 1), (1, 0)])


def shards(
    queries,
    key_cache,
    value_cache,
    new_key,
    new_value,
    cache_length,
    residual,
    out_weight,
    ln_gain,
    gate_weight,
    up_weight,
    down_weight,
    routes,
    route_weight,
):
    attn_count = lax.axis_size("attn")
    core_count = lax.axis_size("expert")
    sharers = attn_count * core_count // HELD
    my_expert = (lax.axis_index("attn") * core_count + lax.axis_index("expert")) // sharers
    dest_expert = [index * core_count // sharers for index in range(attn_count)]
    row_count = routes.shape[0]
    capacity = row_count * TOP // EXPERTS * 2
    cols = residual.shape[1]

    taken, slot_weight = selection(routes, route_weight, capacity)
    pick = taken.astype(jnp.bfloat16)

    gains = gather_attn(ln_gain)

    attended = attend_local(queries, key_cache, value_cache, new_key, new_value, cache_length)
    whole = gather_attn(attended).reshape(row_count, -1)
    partial_proj = jnp.dot(whole, out_weight, preferred_element_type=jnp.float32)
    head_total = pair_sum(partial_proj)
    attn_stream = (residual.astype(jnp.float32) + head_total).astype(jnp.bfloat16)

    chosen = jnp.einsum(
        "esr,rd->esd", pick, attn_stream, preferred_element_type=jnp.float32
    ).astype(jnp.bfloat16)
    outgoing = jnp.stack([chosen[index] for index in dest_expert])
    rows = lax.all_to_all(outgoing, "attn", split_axis=0, concat_axis=0, tiled=True)
    wide = rows.astype(jnp.float32)
    row_mean = jnp.sum(wide, axis=(0, 2)) / D
    row_var = jnp.sum(wide * wide, axis=(0, 2)) / D - row_mean * row_mean
    normed = (
        (wide - row_mean[None, :, None])
        * lax.rsqrt(row_var + EPSILON)[None, :, None]
        * gains.reshape(attn_count, 1, cols)
    ).astype(jnp.bfloat16)
    gate_val = jnp.einsum(
        "asd,adf->sf", normed, gate_weight.reshape(attn_count, cols, -1),
        preferred_element_type=jnp.float32,
    )
    up_val = jnp.einsum(
        "asd,adf->sf", normed, up_weight.reshape(attn_count, cols, -1),
        preferred_element_type=jnp.float32,
    )
    hidden = (jax.nn.silu(gate_val) * up_val).astype(jnp.bfloat16)
    piece = jnp.dot(hidden, down_weight, preferred_element_type=jnp.float32)
    mine = jnp.take(slot_weight, my_expert, axis=0)
    piece = (piece * mine[:, None]).astype(jnp.bfloat16)
    returned = lax.all_to_all(
        piece.reshape(capacity, attn_count, cols).swapaxes(0, 1),
        "attn", split_axis=0, concat_axis=0, tiled=True,
    )
    spread = jnp.stack([pick[index] for index in dest_expert])
    combined = jnp.einsum(
        "asr,asd->rd", spread, returned, preferred_element_type=jnp.float32
    )
    expert_out = pair_sum(combined).astype(jnp.bfloat16)
    return (attn_stream, expert_out)


def solution(mesh):
    return jax.shard_map(
        shards,
        mesh=mesh,
        in_specs=(
            P(("group", "attn"), "expert"),
            P(("group", "attn"), None, "expert"),
            P(("group", "attn"), None, "expert"),
            P(("group", "attn"), "expert"),
            P(("group", "attn"), "expert"),
            P(("group", "attn")),
            P("group", "attn"),
            P("expert", "attn"),
            P("attn"),
            P(None, ("attn", "expert")),
            P(None, ("attn", "expert")),
            P(("attn", "expert"), None),
            P("group", None),
            P("group", None),
        ),
        out_specs=(P("group", "attn"), P("group", "attn")),
        check_vma=False,
    )
```

time: 190 us -> 70.2 us (0.37)
  blocking collectives: 89.6 us -> 0 us
  local copies, waits for them, and re-layouts: 32.4 us -> 8.11 us
  other arithmetic: 25.9 us -> 2.07 us
  starting transfers between devices: 3.61 us -> 20 us
  waiting for transfers between devices: 9.9 us -> 26.2 us
  between operations: 14.5 us -> 0.82 us
    all_gather x2 -> x0, blocking collectives: 63.6 us -> none  [the longest x1 32.4 us: shards(): lax.all_gather(attended, 'attn', axis=0, tiled=True)]
    psum x2 -> x0, blocking collectives: 25.9 us -> none  [the longest x1 21.7 us: shards(): lax.psum((jnp.sum(stream_wide, axis=1), jnp.sum(stream_wide * stream_wide...]
    all_to_all x1 -> x4, waiting for transfers between devices: 5.58 us -> 23.6 us  [the longest x1 8.15 us: shards(): lax.all_to_all(outgoing, 'attn', split_axis=0, concat_axis=0, tiled=True)]
    all_to_all x1 -> x4, starting transfers between devices: 3.57 us -> 19.9 us  [the longest x2 10.6 us: gather_attn(): lax.all_to_all(copies, 'attn', split_axis=0, concat_axis=0, tiled=True)]
    gather x9 -> x0, local copies, waits for them, and re-layouts: 11.7 us -> none  [the longest x8 11 us: shards(): jnp.take(returned, source_rows.reshape(-1), axis=0)]
    convert_element_type x10 -> x3, other arithmetic: 11.3 us -> 0.66 us  [the longest x1 0.63 us: shards(): expert_out = pair_sum(combined).astype(jnp.bfloat16)]
    convert_element_type x8 -> x1, local copies, waits for them, and re-layouts: 10.6 us -> 0.04 us  [attend_local(): result.reshape(row_count, kv_local * group * HEAD_DIM).astype(jnp.bfloat16)]
    scatter x1 -> x0, local copies, waits for them, and re-layouts: 6.4 us -> none  [slot_table(): jnp.full((HELD, capacity), row_count, jnp.int32).at[flat, slots]]
  transfers between devices with their start and end apart: 2 -> 6, of which waited for: 2 -> 5; matrix products, arithmetic and copies ran while one was open for 9% -> 11% of each run, Pallas kernels for 0% -> 0%
where the time goes in v1:
time: 70.2 us; the launch traced here: 69.6 us
  waiting for transfers between devices  26.2 us (37%)
  starting transfers between devices  20 us (28%)
  matrix products  12.5 us (18%)
  local copies, waits for them, and re-layouts  8.11 us (12%)
  other arithmetic  2.07 us (3%)
  between operations  0.82 us (1%)
    all_to_all x2, starting transfers between devices, gather_attn(): lax.all_to_all(copies, 'attn', split_axis=0, concat_axis=0, tiled=True)  10.6 us
    all_to_all x1, waiting for transfers between devices, shards(): lax.all_to_all(outgoing, 'attn', split_axis=0, concat_axis=0, tiled=True)  8.15 us
    all_to_all x2, waiting for transfers between devices, gather_attn(): lax.all_to_all(copies, 'attn', split_axis=0, concat_axis=0, tiled=True)  7.75 us
    all_to_all x1, waiting for transfers between devices, shards(): lax.all_to_all(piece.reshape(capacity, attn_count, cols).swapaxes(0, 1),...  7.7 us
    all_to_all x1, starting transfers between devices, shards(): lax.all_to_all(outgoing, 'attn', split_axis=0, concat_axis=0, tiled=True)  5.93 us
    dot_general x1, matrix products, shards(): piece = jnp.dot(hidden, down_weight, preferred_element_type=jnp.float32)  3.79 us
    unnamed x26, local copies, waits for them, and re-layouts  3.74 us
    all_to_all x1, starting transfers between devices, shards(): lax.all_to_all(piece.reshape(capacity, attn_count, cols).swapaxes(0, 1),...  3.39 us
  transfers between devices with their start and end apart: 6, of which 5 were waited for; matrix products, arithmetic and copies ran while one was open for 11% of the time, Pallas kernels for 0%

profile of v1, /device:TPU:0, one launch (start us, length us, event | category | flops | bytes accessed | tf_op | source)
XLA Modules:
  0.0 69.6 jit_solution(8530634909979213290)
XLA Ops:
  0.6 0.0 copy-start
  0.6 0.0 copy-start.4
  0.7 0.9 %reshape.106 = bf16[4,4,6,128]{3,2,1,0:T(8,128)(2,1)S(1)} reshape(bf16[4,3072]{1,0:T(4,128)(2,1)} %param.14) | data formatting | bytes 49152 | tf_op jit(solution)/shard_map/reshape | solution.py:26
  1.6 0.7 %iota_compare_fusion.2 = pred[4,512]{1,0:T(4,128)(4,1)S(1)} fusion(s32[4]{0:T(128)} %param.19), kind=kLoop, calls=%fused_computation.69 | loop fusion | flops 2048 | bytes 2064 | tf_op jit(solution)/shard_map/lt | solution.py:36
  2.3 0.7 %reshape.152 = bf16[4,4,128,1]{2,3,1,0:T(2,128)(2,1)S(1)} reshape(bf16[4,512]{1,0:T(4,128)(2,1)} %param.17) | data formatting | bytes 8192 | tf_op jit(solution)/shard_map/reshape | solution.py:29
  3.0 0.1 fusion.67
  3.1 0.0 copy-done
  3.1 0.7 %fusion.66 = (f32[4,4,6]{2,1,0:T(4,128)S(1)}, f32[4,4,6,512]{3,2,1,0:T(8,128)S(1)}) fusion(bf16[4,4,6,128]{3,2,1,0:T(8,128)(2,1)S(1)} %reshape.106, pred[4,512]{1,0:T(4,128)(4,1)S(1)} %iota_compare_fusion.2, bf16[4,512,512]{2,1,0:T(8,128)(2,1)S(1)} %copy-done), kind=kOutput, calls=%fused_computation.83 | convolution fusion | flops 12730272 | bytes 2320768 | tf_op jit(solution)/shard_map/rkgd,rlkd->rkgl/dot_general | solution.py:33
  3.9 0.0 copy-start.3
  3.9 0.2 fusion.43
  4.1 0.0 copy-start.5
  4.1 0.0 copy-done.4
  4.2 2.0 %fusion.22 = bf16[4,4,6,128]{3,2,1,0:T(8,128)(2,1)S(1)} fusion(f32[4,4,6,512]{3,2,1,0:T(8,128)S(1)} %get-tuple-element.20, f32[4,4,6]{2,1,0:T(4,128)S(1)} %get-tuple-element.16, f32[4,4,6]{2,1,0:T(4,128)S(1)} %multiply_maximum_fusion, f32[4,4,128]{2,1,0:T(4,128)S(1)} %reshape.134, f32[4,4,6]{2,1,0:T(4,128)S(1)} %get-tuple-element.15, ...), kind=kOutput, calls=%fused_computation.19 | convolution fusion | flops 12767232 | bytes 2327680 | tf_op jit(solution)/shard_map/rkgl,rlkd->rkgd/dot_general | solution.py:48
  6.2 0.7 %broadcast_in_dim.56 = bf16[8,4,3072]{2,1,0:T(4,128)(2,1)} broadcast(bf16[4,3072]{1,0:T(4,128)(2,1)S(1)} %convert_element_type.63), dimensions={1,2} | broadcast | bytes 221184 | tf_op jit(solution)/shard_map/broadcast_in_dim | solution.py:73
  7.0 7.3 %all-to-all-start = ((bf16[8,4,3072]{2,1,0:T(4,128)(2,1)}), bf16[8,4,3072]{2,1,0:T(4,128)(2,1)S(1)}, u32[]{:S(2)}, u32[]{:S(2)}) async-start(bf16[8,4,3072]{2,1,0:T(4,128)(2,1)} %broadcast_in_dim.56), calls=%async_computation | async-start | bytes 393216 | tf_op jit(solution)/shard_map/all_to_all | solution.py:74
  14.3 0.0 copy-done.3
  14.3 0.1 select_reduce_fusion
  14.4 7.7 %all-to-all-done = bf16[8,4,3072]{2,1,0:T(4,128)(2,1)S(1)} async-done(((bf16[8,4,3072]{2,1,0:T(4,128)(2,1)}), bf16[8,4,3072]{2,1,0:T(4,128)(2,1)S(1)}, u32[]{:S(2)}, u32[]{:S(2)}) %all-to-all-start) | async-done | bytes 196640 | tf_op jit(solution)/shard_map/all_to_all | solution.py:74
  22.2 0.6 broadcast_in_dim.90
  22.8 3.3 %all-to-all-start.2 = ((f32[8,1,768]{2,1,0:T(1,128)}), f32[8,1,768]{2,1,0:T(1,128)S(1)}, u32[]{:S(2)}, u32[]{:S(2)}) async-start(f32[8,1,768]{2,1,0:T(1,128)} %broadcast_in_dim.90), calls=%async_computation.2 | async-start | bytes 49152 | tf_op jit(solution)/shard_map/all_to_all | solution.py:74
  26.2 0.0 copy-start.6
  26.2 0.0 copy-start.2
  26.2 3.2 %fusion.68 = f32[32,768]{1,0:T(8,128)S(1)} fusion(bf16[32,3072]{1,0:T(8,128)(2,1)S(1)} %reshape.110, bf16[3072,768]{1,0:T(8,128)(2,1)} %param.21), kind=kOutput, calls=%fused_computation.85 | convolution fusion | flops 150994944 | bytes 5013504 | tf_op jit(solution)/shard_map/dot_general | solution.py:113
  29.5 0.0 collective-permute-start
  29.5 1.3 %collective-permute-done = f32[32,768]{1,0:T(8,128)S(1)} collective-permute-done((f32[32,768]{1,0:T(8,128)S(1)}, f32[32,768]{1,0:T(8,128)S(1)}, u32[]{:S(2)}, u32[]{:S(2)}) %collective-permute-start) | collective-permute-done | bytes 98336 | tf_op jit(solution)/shard_map/ppermute | solution.py:78
  30.8 0.0 copy-start.1
  30.8 0.1 convolution_convert_fusion
  30.9 0.6 constant_dynamic-update-slice_fusion.13
  31.5 0.6 constant_dynamic-update-slice_fusion.12
  32.2 0.6 constant_dynamic-update-slice_fusion.11
  32.8 0.6 constant_dynamic-update-slice_fusion.10
  33.4 0.6 constant_dynamic-update-slice_fusion.9
  34.0 0.6 constant_dynamic-update-slice_fusion.8
  34.6 0.6 constant_dynamic-update-slice_fusion.7
  35.2 0.0 all-to-all-done.2
  35.2 5.9 %all-to-all-start.1 = ((bf16[8,16,768]{2,1,0:T(8,128)(2,1)}), bf16[8,16,768]{2,1,0:T(8,128)(2,1)S(1)}, u32[]{:S(2)}, u32[]{:S(2)}) async-start(bf16[8,16,768]{2,1,0:T(8,128)(2,1)} %constant_dynamic-update-slice_fusion.7), calls=%async_computation.1 | async-start | bytes 393216 | tf_op jit(solution)/shard_map/all_to_all | solution.py:121
  41.1 0.1 select_reduce_fusion.1
  41.3 8.2 %all-to-all-done.1 = bf16[8,16,768]{2,1,0:T(8,128)(2,1)S(1)} async-done(((bf16[8,16,768]{2,1,0:T(8,128)(2,1)}), bf16[8,16,768]{2,1,0:T(8,128)(2,1)S(1)}, u32[]{:S(2)}, u32[]{:S(2)}) %all-to-all-start.1) | async-done | bytes 196640 | tf_op jit(solution)/shard_map/all_to_all | solution.py:121
  49.4 0.2 convert_reduce_fusion
  49.6 2.2 %fusion.25 = f32[16,168]{1,0:T(8,128)S(1)} fusion(bf16[21,8,8,768]{3,2,1,0:T(8,128)(2,1)} %bitcast.85, bf16[8,16,768]{2,1,0:T(8,128)(2,1)S(1)} %all-to-all-done.1, f32[8,768]{1,0:T(8,128)S(1)} %bitcast.81, f32[16]{0:T(128)S(1)} %get-tuple-element.18, f32[16]{0:T(128)S(1)} %get-tuple-element.17), kind=kOutput, calls=%fused_computation.20 | convolution fusion | flops 33521664 | bytes 2296448 | tf_op jit(solution)/shard_map/asd,adf->sf/dot_general | solution.py:130
  51.9 3.8 %fusion = bf16[16,6144]{1,0:T(8,128)(2,1)S(1)} fusion(bf16[168,6144]{1,0:T(8,128)(2,1)} %param.25, bf16[21,8,8,768]{3,2,1,0:T(8,128)(2,1)} %bitcast.79, f32[16]{0:T(128)S(1)} %fusion.61, f32[16,168]{1,0:T(8,128)S(1)} %fusion.25, bf16[8,16,768]{2,1,0:T(8,128)(2,1)S(1)} %all-to-all-done.1, f32[8,768]{1,0:T(8,128)S(1)} %bitcast.82, ...), kind=kOutput, calls=%fused_computation.1 | convolution fusion | flops 66764544 | bytes 4557504 | tf_op jit(solution)/shard_map/dot_general | solution.py:139
  55.7 0.7 %copy.86 = bf16[2,8,8,768]{3,2,0,1:T(8,128)(2,1)} copy(bf16[2,8,8,768]{3,2,1,0:T(8,128)(2,1)S(1)} %bitcast.80) | data formatting | bytes 393216 | tf_op jit(solution)/shard_map/reshape | solution.py:143
  56.3 3.4 %all-to-all-start.3 = ((bf16[8,16,768]{2,1,0:T(8,128)(2,1)}), bf16[8,16,768]{2,1,0:T(8,128)(2,1)S(1)}, u32[]{:S(2)}, u32[]{:S(2)}) async-start(bf16[8,16,768]{2,1,0:T(8,128)(2,1)} %bitcast.77), calls=%async_computation.3 | async-start | bytes 393216 | tf_op jit(solution)/shard_map/all_to_all | solution.py:142
  59.8 7.7 %all-to-all-done.3 = bf16[8,16,768]{2,1,0:T(8,128)(2,1)S(1)} async-done(((bf16[8,16,768]{2,1,0:T(8,128)(2,1)}), bf16[8,16,768]{2,1,0:T(8,128)(2,1)S(1)}, u32[]{:S(2)}, u32[]{:S(2)}) %all-to-all-start.3) | async-done | bytes 196640 | tf_op jit(solution)/shard_map/all_to_all | solution.py:142
  67.5 0.2 convolution_bitcast_fusion
  67.7 0.0 collective-permute-start.1
  67.7 1.3 %collective-permute-done.1 = f32[32,768]{1,0:T(8,128)S(1)} collective-permute-done((f32[32,768]{1,0:T(8,128)S(1)}, f32[32,768]{1,0:T(8,128)S(1)}, u32[]{:S(2)}, u32[]{:S(2)}) %collective-permute-start.1) | collective-permute-done | bytes 98336 | tf_op jit(solution)/shard_map/ppermute | solution.py:78
  69.0 0.6 add_convert_fusion
  (24 shorter events, 0.3 us)
Async XLA Ops:
  0.6 2.5 %copy-start = (bf16[4,512,512]{2,1,0:T(8,128)(2,1)S(1)}, bf16[4,512,512]{2,1,0:T(8,128)(2,1)}, u32[]{:S(2)}) copy-start(bf16[4,512,512]{2,1,0:T(8,128)(2,1)} %param.15) | copy-start | bytes 6291460
  0.6 3.5 %copy-start.4 = (bf16[4,512]{1,0:T(4,128)(2,1)S(1)}, bf16[4,512]{1,0:T(4,128)(2,1)}, u32[]{:S(2)}) copy-start(bf16[4,512]{1,0:T(4,128)(2,1)} %param.18) | copy-start | bytes 12292
  3.9 10.4 %copy-start.3 = (s32[32,4]{0,1:T(4,128)S(1)}, s32[32,4]{0,1:T(4,128)}, u32[]{:S(2)}) copy-start(s32[32,4]{0,1:T(4,128)} %param.26) | copy-start | bytes 1540
  4.1 18.1 %copy-start.5 = (f32[768]{0:T(1024)S(1)}, f32[768]{0:T(1024)}, u32[]{:S(2)}) copy-start(f32[768]{0:T(1024)} %param.22) | copy-start | bytes 9220
  7.0 15.2 %all-to-all-start = ((bf16[8,4,3072]{2,1,0:T(4,128)(2,1)}), bf16[8,4,3072]{2,1,0:T(4,128)(2,1)S(1)}, u32[]{:S(2)}, u32[]{:S(2)}) async-start(bf16[8,4,3072]{2,1,0:T(4,128)(2,1)} %broadcast_in_dim.56), calls=%async_computation | async-start | bytes 393216 | tf_op jit(solution)/shard_map/all_to_all | solution.py:74
  22.8 12.4 %all-to-all-start.2 = ((f32[8,1,768]{2,1,0:T(1,128)}), f32[8,1,768]{2,1,0:T(1,128)S(1)}, u32[]{:S(2)}, u32[]{:S(2)}) async-start(f32[8,1,768]{2,1,0:T(1,128)} %broadcast_in_dim.90), calls=%async_computation.2 | async-start | bytes 49152 | tf_op jit(solution)/shard_map/all_to_all | solution.py:74
  26.2 3.3 %copy-start.6 = (f32[32,4]{0,1:T(4,128)S(1)}, f32[32,4]{0,1:T(4,128)}, u32[]{:S(2)}) copy-start(f32[32,4]{0,1:T(4,128)} %param.27) | copy-start | bytes 1540
  26.2 4.5 %copy-start.2 = (bf16[32,768]{1,0:T(8,128)(2,1)S(1)}, bf16[32,768]{1,0:T(8,128)(2,1)}, u32[]{:S(2)}) copy-start(bf16[32,768]{1,0:T(8,128)(2,1)} %param.20) | copy-start | bytes 147460
  29.5 1.3 %collective-permute-start = (f32[32,768]{1,0:T(8,128)S(1)}, f32[32,768]{1,0:T(8,128)S(1)}, u32[]{:S(2)}, u32[]{:S(2)}) collective-permute-start(f32[32,768]{1,0:T(8,128)S(1)} %fusion.68), channel_id=1, source_target_pairs={{0,1},{1,0},{2,3},{3,2},{4,5},{5,4},{6,7},{7,6},{8,9},{9,8},{10,11... | collective-permute-start | bytes 294920 | tf_op jit(solution)/shard_map/ppermute | solution.py:78
  30.8 24.9 %copy-start.1 = (bf16[32,768]{1,0:T(8,128)(2,1)}, bf16[32,768]{1,0:T(8,128)(2,1)S(1)}, u32[]{:S(2)}) copy-start(bf16[32,768]{1,0:T(8,128)(2,1)S(1)} %add_convert_fusion.1) | copy-start | bytes 147460
  35.2 14.2 %all-to-all-start.1 = ((bf16[8,16,768]{2,1,0:T(8,128)(2,1)}), bf16[8,16,768]{2,1,0:T(8,128)(2,1)S(1)}, u32[]{:S(2)}, u32[]{:S(2)}) async-start(bf16[8,16,768]{2,1,0:T(8,128)(2,1)} %constant_dynamic-update-slice_fusion.7), calls=%async_computation.1 | async-start | bytes 393216 | tf_op jit(solution)/shard_map/all_to_all | solution.py:121
  56.3 11.1 %all-to-all-start.3 = ((bf16[8,16,768]{2,1,0:T(8,128)(2,1)}), bf16[8,16,768]{2,1,0:T(8,128)(2,1)S(1)}, u32[]{:S(2)}, u32[]{:S(2)}) async-start(bf16[8,16,768]{2,1,0:T(8,128)(2,1)} %bitcast.77), calls=%async_computation.3 | async-start | bytes 393216 | tf_op jit(solution)/shard_map/all_to_all | solution.py:142
  67.7 1.3 %collective-permute-start.1 = (f32[32,768]{1,0:T(8,128)S(1)}, f32[32,768]{1,0:T(8,128)S(1)}, u32[]{:S(2)}, u32[]{:S(2)}) collective-permute-start(f32[32,768]{1,0:T(8,128)S(1)} %convolution_bitcast_fusion), channel_id=1, source_target_pairs={{0,1},{1,0},{2,3},{3,2},{4,5},{5,4},{6,7},{7,6},{8,9},{9,8},{10,11... | collective-permute-start | bytes 294920 | tf_op jit(solution)/shard_map/ppermute | solution.py:78

commit v2 on v1

--- a/solution.py
+++ b/solution.py
@@ -1,8 +1,11 @@
+import functools
 import math
 
 import jax
 import jax.numpy as jnp
 from jax import lax
+from jax.experimental import pallas as pl
+from jax.experimental.pallas import tpu as pltpu
 from jax.sharding import PartitionSpec as P
 
 D = 6144
@@ -78,7 +81,7 @@
     return block + lax.ppermute(block, "expert", [(0, 1), (1, 0)])
 
 
-def shards(
+def shards_plain(
     queries,
     key_cache,
     value_cache,
@@ -151,9 +154,420 @@
     return (attn_stream, expert_out)
 
 
+MIB = 1024 * 1024
+VMEM_SPEC = pl.BlockSpec(memory_space=pltpu.VMEM)
+SMEM_SPEC = pl.BlockSpec(memory_space=pltpu.SMEM)
+ANY_SPEC = pl.BlockSpec(memory_space=pl.ANY)
+
+
+def call(kernel, outs, in_specs, scratch, flops, nbytes, vmem_mib):
+    single = not isinstance(outs, (list, tuple))
+    return pl.pallas_call(
+        kernel,
+        out_shape=outs,
+        in_specs=in_specs,
+        out_specs=VMEM_SPEC if single else [VMEM_SPEC] * len(outs),
+        scratch_shapes=scratch,
+        cost_estimate=pl.CostEstimate(flops=flops, bytes_accessed=nbytes, transcendentals=0),
+        compiler_params=pltpu.CompilerParams(vmem_limit_bytes=vmem_mib * MIB),
+    )
+
+
+def attend_kernel(
+    length_ref, query_ref, key_hbm, value_hbm, own_key_ref, own_value_ref, out_ref,
+    key_buf, value_buf, query_rows, key_rows, value_rows, result_rows, key_sem, value_sem,
+):
+    row_count, length_max = key_hbm.shape[0], key_hbm.shape[1]
+    kv_local = own_key_ref.shape[1] // HEAD_DIM
+    group = HEADS // KV_HEADS
+    block = group * row_count
+    key_copies = [
+        pltpu.make_async_copy(key_hbm.at[r], key_buf.at[r], key_sem.at[r]) for r in range(row_count)
+    ]
+    value_copies = [
+        pltpu.make_async_copy(value_hbm.at[r], value_buf.at[r], value_sem.at[r])
+        for r in range(row_count)
+    ]
+    for copy in key_copies + value_copies:
+        copy.start()
+    for g in range(kv_local):
+        lanes = slice(g * HEAD_DIM, (g + 1) * HEAD_DIM)
+        own_key = own_key_ref[:, lanes].astype(jnp.float32)
+        own_value = own_value_ref[:, lanes].astype(jnp.float32)
+        for i in range(group):
+            head = g * group + i
+            rows = pl.ds(g * block + i * row_count, row_count)
+            query_rows[rows, :] = query_ref[
+                :, head * HEAD_DIM : (head + 1) * HEAD_DIM
+            ].astype(jnp.float32)
+            key_rows[rows, :] = own_key
+            value_rows[rows, :] = own_value
+    scale = 1.0 / math.sqrt(HEAD_DIM)
+    pair_rows = 2 * block
+    request = lax.broadcasted_iota(jnp.int32, (pair_rows, 1), 0) % row_count
+    lengths = jnp.zeros((pair_rows, 1), jnp.int32)
+    for r in range(row_count):
+        lengths = jnp.where(request == r, length_ref[r], lengths)
+    position = lax.broadcasted_iota(jnp.int32, (pair_rows, length_max), 1)
+    valid = position < lengths
+    pairs = kv_local // 2
+    past = [jnp.zeros((pair_rows, length_max), jnp.float32) for _ in range(pairs)]
+    packed = []
+    for p in range(pairs):
+        rows = query_rows[pl.ds(p * pair_rows, pair_rows), :]
+        lower = rows[:block].astype(jnp.bfloat16)
+        upper = rows[block:].astype(jnp.bfloat16)
+        zero = jnp.zeros_like(lower)
+        packed.append(
+            jnp.concatenate(
+                [
+                    jnp.concatenate([lower, zero], axis=1),
+                    jnp.concatenate([zero, upper], axis=1),
+                ],
+                axis=0,
+            )
+        )
+    for r in range(row_count):
+        key_copies[r].wait()
+        for p in range(pairs):
+            keys = key_buf[r, :, p * 2 * HEAD_DIM : (p + 1) * 2 * HEAD_DIM]
+            scores = lax.dot_general(
+                packed[p], keys, (((1,), (1,)), ((), ())), preferred_element_type=jnp.float32
+            )
+            past[p] = jnp.where(request == r, scores, past[p])
+    probs, own_probs = [], []
+    for p in range(pairs):
+        rows = pl.ds(p * pair_rows, pair_rows)
+        scores = jnp.where(valid, past[p] * scale, NEG_FILL)
+        own = jnp.sum(query_rows[rows, :] * key_rows[rows, :], axis=1, keepdims=True) * scale
+        largest = jnp.maximum(jnp.max(scores, axis=1, keepdims=True), own)
+        weight = jnp.exp(scores - largest)
+        own_weight = jnp.exp(own - largest)
+        total = jnp.sum(weight, axis=1, keepdims=True) + own_weight
+        probs.append((weight / total).astype(jnp.bfloat16))
+        own_probs.append((own_weight / total).astype(jnp.bfloat16).astype(jnp.float32))
+    sums = [jnp.zeros((pair_rows, 2 * HEAD_DIM), jnp.float32) for _ in range(pairs)]
+    for r in range(row_count):
+        value_copies[r].wait()
+        for p in range(pairs):
+            values = value_buf[r, :, p * 2 * HEAD_DIM : (p + 1) * 2 * HEAD_DIM]
+            product = jnp.dot(probs[p], values, preferred_element_type=jnp.float32)
+            sums[p] = jnp.where(request == r, product, sums[p])
+    for p in range(pairs):
+        rows = pl.ds(p * pair_rows, pair_rows)
+        own_part = own_probs[p] * value_rows[rows, :]
+        lower = sums[p][:block, :HEAD_DIM] + own_part[:block]
+        upper = sums[p][block:, HEAD_DIM:] + own_part[block:]
+        result_rows[pl.ds(p * pair_rows, block), :] = lower
+        result_rows[pl.ds(p * pair_rows + block, block), :] = upper
+    for head in range(kv_local * group):
+        out_ref[:, head * HEAD_DIM : (head + 1) * HEAD_DIM] = result_rows[
+            pl.ds(head * row_count, row_count), :
+        ].astype(jnp.bfloat16)
+
+
+def attend(queries, key_cache, value_cache, new_key, new_value, cache_length):
+    row_count = queries.shape[0]
+    heads = queries.shape[1] // HEAD_DIM
+    table = pltpu.VMEM((heads * row_count, HEAD_DIM), jnp.float32)
+    nbytes = 2 * key_cache.size * 2
+    return call(
+        attend_kernel,
+        jax.ShapeDtypeStruct(queries.shape, jnp.bfloat16),
+        [SMEM_SPEC, VMEM_SPEC, ANY_SPEC, ANY_SPEC, VMEM_SPEC, VMEM_SPEC],
+        [
+            pltpu.VMEM(key_cache.shape, jnp.bfloat16),
+            pltpu.VMEM(value_cache.shape, jnp.bfloat16),
+            table, table, table, table,
+            pltpu.SemaphoreType.DMA((row_count,)),
+            pltpu.SemaphoreType.DMA((row_count,)),
+        ],
+        4 * key_cache.size * 6, nbytes, 12,
+    )(cache_length, queries, key_cache, value_cache, new_key, new_value)
+
+
+def project_kernel(count, chunks, place_ref, *refs):
+    pieces, weight_hbm, out_ref, stack, weight_buf, sem = (
+        refs[:count], refs[count], refs[count + 1], refs[count + 2], refs[count + 3], refs[count + 4],
+    )
+    height = weight_hbm.shape[0] // chunks
+    copies = [
+        pltpu.make_async_copy(
+            weight_hbm.at[pl.ds(c * height, height)],
+            weight_buf.at[pl.ds(c * height, height)],
+            sem.at[c],
+        )
+        for c in range(chunks)
+    ]
+    for copy in copies:
+        copy.start()
+    rows = pieces[0].shape[0]
+    total = rows * count
+    for k in range(count):
+        stack[pl.ds(k * rows, rows), :] = pieces[k][...].astype(jnp.float32)
+    place = place_ref[0]
+    target = lax.broadcasted_iota(jnp.int32, (total, total), 0)
+    source = lax.broadcasted_iota(jnp.int32, (total, total), 1)
+    owner = place - source // rows
+    owner = jnp.where(owner < 0, owner + count, owner)
+    order = (target == owner * rows + source % rows).astype(jnp.bfloat16)
+    whole = jnp.dot(
+        order, stack[...].astype(jnp.bfloat16), preferred_element_type=jnp.float32
+    ).astype(jnp.bfloat16)
+    result = None
+    for c in range(chunks):
+        copies[c].wait()
+        part = jnp.dot(
+            whole[:, c * height : (c + 1) * height],
+            weight_buf[pl.ds(c * height, height), :],
+            preferred_element_type=jnp.float32,
+        )
+        result = part if result is None else result + part
+    out_ref[...] = result
+
+
+def project(place, pieces, out_weight):
+    count = len(pieces)
+    rows, depth = pieces[0].shape
+    cols = out_weight.shape[1]
+    chunks = 6
+    return call(
+        functools.partial(project_kernel, count, chunks),
+        jax.ShapeDtypeStruct((rows * count, cols), jnp.float32),
+        [SMEM_SPEC] + [VMEM_SPEC] * count + [ANY_SPEC],
+        [
+            pltpu.VMEM((rows * count, depth), jnp.float32),
+            pltpu.VMEM(out_weight.shape, jnp.bfloat16),
+            pltpu.SemaphoreType.DMA((chunks,)),
+        ],
+        2 * rows * count * out_weight.size, out_weight.size * 2, 10,
+    )(place, *pieces, out_weight)
+
+
+def expert_rows(routes, expert, capacity):
+    row_count = routes.shape[1]
+    hit = jnp.max((routes == expert).astype(jnp.float32), axis=0, keepdims=True)
+    earlier = lax.broadcasted_iota(jnp.int32, (row_count, row_count), 0) < lax.broadcasted_iota(
+        jnp.int32, (row_count, row_count), 1
+    )
+    slot = jnp.dot(
+        jnp.broadcast_to(hit, (8, row_count)).astype(jnp.bfloat16),
+        earlier.astype(jnp.bfloat16),
+        preferred_element_type=jnp.float32,
+    )[:1]
+    place = lax.broadcasted_iota(jnp.int32, (capacity, row_count), 0).astype(jnp.float32)
+    return jnp.where((slot == place) & (hit > 0.5), 1.0, 0.0)
+
+
+def wrapped(value, count):
+    value = jnp.where(value < 0, value + count, value)
+    return jnp.where(value >= count, value - count, value)
+
+
+def pick_kernel(count, cores, capacity, place_ref, mine_ref, other_ref, residual_ref, routes_ref,
+                stream_ref, *out_refs):
+    stream = (
+        residual_ref[...].astype(jnp.float32) + (mine_ref[...] + other_ref[...])
+    ).astype(jnp.bfloat16)
+    stream_ref[...] = stream
+    routes = routes_ref[...]
+    chosen = [
+        jnp.dot(
+            expert_rows(routes, e, capacity).astype(jnp.bfloat16),
+            stream,
+            preferred_element_type=jnp.float32,
+        )
+        for e in range(HELD)
+    ]
+    sharers = count * cores // HELD
+    for k in range(count):
+        dest = wrapped(place_ref[0] + k, count)
+        out_refs[k][...] = jnp.where(
+            dest * cores < sharers, chosen[0], chosen[1]
+        ).astype(jnp.bfloat16)
+
+
+def pick(place, cores, count, capacity, mine, other, residual, routes):
+    rows, cols = mine.shape
+    return call(
+        functools.partial(pick_kernel, count, cores, capacity),
+        [jax.ShapeDtypeStruct((rows, cols), jnp.bfloat16)]
+        + [jax.ShapeDtypeStruct((capacity, cols), jnp.bfloat16)] * count,
+        [SMEM_SPEC] + [VMEM_SPEC] * 4,
+        [],
+        2 * HELD * capacity * rows * cols, rows * cols * 12, 4,
+    )(place, mine, other, residual, routes)
+
+
+def expert_kernel(count, cores, place_ref, routes_ref, weight_ref, *refs):
+    pieces, gains = refs[:count], refs[count : 2 * count]
+    gate_hbm, up_hbm, down_hbm = refs[2 * count : 2 * count + 3]
+    outs = refs[2 * count + 3 : 3 * count + 3]
+    gate_buf, up_buf, down_buf, sem = refs[3 * count + 3 :]
+    capacity, cols = pieces[0].shape
+    place = place_ref[0]
+    copies = []
+    for k in range(count):
+        source = pl.ds(pl.multiple_of(wrapped(place - k, count) * cols, 128), cols)
+        copies.append(
+            (
+                pltpu.make_async_copy(gate_hbm.at[:, source], gate_buf.at[k], sem.at[0, k]),
+                pltpu.make_async_copy(up_hbm.at[:, source], up_buf.at[k], sem.at[1, k]),
+            )
+        )
+    returns = []
+    for k in range(count):
+        target = pl.ds(pl.multiple_of(wrapped(place + k, count) * cols, 128), cols)
+        returns.append(
+            pltpu.make_async_copy(down_hbm.at[:, target], down_buf.at[k], sem.at[2, k])
+        )
+    for pair in copies:
+        pair[0].start()
+        pair[1].start()
+    for copy in returns:
+        copy.start()
+    sharers = count * cores // HELD
+    expert = jnp.where(place * cores < sharers, 0, 1)
+    routes = routes_ref[...]
+    taken = expert_rows(routes, expert, capacity)
+    row_weight = jnp.sum(
+        jnp.where(routes == expert, weight_ref[...], 0.0), axis=0, keepdims=True
+    )
+    slot_weight = jnp.sum(taken * row_weight, axis=1, keepdims=True)
+    wide = [piece[...].astype(jnp.float32) for piece in pieces]
+    first = wide[0]
+    second = wide[0] * wide[0]
+    for value in wide[1:]:
+        first = first + value
+        second = second + value * value
+    row_mean = jnp.sum(first, axis=1, keepdims=True) / D
+    row_var = jnp.sum(second, axis=1, keepdims=True) / D - row_mean * row_mean
+    inverse = lax.rsqrt(row_var + EPSILON)
+    contract = (((1,), (1,)), ((), ()))
+    gate_val = up_val = None
+    for k in range(count):
+        normed = ((wide[k] - row_mean) * inverse * gains[k][...]).astype(jnp.bfloat16)
+        copies[k][0].wait()
+        gate_part = lax.dot_general(
+            normed, gate_buf[k], contract, preferred_element_type=jnp.float32
+        )
+        copies[k][1].wait()
+        up_part = lax.dot_general(
+            normed, up_buf[k], contract, preferred_element_type=jnp.float32
+        )
+        gate_val = gate_part if gate_val is None else gate_val + gate_part
+        up_val = up_part if up_val is None else up_val + up_part
+    hidden = (gate_val / (1.0 + jnp.exp(-gate_val)) * up_val).astype(jnp.bfloat16)
+    for k in range(count):
+        returns[k].wait()
+        outs[k][...] = (
+            jnp.dot(hidden, down_buf[k], preferred_element_type=jnp.float32) * slot_weight
+        ).astype(jnp.bfloat16)
+
+
+def run_experts(place, cores, routes, route_weight, pieces, gains, gate, up, down):
+    count = len(pieces)
+    capacity, cols = pieces[0].shape
+    hidden = gate.shape[0]
+    buf = pltpu.VMEM((count, hidden, cols), jnp.bfloat16)
+    return call(
+        functools.partial(expert_kernel, count, cores),
+        [jax.ShapeDtypeStruct((capacity, cols), jnp.bfloat16)] * count,
+        [SMEM_SPEC] + [VMEM_SPEC] * (2 + 2 * count) + [ANY_SPEC] * 3,
+        [buf, buf, buf, pltpu.SemaphoreType.DMA((3, count))],
+        6 * capacity * gate.size, gate.size * 6, 14,
+    )(place, routes, route_weight, *pieces, *gains, gate, up, down)
+
+
+def combine_kernel(count, cores, place_ref, routes_ref, *refs):
+    pieces, out_ref = refs[:count], refs[count]
+    capacity = pieces[0].shape[0]
+    sharers = count * cores // HELD
+    routes = routes_ref[...]
+    taken = [expert_rows(routes, e, capacity) for e in range(HELD)]
+    spread = []
+    for k in range(count):
+        source = wrapped(place_ref[0] - k, count)
+        spread.append(jnp.where(source * cores < sharers, taken[0], taken[1]))
+    out_ref[...] = lax.dot_general(
+        jnp.concatenate(spread, axis=0).astype(jnp.bfloat16),
+        jnp.concatenate([piece[...] for piece in pieces], axis=0),
+        (((0,), (0,)), ((), ())),
+        preferred_element_type=jnp.float32,
+    )
+
+
+def combine(place, cores, routes, pieces):
+    count = len(pieces)
+    capacity, cols = pieces[0].shape
+    rows = routes.shape[1]
+    return call(
+        functools.partial(combine_kernel, count, cores),
+        jax.ShapeDtypeStruct((rows, cols), jnp.float32),
+        [SMEM_SPEC] + [VMEM_SPEC] * (1 + count),
+        [],
+        2 * rows * capacity * count * cols, (count * capacity * 2 + rows * 4) * cols, 4,
+    )(place, routes, *pieces)
+
+
+def shifted(block, count, distance):
+    pairs = [(index, (index + distance) % count) for index in range(count)]
+    return lax.ppermute(block, "attn", pairs)
+
+
+def swap(block):
+    return lax.ppermute(block, "expert", [(0, 1), (1, 0)])
+
+
+def shards(
+    queries,
+    key_cache,
+    value_cache,
+    new_key,
+    new_value,
+    cache_length,
+    residual,
+    out_weight,
+    ln_gain,
+    gate_weight,
+    up_weight,
+    down_weight,
+    routes,
+    route_weight,
+):
+    count = lax.axis_size("attn")
+    cores = lax.axis_size("expert")
+    row_count = routes.shape[0]
+    capacity = row_count * TOP // EXPERTS * 2
+    place = lax.axis_index("attn").astype(jnp.int32).reshape(1)
+    routes = routes.T
+    route_weight = route_weight.T
+
+    gain = ln_gain.reshape(1, -1)
+    gains = [gain] + [shifted(gain, count, k) for k in range(1, count)]
+
+    attended = attend(queries, key_cache, value_cache, new_key, new_value, cache_length)
+    pieces = [attended] + [shifted(attended, count, k) for k in range(1, count)]
+    mine = project(place, pieces, out_weight)
+    other = swap(mine)
+    attn_stream, *chosen = pick(
+        place, cores, count, capacity, mine, other, residual, routes
+    )
+    rows = [chosen[0]] + [shifted(chosen[k], count, k) for k in range(1, count)]
+    outgoing = run_experts(
+        place, cores, routes, route_weight, rows, gains,
+        gate_weight.T, up_weight.T, down_weight,
+    )
+    returned = [outgoing[0]] + [shifted(outgoing[k], count, k) for k in range(1, count)]
+    combined = combine(place, cores, routes, returned)
+    expert_out = (combined + swap(combined)).astype(jnp.bfloat16)
+    return (attn_stream, expert_out)
+
+
 def solution(mesh):
+    cols = D // mesh.shape["attn"]
     return jax.shard_map(
-        shards,
+        shards if cols % 128 == 0 else shards_plain,
         mesh=mesh,
         in_specs=(
             P(("group", "attn"), "expert"),

time: 70.2 us -> 78.2 us (1.11)
  starting transfers between devices: 20 us -> 47 us
  waiting for transfers between devices: 26.2 us -> 10.3 us
  matrix products: 12.5 us -> 0 us
  Pallas kernels: 0 us -> 10.8 us
  other arithmetic: 2.07 us -> 0.63 us
    ppermute x2 -> x30, starting transfers between devices: 0.01 us -> 47 us  [the longest x28 46.9 us: shifted(): return lax.ppermute(block, 'attn', pairs)]
    all_to_all x4 -> x0, waiting for transfers between devices: 23.6 us -> none  [the longest x1 8.15 us: shards(): lax.all_to_all(outgoing, 'attn', split_axis=0, concat_axis=0, tiled=True)]
    all_to_all x4 -> x0, starting transfers between devices: 19.9 us -> none  [the longest x2 10.6 us: gather_attn(): lax.all_to_all(copies, 'attn', split_axis=0, concat_axis=0, tiled=True)]
    dot_general x8 -> x0, matrix products: 12.5 us -> none  [the longest x1 3.79 us: shards(): piece = jnp.dot(hidden, down_weight, preferred_element_type=jnp.float32)]
    pallas_call x0 -> x5, Pallas kernels: none -> 10.8 us  [the longest x1 5.12 us: run_experts(): call(functools.partial(expert_kernel, count, cores), [jax.ShapeDtypeStruc...]
    ppermute x2 -> x30, waiting for transfers between devices: 2.58 us -> 10.3 us  [the longest x28 7.72 us: shifted(): return lax.ppermute(block, 'attn', pairs)]
    unnamed x26 -> x28, local copies, waits for them, and re-layouts: 3.74 us -> 8.31 us
    reshape x4 -> x1, local copies, waits for them, and re-layouts: 2.36 us -> 0.01 us  [shards(): gain = ln_gain.reshape(1, -1)]
  transfers between devices with their start and end apart: 6 -> 30, of which waited for: 5 -> 9; matrix products, arithmetic and copies ran while one was open for 11% -> 0% of each run, Pallas kernels for 0% -> 0%
where the time goes in v2:
time: 78.2 us; the launch traced here: 77.9 us
  starting transfers between devices  47 us (60%)
  Pallas kernels  10.8 us (14%)
  waiting for transfers between devices  10.3 us (13%)
  local copies, waits for them, and re-layouts  8.31 us (11%)
    ppermute x28, starting transfers between devices, shifted(): return lax.ppermute(block, 'attn', pairs)  46.9 us
    unnamed x28, local copies, waits for them, and re-layouts  8.31 us
    ppermute x28, waiting for transfers between devices, shifted(): return lax.ppermute(block, 'attn', pairs)  7.72 us
    pallas_call x1, Pallas kernels, run_experts(): call(functools.partial(expert_kernel, count, cores), [jax.ShapeDtypeStruc...  5.12 us
    pallas_call x1, Pallas kernels, attend(): call(attend_kernel, jax.ShapeDtypeStruct(queries.shape, jnp.bfloat16), [S...  3.01 us
    ppermute x2, waiting for transfers between devices, swap(): return lax.ppermute(block, 'expert', [(0, 1), (1, 0)])  2.58 us
    pallas_call x1, Pallas kernels, project(): call(functools.partial(project_kernel, count, chunks), jax.ShapeDtypeStru...  1.77 us
  transfers between devices with their start and end apart: 30, of which 9 were waited for; matrix products, arithmetic and copies ran while one was open for 0% of the time, Pallas kernels for 0%

profile of v2, /device:TPU:0, one launch (start us, length us, event | category | flops | bytes accessed | tf_op | source)
XLA Modules:
  0.0 77.9 jit_solution(7016375540112437640)
XLA Ops:
  0.6 1.6 %copy-done.1 = bf16[4,512,512]{2,1,0:T(8,128)(2,1)S(1)} copy-done((bf16[4,512,512]{2,1,0:T(8,128)(2,1)S(1)}, bf16[4,512,512]{2,1,0:T(8,128)(2,1)}, u32[]{:S(2)}) %copy-start.1) | copy-done | bytes 2097176
  2.2 1.6 %copy-done.2 = bf16[4,512,512]{2,1,0:T(8,128)(2,1)S(1)} copy-done((bf16[4,512,512]{2,1,0:T(8,128)(2,1)S(1)}, bf16[4,512,512]{2,1,0:T(8,128)(2,1)}, u32[]{:S(2)}) %copy-start.2) | copy-done | bytes 2097176
  3.8 0.7 copy-done.7
  4.6 0.7 copy-done.9
  5.2 0.7 copy-done.10
  5.9 0.7 copy-done.12
  6.6 3.0 %shard_map.149.refs_0_ = bf16[4,3072]{1,0:T(4,128)(2,1)S(1)} custom-call(s32[4]{0:T(128)S(1)} %copy-done.12, bf16[4,3072]{1,0:T(4,128)(2,1)S(1)} %copy-done.7, bf16[4,512,512]{2,1,0:T(8,128)(2,1)S(1)} %copy-done.1, bf16[4,512,512]{2,1,0:T(8,128)(2,1)S(1)} %copy-done.2, bf16[4,512]{1,0:T(4,128)(2,1)S(1)} %copy-done.9, bf16[4,512]{1,0:T(4,128)(2,1)S(1)} %copy-done.10), custom_call_target="tpu_custom_call" | custom-call | flops 25165824 | bytes 4194304 | tf_op jit(solution)/shard_map/pallas_call | solution.py:274
  9.6 3.0 %collective-permute-start = (bf16[4,3072]{1,0:T(4,128)(2,1)S(1)}, bf16[4,3072]{1,0:T(4,128)(2,1)S(1)}, u32[]{:S(2)}, u32[]{:S(2)}) collective-permute-start(bf16[4,3072]{1,0:T(4,128)(2,1)S(1)} %shard_map.149.refs_0_), channel_id=1, source_target_pairs={{0,2},{2,4},{4,6},{6,8},{8,10},{10,12},{12,14},{14,0},{1,3},{3,5},... | collective-permute-start | bytes 73736 | tf_op jit(solution)/shard_map/ppermute | solution.py:515
  12.6 1.6 %collective-permute-start.1 = (bf16[4,3072]{1,0:T(4,128)(2,1)S(1)}, bf16[4,3072]{1,0:T(4,128)(2,1)S(1)}, u32[]{:S(2)}, u32[]{:S(2)}) collective-permute-start(bf16[4,3072]{1,0:T(4,128)(2,1)S(1)} %shard_map.149.refs_0_), channel_id=1, source_target_pairs={{0,4},{2,6},{4,8},{6,10},{8,12},{10,14},{12,0},{14,2},{1,5},{3,7},... | collective-permute-start | bytes 73736 | tf_op jit(solution)/shard_map/ppermute | solution.py:515
  14.2 2.5 %collective-permute-start.2 = (bf16[4,3072]{1,0:T(4,128)(2,1)S(1)}, bf16[4,3072]{1,0:T(4,128)(2,1)S(1)}, u32[]{:S(2)}, u32[]{:S(2)}) collective-permute-start(bf16[4,3072]{1,0:T(4,128)(2,1)S(1)} %shard_map.149.refs_0_), channel_id=1, source_target_pairs={{0,6},{2,8},{4,10},{6,12},{8,14},{10,0},{12,2},{14,4},{1,7},{3,9},... | collective-permute-start | bytes 73736 | tf_op jit(solution)/shard_map/ppermute | solution.py:515
  16.7 1.2 %collective-permute-start.3 = (bf16[4,3072]{1,0:T(4,128)(2,1)S(1)}, bf16[4,3072]{1,0:T(4,128)(2,1)S(1)}, u32[]{:S(2)}, u32[]{:S(2)}) collective-permute-start(bf16[4,3072]{1,0:T(4,128)(2,1)S(1)} %shard_map.149.refs_0_), channel_id=1, source_target_pairs={{0,8},{2,10},{4,12},{6,14},{8,0},{10,2},{12,4},{14,6},{1,9},{3,11}... | collective-permute-start | bytes 73736 | tf_op jit(solution)/shard_map/ppermute | solution.py:515
  18.0 2.6 %collective-permute-start.4 = (bf16[4,3072]{1,0:T(4,128)(2,1)S(1)}, bf16[4,3072]{1,0:T(4,128)(2,1)S(1)}, u32[]{:S(2)}, u32[]{:S(2)}) collective-permute-start(bf16[4,3072]{1,0:T(4,128)(2,1)S(1)} %shard_map.149.refs_0_), channel_id=1, source_target_pairs={{0,10},{2,12},{4,14},{6,0},{8,2},{10,4},{12,6},{14,8},{1,11},{3,13... | collective-permute-start | bytes 73736 | tf_op jit(solution)/shard_map/ppermute | solution.py:515
  20.6 1.3 %collective-permute-start.5 = (bf16[4,3072]{1,0:T(4,128)(2,1)S(1)}, bf16[4,3072]{1,0:T(4,128)(2,1)S(1)}, u32[]{:S(2)}, u32[]{:S(2)}) collective-permute-start(bf16[4,3072]{1,0:T(4,128)(2,1)S(1)} %shard_map.149.refs_0_), channel_id=1, source_target_pairs={{0,12},{2,14},{4,0},{6,2},{8,4},{10,6},{12,8},{14,10},{1,13},{3,15... | collective-permute-start | bytes 73736 | tf_op jit(solution)/shard_map/ppermute | solution.py:515
  22.0 1.4 %collective-permute-start.6 = (bf16[4,3072]{1,0:T(4,128)(2,1)S(1)}, bf16[4,3072]{1,0:T(4,128)(2,1)S(1)}, u32[]{:S(2)}, u32[]{:S(2)}) collective-permute-start(bf16[4,3072]{1,0:T(4,128)(2,1)S(1)} %shard_map.149.refs_0_), channel_id=1, source_target_pairs={{0,14},{2,0},{4,2},{6,4},{8,6},{10,8},{12,10},{14,12},{1,15},{3,1}... | collective-permute-start | bytes 73736 | tf_op jit(solution)/shard_map/ppermute | solution.py:515
  23.4 1.1 %collective-permute-done.5.refs_6_ = bf16[4,3072]{1,0:T(4,128)(2,1)S(1)} collective-permute-done((bf16[4,3072]{1,0:T(4,128)(2,1)S(1)}, bf16[4,3072]{1,0:T(4,128)(2,1)S(1)}, u32[]{:S(2)}, u32[]{:S(2)}) %collective-permute-start.5) | collective-permute-done | bytes 24608 | tf_op jit(solution)/shard_map/ppermute | solution.py:515
  24.5 1.4 %collective-permute-done.6.refs_7_ = bf16[4,3072]{1,0:T(4,128)(2,1)S(1)} collective-permute-done((bf16[4,3072]{1,0:T(4,128)(2,1)S(1)}, bf16[4,3072]{1,0:T(4,128)(2,1)S(1)}, u32[]{:S(2)}, u32[]{:S(2)}) %collective-permute-start.6) | collective-permute-done | bytes 24608 | tf_op jit(solution)/shard_map/ppermute | solution.py:515
  25.8 2.3 %copy-done = bf16[3072,768]{1,0:T(8,128)(2,1)S(1)} copy-done((bf16[3072,768]{1,0:T(8,128)(2,1)S(1)}, bf16[3072,768]{1,0:T(8,128)(2,1)}, u32[]{:S(2)}) %copy-start) | copy-done | bytes 4718616
  28.2 1.8 %shard_map.150.mine_ref = f32[32,768]{1,0:T(8,128)S(1)} custom-call(s32[1]{0:T(128)} %bitcast.place_ref, bf16[4,3072]{1,0:T(4,128)(2,1)S(1)} %shard_map.149.refs_0_, bf16[4,3072]{1,0:T(4,128)(2,1)S(1)} %collective-permute-done.refs_1_, bf16[4,3072]{1,0:T(4,128)(2,1)S(1)} %collective-permute-done.1.refs_2_, ...), custom_call_target="tpu_custom_call" | custom-call | flops 150994944 | bytes 4718592 | tf_op jit(solution)/shard_map/pallas_call | solution.py:334
  30.0 1.3 %collective-permute-done.7.other_ref = f32[32,768]{1,0:T(8,128)S(1)} collective-permute-done((f32[32,768]{1,0:T(8,128)S(1)}, f32[32,768]{1,0:T(8,128)S(1)}, u32[]{:S(2)}, u32[]{:S(2)}) %collective-permute-start.7) | collective-permute-done | bytes 98336 | tf_op jit(solution)/shard_map/ppermute | solution.py:519
  31.3 0.6 shard_map.151
  32.0 1.5 %collective-permute-start.8 = (bf16[16,768]{1,0:T(8,128)(2,1)S(1)}, bf16[16,768]{1,0:T(8,128)(2,1)S(1)}, u32[]{:S(2)}, u32[]{:S(2)}) collective-permute-start(bf16[16,768]{1,0:T(8,128)(2,1)S(1)} %get-tuple-element.21), channel_id=1, source_target_pairs={{0,2},{2,4},{4,6},{6,8},{8,10},{10,12},{12,14},{14,0},{1,3},{3,5},... | collective-permute-start | bytes 73736 | tf_op jit(solution)/shard_map/ppermute | solution.py:515
  33.6 0.7 collective-permute-start.15
  34.3 2.0 %collective-permute-start.16 = (f32[1,768]{1,0:T(1,128)S(1)}, f32[1,768]{1,0:T(1,128)S(1)}, u32[]{:S(2)}, u32[]{:S(2)}) collective-permute-start(f32[1,768]{1,0:T(1,128)S(1)} %reshape.11.refs_8_), channel_id=1, source_target_pairs={{0,4},{2,6},{4,8},{6,10},{8,12},{10,14},{12,0},{14,2},{1,5},{3,7},... | collective-permute-start | bytes 9224 | tf_op jit(solution)/shard_map/ppermute | solution.py:515
  36.4 3.0 %collective-permute-start.17 = (f32[1,768]{1,0:T(1,128)S(1)}, f32[1,768]{1,0:T(1,128)S(1)}, u32[]{:S(2)}, u32[]{:S(2)}) collective-permute-start(f32[1,768]{1,0:T(1,128)S(1)} %reshape.11.refs_8_), channel_id=1, source_target_pairs={{0,6},{2,8},{4,10},{6,12},{8,14},{10,0},{12,2},{14,4},{1,7},{3,9},... | collective-permute-start | bytes 9224 | tf_op jit(solution)/shard_map/ppermute | solution.py:515
  39.3 0.6 collective-permute-done.15.refs_9_
  39.9 1.8 %collective-permute-start.18 = (f32[1,768]{1,0:T(1,128)S(1)}, f32[1,768]{1,0:T(1,128)S(1)}, u32[]{:S(2)}, u32[]{:S(2)}) collective-permute-start(f32[1,768]{1,0:T(1,128)S(1)} %reshape.11.refs_8_), channel_id=1, source_target_pairs={{0,8},{2,10},{4,12},{6,14},{8,0},{10,2},{12,4},{14,6},{1,9},{3,11}... | collective-permute-start | bytes 9224 | tf_op jit(solution)/shard_map/ppermute | solution.py:515
  41.7 0.7 collective-permute-start.19
  42.4 2.2 %collective-permute-start.20 = (f32[1,768]{1,0:T(1,128)S(1)}, f32[1,768]{1,0:T(1,128)S(1)}, u32[]{:S(2)}, u32[]{:S(2)}) collective-permute-start(f32[1,768]{1,0:T(1,128)S(1)} %reshape.11.refs_8_), channel_id=1, source_target_pairs={{0,12},{2,14},{4,0},{6,2},{8,4},{10,6},{12,8},{14,10},{1,13},{3,15... | collective-permute-start | bytes 9224 | tf_op jit(solution)/shard_map/ppermute | solution.py:515
  44.6 2.3 %collective-permute-start.21 = (f32[1,768]{1,0:T(1,128)S(1)}, f32[1,768]{1,0:T(1,128)S(1)}, u32[]{:S(2)}, u32[]{:S(2)}) collective-permute-start(f32[1,768]{1,0:T(1,128)S(1)} %reshape.11.refs_8_), channel_id=1, source_target_pairs={{0,14},{2,0},{4,2},{6,4},{8,6},{10,8},{12,10},{14,12},{1,15},{3,1}... | collective-permute-start | bytes 9224 | tf_op jit(solution)/shard_map/ppermute | solution.py:515
  46.9 0.8 collective-permute-start.10
  47.7 1.4 %collective-permute-start.11 = (bf16[16,768]{1,0:T(8,128)(2,1)S(1)}, bf16[16,768]{1,0:T(8,128)(2,1)S(1)}, u32[]{:S(2)}, u32[]{:S(2)}) collective-permute-start(bf16[16,768]{1,0:T(8,128)(2,1)S(1)} %get-tuple-element.24), channel_id=1, source_target_pairs={{0,8},{2,10},{4,12},{6,14},{8,0},{10,2},{12,4},{14,6},{1,9},{3,11}... | collective-permute-start | bytes 73736 | tf_op jit(solution)/shard_map/ppermute | solution.py:515
  49.0 3.3 %collective-permute-start.12 = (bf16[16,768]{1,0:T(8,128)(2,1)S(1)}, bf16[16,768]{1,0:T(8,128)(2,1)S(1)}, u32[]{:S(2)}, u32[]{:S(2)}) collective-permute-start(bf16[16,768]{1,0:T(8,128)(2,1)S(1)} %get-tuple-element.25), channel_id=1, source_target_pairs={{0,10},{2,12},{4,14},{6,0},{8,2},{10,4},{12,6},{14,8},{1,11},{3,13... | collective-permute-start | bytes 73736 | tf_op jit(solution)/shard_map/ppermute | solution.py:515
  52.3 1.6 %collective-permute-start.13 = (bf16[16,768]{1,0:T(8,128)(2,1)S(1)}, bf16[16,768]{1,0:T(8,128)(2,1)S(1)}, u32[]{:S(2)}, u32[]{:S(2)}) collective-permute-start(bf16[16,768]{1,0:T(8,128)(2,1)S(1)} %get-tuple-element.26), channel_id=1, source_target_pairs={{0,12},{2,14},{4,0},{6,2},{8,4},{10,6},{12,8},{14,10},{1,13},{3,15... | collective-permute-start | bytes 73736 | tf_op jit(solution)/shard_map/ppermute | solution.py:515
  53.9 0.6 collective-permute-start.14
  54.5 1.6 %collective-permute-done.13.refs_6_ = bf16[16,768]{1,0:T(8,128)(2,1)S(1)} collective-permute-done((bf16[16,768]{1,0:T(8,128)(2,1)S(1)}, bf16[16,768]{1,0:T(8,128)(2,1)S(1)}, u32[]{:S(2)}, u32[]{:S(2)}) %collective-permute-start.13) | collective-permute-done | bytes 24608 | tf_op jit(solution)/shard_map/ppermute | solution.py:515
  56.1 1.6 %collective-permute-done.14.refs_7_ = bf16[16,768]{1,0:T(8,128)(2,1)S(1)} collective-permute-done((bf16[16,768]{1,0:T(8,128)(2,1)S(1)}, bf16[16,768]{1,0:T(8,128)(2,1)S(1)}, u32[]{:S(2)}, u32[]{:S(2)}) %collective-permute-start.14) | collective-permute-done | bytes 24608 | tf_op jit(solution)/shard_map/ppermute | solution.py:515
  57.7 5.1 %shard_map.152 = (bf16[16,768]{1,0:T(8,128)(2,1)S(1)}, bf16[16,768]{1,0:T(8,128)(2,1)S(1)}, bf16[16,768]{1,0:T(8,128)(2,1)S(1)}, bf16[16,768]{1,0:T(8,128)(2,1)S...) custom-call(s32[1]{0:T(128)} %bitcast.place_ref, ...), custom_call_target="tpu_custom_call" | custom-call | flops 99090432 | bytes 6193152 | tf_op jit(solution)/shard_map/pallas_call | solution.py:473
  62.8 1.0 %collective-permute-start.22 = (bf16[16,768]{1,0:T(8,128)(2,1)S(1)}, bf16[16,768]{1,0:T(8,128)(2,1)S(1)}, u32[]{:S(2)}, u32[]{:S(2)}) collective-permute-start(bf16[16,768]{1,0:T(8,128)(2,1)S(1)} %get-tuple-element.29), channel_id=1, source_target_pairs={{0,2},{2,4},{4,6},{6,8},{8,10},{10,12},{12,14},{14,0},{1,3},{3,5},... | collective-permute-start | bytes 73736 | tf_op jit(solution)/shard_map/ppermute | solution.py:515
  63.8 0.8 %collective-permute-start.23 = (bf16[16,768]{1,0:T(8,128)(2,1)S(1)}, bf16[16,768]{1,0:T(8,128)(2,1)S(1)}, u32[]{:S(2)}, u32[]{:S(2)}) collective-permute-start(bf16[16,768]{1,0:T(8,128)(2,1)S(1)} %get-tuple-element.30), channel_id=1, source_target_pairs={{0,4},{2,6},{4,8},{6,10},{8,12},{10,14},{12,0},{14,2},{1,5},{3,7},... | collective-permute-start | bytes 73736 | tf_op jit(solution)/shard_map/ppermute | solution.py:515
  64.6 2.1 %collective-permute-start.24 = (bf16[16,768]{1,0:T(8,128)(2,1)S(1)}, bf16[16,768]{1,0:T(8,128)(2,1)S(1)}, u32[]{:S(2)}, u32[]{:S(2)}) collective-permute-start(bf16[16,768]{1,0:T(8,128)(2,1)S(1)} %get-tuple-element.31), channel_id=1, source_target_pairs={{0,6},{2,8},{4,10},{6,12},{8,14},{10,0},{12,2},{14,4},{1,7},{3,9},... | collective-permute-start | bytes 73736 | tf_op jit(solution)/shard_map/ppermute | solution.py:515
  66.7 1.9 %collective-permute-start.25 = (bf16[16,768]{1,0:T(8,128)(2,1)S(1)}, bf16[16,768]{1,0:T(8,128)(2,1)S(1)}, u32[]{:S(2)}, u32[]{:S(2)}) collective-permute-start(bf16[16,768]{1,0:T(8,128)(2,1)S(1)} %get-tuple-element.32), channel_id=1, source_target_pairs={{0,8},{2,10},{4,12},{6,14},{8,0},{10,2},{12,4},{14,6},{1,9},{3,11}... | collective-permute-start | bytes 73736 | tf_op jit(solution)/shard_map/ppermute | solution.py:515
  68.6 2.5 %collective-permute-start.26 = (bf16[16,768]{1,0:T(8,128)(2,1)S(1)}, bf16[16,768]{1,0:T(8,128)(2,1)S(1)}, u32[]{:S(2)}, u32[]{:S(2)}) collective-permute-start(bf16[16,768]{1,0:T(8,128)(2,1)S(1)} %get-tuple-element.33), channel_id=1, source_target_pairs={{0,10},{2,12},{4,14},{6,0},{8,2},{10,4},{12,6},{14,8},{1,11},{3,13... | collective-permute-start | bytes 73736 | tf_op jit(solution)/shard_map/ppermute | solution.py:515
  71.5 2.6 %collective-permute-start.28 = (bf16[16,768]{1,0:T(8,128)(2,1)S(1)}, bf16[16,768]{1,0:T(8,128)(2,1)S(1)}, u32[]{:S(2)}, u32[]{:S(2)}) collective-permute-start(bf16[16,768]{1,0:T(8,128)(2,1)S(1)} %get-tuple-element.35), channel_id=1, source_target_pairs={{0,14},{2,0},{4,2},{6,4},{8,6},{10,8},{12,10},{14,12},{1,15},{3,1}... | collective-permute-start | bytes 73736 | tf_op jit(solution)/shard_map/ppermute | solution.py:515
  74.0 0.9 %collective-permute-done.27.refs_6_ = bf16[16,768]{1,0:T(8,128)(2,1)S(1)} collective-permute-done((bf16[16,768]{1,0:T(8,128)(2,1)S(1)}, bf16[16,768]{1,0:T(8,128)(2,1)S(1)}, u32[]{:S(2)}, u32[]{:S(2)}) %collective-permute-start.27) | collective-permute-done | bytes 24608 | tf_op jit(solution)/shard_map/ppermute | solution.py:515
  75.0 0.6 collective-permute-done.28.refs_7_
  75.6 0.3 shard_map.153
  75.9 1.3 %collective-permute-done.29 = f32[32,768]{1,0:T(8,128)S(1)} collective-permute-done((f32[32,768]{1,0:T(8,128)S(1)}, f32[32,768]{1,0:T(8,128)S(1)}, u32[]{:S(2)}, u32[]{:S(2)}) %collective-permute-start.29) | collective-permute-done | bytes 98336 | tf_op jit(solution)/shard_map/ppermute | solution.py:519
  77.2 0.6 add_convert_fusion
  (47 shorter events, 0.6 us)
Async XLA Ops:
  0.6 1.6 %copy-start.1 = (bf16[4,512,512]{2,1,0:T(8,128)(2,1)S(1)}, bf16[4,512,512]{2,1,0:T(8,128)(2,1)}, u32[]{:S(2)}) copy-start(bf16[4,512,512]{2,1,0:T(8,128)(2,1)} %key_hbm.1) | copy-start | bytes 6291460
  2.2 1.6 %copy-start.2 = (bf16[4,512,512]{2,1,0:T(8,128)(2,1)S(1)}, bf16[4,512,512]{2,1,0:T(8,128)(2,1)}, u32[]{:S(2)}) copy-start(bf16[4,512,512]{2,1,0:T(8,128)(2,1)} %value_hbm.1) | copy-start | bytes 6291460
  3.8 0.7 copy-start.7
  4.6 0.7 copy-start.9
  5.2 0.7 copy-start.10
  5.9 0.7 copy-start.12
  6.6 51.1 %copy-start.5 = (bf16[168,6144]{1,0:T(8,128)(2,1)S(1)}, bf16[168,6144]{1,0:T(8,128)(2,1)}, u32[]{:S(2)}) copy-start(bf16[168,6144]{1,0:T(8,128)(2,1)} %refs_18_.1) | copy-start | bytes 6193156
  9.6 11.0 %collective-permute-start = (bf16[4,3072]{1,0:T(4,128)(2,1)S(1)}, bf16[4,3072]{1,0:T(4,128)(2,1)S(1)}, u32[]{:S(2)}, u32[]{:S(2)}) collective-permute-start(bf16[4,3072]{1,0:T(4,128)(2,1)S(1)} %shard_map.149.refs_0_), channel_id=1, source_target_pairs={{0,2},{2,4},{4,6},{6,8},{8,10},{10,12},{12,14},{14,0},{1,3},{3,5},... | collective-permute-start | bytes 73736 | tf_op jit(solution)/shard_map/ppermute | solution.py:515
  12.6 9.3 %collective-permute-start.1 = (bf16[4,3072]{1,0:T(4,128)(2,1)S(1)}, bf16[4,3072]{1,0:T(4,128)(2,1)S(1)}, u32[]{:S(2)}, u32[]{:S(2)}) collective-permute-start(bf16[4,3072]{1,0:T(4,128)(2,1)S(1)} %shard_map.149.refs_0_), channel_id=1, source_target_pairs={{0,4},{2,6},{4,8},{6,10},{8,12},{10,14},{12,0},{14,2},{1,5},{3,7},... | collective-permute-start | bytes 73736 | tf_op jit(solution)/shard_map/ppermute | solution.py:515
  14.2 9.2 %collective-permute-start.2 = (bf16[4,3072]{1,0:T(4,128)(2,1)S(1)}, bf16[4,3072]{1,0:T(4,128)(2,1)S(1)}, u32[]{:S(2)}, u32[]{:S(2)}) collective-permute-start(bf16[4,3072]{1,0:T(4,128)(2,1)S(1)} %shard_map.149.refs_0_), channel_id=1, source_target_pairs={{0,6},{2,8},{4,10},{6,12},{8,14},{10,0},{12,2},{14,4},{1,7},{3,9},... | collective-permute-start | bytes 73736 | tf_op jit(solution)/shard_map/ppermute | solution.py:515
  16.7 6.6 %collective-permute-start.3 = (bf16[4,3072]{1,0:T(4,128)(2,1)S(1)}, bf16[4,3072]{1,0:T(4,128)(2,1)S(1)}, u32[]{:S(2)}, u32[]{:S(2)}) collective-permute-start(bf16[4,3072]{1,0:T(4,128)(2,1)S(1)} %shard_map.149.refs_0_), channel_id=1, source_target_pairs={{0,8},{2,10},{4,12},{6,14},{8,0},{10,2},{12,4},{14,6},{1,9},{3,11}... | collective-permute-start | bytes 73736 | tf_op jit(solution)/shard_map/ppermute | solution.py:515
  18.0 5.4 %collective-permute-start.4 = (bf16[4,3072]{1,0:T(4,128)(2,1)S(1)}, bf16[4,3072]{1,0:T(4,128)(2,1)S(1)}, u32[]{:S(2)}, u32[]{:S(2)}) collective-permute-start(bf16[4,3072]{1,0:T(4,128)(2,1)S(1)} %shard_map.149.refs_0_), channel_id=1, source_target_pairs={{0,10},{2,12},{4,14},{6,0},{8,2},{10,4},{12,6},{14,8},{1,11},{3,13... | collective-permute-start | bytes 73736 | tf_op jit(solution)/shard_map/ppermute | solution.py:515
  20.6 3.8 %collective-permute-start.5 = (bf16[4,3072]{1,0:T(4,128)(2,1)S(1)}, bf16[4,3072]{1,0:T(4,128)(2,1)S(1)}, u32[]{:S(2)}, u32[]{:S(2)}) collective-permute-start(bf16[4,3072]{1,0:T(4,128)(2,1)S(1)} %shard_map.149.refs_0_), channel_id=1, source_target_pairs={{0,12},{2,14},{4,0},{6,2},{8,4},{10,6},{12,8},{14,10},{1,13},{3,15... | collective-permute-start | bytes 73736 | tf_op jit(solution)/shard_map/ppermute | solution.py:515
  22.0 3.8 %collective-permute-start.6 = (bf16[4,3072]{1,0:T(4,128)(2,1)S(1)}, bf16[4,3072]{1,0:T(4,128)(2,1)S(1)}, u32[]{:S(2)}, u32[]{:S(2)}) collective-permute-start(bf16[4,3072]{1,0:T(4,128)(2,1)S(1)} %shard_map.149.refs_0_), channel_id=1, source_target_pairs={{0,14},{2,0},{4,2},{6,4},{8,6},{10,8},{12,10},{14,12},{1,15},{3,1}... | collective-permute-start | bytes 73736 | tf_op jit(solution)/shard_map/ppermute | solution.py:515
  25.8 2.3 %copy-start = (bf16[3072,768]{1,0:T(8,128)(2,1)S(1)}, bf16[3072,768]{1,0:T(8,128)(2,1)}, u32[]{:S(2)}) copy-start(bf16[3072,768]{1,0:T(8,128)(2,1)} %refs_8_.1) | copy-start | bytes 14155780
  28.1 3.2 %copy-start.6 = (bf16[32,768]{1,0:T(8,128)(2,1)S(1)}, bf16[32,768]{1,0:T(8,128)(2,1)}, u32[]{:S(2)}) copy-start(bf16[32,768]{1,0:T(8,128)(2,1)} %residual_ref.1) | copy-start | bytes 147460
  28.1 3.2 %copy-start.8 = (s32[32,4]{0,1:T(4,128)S(1)}, s32[32,4]{0,1:T(4,128)}, u32[]{:S(2)}) copy-start(s32[32,4]{0,1:T(4,128)} %param.26) | copy-start | bytes 1540
  28.1 5.5 %copy-start.13 = (f32[768]{0:T(1024)S(1)}, f32[768]{0:T(1024)}, u32[]{:S(2)}) copy-start(f32[768]{0:T(1024)} %param.22) | copy-start | bytes 9220
  28.1 29.5 %copy-start.3 = (bf16[6144,168]{0,1:T(8,128)(2,1)S(1)}, bf16[6144,168]{0,1:T(8,128)(2,1)}, u32[]{:S(2)}) copy-start(bf16[6144,168]{0,1:T(8,128)(2,1)} %param.23) | copy-start | bytes 6193156
  28.2 29.5 %copy-start.4 = (bf16[6144,168]{0,1:T(8,128)(2,1)S(1)}, bf16[6144,168]{0,1:T(8,128)(2,1)}, u32[]{:S(2)}) copy-start(bf16[6144,168]{0,1:T(8,128)(2,1)} %param.24) | copy-start | bytes 6193156
  28.2 29.5 %copy-start.11 = (f32[32,4]{0,1:T(4,128)S(1)}, f32[32,4]{0,1:T(4,128)}, u32[]{:S(2)}) copy-start(f32[32,4]{0,1:T(4,128)} %param.27) | copy-start | bytes 1540
  30.0 1.4 %collective-permute-start.7 = (f32[32,768]{1,0:T(8,128)S(1)}, f32[32,768]{1,0:T(8,128)S(1)}, u32[]{:S(2)}, u32[]{:S(2)}) collective-permute-start(f32[32,768]{1,0:T(8,128)S(1)} %shard_map.150.mine_ref), channel_id=1, source_target_pairs={{0,1},{1,0},{2,3},{3,2},{4,5},{5,4},{6,7},{7,6},{8,9},{9,8},{10,11... | collective-permute-start | bytes 294920 | tf_op jit(solution)/shard_map/ppermute | solution.py:519
  32.0 20.3 %collective-permute-start.8 = (bf16[16,768]{1,0:T(8,128)(2,1)S(1)}, bf16[16,768]{1,0:T(8,128)(2,1)S(1)}, u32[]{:S(2)}, u32[]{:S(2)}) collective-permute-start(bf16[16,768]{1,0:T(8,128)(2,1)S(1)} %get-tuple-element.21), channel_id=1, source_target_pairs={{0,2},{2,4},{4,6},{6,8},{8,10},{10,12},{12,14},{14,0},{1,3},{3,5},... | collective-permute-start | bytes 73736 | tf_op jit(solution)/shard_map/ppermute | solution.py:515
  33.5 20.4 %collective-permute-start.9 = (bf16[16,768]{1,0:T(8,128)(2,1)S(1)}, bf16[16,768]{1,0:T(8,128)(2,1)S(1)}, u32[]{:S(2)}, u32[]{:S(2)}) collective-permute-start(bf16[16,768]{1,0:T(8,128)(2,1)S(1)} %get-tuple-element.22), channel_id=1, source_target_pairs={{0,4},{2,6},{4,8},{6,10},{8,12},{10,14},{12,0},{14,2},{1,5},{3,7},... | collective-permute-start | bytes 73736 | tf_op jit(solution)/shard_map/ppermute | solution.py:515
  33.6 6.3 %collective-permute-start.15 = (f32[1,768]{1,0:T(1,128)S(1)}, f32[1,768]{1,0:T(1,128)S(1)}, u32[]{:S(2)}, u32[]{:S(2)}) collective-permute-start(f32[1,768]{1,0:T(1,128)S(1)} %reshape.11.refs_8_), channel_id=1, source_target_pairs={{0,2},{2,4},{4,6},{6,8},{8,10},{10,12},{12,14},{14,0},{1,3},{3,5},... | collective-permute-start | bytes 9224 | tf_op jit(solution)/shard_map/ppermute | solution.py:515
  34.3 7.4 %collective-permute-start.16 = (f32[1,768]{1,0:T(1,128)S(1)}, f32[1,768]{1,0:T(1,128)S(1)}, u32[]{:S(2)}, u32[]{:S(2)}) collective-permute-start(f32[1,768]{1,0:T(1,128)S(1)} %reshape.11.refs_8_), channel_id=1, source_target_pairs={{0,4},{2,6},{4,8},{6,10},{8,12},{10,14},{12,0},{14,2},{1,5},{3,7},... | collective-permute-start | bytes 9224 | tf_op jit(solution)/shard_map/ppermute | solution.py:515
  36.4 6.0 %collective-permute-start.17 = (f32[1,768]{1,0:T(1,128)S(1)}, f32[1,768]{1,0:T(1,128)S(1)}, u32[]{:S(2)}, u32[]{:S(2)}) collective-permute-start(f32[1,768]{1,0:T(1,128)S(1)} %reshape.11.refs_8_), channel_id=1, source_target_pairs={{0,6},{2,8},{4,10},{6,12},{8,14},{10,0},{12,2},{14,4},{1,7},{3,9},... | collective-permute-start | bytes 9224 | tf_op jit(solution)/shard_map/ppermute | solution.py:515
  39.9 4.7 %collective-permute-start.18 = (f32[1,768]{1,0:T(1,128)S(1)}, f32[1,768]{1,0:T(1,128)S(1)}, u32[]{:S(2)}, u32[]{:S(2)}) collective-permute-start(f32[1,768]{1,0:T(1,128)S(1)} %reshape.11.refs_8_), channel_id=1, source_target_pairs={{0,8},{2,10},{4,12},{6,14},{8,0},{10,2},{12,4},{14,6},{1,9},{3,11}... | collective-permute-start | bytes 9224 | tf_op jit(solution)/shard_map/ppermute | solution.py:515
  41.7 5.2 %collective-permute-start.19 = (f32[1,768]{1,0:T(1,128)S(1)}, f32[1,768]{1,0:T(1,128)S(1)}, u32[]{:S(2)}, u32[]{:S(2)}) collective-permute-start(f32[1,768]{1,0:T(1,128)S(1)} %reshape.11.refs_8_), channel_id=1, source_target_pairs={{0,10},{2,12},{4,14},{6,0},{8,2},{10,4},{12,6},{14,8},{1,11},{3,13... | collective-permute-start | bytes 9224 | tf_op jit(solution)/shard_map/ppermute | solution.py:515
  42.4 5.3 %collective-permute-start.20 = (f32[1,768]{1,0:T(1,128)S(1)}, f32[1,768]{1,0:T(1,128)S(1)}, u32[]{:S(2)}, u32[]{:S(2)}) collective-permute-start(f32[1,768]{1,0:T(1,128)S(1)} %reshape.11.refs_8_), channel_id=1, source_target_pairs={{0,12},{2,14},{4,0},{6,2},{8,4},{10,6},{12,8},{14,10},{1,13},{3,15... | collective-permute-start | bytes 9224 | tf_op jit(solution)/shard_map/ppermute | solution.py:515
  44.6 4.4 %collective-permute-start.21 = (f32[1,768]{1,0:T(1,128)S(1)}, f32[1,768]{1,0:T(1,128)S(1)}, u32[]{:S(2)}, u32[]{:S(2)}) collective-permute-start(f32[1,768]{1,0:T(1,128)S(1)} %reshape.11.refs_8_), channel_id=1, source_target_pairs={{0,14},{2,0},{4,2},{6,4},{8,6},{10,8},{12,10},{14,12},{1,15},{3,1}... | collective-permute-start | bytes 9224 | tf_op jit(solution)/shard_map/ppermute | solution.py:515
  46.9 7.6 %collective-permute-start.10 = (bf16[16,768]{1,0:T(8,128)(2,1)S(1)}, bf16[16,768]{1,0:T(8,128)(2,1)S(1)}, u32[]{:S(2)}, u32[]{:S(2)}) collective-permute-start(bf16[16,768]{1,0:T(8,128)(2,1)S(1)} %get-tuple-element.23), channel_id=1, source_target_pairs={{0,6},{2,8},{4,10},{6,12},{8,14},{10,0},{12,2},{14,4},{1,7},{3,9},... | collective-permute-start | bytes 73736 | tf_op jit(solution)/shard_map/ppermute | solution.py:515
  47.7 6.8 %collective-permute-start.11 = (bf16[16,768]{1,0:T(8,128)(2,1)S(1)}, bf16[16,768]{1,0:T(8,128)(2,1)S(1)}, u32[]{:S(2)}, u32[]{:S(2)}) collective-permute-start(bf16[16,768]{1,0:T(8,128)(2,1)S(1)} %get-tuple-element.24), channel_id=1, source_target_pairs={{0,8},{2,10},{4,12},{6,14},{8,0},{10,2},{12,4},{14,6},{1,9},{3,11}... | collective-permute-start | bytes 73736 | tf_op jit(solution)/shard_map/ppermute | solution.py:515
  49.0 5.5 %collective-permute-start.12 = (bf16[16,768]{1,0:T(8,128)(2,1)S(1)}, bf16[16,768]{1,0:T(8,128)(2,1)S(1)}, u32[]{:S(2)}, u32[]{:S(2)}) collective-permute-start(bf16[16,768]{1,0:T(8,128)(2,1)S(1)} %get-tuple-element.25), channel_id=1, source_target_pairs={{0,10},{2,12},{4,14},{6,0},{8,2},{10,4},{12,6},{14,8},{1,11},{3,13... | collective-permute-start | bytes 73736 | tf_op jit(solution)/shard_map/ppermute | solution.py:515
  52.3 3.8 %collective-permute-start.13 = (bf16[16,768]{1,0:T(8,128)(2,1)S(1)}, bf16[16,768]{1,0:T(8,128)(2,1)S(1)}, u32[]{:S(2)}, u32[]{:S(2)}) collective-permute-start(bf16[16,768]{1,0:T(8,128)(2,1)S(1)} %get-tuple-element.26), channel_id=1, source_target_pairs={{0,12},{2,14},{4,0},{6,2},{8,4},{10,6},{12,8},{14,10},{1,13},{3,15... | collective-permute-start | bytes 73736 | tf_op jit(solution)/shard_map/ppermute | solution.py:515
  53.9 3.8 %collective-permute-start.14 = (bf16[16,768]{1,0:T(8,128)(2,1)S(1)}, bf16[16,768]{1,0:T(8,128)(2,1)S(1)}, u32[]{:S(2)}, u32[]{:S(2)}) collective-permute-start(bf16[16,768]{1,0:T(8,128)(2,1)S(1)} %get-tuple-element.27), channel_id=1, source_target_pairs={{0,14},{2,0},{4,2},{6,4},{8,6},{10,8},{12,10},{14,12},{1,15},{3,1}... | collective-permute-start | bytes 73736 | tf_op jit(solution)/shard_map/ppermute | solution.py:515
  62.8 8.3 %collective-permute-start.22 = (bf16[16,768]{1,0:T(8,128)(2,1)S(1)}, bf16[16,768]{1,0:T(8,128)(2,1)S(1)}, u32[]{:S(2)}, u32[]{:S(2)}) collective-permute-start(bf16[16,768]{1,0:T(8,128)(2,1)S(1)} %get-tuple-element.29), channel_id=1, source_target_pairs={{0,2},{2,4},{4,6},{6,8},{8,10},{10,12},{12,14},{14,0},{1,3},{3,5},... | collective-permute-start | bytes 73736 | tf_op jit(solution)/shard_map/ppermute | solution.py:515
  63.8 7.7 %collective-permute-start.23 = (bf16[16,768]{1,0:T(8,128)(2,1)S(1)}, bf16[16,768]{1,0:T(8,128)(2,1)S(1)}, u32[]{:S(2)}, u32[]{:S(2)}) collective-permute-start(bf16[16,768]{1,0:T(8,128)(2,1)S(1)} %get-tuple-element.30), channel_id=1, source_target_pairs={{0,4},{2,6},{4,8},{6,10},{8,12},{10,14},{12,0},{14,2},{1,5},{3,7},... | collective-permute-start | bytes 73736 | tf_op jit(solution)/shard_map/ppermute | solution.py:515
  64.6 9.4 %collective-permute-start.24 = (bf16[16,768]{1,0:T(8,128)(2,1)S(1)}, bf16[16,768]{1,0:T(8,128)(2,1)S(1)}, u32[]{:S(2)}, u32[]{:S(2)}) collective-permute-start(bf16[16,768]{1,0:T(8,128)(2,1)S(1)} %get-tuple-element.31), channel_id=1, source_target_pairs={{0,6},{2,8},{4,10},{6,12},{8,14},{10,0},{12,2},{14,4},{1,7},{3,9},... | collective-permute-start | bytes 73736 | tf_op jit(solution)/shard_map/ppermute | solution.py:515
  66.7 7.3 %collective-permute-start.25 = (bf16[16,768]{1,0:T(8,128)(2,1)S(1)}, bf16[16,768]{1,0:T(8,128)(2,1)S(1)}, u32[]{:S(2)}, u32[]{:S(2)}) collective-permute-start(bf16[16,768]{1,0:T(8,128)(2,1)S(1)} %get-tuple-element.32), channel_id=1, source_target_pairs={{0,8},{2,10},{4,12},{6,14},{8,0},{10,2},{12,4},{14,6},{1,9},{3,11}... | collective-permute-start | bytes 73736 | tf_op jit(solution)/shard_map/ppermute | solution.py:515
  68.6 5.4 %collective-permute-start.26 = (bf16[16,768]{1,0:T(8,128)(2,1)S(1)}, bf16[16,768]{1,0:T(8,128)(2,1)S(1)}, u32[]{:S(2)}, u32[]{:S(2)}) collective-permute-start(bf16[16,768]{1,0:T(8,128)(2,1)S(1)} %get-tuple-element.33), channel_id=1, source_target_pairs={{0,10},{2,12},{4,14},{6,0},{8,2},{10,4},{12,6},{14,8},{1,11},{3,13... | collective-permute-start | bytes 73736 | tf_op jit(solution)/shard_map/ppermute | solution.py:515
  71.2 3.8 %collective-permute-start.27 = (bf16[16,768]{1,0:T(8,128)(2,1)S(1)}, bf16[16,768]{1,0:T(8,128)(2,1)S(1)}, u32[]{:S(2)}, u32[]{:S(2)}) collective-permute-start(bf16[16,768]{1,0:T(8,128)(2,1)S(1)} %get-tuple-element.34), channel_id=1, source_target_pairs={{0,12},{2,14},{4,0},{6,2},{8,4},{10,6},{12,8},{14,10},{1,13},{3,15... | collective-permute-start | bytes 73736 | tf_op jit(solution)/shard_map/ppermute | solution.py:515
  71.5 4.1 %collective-permute-start.28 = (bf16[16,768]{1,0:T(8,128)(2,1)S(1)}, bf16[16,768]{1,0:T(8,128)(2,1)S(1)}, u32[]{:S(2)}, u32[]{:S(2)}) collective-permute-start(bf16[16,768]{1,0:T(8,128)(2,1)S(1)} %get-tuple-element.35), channel_id=1, source_target_pairs={{0,14},{2,0},{4,2},{6,4},{8,6},{10,8},{12,10},{14,12},{1,15},{3,1}... | collective-permute-start | bytes 73736 | tf_op jit(solution)/shard_map/ppermute | solution.py:515
  75.9 1.4 %collective-permute-start.29 = (f32[32,768]{1,0:T(8,128)S(1)}, f32[32,768]{1,0:T(8,128)S(1)}, u32[]{:S(2)}, u32[]{:S(2)}) collective-permute-start(f32[32,768]{1,0:T(8,128)S(1)} %shard_map.153), channel_id=1, source_target_pairs={{0,1},{1,0},{2,3},{3,2},{4,5},{5,4},{6,7},{7,6},{8,9},{9,8},{10,11... | collective-permute-start | bytes 294920 | tf_op jit(solution)/shard_map/ppermute | solution.py:519

commit v3 on v2

--- a/solution.py
+++ b/solution.py
@@ -157,7 +157,7 @@
 MIB = 1024 * 1024
 VMEM_SPEC = pl.BlockSpec(memory_space=pltpu.VMEM)
 SMEM_SPEC = pl.BlockSpec(memory_space=pltpu.SMEM)
-ANY_SPEC = pl.BlockSpec(memory_space=pl.ANY)
+HBM_SPEC = pl.BlockSpec(memory_space=pltpu.HBM)
 
 
 def call(kernel, outs, in_specs, scratch, flops, nbytes, vmem_mib):
@@ -174,8 +174,9 @@
 
 
 def attend_kernel(
-    length_ref, query_ref, key_hbm, value_hbm, own_key_ref, own_value_ref, out_ref,
-    key_buf, value_buf, query_rows, key_rows, value_rows, result_rows, key_sem, value_sem,
+    length_ref, query_hbm, key_hbm, value_hbm, own_key_hbm, own_value_hbm, gain_hbm, out_ref,
+    query_ref, key_buf, value_buf, own_key_ref, own_value_ref, gain_ref,
+    query_rows, key_rows, value_rows, result_rows, key_sem, value_sem, small_sem,
 ):
     row_count, length_max = key_hbm.shape[0], key_hbm.shape[1]
     kv_local = own_key_ref.shape[1] // HEAD_DIM
@@ -188,8 +189,21 @@
         pltpu.make_async_copy(value_hbm.at[r], value_buf.at[r], value_sem.at[r])
         for r in range(row_count)
     ]
-    for copy in key_copies + value_copies:
+    small_copies = [
+        pltpu.make_async_copy(source, target, small_sem.at[index])
+        for index, (source, target) in enumerate(
+            (
+                (query_hbm, query_ref),
+                (own_key_hbm, own_key_ref),
+                (own_value_hbm, own_value_ref),
+                (gain_hbm, gain_ref),
+            )
+        )
+    ]
+    for copy in small_copies + key_copies + value_copies:
         copy.start()
+    for copy in small_copies:
+        copy.wait()
     for g in range(kv_local):
         lanes = slice(g * HEAD_DIM, (g + 1) * HEAD_DIM)
         own_key = own_key_ref[:, lanes].astype(jnp.float32)
@@ -260,36 +274,48 @@
         upper = sums[p][block:, HEAD_DIM:] + own_part[block:]
         result_rows[pl.ds(p * pair_rows, block), :] = lower
         result_rows[pl.ds(p * pair_rows + block, block), :] = upper
+    width = query_hbm.shape[1]
     for head in range(kv_local * group):
-        out_ref[:, head * HEAD_DIM : (head + 1) * HEAD_DIM] = result_rows[
-            pl.ds(head * row_count, row_count), :
-        ].astype(jnp.bfloat16)
-
-
-def attend(queries, key_cache, value_cache, new_key, new_value, cache_length):
-    row_count = queries.shape[0]
-    heads = queries.shape[1] // HEAD_DIM
+        rows = result_rows[pl.ds(head * row_count, row_count), :].astype(jnp.bfloat16)
+        for index in range(out_ref.shape[0]):
+            out_ref[index, :, head * HEAD_DIM : (head + 1) * HEAD_DIM] = rows
+    half = gain_ref.shape[1] // 2
+    row = lax.broadcasted_iota(jnp.int32, (row_count, half), 0)
+    left = jnp.broadcast_to(gain_ref[:, :half], (row_count, half))
+    right = jnp.broadcast_to(gain_ref[:, half:], (row_count, half))
+    gain = jnp.where(row % 2 == 0, left, right)
+    upper = gain.astype(jnp.bfloat16).astype(jnp.float32)
+    parts = jnp.where(row < 2, upper, gain - upper).astype(jnp.bfloat16)
+    for index in range(out_ref.shape[0]):
+        out_ref[index, :, width:] = parts
+
+
+def attend(count, queries, key_cache, value_cache, new_key, new_value, cache_length, gain):
+    row_count, width = queries.shape
+    heads = width // HEAD_DIM
     table = pltpu.VMEM((heads * row_count, HEAD_DIM), jnp.float32)
     nbytes = 2 * key_cache.size * 2
     return call(
         attend_kernel,
-        jax.ShapeDtypeStruct(queries.shape, jnp.bfloat16),
-        [SMEM_SPEC, VMEM_SPEC, ANY_SPEC, ANY_SPEC, VMEM_SPEC, VMEM_SPEC],
+        jax.ShapeDtypeStruct((count, row_count, width + gain.shape[1] // 2), jnp.bfloat16),
+        [SMEM_SPEC] + [HBM_SPEC] * 6,
         [
+            pltpu.VMEM(queries.shape, jnp.bfloat16),
             pltpu.VMEM(key_cache.shape, jnp.bfloat16),
             pltpu.VMEM(value_cache.shape, jnp.bfloat16),
+            pltpu.VMEM(new_key.shape, jnp.bfloat16),
+            pltpu.VMEM(new_value.shape, jnp.bfloat16),
+            pltpu.VMEM(gain.shape, jnp.float32),
             table, table, table, table,
             pltpu.SemaphoreType.DMA((row_count,)),
             pltpu.SemaphoreType.DMA((row_count,)),
+            pltpu.SemaphoreType.DMA((4,)),
         ],
         4 * key_cache.size * 6, nbytes, 12,
-    )(cache_length, queries, key_cache, value_cache, new_key, new_value)
-
-
-def project_kernel(count, chunks, place_ref, *refs):
-    pieces, weight_hbm, out_ref, stack, weight_buf, sem = (
-        refs[:count], refs[count], refs[count + 1], refs[count + 2], refs[count + 3], refs[count + 4],
-    )
+    )(cache_length, queries, key_cache, value_cache, new_key, new_value, gain)
+
+
+def project_kernel(chunks, pieces, weight_hbm, out_ref, gain_ref, stack, weight_buf, sem):
     height = weight_hbm.shape[0] // chunks
     copies = [
         pltpu.make_async_copy(
@@ -301,24 +327,19 @@
     ]
     for copy in copies:
         copy.start()
-    rows = pieces[0].shape[0]
-    total = rows * count
+    count, rows, _ = pieces.shape
+    width = weight_hbm.shape[0]
+    half = gain_ref.shape[1] // 2
     for k in range(count):
-        stack[pl.ds(k * rows, rows), :] = pieces[k][...].astype(jnp.float32)
-    place = place_ref[0]
-    target = lax.broadcasted_iota(jnp.int32, (total, total), 0)
-    source = lax.broadcasted_iota(jnp.int32, (total, total), 1)
-    owner = place - source // rows
-    owner = jnp.where(owner < 0, owner + count, owner)
-    order = (target == owner * rows + source % rows).astype(jnp.bfloat16)
-    whole = jnp.dot(
-        order, stack[...].astype(jnp.bfloat16), preferred_element_type=jnp.float32
-    ).astype(jnp.bfloat16)
+        stack[pl.ds(k * rows, rows), :] = pieces[k, :, :width].astype(jnp.float32)
+        parts = pieces[k, :, width:].astype(jnp.float32)
+        gain_ref[pl.ds(k, 1), :half] = parts[0:1] + parts[2:3]
+        gain_ref[pl.ds(k, 1), half:] = parts[1:2] + parts[3:4]
     result = None
     for c in range(chunks):
         copies[c].wait()
         part = jnp.dot(
-            whole[:, c * height : (c + 1) * height],
+            stack[:, pl.ds(c * height, height)].astype(jnp.bfloat16),
             weight_buf[pl.ds(c * height, height), :],
             preferred_element_type=jnp.float32,
         )
@@ -326,22 +347,24 @@
     out_ref[...] = result
 
 
-def project(place, pieces, out_weight):
-    count = len(pieces)
-    rows, depth = pieces[0].shape
-    cols = out_weight.shape[1]
+def project(pieces, out_weight):
+    count, rows, _ = pieces.shape
+    depth, cols = out_weight.shape
     chunks = 6
     return call(
-        functools.partial(project_kernel, count, chunks),
-        jax.ShapeDtypeStruct((rows * count, cols), jnp.float32),
-        [SMEM_SPEC] + [VMEM_SPEC] * count + [ANY_SPEC],
+        functools.partial(project_kernel, chunks),
+        [
+            jax.ShapeDtypeStruct((rows * count, cols), jnp.float32),
+            jax.ShapeDtypeStruct((count, cols), jnp.float32),
+        ],
+        [VMEM_SPEC, HBM_SPEC],
         [
             pltpu.VMEM((rows * count, depth), jnp.float32),
             pltpu.VMEM(out_weight.shape, jnp.bfloat16),
             pltpu.SemaphoreType.DMA((chunks,)),
         ],
         2 * rows * count * out_weight.size, out_weight.size * 2, 10,
-    )(place, *pieces, out_weight)
+    )(pieces, out_weight)
 
 
 def expert_rows(routes, expert, capacity):
@@ -359,13 +382,8 @@
     return jnp.where((slot == place) & (hit > 0.5), 1.0, 0.0)
 
 
-def wrapped(value, count):
-    value = jnp.where(value < 0, value + count, value)
-    return jnp.where(value >= count, value - count, value)
-
-
-def pick_kernel(count, cores, capacity, place_ref, mine_ref, other_ref, residual_ref, routes_ref,
-                stream_ref, *out_refs):
+def pick_kernel(cores, mine_ref, other_ref, residual_ref, routes_ref, stream_ref, out_ref):
+    count, capacity, _ = out_ref.shape
     stream = (
         residual_ref[...].astype(jnp.float32) + (mine_ref[...] + other_ref[...])
     ).astype(jnp.bfloat16)
@@ -376,50 +394,42 @@
             expert_rows(routes, e, capacity).astype(jnp.bfloat16),
             stream,
             preferred_element_type=jnp.float32,
-        )
+        ).astype(jnp.bfloat16)
         for e in range(HELD)
     ]
     sharers = count * cores // HELD
     for k in range(count):
-        dest = wrapped(place_ref[0] + k, count)
-        out_refs[k][...] = jnp.where(
-            dest * cores < sharers, chosen[0], chosen[1]
-        ).astype(jnp.bfloat16)
-
-
-def pick(place, cores, count, capacity, mine, other, residual, routes):
+        out_ref[k] = chosen[k * cores // sharers]
+
+
+def pick(cores, count, capacity, mine, other, residual, routes):
     rows, cols = mine.shape
     return call(
-        functools.partial(pick_kernel, count, cores, capacity),
-        [jax.ShapeDtypeStruct((rows, cols), jnp.bfloat16)]
-        + [jax.ShapeDtypeStruct((capacity, cols), jnp.bfloat16)] * count,
-        [SMEM_SPEC] + [VMEM_SPEC] * 4,
+        functools.partial(pick_kernel, cores),
+        [
+            jax.ShapeDtypeStruct((rows, cols), jnp.bfloat16),
+            jax.ShapeDtypeStruct((count, capacity, cols), jnp.bfloat16),
+        ],
+        [VMEM_SPEC] * 4,
         [],
         2 * HELD * capacity * rows * cols, rows * cols * 12, 4,
-    )(place, mine, other, residual, routes)
-
-
-def expert_kernel(count, cores, place_ref, routes_ref, weight_ref, *refs):
-    pieces, gains = refs[:count], refs[count : 2 * count]
-    gate_hbm, up_hbm, down_hbm = refs[2 * count : 2 * count + 3]
-    outs = refs[2 * count + 3 : 3 * count + 3]
-    gate_buf, up_buf, down_buf, sem = refs[3 * count + 3 :]
-    capacity, cols = pieces[0].shape
-    place = place_ref[0]
-    copies = []
+    )(mine, other, residual, routes)
+
+
+def expert_kernel(cores, place_ref, routes_ref, weight_ref, pieces, gains, gate_hbm, up_hbm,
+                  down_hbm, out_ref, gate_buf, up_buf, down_buf, sem):
+    count, capacity, cols = pieces.shape
+    copies, returns = [], []
     for k in range(count):
-        source = pl.ds(pl.multiple_of(wrapped(place - k, count) * cols, 128), cols)
+        block = pl.ds(k * cols, cols)
         copies.append(
             (
-                pltpu.make_async_copy(gate_hbm.at[:, source], gate_buf.at[k], sem.at[0, k]),
-                pltpu.make_async_copy(up_hbm.at[:, source], up_buf.at[k], sem.at[1, k]),
+                pltpu.make_async_copy(gate_hbm.at[:, block], gate_buf.at[k], sem.at[0, k]),
+                pltpu.make_async_copy(up_hbm.at[:, block], up_buf.at[k], sem.at[1, k]),
             )
         )
-    returns = []
-    for k in range(count):
-        target = pl.ds(pl.multiple_of(wrapped(place + k, count) * cols, 128), cols)
         returns.append(
-            pltpu.make_async_copy(down_hbm.at[:, target], down_buf.at[k], sem.at[2, k])
+            pltpu.make_async_copy(down_hbm.at[:, block], down_buf.at[k], sem.at[2, k])
         )
     for pair in copies:
         pair[0].start()
@@ -427,92 +437,83 @@
     for copy in returns:
         copy.start()
     sharers = count * cores // HELD
-    expert = jnp.where(place * cores < sharers, 0, 1)
+    expert = jnp.where(place_ref[0] * cores < sharers, 0, 1)
     routes = routes_ref[...]
     taken = expert_rows(routes, expert, capacity)
     row_weight = jnp.sum(
         jnp.where(routes == expert, weight_ref[...], 0.0), axis=0, keepdims=True
     )
     slot_weight = jnp.sum(taken * row_weight, axis=1, keepdims=True)
-    wide = [piece[...].astype(jnp.float32) for piece in pieces]
-    first = wide[0]
-    second = wide[0] * wide[0]
-    for value in wide[1:]:
-        first = first + value
-        second = second + value * value
+    first = second = 0.0
+    for k in range(count):
+        wide = pieces[k].astype(jnp.float32)
+        first = first + wide
+        second = second + wide * wide
     row_mean = jnp.sum(first, axis=1, keepdims=True) / D
     row_var = jnp.sum(second, axis=1, keepdims=True) / D - row_mean * row_mean
     inverse = lax.rsqrt(row_var + EPSILON)
     contract = (((1,), (1,)), ((), ()))
-    gate_val = up_val = None
+    gate_val = up_val = 0.0
     for k in range(count):
-        normed = ((wide[k] - row_mean) * inverse * gains[k][...]).astype(jnp.bfloat16)
+        wide = pieces[k].astype(jnp.float32)
+        normed = ((wide - row_mean) * inverse * gains[pl.ds(k, 1), :]).astype(jnp.bfloat16)
         copies[k][0].wait()
-        gate_part = lax.dot_general(
-            normed, gate_buf[k], contract, preferred_element_type=jnp.float32
+        gate_val = gate_val + lax.dot_general(
+            gate_buf[k], normed, contract, preferred_element_type=jnp.float32
         )
         copies[k][1].wait()
-        up_part = lax.dot_general(
-            normed, up_buf[k], contract, preferred_element_type=jnp.float32
-        )
-        gate_val = gate_part if gate_val is None else gate_val + gate_part
-        up_val = up_part if up_val is None else up_val + up_part
-    hidden = (gate_val / (1.0 + jnp.exp(-gate_val)) * up_val).astype(jnp.bfloat16)
+        up_val = up_val + lax.dot_general(
+            up_buf[k], normed, contract, preferred_element_type=jnp.float32
+        )
+    hidden = (gate_val / (1.0 + jnp.exp(-gate_val)) * up_val).T.astype(jnp.bfloat16)
     for k in range(count):
         returns[k].wait()
-        outs[k][...] = (
+        out_ref[k] = (
             jnp.dot(hidden, down_buf[k], preferred_element_type=jnp.float32) * slot_weight
         ).astype(jnp.bfloat16)
 
 
 def run_experts(place, cores, routes, route_weight, pieces, gains, gate, up, down):
-    count = len(pieces)
-    capacity, cols = pieces[0].shape
+    count, capacity, cols = pieces.shape
     hidden = gate.shape[0]
     buf = pltpu.VMEM((count, hidden, cols), jnp.bfloat16)
     return call(
-        functools.partial(expert_kernel, count, cores),
-        [jax.ShapeDtypeStruct((capacity, cols), jnp.bfloat16)] * count,
-        [SMEM_SPEC] + [VMEM_SPEC] * (2 + 2 * count) + [ANY_SPEC] * 3,
+        functools.partial(expert_kernel, cores),
+        jax.ShapeDtypeStruct((count, capacity, cols), jnp.bfloat16),
+        [SMEM_SPEC] + [VMEM_SPEC] * 4 + [HBM_SPEC] * 3,
         [buf, buf, buf, pltpu.SemaphoreType.DMA((3, count))],
         6 * capacity * gate.size, gate.size * 6, 14,
-    )(place, routes, route_weight, *pieces, *gains, gate, up, down)
-
-
-def combine_kernel(count, cores, place_ref, routes_ref, *refs):
-    pieces, out_ref = refs[:count], refs[count]
-    capacity = pieces[0].shape[0]
+    )(place, routes, route_weight, pieces, gains, gate, up, down)
+
+
+def combine_kernel(cores, routes_ref, pieces, out_ref):
+    count, capacity, cols = pieces.shape
     sharers = count * cores // HELD
     routes = routes_ref[...]
     taken = [expert_rows(routes, e, capacity) for e in range(HELD)]
-    spread = []
-    for k in range(count):
-        source = wrapped(place_ref[0] - k, count)
-        spread.append(jnp.where(source * cores < sharers, taken[0], taken[1]))
+    spread = [taken[k * cores // sharers] for k in range(count)]
     out_ref[...] = lax.dot_general(
         jnp.concatenate(spread, axis=0).astype(jnp.bfloat16),
-        jnp.concatenate([piece[...] for piece in pieces], axis=0),
+        pieces[...].reshape(count * capacity, cols),
         (((0,), (0,)), ((), ())),
         preferred_element_type=jnp.float32,
     )
 
 
-def combine(place, cores, routes, pieces):
-    count = len(pieces)
-    capacity, cols = pieces[0].shape
+def combine(cores, routes, pieces):
+    count, capacity, cols = pieces.shape
     rows = routes.shape[1]
     return call(
-        functools.partial(combine_kernel, count, cores),
+        functools.partial(combine_kernel, cores),
         jax.ShapeDtypeStruct((rows, cols), jnp.float32),
-        [SMEM_SPEC] + [VMEM_SPEC] * (1 + count),
+        [VMEM_SPEC] * 2,
         [],
         2 * rows * capacity * count * cols, (count * capacity * 2 + rows * 4) * cols, 4,
-    )(place, routes, *pieces)
-
-
-def shifted(block, count, distance):
-    pairs = [(index, (index + distance) % count) for index in range(count)]
-    return lax.ppermute(block, "attn", pairs)
+    )(routes, pieces)
+
+
+def exchange(blocks):
+    return lax.all_to_all(blocks, "attn", split_axis=0, concat_axis=0, tiled=True)
 
 
 def swap(block):
@@ -537,29 +538,24 @@
 ):
     count = lax.axis_size("attn")
     cores = lax.axis_size("expert")
-    row_count = routes.shape[0]
-    capacity = row_count * TOP // EXPERTS * 2
+    capacity = routes.shape[0] * TOP // EXPERTS * 2
     place = lax.axis_index("attn").astype(jnp.int32).reshape(1)
     routes = routes.T
     route_weight = route_weight.T
 
-    gain = ln_gain.reshape(1, -1)
-    gains = [gain] + [shifted(gain, count, k) for k in range(1, count)]
-
-    attended = attend(queries, key_cache, value_cache, new_key, new_value, cache_length)
-    pieces = [attended] + [shifted(attended, count, k) for k in range(1, count)]
-    mine = project(place, pieces, out_weight)
-    other = swap(mine)
-    attn_stream, *chosen = pick(
-        place, cores, count, capacity, mine, other, residual, routes
-    )
-    rows = [chosen[0]] + [shifted(chosen[k], count, k) for k in range(1, count)]
+    attended = exchange(
+        attend(
+            count, queries, key_cache, value_cache, new_key, new_value, cache_length,
+            ln_gain.reshape(1, -1),
+        )
+    )
+    mine, gains = project(attended, out_weight)
+    attn_stream, chosen = pick(cores, count, capacity, mine, swap(mine), residual, routes)
     outgoing = run_experts(
-        place, cores, routes, route_weight, rows, gains,
+        place, cores, routes, route_weight, exchange(chosen), gains,
         gate_weight.T, up_weight.T, down_weight,
     )
-    returned = [outgoing[0]] + [shifted(outgoing[k], count, k) for k in range(1, count)]
-    combined = combine(place, cores, routes, returned)
+    combined = combine(cores, routes, exchange(outgoing))
     expert_out = (combined + swap(combined)).astype(jnp.bfloat16)
     return (attn_stream, expert_out)
 
@@ -567,7 +563,7 @@
 def solution(mesh):
     cols = D // mesh.shape["attn"]
     return jax.shard_map(
-        shards if cols % 128 == 0 else shards_plain,
+        shards if cols % 256 == 0 else shards_plain,
         mesh=mesh,
         in_specs=(
             P(("group", "attn"), "expert"),

time: 78.2 us -> 63.7 us (0.81)
  starting transfers between devices: 47 us -> 3.53 us
  blocking collectives: 0 us -> 26.1 us
  local copies, waits for them, and re-layouts: 8.31 us -> 9.82 us
  waiting for transfers between devices: 10.3 us -> 11.1 us
    ppermute x28 -> x0, starting transfers between devices: 46.9 us -> none  [shifted(): return lax.ppermute(block, 'attn', pairs)]
    all_to_all x0 -> x2, blocking collectives: none -> 26.1 us  [exchange(): lax.all_to_all(blocks, 'attn', split_axis=0, concat_axis=0, tiled=True)]
    all_to_all x0 -> x1, waiting for transfers between devices: none -> 8.48 us  [exchange(): lax.all_to_all(blocks, 'attn', split_axis=0, concat_axis=0, tiled=True)]
    ppermute x28 -> x0, waiting for transfers between devices: 7.72 us -> none  [shifted(): return lax.ppermute(block, 'attn', pairs)]
    all_to_all x0 -> x1, starting transfers between devices: none -> 3.39 us  [exchange(): lax.all_to_all(blocks, 'attn', split_axis=0, concat_axis=0, tiled=True)]
    unnamed x28 -> x26, local copies, waits for them, and re-layouts: 8.31 us -> 9.13 us
  transfers between devices with their start and end apart: 30 -> 3, of which waited for: 9 -> 3; matrix products, arithmetic and copies ran while one was open for 0% -> 0% of each run, Pallas kernels for 0% -> 0%
where the time goes in v3:
time: 63.7 us; the launch traced here: 63.1 us
  blocking collectives  26.1 us (41%)
  Pallas kernels  11.3 us (18%)
  waiting for transfers between devices  11.1 us (17%)
  local copies, waits for them, and re-layouts  9.82 us (15%)
  starting transfers between devices  3.53 us (6%)
  between operations  0.72 us (1%)
    all_to_all x2, blocking collectives, exchange(): lax.all_to_all(blocks, 'attn', split_axis=0, concat_axis=0, tiled=True)  26.1 us
    unnamed x26, local copies, waits for them, and re-layouts  9.13 us
    all_to_all x1, waiting for transfers between devices, exchange(): lax.all_to_all(blocks, 'attn', split_axis=0, concat_axis=0, tiled=True)  8.48 us
    pallas_call x1, Pallas kernels, run_experts(): call(functools.partial(expert_kernel, cores), jax.ShapeDtypeStruct((count...  5.18 us
    all_to_all x1, starting transfers between devices, exchange(): lax.all_to_all(blocks, 'attn', split_axis=0, concat_axis=0, tiled=True)  3.39 us
    pallas_call x1, Pallas kernels, attend(): call(attend_kernel, jax.ShapeDtypeStruct((count, row_count, width + gain....  3.15 us
    ppermute x2, waiting for transfers between devices, swap(): return lax.ppermute(block, 'expert', [(0, 1), (1, 0)])  2.58 us
    pallas_call x1, Pallas kernels, project(): call(functools.partial(project_kernel, chunks), [jax.ShapeDtypeStruct((ro...  1.58 us
  transfers between devices with their start and end apart: 3, of which 3 were waited for; matrix products, arithmetic and copies ran while one was open for 0% of the time, Pallas kernels for 0%

profile of v3, /device:TPU:0, one launch (start us, length us, event | category | flops | bytes accessed | tf_op | source)
XLA Modules:
  0.0 63.1 jit_solution(17270691840149652195)
XLA Ops:
  0.6 0.7 %reshape.10.gain_hbm = f32[1,768]{1,0:T(1,128)S(1)} reshape(f32[768]{0:T(1024)} %param.22) | data formatting | bytes 6144 | tf_op jit(solution)/shard_map/reshape | solution.py:549
  1.3 0.0 copy-start.1
  1.3 1.6 %copy-done.1 = bf16[4,512,512]{2,1,0:T(8,128)(2,1)S(1)} copy-done((bf16[4,512,512]{2,1,0:T(8,128)(2,1)S(1)}, bf16[4,512,512]{2,1,0:T(8,128)(2,1)}, u32[]{:S(2)}) %copy-start.1) | copy-done | bytes 2097176
  2.9 0.0 copy-start.2
  2.9 1.6 %copy-done.2 = bf16[4,512,512]{2,1,0:T(8,128)(2,1)S(1)} copy-done((bf16[4,512,512]{2,1,0:T(8,128)(2,1)S(1)}, bf16[4,512,512]{2,1,0:T(8,128)(2,1)}, u32[]{:S(2)}) %copy-start.2) | copy-done | bytes 2097176
  4.5 0.0 copy-start.7
  4.5 0.7 %copy-done.7 = bf16[4,3072]{1,0:T(4,128)(2,1)S(1)} copy-done((bf16[4,3072]{1,0:T(4,128)(2,1)S(1)}, bf16[4,3072]{1,0:T(4,128)(2,1)}, u32[]{:S(2)}) %copy-start.7) | copy-done | bytes 24600
  5.2 0.0 copy-start.9
  5.2 0.7 %copy-done.9 = bf16[4,512]{1,0:T(4,128)(2,1)S(1)} copy-done((bf16[4,512]{1,0:T(4,128)(2,1)S(1)}, bf16[4,512]{1,0:T(4,128)(2,1)}, u32[]{:S(2)}) %copy-start.9) | copy-done | bytes 4120
  5.9 0.0 copy-start.10
  5.9 0.7 %copy-done.10 = bf16[4,512]{1,0:T(4,128)(2,1)S(1)} copy-done((bf16[4,512]{1,0:T(4,128)(2,1)S(1)}, bf16[4,512]{1,0:T(4,128)(2,1)}, u32[]{:S(2)}) %copy-start.10) | copy-done | bytes 4120
  6.6 0.0 copy-start.12
  6.6 0.7 %copy-done.12 = s32[4]{0:T(128)S(1)} copy-done((s32[4]{0:T(128)S(1)}, s32[4]{0:T(128)}, u32[]{:S(2)}) %copy-start.12) | copy-done | bytes 40
  7.3 0.0 copy-start
  7.3 3.1 %shard_map.149 = bf16[8,4,3456]{2,1,0:T(4,128)(2,1)S(1)} custom-call(s32[4]{0:T(128)S(1)} %copy-done.12, bf16[4,3072]{1,0:T(4,128)(2,1)S(1)} %copy-done.7, bf16[4,512,512]{2,1,0:T(8,128)(2,1)S(1)} %copy-done.1, bf16[4,512,512]{2,1,0:T(8,128)(2,1)S(1)} %copy-done.2, bf16[4,512]{1,0:T(4,128)(2,1)S(1)} %copy-done.9, bf16[4,512]{1,0:T(4,128)(2,1)S(1)} %copy-done.10, ...), custom_call_target="tpu_custom_call" | custom-call | flops 25165824 | bytes 4194304 | tf_op jit(solution)/shard_map/pallas_call | solution.py:298
  10.4 15.4 %all_to_all.15.pieces = bf16[8,4,3456]{2,1,0:T(4,128)(2,1)S(1)} all-to-all(bf16[8,4,3456]{2,1,0:T(4,128)(2,1)S(1)} %shard_map.149), channel_id=1, replica_groups=mesh['group'=2,'attn'=8,'expert'=2] {'attn'}, dimensions={0} | all-to-all | bytes 442368 | tf_op jit(solution)/shard_map/all_to_all | solution.py:516
  25.8 0.0 copy-done
  25.8 0.0 copy-start.6
  25.8 0.0 copy-start.8
  25.8 0.0 copy-start.3
  25.8 0.0 copy-start.11
  25.9 1.6 %shard_map.150 = (f32[32,768]{1,0:T(8,128)S(1)}, f32[8,768]{1,0:T(8,128)S(1)}) custom-call(bf16[8,4,3456]{2,1,0:T(4,128)(2,1)S(1)} %all_to_all.15.pieces, bf16[3072,768]{1,0:T(8,128)(2,1)S(1)} %copy-done), custom_call_target="tpu_custom_call" | custom-call | flops 150994944 | bytes 4718592 | tf_op jit(solution)/shard_map/pallas_call | solution.py:354
  27.4 0.1 collective-permute-start
  27.5 1.3 %collective-permute-done.other_ref = f32[32,768]{1,0:T(8,128)S(1)} collective-permute-done((f32[32,768]{1,0:T(8,128)S(1)}, f32[32,768]{1,0:T(8,128)S(1)}, u32[]{:S(2)}, u32[]{:S(2)}) %collective-permute-start) | collective-permute-done | bytes 98336 | tf_op jit(solution)/shard_map/ppermute | solution.py:520
  28.8 0.0 copy-done.6
  28.8 0.0 copy-done.8
  28.8 1.1 %shard_map.151 = (bf16[32,768]{1,0:T(8,128)(2,1)}, bf16[8,16,768]{2,1,0:T(8,128)(2,1)}) custom-call(f32[32,768]{1,0:T(8,128)S(1)} %get-tuple-element.6.mine_ref, f32[32,768]{1,0:T(8,128)S(1)} %collective-permute-done.other_ref, bf16[32,768]{1,0:T(8,128)(2,1)S(1)} %copy-done.6, s32[4,32]{1,0:T(4,128)S(1)} %bitcast.7), custom_call_target="tpu_custom_call" | custom-call | flops 1572864 | bytes 294912 | tf_op jit(solution)/shard_map/pallas_call | solution.py:407
  29.9 3.4 %all-to-all-start.1 = ((bf16[8,16,768]{2,1,0:T(8,128)(2,1)}), bf16[8,16,768]{2,1,0:T(8,128)(2,1)S(1)}, u32[]{:S(2)}, u32[]{:S(2)}) async-start(bf16[8,16,768]{2,1,0:T(8,128)(2,1)} %get-tuple-element.8), calls=%async_computation.1 | async-start | bytes 393216 | tf_op jit(solution)/shard_map/all_to_all | solution.py:516
  33.3 8.5 %all-to-all-done.1.pieces = bf16[8,16,768]{2,1,0:T(8,128)(2,1)S(1)} async-done(((bf16[8,16,768]{2,1,0:T(8,128)(2,1)}), bf16[8,16,768]{2,1,0:T(8,128)(2,1)S(1)}, u32[]{:S(2)}, u32[]{:S(2)}) %all-to-all-start.1) | async-done | bytes 196640 | tf_op jit(solution)/shard_map/all_to_all | solution.py:516
  41.8 0.0 copy-done.3
  41.8 0.0 copy-done.11
  41.8 0.0 copy-start.4
  41.8 1.6 %copy-done.4 = bf16[6144,168]{0,1:T(8,128)(2,1)S(1)} copy-done((bf16[6144,168]{0,1:T(8,128)(2,1)S(1)}, bf16[6144,168]{0,1:T(8,128)(2,1)}, u32[]{:S(2)}) %copy-start.4) | copy-done | bytes 2064408
  43.3 0.0 copy-start.5
  43.3 1.6 %copy-done.5 = bf16[168,6144]{1,0:T(8,128)(2,1)S(1)} copy-done((bf16[168,6144]{1,0:T(8,128)(2,1)S(1)}, bf16[168,6144]{1,0:T(8,128)(2,1)}, u32[]{:S(2)}) %copy-start.5) | copy-done | bytes 2064408
  44.9 5.2 %shard_map.152 = bf16[8,16,768]{2,1,0:T(8,128)(2,1)S(1)} custom-call(s32[1]{0:T(128)} %bitcast.1.place_ref, s32[4,32]{1,0:T(4,128)S(1)} %bitcast.8, f32[4,32]{1,0:T(4,128)S(1)} %bitcast.10, bf16[8,16,768]{2,1,0:T(8,128)(2,1)S(1)} %all-to-all-done.1.pieces, f32[8,768]{1,0:T(8,128)S(1)} %get-tuple-element.9.gains, bf16[168,6144]{1,0:T(8,128)(2,1)S(1)} %bitcast.5, ...), custom_call_target="tpu_custom_call" | custom-call | flops 99090432 | bytes 6193152 | tf_op jit(solution)/shard_map/pallas_call | solution.py:480
  50.1 10.7 %all_to_all.16.pieces = bf16[8,16,768]{2,1,0:T(8,128)(2,1)S(1)} all-to-all(bf16[8,16,768]{2,1,0:T(8,128)(2,1)S(1)} %shard_map.152), channel_id=1, replica_groups=mesh['group'=2,'attn'=8,'expert'=2] {'attn'}, dimensions={0} | all-to-all | bytes 393216 | tf_op jit(solution)/shard_map/all_to_all | solution.py:516
  60.8 0.3 shard_map.153
  61.1 0.1 collective-permute-start.1
  61.2 1.3 %collective-permute-done.1 = f32[32,768]{1,0:T(8,128)S(1)} collective-permute-done((f32[32,768]{1,0:T(8,128)S(1)}, f32[32,768]{1,0:T(8,128)S(1)}, u32[]{:S(2)}, u32[]{:S(2)}) %collective-permute-start.1) | collective-permute-done | bytes 98336 | tf_op jit(solution)/shard_map/ppermute | solution.py:520
  62.5 0.6 %add_convert_fusion = bf16[32,768]{1,0:T(8,128)(2,1)} fusion(f32[32,768]{1,0:T(8,128)S(1)} %shard_map.153, f32[32,768]{1,0:T(8,128)S(1)} %collective-permute-done.1), kind=kLoop, calls=%fused_computation | loop fusion | flops 49152 | bytes 245760 | tf_op jit(solution)/shard_map/convert_element_type | solution.py:559
Async XLA Ops:
  1.3 1.6 %copy-start.1 = (bf16[4,512,512]{2,1,0:T(8,128)(2,1)S(1)}, bf16[4,512,512]{2,1,0:T(8,128)(2,1)}, u32[]{:S(2)}) copy-start(bf16[4,512,512]{2,1,0:T(8,128)(2,1)} %key_hbm.1) | copy-start | bytes 6291460
  2.9 1.6 %copy-start.2 = (bf16[4,512,512]{2,1,0:T(8,128)(2,1)S(1)}, bf16[4,512,512]{2,1,0:T(8,128)(2,1)}, u32[]{:S(2)}) copy-start(bf16[4,512,512]{2,1,0:T(8,128)(2,1)} %value_hbm.1) | copy-start | bytes 6291460
  4.5 0.7 %copy-start.7 = (bf16[4,3072]{1,0:T(4,128)(2,1)S(1)}, bf16[4,3072]{1,0:T(4,128)(2,1)}, u32[]{:S(2)}) copy-start(bf16[4,3072]{1,0:T(4,128)(2,1)} %query_hbm.1) | copy-start | bytes 73732
  5.2 0.7 %copy-start.9 = (bf16[4,512]{1,0:T(4,128)(2,1)S(1)}, bf16[4,512]{1,0:T(4,128)(2,1)}, u32[]{:S(2)}) copy-start(bf16[4,512]{1,0:T(4,128)(2,1)} %own_key_hbm.1) | copy-start | bytes 12292
  5.9 0.7 %copy-start.10 = (bf16[4,512]{1,0:T(4,128)(2,1)S(1)}, bf16[4,512]{1,0:T(4,128)(2,1)}, u32[]{:S(2)}) copy-start(bf16[4,512]{1,0:T(4,128)(2,1)} %own_value_hbm.1) | copy-start | bytes 12292
  6.6 0.7 %copy-start.12 = (s32[4]{0:T(128)S(1)}, s32[4]{0:T(128)}, u32[]{:S(2)}) copy-start(s32[4]{0:T(128)} %length_ref.1) | copy-start | bytes 52
  7.3 18.6 %copy-start = (bf16[3072,768]{1,0:T(8,128)(2,1)S(1)}, bf16[3072,768]{1,0:T(8,128)(2,1)}, u32[]{:S(2)}) copy-start(bf16[3072,768]{1,0:T(8,128)(2,1)} %weight_hbm.1) | copy-start | bytes 14155780
  25.8 3.0 %copy-start.6 = (bf16[32,768]{1,0:T(8,128)(2,1)S(1)}, bf16[32,768]{1,0:T(8,128)(2,1)}, u32[]{:S(2)}) copy-start(bf16[32,768]{1,0:T(8,128)(2,1)} %residual_ref.1) | copy-start | bytes 147460
  25.8 3.0 %copy-start.8 = (s32[32,4]{0,1:T(4,128)S(1)}, s32[32,4]{0,1:T(4,128)}, u32[]{:S(2)}) copy-start(s32[32,4]{0,1:T(4,128)} %param.26) | copy-start | bytes 1540
  25.8 15.9 %copy-start.3 = (bf16[6144,168]{0,1:T(8,128)(2,1)S(1)}, bf16[6144,168]{0,1:T(8,128)(2,1)}, u32[]{:S(2)}) copy-start(bf16[6144,168]{0,1:T(8,128)(2,1)} %param.23) | copy-start | bytes 6193156
  25.8 15.9 %copy-start.11 = (f32[32,4]{0,1:T(4,128)S(1)}, f32[32,4]{0,1:T(4,128)}, u32[]{:S(2)}) copy-start(f32[32,4]{0,1:T(4,128)} %param.27) | copy-start | bytes 1540
  27.4 1.4 %collective-permute-start = (f32[32,768]{1,0:T(8,128)S(1)}, f32[32,768]{1,0:T(8,128)S(1)}, u32[]{:S(2)}, u32[]{:S(2)}) collective-permute-start(f32[32,768]{1,0:T(8,128)S(1)} %get-tuple-element.6.mine_ref), channel_id=1, source_target_pairs={{0,1},{1,0},{2,3},{3,2},{4,5},{5,4},{6,7},{7,6},{8,9},{9,8},{10,11... | collective-permute-start | bytes 294920 | tf_op jit(solution)/shard_map/ppermute | solution.py:520
  29.9 11.9 %all-to-all-start.1 = ((bf16[8,16,768]{2,1,0:T(8,128)(2,1)}), bf16[8,16,768]{2,1,0:T(8,128)(2,1)S(1)}, u32[]{:S(2)}, u32[]{:S(2)}) async-start(bf16[8,16,768]{2,1,0:T(8,128)(2,1)} %get-tuple-element.8), calls=%async_computation.1 | async-start | bytes 393216 | tf_op jit(solution)/shard_map/all_to_all | solution.py:516
  41.8 1.6 %copy-start.4 = (bf16[6144,168]{0,1:T(8,128)(2,1)S(1)}, bf16[6144,168]{0,1:T(8,128)(2,1)}, u32[]{:S(2)}) copy-start(bf16[6144,168]{0,1:T(8,128)(2,1)} %param.24) | copy-start | bytes 6193156
  43.3 1.6 %copy-start.5 = (bf16[168,6144]{1,0:T(8,128)(2,1)S(1)}, bf16[168,6144]{1,0:T(8,128)(2,1)}, u32[]{:S(2)}) copy-start(bf16[168,6144]{1,0:T(8,128)(2,1)} %down_hbm.1) | copy-start | bytes 6193156
  61.1 1.4 %collective-permute-start.1 = (f32[32,768]{1,0:T(8,128)S(1)}, f32[32,768]{1,0:T(8,128)S(1)}, u32[]{:S(2)}, u32[]{:S(2)}) collective-permute-start(f32[32,768]{1,0:T(8,128)S(1)} %shard_map.153), channel_id=1, source_target_pairs={{0,1},{1,0},{2,3},{3,2},{4,5},{5,4},{6,7},{7,6},{8,9},{9,8},{10,11... | collective-permute-start | bytes 294920 | tf_op jit(solution)/shard_map/ppermute | solution.py:520

commit v4 on v3

--- a/solution.py
+++ b/solution.py
@@ -155,6 +155,8 @@
 
 
 MIB = 1024 * 1024
+ATTEND_MIB = 58_000_000 / MIB
+EXCHANGE_FLOPS = 10**10
 VMEM_SPEC = pl.BlockSpec(memory_space=pltpu.VMEM)
 SMEM_SPEC = pl.BlockSpec(memory_space=pltpu.SMEM)
 HBM_SPEC = pl.BlockSpec(memory_space=pltpu.HBM)
@@ -169,7 +171,7 @@
         out_specs=VMEM_SPEC if single else [VMEM_SPEC] * len(outs),
         scratch_shapes=scratch,
         cost_estimate=pl.CostEstimate(flops=flops, bytes_accessed=nbytes, transcendentals=0),
-        compiler_params=pltpu.CompilerParams(vmem_limit_bytes=vmem_mib * MIB),
+        compiler_params=pltpu.CompilerParams(vmem_limit_bytes=int(vmem_mib * MIB)),
     )
 
 
@@ -279,10 +281,11 @@
         rows = result_rows[pl.ds(head * row_count, row_count), :].astype(jnp.bfloat16)
         for index in range(out_ref.shape[0]):
             out_ref[index, :, head * HEAD_DIM : (head + 1) * HEAD_DIM] = rows
-    half = gain_ref.shape[1] // 2
+    gain_row = gain_ref[...].reshape(1, -1)
+    half = gain_row.shape[1] // 2
     row = lax.broadcasted_iota(jnp.int32, (row_count, half), 0)
-    left = jnp.broadcast_to(gain_ref[:, :half], (row_count, half))
-    right = jnp.broadcast_to(gain_ref[:, half:], (row_count, half))
+    left = jnp.broadcast_to(gain_row[:, :half], (row_count, half))
+    right = jnp.broadcast_to(gain_row[:, half:], (row_count, half))
     gain = jnp.where(row % 2 == 0, left, right)
     upper = gain.astype(jnp.bfloat16).astype(jnp.float32)
     parts = jnp.where(row < 2, upper, gain - upper).astype(jnp.bfloat16)
@@ -297,7 +300,7 @@
     nbytes = 2 * key_cache.size * 2
     return call(
         attend_kernel,
-        jax.ShapeDtypeStruct((count, row_count, width + gain.shape[1] // 2), jnp.bfloat16),
+        jax.ShapeDtypeStruct((count, row_count, width + gain.shape[0] // 2), jnp.bfloat16),
         [SMEM_SPEC] + [HBM_SPEC] * 6,
         [
             pltpu.VMEM(queries.shape, jnp.bfloat16),
@@ -311,58 +314,35 @@
             pltpu.SemaphoreType.DMA((row_count,)),
             pltpu.SemaphoreType.DMA((4,)),
         ],
-        4 * key_cache.size * 6, nbytes, 12,
+        4 * key_cache.size * 6, nbytes, ATTEND_MIB,
     )(cache_length, queries, key_cache, value_cache, new_key, new_value, gain)
 
 
-def project_kernel(chunks, pieces, weight_hbm, out_ref, gain_ref, stack, weight_buf, sem):
-    height = weight_hbm.shape[0] // chunks
-    copies = [
-        pltpu.make_async_copy(
-            weight_hbm.at[pl.ds(c * height, height)],
-            weight_buf.at[pl.ds(c * height, height)],
-            sem.at[c],
-        )
-        for c in range(chunks)
-    ]
-    for copy in copies:
-        copy.start()
+def project_kernel(pieces, weight_ref, out_ref, gain_ref, stack):
     count, rows, _ = pieces.shape
-    width = weight_hbm.shape[0]
+    width = weight_ref.shape[0]
     half = gain_ref.shape[1] // 2
     for k in range(count):
         stack[pl.ds(k * rows, rows), :] = pieces[k, :, :width].astype(jnp.float32)
         parts = pieces[k, :, width:].astype(jnp.float32)
         gain_ref[pl.ds(k, 1), :half] = parts[0:1] + parts[2:3]
         gain_ref[pl.ds(k, 1), half:] = parts[1:2] + parts[3:4]
-    result = None
-    for c in range(chunks):
-        copies[c].wait()
-        part = jnp.dot(
-            stack[:, pl.ds(c * height, height)].astype(jnp.bfloat16),
-            weight_buf[pl.ds(c * height, height), :],
-            preferred_element_type=jnp.float32,
-        )
-        result = part if result is None else result + part
-    out_ref[...] = result
+    out_ref[...] = jnp.dot(
+        stack[...].astype(jnp.bfloat16), weight_ref[...], preferred_element_type=jnp.float32
+    )
 
 
 def project(pieces, out_weight):
     count, rows, _ = pieces.shape
     depth, cols = out_weight.shape
-    chunks = 6
     return call(
-        functools.partial(project_kernel, chunks),
+        project_kernel,
         [
             jax.ShapeDtypeStruct((rows * count, cols), jnp.float32),
             jax.ShapeDtypeStruct((count, cols), jnp.float32),
         ],
-        [VMEM_SPEC, HBM_SPEC],
-        [
-            pltpu.VMEM((rows * count, depth), jnp.float32),
-            pltpu.VMEM(out_weight.shape, jnp.bfloat16),
-            pltpu.SemaphoreType.DMA((chunks,)),
-        ],
+        [VMEM_SPEC, VMEM_SPEC],
+        [pltpu.VMEM((rows * count, depth), jnp.float32)],
         2 * rows * count * out_weight.size, out_weight.size * 2, 10,
     )(pieces, out_weight)
 
@@ -382,68 +362,52 @@
     return jnp.where((slot == place) & (hit > 0.5), 1.0, 0.0)
 
 
-def pick_kernel(cores, mine_ref, other_ref, residual_ref, routes_ref, stream_ref, out_ref):
+def pick_kernel(cores, place_ref, mine_ref, other_ref, residual_ref, routes_ref, weight_ref,
+                stream_ref, out_ref, slot_ref):
     count, capacity, _ = out_ref.shape
     stream = (
         residual_ref[...].astype(jnp.float32) + (mine_ref[...] + other_ref[...])
     ).astype(jnp.bfloat16)
     stream_ref[...] = stream
     routes = routes_ref[...]
+    sharers = count * cores // HELD
+    taken = [expert_rows(routes, e, capacity) for e in range(HELD)]
     chosen = [
         jnp.dot(
-            expert_rows(routes, e, capacity).astype(jnp.bfloat16),
-            stream,
-            preferred_element_type=jnp.float32,
+            taken[e].astype(jnp.bfloat16), stream, preferred_element_type=jnp.float32
         ).astype(jnp.bfloat16)
         for e in range(HELD)
     ]
-    sharers = count * cores // HELD
     for k in range(count):
         out_ref[k] = chosen[k * cores // sharers]
-
-
-def pick(cores, count, capacity, mine, other, residual, routes):
+    first = place_ref[0] * cores < sharers
+    expert = jnp.where(first, 0, 1)
+    row_weight = jnp.sum(
+        jnp.where(routes == expert, weight_ref[...], 0.0), axis=0, keepdims=True
+    )
+    mine = jnp.where(first, taken[0], taken[1])
+    slot_ref[...] = jnp.broadcast_to(
+        jnp.sum(mine * row_weight, axis=1, keepdims=True), slot_ref.shape
+    )
+
+
+def pick(place, cores, count, capacity, mine, other, residual, routes, route_weight):
     rows, cols = mine.shape
     return call(
         functools.partial(pick_kernel, cores),
         [
             jax.ShapeDtypeStruct((rows, cols), jnp.bfloat16),
             jax.ShapeDtypeStruct((count, capacity, cols), jnp.bfloat16),
+            jax.ShapeDtypeStruct((capacity, 128), jnp.float32),
         ],
-        [VMEM_SPEC] * 4,
+        [SMEM_SPEC] + [VMEM_SPEC] * 5,
         [],
-        2 * HELD * capacity * rows * cols, rows * cols * 12, 4,
-    )(mine, other, residual, routes)
-
-
-def expert_kernel(cores, place_ref, routes_ref, weight_ref, pieces, gains, gate_hbm, up_hbm,
-                  down_hbm, out_ref, gate_buf, up_buf, down_buf, sem):
+        EXCHANGE_FLOPS, rows * cols * 12, 4,
+    )(place, mine, other, residual, routes, route_weight)
+
+
+def expert_kernel(slot_ref, pieces, gains, gate_ref, up_ref, down_ref, out_ref):
     count, capacity, cols = pieces.shape
-    copies, returns = [], []
-    for k in range(count):
-        block = pl.ds(k * cols, cols)
-        copies.append(
-            (
-                pltpu.make_async_copy(gate_hbm.at[:, block], gate_buf.at[k], sem.at[0, k]),
-                pltpu.make_async_copy(up_hbm.at[:, block], up_buf.at[k], sem.at[1, k]),
-            )
-        )
-        returns.append(
-            pltpu.make_async_copy(down_hbm.at[:, block], down_buf.at[k], sem.at[2, k])
-        )
-    for pair in copies:
-        pair[0].start()
-        pair[1].start()
-    for copy in returns:
-        copy.start()
-    sharers = count * cores // HELD
-    expert = jnp.where(place_ref[0] * cores < sharers, 0, 1)
-    routes = routes_ref[...]
-    taken = expert_rows(routes, expert, capacity)
-    row_weight = jnp.sum(
-        jnp.where(routes == expert, weight_ref[...], 0.0), axis=0, keepdims=True
-    )
-    slot_weight = jnp.sum(taken * row_weight, axis=1, keepdims=True)
     first = second = 0.0
     for k in range(count):
         wide = pieces[k].astype(jnp.float32)
@@ -455,35 +419,32 @@
     contract = (((1,), (1,)), ((), ()))
     gate_val = up_val = 0.0
     for k in range(count):
+        block = slice(k * cols, (k + 1) * cols)
         wide = pieces[k].astype(jnp.float32)
         normed = ((wide - row_mean) * inverse * gains[pl.ds(k, 1), :]).astype(jnp.bfloat16)
-        copies[k][0].wait()
         gate_val = gate_val + lax.dot_general(
-            gate_buf[k], normed, contract, preferred_element_type=jnp.float32
+            gate_ref[:, block], normed, contract, preferred_element_type=jnp.float32
         )
-        copies[k][1].wait()
         up_val = up_val + lax.dot_general(
-            up_buf[k], normed, contract, preferred_element_type=jnp.float32
+            up_ref[:, block], normed, contract, preferred_element_type=jnp.float32
         )
     hidden = (gate_val / (1.0 + jnp.exp(-gate_val)) * up_val).T.astype(jnp.bfloat16)
+    slot_weight = slot_ref[:, :1]
     for k in range(count):
-        returns[k].wait()
+        block = slice(k * cols, (k + 1) * cols)
         out_ref[k] = (
-            jnp.dot(hidden, down_buf[k], preferred_element_type=jnp.float32) * slot_weight
+            jnp.dot(hidden, down_ref[:, block], preferred_element_type=jnp.float32) * slot_weight
         ).astype(jnp.bfloat16)
 
 
-def run_experts(place, cores, routes, route_weight, pieces, gains, gate, up, down):
-    count, capacity, cols = pieces.shape
-    hidden = gate.shape[0]
-    buf = pltpu.VMEM((count, hidden, cols), jnp.bfloat16)
+def run_experts(slots, pieces, gains, gate, up, down):
     return call(
-        functools.partial(expert_kernel, cores),
-        jax.ShapeDtypeStruct((count, capacity, cols), jnp.bfloat16),
-        [SMEM_SPEC] + [VMEM_SPEC] * 4 + [HBM_SPEC] * 3,
-        [buf, buf, buf, pltpu.SemaphoreType.DMA((3, count))],
-        6 * capacity * gate.size, gate.size * 6, 14,
-    )(place, routes, route_weight, pieces, gains, gate, up, down)
+        expert_kernel,
+        jax.ShapeDtypeStruct(pieces.shape, jnp.bfloat16),
+        [VMEM_SPEC] * 6,
+        [],
+        6 * pieces.shape[1] * gate.size, gate.size * 6, 14,
+    )(slots, pieces, gains, gate, up, down)
 
 
 def combine_kernel(cores, routes_ref, pieces, out_ref):
@@ -546,14 +507,15 @@
     attended = exchange(
         attend(
             count, queries, key_cache, value_cache, new_key, new_value, cache_length,
-            ln_gain.reshape(1, -1),
+            ln_gain,
         )
     )
     mine, gains = project(attended, out_weight)
-    attn_stream, chosen = pick(cores, count, capacity, mine, swap(mine), residual, routes)
+    attn_stream, chosen, slots = pick(
+        place, cores, count, capacity, mine, swap(mine), residual, routes, route_weight
+    )
     outgoing = run_experts(
-        place, cores, routes, route_weight, exchange(chosen), gains,
-        gate_weight.T, up_weight.T, down_weight,
+        slots, exchange(chosen), gains, gate_weight.T, up_weight.T, down_weight
     )
     combined = combine(cores, routes, exchange(outgoing))
     expert_out = (combined + swap(combined)).astype(jnp.bfloat16)

time: 63.7 us -> 51.8 us (0.81)
  blocking collectives: 26.1 us -> 38 us
  local copies, waits for them, and re-layouts: 9.82 us -> 0.03 us
  waiting for transfers between devices: 11.1 us -> 2.57 us
  starting transfers between devices: 3.53 us -> 0.12 us
  Pallas kernels: 11.3 us -> 9.52 us
    all_to_all x2 -> x3, blocking collectives: 26.1 us -> 38 us  [exchange(): lax.all_to_all(blocks, 'attn', split_axis=0, concat_axis=0, tiled=True)]
    unnamed x26 -> x14, local copies, waits for them, and re-layouts: 9.13 us -> 0.03 us
    all_to_all x1 -> x0, waiting for transfers between devices: 8.48 us -> none  [exchange(): lax.all_to_all(blocks, 'attn', split_axis=0, concat_axis=0, tiled=True)]
    pallas_call x2, Pallas kernels: 6.76 us -> 2.75 us  [the longest x1 1.87 us: run_experts(): call(expert_kernel, jax.ShapeDtypeStruct(pieces.shape, jnp.bfloat16), [VM...]
    all_to_all x1 -> x0, starting transfers between devices: 3.39 us -> none  [exchange(): lax.all_to_all(blocks, 'attn', split_axis=0, concat_axis=0, tiled=True)]
    pallas_call x1, Pallas kernels: 3.15 us -> 5.82 us  [attend(): call(attend_kernel, jax.ShapeDtypeStruct((count, row_count, width + gain....]
    reshape x1 -> x0, local copies, waits for them, and re-layouts: 0.69 us -> none  [shards(): ln_gain.reshape(1, -1)]
  transfers between devices with their start and end apart: 3 -> 2, of which waited for: 3 -> 2; matrix products, arithmetic and copies ran while one was open for 0% -> 0% of each run, Pallas kernels for 0% -> 0%
where the time goes in v4:
time: 51.8 us; the launch traced here: 51.5 us
  blocking collectives  38 us (73%)
  Pallas kernels  9.52 us (18%)
  waiting for transfers between devices  2.57 us (5%)
  between operations  0.72 us (1%)
  other arithmetic  0.63 us (1%)
    all_to_all x3, blocking collectives, exchange(): lax.all_to_all(blocks, 'attn', split_axis=0, concat_axis=0, tiled=True)  38 us
    pallas_call x1, Pallas kernels, attend(): call(attend_kernel, jax.ShapeDtypeStruct((count, row_count, width + gain....  5.82 us
    ppermute x2, waiting for transfers between devices, swap(): return lax.ppermute(block, 'expert', [(0, 1), (1, 0)])  2.57 us
    pallas_call x1, Pallas kernels, run_experts(): call(expert_kernel, jax.ShapeDtypeStruct(pieces.shape, jnp.bfloat16), [VM...  1.87 us
  transfers between devices with their start and end apart: 2, of which 2 were waited for; matrix products, arithmetic and copies ran while one was open for 0% of the time, Pallas kernels for 0%

profile of v4, /device:TPU:0, one launch (start us, length us, event | category | flops | bytes accessed | tf_op | source)
XLA Modules:
  0.0 51.5 jit_solution(1590896940428867163)
XLA Ops:
  0.6 0.0 copy-start
  0.6 5.8 %shard_map.149 = bf16[8,4,3456]{2,1,0:T(4,128)(2,1)} custom-call(s32[4]{0:T(128)} %length_ref.1, bf16[4,3072]{1,0:T(4,128)(2,1)} %query_hbm.1, bf16[4,512,512]{2,1,0:T(8,128)(2,1)} %key_hbm.1, bf16[4,512,512]{2,1,0:T(8,128)(2,1)} %value_hbm.1, bf16[4,512]{1,0:T(4,128)(2,1)} %own_key_hbm.1, bf16[4,512]{1,0:T(4,128)(2,1)} %own_value_hbm.1, f32[768]{0:T(1024)} %gain_hbm.1), custom_call_target="tpu_custom_call" | custom-call | flops 25165824 | bytes 4194304 | tf_op jit(solution)/shard_map/pallas_call | solution.py:301
  6.5 15.6 %all_to_all.15.pieces = bf16[8,4,3456]{2,1,0:T(4,128)(2,1)S(1)} all-to-all(bf16[8,4,3456]{2,1,0:T(4,128)(2,1)} %shard_map.149), channel_id=1, replica_groups=mesh['group'=2,'attn'=8,'expert'=2] {'attn'}, dimensions={0} | all-to-all | bytes 442368 | tf_op jit(solution)/shard_map/all_to_all | solution.py:477
  22.1 0.0 copy-done
  22.1 0.0 copy-start.4
  22.1 0.0 copy-start.5
  22.1 0.0 copy-start.6
  22.1 0.9 %shard_map.150 = (f32[32,768]{1,0:T(8,128)S(1)}, f32[8,768]{1,0:T(8,128)S(1)}) custom-call(bf16[8,4,3456]{2,1,0:T(4,128)(2,1)S(1)} %all_to_all.15.pieces, bf16[3072,768]{1,0:T(8,128)(2,1)S(1)} %copy-done), custom_call_target="tpu_custom_call" | custom-call | flops 150994944 | bytes 4718592 | tf_op jit(solution)/shard_map/pallas_call | solution.py:338
  23.0 0.0 collective-permute-start
  23.0 1.3 %collective-permute-done.other_ref = f32[32,768]{1,0:T(8,128)S(1)} collective-permute-done((f32[32,768]{1,0:T(8,128)S(1)}, f32[32,768]{1,0:T(8,128)S(1)}, u32[]{:S(2)}, u32[]{:S(2)}) %collective-permute-start) | collective-permute-done | bytes 98336 | tf_op jit(solution)/shard_map/ppermute | solution.py:481
  24.3 0.0 copy-done.4
  24.3 0.0 copy-done.5
  24.3 0.0 copy-done.6
  24.3 0.0 copy-start.1
  24.3 0.0 copy-start.2
  24.4 0.0 copy-start.3
  24.4 0.6 %shard_map.151 = (bf16[32,768]{1,0:T(8,128)(2,1)}, bf16[8,16,768]{2,1,0:T(8,128)(2,1)S(1)}, f32[16,128]{1,0:T(8,128)S(1)}) custom-call(s32[1]{0:T(128)} %bitcast.place_ref, f32[32,768]{1,0:T(8,128)S(1)} %get-tuple-element.7.mine_ref, f32[32,768]{1,0:T(8,128)S(1)} %collective-permute-done.other_ref, bf16[32,768]{1,0:T(8,128)(2,1)S(1)} %copy-done.5, ...), custom_call_target="tpu_custom_call" | custom-call | flops 10000000000 | bytes 294912 | tf_op jit(solution)/shard_map/pallas_call | solution.py:396
  25.0 11.6 %all_to_all.16.pieces = bf16[8,16,768]{2,1,0:T(8,128)(2,1)S(1)} all-to-all(bf16[8,16,768]{2,1,0:T(8,128)(2,1)S(1)} %get-tuple-element.10), channel_id=1, replica_groups=mesh['group'=2,'attn'=8,'expert'=2] {'attn'}, dimensions={0} | all-to-all | bytes 393216 | tf_op jit(solution)/shard_map/all_to_all | solution.py:477
  36.6 0.0 copy-done.1
  36.6 0.0 copy-done.2
  36.6 0.0 copy-done.3
  36.7 1.9 %shard_map.152 = bf16[8,16,768]{2,1,0:T(8,128)(2,1)S(1)} custom-call(f32[16,128]{1,0:T(8,128)S(1)} %get-tuple-element.9.slot_ref, bf16[8,16,768]{2,1,0:T(8,128)(2,1)S(1)} %all_to_all.16.pieces, f32[8,768]{1,0:T(8,128)S(1)} %get-tuple-element.11.gains, bf16[168,6144]{1,0:T(8,128)(2,1)S(1)} %bitcast.5, bf16[168,6144]{1,0:T(8,128)(2,1)S(1)} %bitcast.6, ...), custom_call_target="tpu_custom_call" | custom-call | flops 99090432 | bytes 6193152 | tf_op jit(solution)/shard_map/pallas_call | solution.py:441
  38.5 10.7 %all_to_all.17.pieces = bf16[8,16,768]{2,1,0:T(8,128)(2,1)S(1)} all-to-all(bf16[8,16,768]{2,1,0:T(8,128)(2,1)S(1)} %shard_map.152), channel_id=1, replica_groups=mesh['group'=2,'attn'=8,'expert'=2] {'attn'}, dimensions={0} | all-to-all | bytes 393216 | tf_op jit(solution)/shard_map/all_to_all | solution.py:477
  49.2 0.3 shard_map.153
  49.5 0.1 collective-permute-start.1
  49.6 1.3 %collective-permute-done.1 = f32[32,768]{1,0:T(8,128)S(1)} collective-permute-done((f32[32,768]{1,0:T(8,128)S(1)}, f32[32,768]{1,0:T(8,128)S(1)}, u32[]{:S(2)}, u32[]{:S(2)}) %collective-permute-start.1) | collective-permute-done | bytes 98336 | tf_op jit(solution)/shard_map/ppermute | solution.py:481
  50.9 0.6 %add_convert_fusion = bf16[32,768]{1,0:T(8,128)(2,1)} fusion(f32[32,768]{1,0:T(8,128)S(1)} %shard_map.153, f32[32,768]{1,0:T(8,128)S(1)} %collective-permute-done.1), kind=kLoop, calls=%fused_computation | loop fusion | flops 49152 | bytes 245760 | tf_op jit(solution)/shard_map/convert_element_type | solution.py:521
Async XLA Ops:
  0.6 21.4 %copy-start = (bf16[3072,768]{1,0:T(8,128)(2,1)S(1)}, bf16[3072,768]{1,0:T(8,128)(2,1)}, u32[]{:S(2)}) copy-start(bf16[3072,768]{1,0:T(8,128)(2,1)} %weight_ref.1) | copy-start | bytes 14155780
  22.1 2.2 %copy-start.4 = (s32[32,4]{0,1:T(4,128)S(1)}, s32[32,4]{0,1:T(4,128)}, u32[]{:S(2)}) copy-start(s32[32,4]{0,1:T(4,128)} %param.26) | copy-start | bytes 1540
  22.1 2.2 %copy-start.5 = (bf16[32,768]{1,0:T(8,128)(2,1)S(1)}, bf16[32,768]{1,0:T(8,128)(2,1)}, u32[]{:S(2)}) copy-start(bf16[32,768]{1,0:T(8,128)(2,1)} %residual_ref.1) | copy-start | bytes 147460
  22.1 2.2 %copy-start.6 = (f32[32,4]{0,1:T(4,128)S(1)}, f32[32,4]{0,1:T(4,128)}, u32[]{:S(2)}) copy-start(f32[32,4]{0,1:T(4,128)} %param.27) | copy-start | bytes 1540
  23.0 1.3 %collective-permute-start = (f32[32,768]{1,0:T(8,128)S(1)}, f32[32,768]{1,0:T(8,128)S(1)}, u32[]{:S(2)}, u32[]{:S(2)}) collective-permute-start(f32[32,768]{1,0:T(8,128)S(1)} %get-tuple-element.7.mine_ref), channel_id=1, source_target_pairs={{0,1},{1,0},{2,3},{3,2},{4,5},{5,4},{6,7},{7,6},{8,9},{9,8},{10,11... | collective-permute-start | bytes 294920 | tf_op jit(solution)/shard_map/ppermute | solution.py:481
  24.3 12.3 %copy-start.1 = (bf16[6144,168]{0,1:T(8,128)(2,1)S(1)}, bf16[6144,168]{0,1:T(8,128)(2,1)}, u32[]{:S(2)}) copy-start(bf16[6144,168]{0,1:T(8,128)(2,1)} %param.23) | copy-start | bytes 6193156
  24.3 12.3 %copy-start.2 = (bf16[6144,168]{0,1:T(8,128)(2,1)S(1)}, bf16[6144,168]{0,1:T(8,128)(2,1)}, u32[]{:S(2)}) copy-start(bf16[6144,168]{0,1:T(8,128)(2,1)} %param.24) | copy-start | bytes 6193156
  24.4 12.3 %copy-start.3 = (bf16[168,6144]{1,0:T(8,128)(2,1)S(1)}, bf16[168,6144]{1,0:T(8,128)(2,1)}, u32[]{:S(2)}) copy-start(bf16[168,6144]{1,0:T(8,128)(2,1)} %down_ref.1) | copy-start | bytes 6193156
  49.5 1.4 %collective-permute-start.1 = (f32[32,768]{1,0:T(8,128)S(1)}, f32[32,768]{1,0:T(8,128)S(1)}, u32[]{:S(2)}, u32[]{:S(2)}) collective-permute-start(f32[32,768]{1,0:T(8,128)S(1)} %shard_map.153), channel_id=1, source_target_pairs={{0,1},{1,0},{2,3},{3,2},{4,5},{5,4},{6,7},{7,6},{8,9},{9,8},{10,11... | collective-permute-start | bytes 294920 | tf_op jit(solution)/shard_map/ppermute | solution.py:481

commit v5 on v4

--- a/solution.py
+++ b/solution.py
@@ -362,9 +362,13 @@
     return jnp.where((slot == place) & (hit > 0.5), 1.0, 0.0)
 
 
+def own_half(core, left, right):
+    return jnp.where(core == 0, left, right)
+
+
 def pick_kernel(cores, place_ref, mine_ref, other_ref, residual_ref, routes_ref, weight_ref,
                 stream_ref, out_ref, slot_ref):
-    count, capacity, _ = out_ref.shape
+    count, capacity, half = out_ref.shape
     stream = (
         residual_ref[...].astype(jnp.float32) + (mine_ref[...] + other_ref[...])
     ).astype(jnp.bfloat16)
@@ -378,6 +382,8 @@
         ).astype(jnp.bfloat16)
         for e in range(HELD)
     ]
+    core = place_ref[1]
+    chosen = [own_half(core, rows[:, :half], rows[:, half:]) for rows in chosen]
     for k in range(count):
         out_ref[k] = chosen[k * cores // sharers]
     first = place_ref[0] * cores < sharers
@@ -397,7 +403,7 @@
         functools.partial(pick_kernel, cores),
         [
             jax.ShapeDtypeStruct((rows, cols), jnp.bfloat16),
-            jax.ShapeDtypeStruct((count, capacity, cols), jnp.bfloat16),
+            jax.ShapeDtypeStruct((count, capacity, cols // 2), jnp.bfloat16),
             jax.ShapeDtypeStruct((capacity, 128), jnp.float32),
         ],
         [SMEM_SPEC] + [VMEM_SPEC] * 5,
@@ -406,11 +412,17 @@
     )(place, mine, other, residual, routes, route_weight)
 
 
-def expert_kernel(slot_ref, pieces, gains, gate_ref, up_ref, down_ref, out_ref):
-    count, capacity, cols = pieces.shape
+def expert_kernel(place_ref, slot_ref, mine_ref, other_ref, gains, gate_ref, up_ref, down_ref,
+                  keep_ref, give_ref):
+    count, capacity, half = mine_ref.shape
+    core = place_ref[1]
+    blocks = []
+    for k in range(count):
+        mine, other = mine_ref[k], other_ref[k]
+        blocks.append(own_half(core, mine, other).astype(jnp.float32))
+        blocks.append(own_half(core, other, mine).astype(jnp.float32))
     first = second = 0.0
-    for k in range(count):
-        wide = pieces[k].astype(jnp.float32)
+    for wide in blocks:
         first = first + wide
         second = second + wide * wide
     row_mean = jnp.sum(first, axis=1, keepdims=True) / D
@@ -419,58 +431,96 @@
     contract = (((1,), (1,)), ((), ()))
     gate_val = up_val = 0.0
     for k in range(count):
-        block = slice(k * cols, (k + 1) * cols)
-        wide = pieces[k].astype(jnp.float32)
+        columns = slice(2 * k * half, 2 * (k + 1) * half)
+        wide = jnp.concatenate(blocks[2 * k : 2 * k + 2], axis=1)
         normed = ((wide - row_mean) * inverse * gains[pl.ds(k, 1), :]).astype(jnp.bfloat16)
         gate_val = gate_val + lax.dot_general(
-            gate_ref[:, block], normed, contract, preferred_element_type=jnp.float32
+            gate_ref[:, columns], normed, contract, preferred_element_type=jnp.float32
         )
         up_val = up_val + lax.dot_general(
-            up_ref[:, block], normed, contract, preferred_element_type=jnp.float32
+            up_ref[:, columns], normed, contract, preferred_element_type=jnp.float32
         )
     hidden = (gate_val / (1.0 + jnp.exp(-gate_val)) * up_val).T.astype(jnp.bfloat16)
     slot_weight = slot_ref[:, :1]
     for k in range(count):
-        block = slice(k * cols, (k + 1) * cols)
-        out_ref[k] = (
-            jnp.dot(hidden, down_ref[:, block], preferred_element_type=jnp.float32) * slot_weight
+        columns = slice(2 * k * half, 2 * (k + 1) * half)
+        piece = (
+            jnp.dot(hidden, down_ref[:, columns], preferred_element_type=jnp.float32)
+            * slot_weight
         ).astype(jnp.bfloat16)
-
-
-def run_experts(slots, pieces, gains, gate, up, down):
+        keep_ref[k] = own_half(core, piece[:, :half], piece[:, half:])
+        give_ref[k] = own_half(core, piece[:, half:], piece[:, :half])
+
+
+def run_experts(place, slots, mine, other, gains, gate, up, down):
     return call(
         expert_kernel,
-        jax.ShapeDtypeStruct(pieces.shape, jnp.bfloat16),
-        [VMEM_SPEC] * 6,
+        [jax.ShapeDtypeStruct(mine.shape, jnp.bfloat16)] * 2,
+        [SMEM_SPEC] + [VMEM_SPEC] * 7,
         [],
-        6 * pieces.shape[1] * gate.size, gate.size * 6, 14,
-    )(slots, pieces, gains, gate, up, down)
+        6 * mine.shape[1] * gate.size, gate.size * 6, 14,
+    )(place, slots, mine, other, gains, gate, up, down)
+
+
+def add_kernel(keep_ref, given_ref, out_ref):
+    out_ref[...] = (
+        keep_ref[...].astype(jnp.float32) + given_ref[...].astype(jnp.float32)
+    ).astype(jnp.bfloat16)
+
+
+def add(keep, given):
+    return call(
+        add_kernel,
+        jax.ShapeDtypeStruct(keep.shape, jnp.bfloat16),
+        [VMEM_SPEC] * 2,
+        [],
+        keep.size, keep.size * 6, 4,
+    )(keep, given)
 
 
 def combine_kernel(cores, routes_ref, pieces, out_ref):
-    count, capacity, cols = pieces.shape
+    count, capacity, half = pieces.shape
     sharers = count * cores // HELD
     routes = routes_ref[...]
     taken = [expert_rows(routes, e, capacity) for e in range(HELD)]
     spread = [taken[k * cores // sharers] for k in range(count)]
     out_ref[...] = lax.dot_general(
         jnp.concatenate(spread, axis=0).astype(jnp.bfloat16),
-        pieces[...].reshape(count * capacity, cols),
+        pieces[...].reshape(count * capacity, half),
         (((0,), (0,)), ((), ())),
         preferred_element_type=jnp.float32,
-    )
+    ).astype(jnp.bfloat16)
 
 
 def combine(cores, routes, pieces):
-    count, capacity, cols = pieces.shape
+    count, capacity, half = pieces.shape
     rows = routes.shape[1]
     return call(
         functools.partial(combine_kernel, cores),
-        jax.ShapeDtypeStruct((rows, cols), jnp.float32),
+        jax.ShapeDtypeStruct((rows, half), jnp.bfloat16),
         [VMEM_SPEC] * 2,
         [],
-        2 * rows * capacity * count * cols, (count * capacity * 2 + rows * 4) * cols, 4,
+        2 * rows * capacity * count * half, (count * capacity + rows) * 2 * half, 4,
     )(routes, pieces)
+
+
+def join_kernel(place_ref, mine_ref, other_ref, out_ref):
+    half = mine_ref.shape[1]
+    core = place_ref[1]
+    mine, other = mine_ref[...], other_ref[...]
+    out_ref[:, :half] = own_half(core, mine, other)
+    out_ref[:, half:] = own_half(core, other, mine)
+
+
+def join(place, mine, other):
+    rows, half = mine.shape
+    return call(
+        join_kernel,
+        jax.ShapeDtypeStruct((rows, 2 * half), jnp.bfloat16),
+        [SMEM_SPEC] + [VMEM_SPEC] * 2,
+        [],
+        rows * half, rows * half * 8, 4,
+    )(place, mine, other)
 
 
 def exchange(blocks):
@@ -500,7 +550,7 @@
     count = lax.axis_size("attn")
     cores = lax.axis_size("expert")
     capacity = routes.shape[0] * TOP // EXPERTS * 2
-    place = lax.axis_index("attn").astype(jnp.int32).reshape(1)
+    place = jnp.stack([lax.axis_index("attn"), lax.axis_index("expert")]).astype(jnp.int32)
     routes = routes.T
     route_weight = route_weight.T
 
@@ -514,11 +564,12 @@
     attn_stream, chosen, slots = pick(
         place, cores, count, capacity, mine, swap(mine), residual, routes, route_weight
     )
-    outgoing = run_experts(
-        slots, exchange(chosen), gains, gate_weight.T, up_weight.T, down_weight
-    )
-    combined = combine(cores, routes, exchange(outgoing))
-    expert_out = (combined + swap(combined)).astype(jnp.bfloat16)
+    arrived = exchange(chosen)
+    keep, give = run_experts(
+        place, slots, arrived, swap(arrived), gains, gate_weight.T, up_weight.T, down_weight
+    )
+    combined = combine(cores, routes, exchange(add(keep, swap(give))))
+    expert_out = join(place, combined, swap(combined))
     return (attn_stream, expert_out)
 
 

time: 51.8 us -> 55.3 us (1.068)
  blocking collectives: 38 us -> 19.9 us
  waiting for transfers between devices: 2.57 us -> 13.2 us
  starting transfers between devices: 0.12 us -> 7.57 us
  local copies, waits for them, and re-layouts: 0.03 us -> 2.37 us
  Pallas kernels: 9.52 us -> 11.2 us
    all_to_all x3 -> x2, blocking collectives: 38 us -> 19.9 us  [exchange(): lax.all_to_all(blocks, 'attn', split_axis=0, concat_axis=0, tiled=True)]
    all_to_all x0 -> x1, waiting for transfers between devices: none -> 8.32 us  [exchange(): lax.all_to_all(blocks, 'attn', split_axis=0, concat_axis=0, tiled=True)]
    all_to_all x0 -> x1, starting transfers between devices: none -> 7.29 us  [exchange(): lax.all_to_all(blocks, 'attn', split_axis=0, concat_axis=0, tiled=True)]
    unnamed x14, local copies, waits for them, and re-layouts: 0.03 us -> 2.37 us
    ppermute x2 -> x4, waiting for transfers between devices: 2.57 us -> 4.85 us  [swap(): return lax.ppermute(block, 'expert', [(0, 1), (1, 0)])]
    pallas_call x1 -> x3, Pallas kernels: 1.87 us -> 3.62 us  [the longest x1 2.42 us: run_experts(): call(expert_kernel, [jax.ShapeDtypeStruct(mine.shape, jnp.bfloat16)] * 2,...]
    convert_element_type x1 -> x0, other arithmetic: 0.63 us -> none  [shards(): expert_out = (combined + swap(combined)).astype(jnp.bfloat16)]
  transfers between devices with their start and end apart: 2 -> 5, of which waited for: 2 -> 5; matrix products, arithmetic and copies ran while one was open for 0% -> 0% of each run, Pallas kernels for 0% -> 0%
where the time goes in v5:
time: 55.3 us; the launch traced here: 55 us
  blocking collectives  19.9 us (36%)
  waiting for transfers between devices  13.2 us (24%)
  Pallas kernels  11.2 us (20%)
  starting transfers between devices  7.57 us (14%)
  local copies, waits for them, and re-layouts  2.37 us (4%)
  between operations  0.7 us (1%)
    all_to_all x2, blocking collectives, exchange(): lax.all_to_all(blocks, 'attn', split_axis=0, concat_axis=0, tiled=True)  19.9 us
    all_to_all x1, waiting for transfers between devices, exchange(): lax.all_to_all(blocks, 'attn', split_axis=0, concat_axis=0, tiled=True)  8.32 us
    all_to_all x1, starting transfers between devices, exchange(): lax.all_to_all(blocks, 'attn', split_axis=0, concat_axis=0, tiled=True)  7.29 us
    pallas_call x1, Pallas kernels, attend(): call(attend_kernel, jax.ShapeDtypeStruct((count, row_count, width + gain....  5.28 us
    ppermute x4, waiting for transfers between devices, swap(): return lax.ppermute(block, 'expert', [(0, 1), (1, 0)])  4.85 us
    pallas_call x1, Pallas kernels, run_experts(): call(expert_kernel, [jax.ShapeDtypeStruct(mine.shape, jnp.bfloat16)] * 2,...  2.42 us
    unnamed x14, local copies, waits for them, and re-layouts  2.37 us
    pallas_call x1, Pallas kernels, pick(): call(functools.partial(pick_kernel, cores), [jax.ShapeDtypeStruct((rows,...  1.19 us
  transfers between devices with their start and end apart: 5, of which 5 were waited for; matrix products, arithmetic and copies ran while one was open for 0% of the time, Pallas kernels for 0%

profile of v5, /device:TPU:0, one launch (start us, length us, event | category | flops | bytes accessed | tf_op | source)
XLA Modules:
  0.0 55.0 jit_solution(15323074766156794887)
XLA Ops:
  0.6 5.3 %shard_map.149 = bf16[8,4,3456]{2,1,0:T(4,128)(2,1)} custom-call(s32[4]{0:T(128)} %length_ref.1, bf16[4,3072]{1,0:T(4,128)(2,1)} %query_hbm.1, bf16[4,512,512]{2,1,0:T(8,128)(2,1)} %key_hbm.1, bf16[4,512,512]{2,1,0:T(8,128)(2,1)} %value_hbm.1, bf16[4,512]{1,0:T(4,128)(2,1)} %own_key_hbm.1, bf16[4,512]{1,0:T(4,128)(2,1)} %own_value_hbm.1, f32[768]{0:T(1024)} %gain_hbm.1), custom_call_target="tpu_custom_call" | custom-call | flops 25165824 | bytes 4194304 | tf_op jit(solution)/shard_map/pallas_call | solution.py:301
  5.9 7.3 %all-to-all-start = ((bf16[8,4,3456]{2,1,0:T(4,128)(2,1)}), bf16[8,4,3456]{2,1,0:T(4,128)(2,1)S(1)}, u32[]{:S(2)}, u32[]{:S(2)}) async-start(bf16[8,4,3456]{2,1,0:T(4,128)(2,1)} %shard_map.149), calls=%async_computation | async-start | bytes 442368 | tf_op jit(solution)/shard_map/all_to_all | solution.py:527
  13.2 8.3 %all-to-all-done.pieces = bf16[8,4,3456]{2,1,0:T(4,128)(2,1)S(1)} async-done(((bf16[8,4,3456]{2,1,0:T(4,128)(2,1)}), bf16[8,4,3456]{2,1,0:T(4,128)(2,1)S(1)}, u32[]{:S(2)}, u32[]{:S(2)}) %all-to-all-start) | async-done | bytes 221216 | tf_op jit(solution)/shard_map/all_to_all | solution.py:527
  21.5 0.0 copy-start
  21.5 2.3 %copy-done = bf16[3072,768]{1,0:T(8,128)(2,1)S(1)} copy-done((bf16[3072,768]{1,0:T(8,128)(2,1)S(1)}, bf16[3072,768]{1,0:T(8,128)(2,1)}, u32[]{:S(2)}) %copy-start) | copy-done | bytes 4718616
  23.9 0.0 copy-start.4
  23.9 0.0 copy-start.5
  23.9 0.0 copy-start.6
  23.9 0.9 %shard_map.150 = (f32[32,768]{1,0:T(8,128)S(1)}, f32[8,768]{1,0:T(8,128)S(1)}) custom-call(bf16[8,4,3456]{2,1,0:T(4,128)(2,1)S(1)} %all-to-all-done.pieces, bf16[3072,768]{1,0:T(8,128)(2,1)S(1)} %copy-done), custom_call_target="tpu_custom_call" | custom-call | flops 150994944 | bytes 4718592 | tf_op jit(solution)/shard_map/pallas_call | solution.py:338
  24.8 0.0 collective-permute-start
  24.8 0.1 pad_add_fusion.place_ref
  24.9 1.2 %collective-permute-done.other_ref = f32[32,768]{1,0:T(8,128)S(1)} collective-permute-done((f32[32,768]{1,0:T(8,128)S(1)}, f32[32,768]{1,0:T(8,128)S(1)}, u32[]{:S(2)}, u32[]{:S(2)}) %collective-permute-start) | collective-permute-done | bytes 98336 | tf_op jit(solution)/shard_map/ppermute | solution.py:531
  26.1 0.0 copy-done.4
  26.1 0.0 copy-done.5
  26.1 0.0 copy-done.6
  26.1 0.0 copy-start.1
  26.1 0.0 copy-start.2
  26.1 0.0 copy-start.3
  26.1 1.2 %shard_map.151 = (bf16[32,768]{1,0:T(8,128)(2,1)}, bf16[8,16,384]{2,1,0:T(8,128)(2,1)S(1)}, f32[16,128]{1,0:T(8,128)S(1)}) custom-call(s32[2]{0:T(128)S(1)} %pad_add_fusion.place_ref, f32[32,768]{1,0:T(8,128)S(1)} %get-tuple-element.9.mine_ref, f32[32,768]{1,0:T(8,128)S(1)} %collective-permute-done.other_ref, bf16[32,768]{1,0:T(8,128)(2,1)S(1)} %copy-done.5, ...), custom_call_target="tpu_custom_call" | custom-call | flops 10000000000 | bytes 294912 | tf_op jit(solution)/shard_map/pallas_call | solution.py:402
  27.3 10.3 %all_to_all.15.mine_ref = bf16[8,16,384]{2,1,0:T(8,128)(2,1)S(1)} all-to-all(bf16[8,16,384]{2,1,0:T(8,128)(2,1)S(1)} %get-tuple-element.12), channel_id=1, replica_groups=mesh['group'=2,'attn'=8,'expert'=2] {'attn'}, dimensions={0} | all-to-all | bytes 196608 | tf_op jit(solution)/shard_map/all_to_all | solution.py:527
  37.7 0.0 collective-permute-start.1
  37.7 1.3 %collective-permute-done.1.other_ref = bf16[8,16,384]{2,1,0:T(8,128)(2,1)S(1)} collective-permute-done((bf16[8,16,384]{2,1,0:T(8,128)(2,1)S(1)}, bf16[8,16,384]{2,1,0:T(8,128)(2,1)S(1)}, u32[]{:S(2)}, u32[]{:S(2)}) %collective-permute-start.1) | collective-permute-done | bytes 98336 | tf_op jit(solution)/shard_map/ppermute | solution.py:531
  39.0 0.0 copy-done.1
  39.0 0.0 copy-done.2
  39.0 0.0 copy-done.3
  39.0 2.4 %shard_map.152 = (bf16[8,16,384]{2,1,0:T(8,128)(2,1)S(1)}, bf16[8,16,384]{2,1,0:T(8,128)(2,1)S(1)}) custom-call(s32[2]{0:T(128)S(1)} %pad_add_fusion.place_ref, f32[16,128]{1,0:T(8,128)S(1)} %get-tuple-element.11.slot_ref, bf16[8,16,384]{2,1,0:T(8,128)(2,1)S(1)} %all_to_all.15.mine_ref, bf16[8,16,384]{2,1,0:T(8,128)(2,1)S(1)} %collective-permute-done.1.other_ref, ...), custom_call_target="tpu_custom_call" | custom-call | flops 99090432 | bytes 6193152 | tf_op jit(solution)/shard_map/pallas_call | solution.py:456
  41.4 0.2 collective-permute-start.2
  41.6 1.2 %collective-permute-done.2.given_ref = bf16[8,16,384]{2,1,0:T(8,128)(2,1)S(1)} collective-permute-done((bf16[8,16,384]{2,1,0:T(8,128)(2,1)S(1)}, bf16[8,16,384]{2,1,0:T(8,128)(2,1)S(1)}, u32[]{:S(2)}, u32[]{:S(2)}) %collective-permute-start.2) | collective-permute-done | bytes 98336 | tf_op jit(solution)/shard_map/ppermute | solution.py:531
  42.8 9.5 %all_to_all.16.pieces = bf16[8,16,384]{2,1,0:T(8,128)(2,1)S(1)} all-to-all(bf16[8,16,384]{2,1,0:T(8,128)(2,1)S(1)} %shard_map.153), channel_id=1, replica_groups=mesh['group'=2,'attn'=8,'expert'=2] {'attn'}, dimensions={0} | all-to-all | bytes 196608 | tf_op jit(solution)/shard_map/all_to_all | solution.py:527
  52.3 0.3 shard_map.154.mine_ref
  52.6 0.0 collective-permute-start.3
  52.6 1.2 %collective-permute-done.3.other_ref = bf16[32,384]{1,0:T(8,128)(2,1)S(1)} collective-permute-done((bf16[32,384]{1,0:T(8,128)(2,1)S(1)}, bf16[32,384]{1,0:T(8,128)(2,1)S(1)}, u32[]{:S(2)}, u32[]{:S(2)}) %collective-permute-start.3) | collective-permute-done | bytes 24608 | tf_op jit(solution)/shard_map/ppermute | solution.py:531
  53.8 1.2 %shard_map.155 = bf16[32,768]{1,0:T(8,128)(2,1)} custom-call(s32[2]{0:T(128)S(1)} %pad_add_fusion.place_ref, bf16[32,384]{1,0:T(8,128)(2,1)S(1)} %shard_map.154.mine_ref, bf16[32,384]{1,0:T(8,128)(2,1)S(1)} %collective-permute-done.3.other_ref), custom_call_target="tpu_custom_call" | custom-call | flops 12288 | bytes 98304 | tf_op jit(solution)/shard_map/pallas_call | solution.py:517
  (1 shorter events, 0.0 us)
Async XLA Ops:
  5.9 15.6 %all-to-all-start = ((bf16[8,4,3456]{2,1,0:T(4,128)(2,1)}), bf16[8,4,3456]{2,1,0:T(4,128)(2,1)S(1)}, u32[]{:S(2)}, u32[]{:S(2)}) async-start(bf16[8,4,3456]{2,1,0:T(4,128)(2,1)} %shard_map.149), calls=%async_computation | async-start | bytes 442368 | tf_op jit(solution)/shard_map/all_to_all | solution.py:527
  21.5 2.3 %copy-start = (bf16[3072,768]{1,0:T(8,128)(2,1)S(1)}, bf16[3072,768]{1,0:T(8,128)(2,1)}, u32[]{:S(2)}) copy-start(bf16[3072,768]{1,0:T(8,128)(2,1)} %weight_ref.1) | copy-start | bytes 14155780
  23.9 2.2 %copy-start.4 = (s32[32,4]{0,1:T(4,128)S(1)}, s32[32,4]{0,1:T(4,128)}, u32[]{:S(2)}) copy-start(s32[32,4]{0,1:T(4,128)} %param.26) | copy-start | bytes 1540
  23.9 2.2 %copy-start.5 = (bf16[32,768]{1,0:T(8,128)(2,1)S(1)}, bf16[32,768]{1,0:T(8,128)(2,1)}, u32[]{:S(2)}) copy-start(bf16[32,768]{1,0:T(8,128)(2,1)} %residual_ref.1) | copy-start | bytes 147460
  23.9 2.2 %copy-start.6 = (f32[32,4]{0,1:T(4,128)S(1)}, f32[32,4]{0,1:T(4,128)}, u32[]{:S(2)}) copy-start(f32[32,4]{0,1:T(4,128)} %param.27) | copy-start | bytes 1540
  24.8 1.3 %collective-permute-start = (f32[32,768]{1,0:T(8,128)S(1)}, f32[32,768]{1,0:T(8,128)S(1)}, u32[]{:S(2)}, u32[]{:S(2)}) collective-permute-start(f32[32,768]{1,0:T(8,128)S(1)} %get-tuple-element.9.mine_ref), channel_id=1, source_target_pairs={{0,1},{1,0},{2,3},{3,2},{4,5},{5,4},{6,7},{7,6},{8,9},{9,8},{10,11... | collective-permute-start | bytes 294920 | tf_op jit(solution)/shard_map/ppermute | solution.py:531
  26.1 12.9 %copy-start.1 = (bf16[6144,168]{0,1:T(8,128)(2,1)S(1)}, bf16[6144,168]{0,1:T(8,128)(2,1)}, u32[]{:S(2)}) copy-start(bf16[6144,168]{0,1:T(8,128)(2,1)} %param.23) | copy-start | bytes 6193156
  26.1 12.9 %copy-start.2 = (bf16[6144,168]{0,1:T(8,128)(2,1)S(1)}, bf16[6144,168]{0,1:T(8,128)(2,1)}, u32[]{:S(2)}) copy-start(bf16[6144,168]{0,1:T(8,128)(2,1)} %param.24) | copy-start | bytes 6193156
  26.1 12.9 %copy-start.3 = (bf16[168,6144]{1,0:T(8,128)(2,1)S(1)}, bf16[168,6144]{1,0:T(8,128)(2,1)}, u32[]{:S(2)}) copy-start(bf16[168,6144]{1,0:T(8,128)(2,1)} %down_ref.1) | copy-start | bytes 6193156
  37.7 1.3 %collective-permute-start.1 = (bf16[8,16,384]{2,1,0:T(8,128)(2,1)S(1)}, bf16[8,16,384]{2,1,0:T(8,128)(2,1)S(1)}, u32[]{:S(2)}, u32[]{:S(2)}) collective-permute-start(bf16[8,16,384]{2,1,0:T(8,128)(2,1)S(1)} %all_to_all.15.mine_ref), channel_id=1, source_target_pairs={{0,1},{1,0},{2,3},{3,2},{4,5},{5,4},{6,7},{7,6},{8,9},{9,8},{10,11... | collective-permute-start | bytes 294920 | tf_op jit(solution)/shard_map/ppermute | solution.py:531
  41.4 1.4 %collective-permute-start.2 = (bf16[8,16,384]{2,1,0:T(8,128)(2,1)S(1)}, bf16[8,16,384]{2,1,0:T(8,128)(2,1)S(1)}, u32[]{:S(2)}, u32[]{:S(2)}) collective-permute-start(bf16[8,16,384]{2,1,0:T(8,128)(2,1)S(1)} %get-tuple-element.15), channel_id=1, source_target_pairs={{0,1},{1,0},{2,3},{3,2},{4,5},{5,4},{6,7},{7,6},{8,9},{9,8},{10,11... | collective-permute-start | bytes 294920 | tf_op jit(solution)/shard_map/ppermute | solution.py:531
  52.6 1.2 %collective-permute-start.3 = (bf16[32,384]{1,0:T(8,128)(2,1)S(1)}, bf16[32,384]{1,0:T(8,128)(2,1)S(1)}, u32[]{:S(2)}, u32[]{:S(2)}) collective-permute-start(bf16[32,384]{1,0:T(8,128)(2,1)S(1)} %shard_map.154.mine_ref), channel_id=1, source_target_pairs={{0,1},{1,0},{2,3},{3,2},{4,5},{5,4},{6,7},{7,6},{8,9},{9,8},{10,11... | collective-permute-start | bytes 73736 | tf_op jit(solution)/shard_map/ppermute | solution.py:531

commit v6 on v4

--- a/solution.py
+++ b/solution.py
@@ -178,19 +178,13 @@
 def attend_kernel(
     length_ref, query_hbm, key_hbm, value_hbm, own_key_hbm, own_value_hbm, gain_hbm, out_ref,
     query_ref, key_buf, value_buf, own_key_ref, own_value_ref, gain_ref,
-    query_rows, key_rows, value_rows, result_rows, key_sem, value_sem, small_sem,
+    query_table, own_table, value_rows, result_rows, key_sem, value_sem, small_sem,
 ):
     row_count, length_max = key_hbm.shape[0], key_hbm.shape[1]
-    kv_local = own_key_ref.shape[1] // HEAD_DIM
+    kv_local = own_key_hbm.shape[1] // HEAD_DIM
     group = HEADS // KV_HEADS
     block = group * row_count
-    key_copies = [
-        pltpu.make_async_copy(key_hbm.at[r], key_buf.at[r], key_sem.at[r]) for r in range(row_count)
-    ]
-    value_copies = [
-        pltpu.make_async_copy(value_hbm.at[r], value_buf.at[r], value_sem.at[r])
-        for r in range(row_count)
-    ]
+    total_rows = kv_local * block
     small_copies = [
         pltpu.make_async_copy(source, target, small_sem.at[index])
         for index, (source, target) in enumerate(
@@ -202,85 +196,78 @@
             )
         )
     ]
+    key_copies = [
+        pltpu.make_async_copy(key_hbm.at[r], key_buf.at[r], key_sem.at[r]) for r in range(row_count)
+    ]
+    value_copies = [
+        pltpu.make_async_copy(value_hbm.at[r], value_buf.at[r], value_sem.at[r])
+        for r in range(row_count)
+    ]
     for copy in small_copies + key_copies + value_copies:
         copy.start()
+    query_table[...] = jnp.zeros_like(query_table)
+    own_table[...] = jnp.zeros_like(own_table)
+    lane = lax.broadcasted_iota(jnp.int32, (1, total_rows), 1) % row_count
+    lengths = jnp.zeros((1, total_rows), jnp.int32)
+    for r in range(row_count):
+        lengths = jnp.where(lane == r, length_ref[r], lengths)
+    position = lax.broadcasted_iota(jnp.int32, (length_max, total_rows), 0)
     for copy in small_copies:
         copy.wait()
+    own_table[pl.ds(0, row_count), :] = own_key_ref[...].astype(jnp.float32)
     for g in range(kv_local):
         lanes = slice(g * HEAD_DIM, (g + 1) * HEAD_DIM)
-        own_key = own_key_ref[:, lanes].astype(jnp.float32)
         own_value = own_value_ref[:, lanes].astype(jnp.float32)
         for i in range(group):
             head = g * group + i
             rows = pl.ds(g * block + i * row_count, row_count)
-            query_rows[rows, :] = query_ref[
+            query_table[rows, lanes] = query_ref[
                 :, head * HEAD_DIM : (head + 1) * HEAD_DIM
             ].astype(jnp.float32)
-            key_rows[rows, :] = own_key
             value_rows[rows, :] = own_value
+    queries = query_table[...].astype(jnp.bfloat16)
+    contract = (((1,), (1,)), ((), ()))
     scale = 1.0 / math.sqrt(HEAD_DIM)
-    pair_rows = 2 * block
-    request = lax.broadcasted_iota(jnp.int32, (pair_rows, 1), 0) % row_count
-    lengths = jnp.zeros((pair_rows, 1), jnp.int32)
-    for r in range(row_count):
-        lengths = jnp.where(request == r, length_ref[r], lengths)
-    position = lax.broadcasted_iota(jnp.int32, (pair_rows, length_max), 1)
-    valid = position < lengths
-    pairs = kv_local // 2
-    past = [jnp.zeros((pair_rows, length_max), jnp.float32) for _ in range(pairs)]
-    packed = []
-    for p in range(pairs):
-        rows = query_rows[pl.ds(p * pair_rows, pair_rows), :]
-        lower = rows[:block].astype(jnp.bfloat16)
-        upper = rows[block:].astype(jnp.bfloat16)
-        zero = jnp.zeros_like(lower)
-        packed.append(
-            jnp.concatenate(
-                [
-                    jnp.concatenate([lower, zero], axis=1),
-                    jnp.concatenate([zero, upper], axis=1),
-                ],
-                axis=0,
-            )
-        )
+    own_scores = lax.dot_general(
+        own_table[...].astype(jnp.bfloat16), queries, contract, preferred_element_type=jnp.float32
+    )
+    own_row = lax.broadcasted_iota(jnp.int32, own_scores.shape, 0)
+    own = jnp.sum(jnp.where(own_row == lane, own_scores, 0.0), axis=0, keepdims=True) * scale
+    past = None
     for r in range(row_count):
         key_copies[r].wait()
-        for p in range(pairs):
-            keys = key_buf[r, :, p * 2 * HEAD_DIM : (p + 1) * 2 * HEAD_DIM]
-            scores = lax.dot_general(
-                packed[p], keys, (((1,), (1,)), ((), ())), preferred_element_type=jnp.float32
-            )
-            past[p] = jnp.where(request == r, scores, past[p])
-    probs, own_probs = [], []
-    for p in range(pairs):
-        rows = pl.ds(p * pair_rows, pair_rows)
-        scores = jnp.where(valid, past[p] * scale, NEG_FILL)
-        own = jnp.sum(query_rows[rows, :] * key_rows[rows, :], axis=1, keepdims=True) * scale
-        largest = jnp.maximum(jnp.max(scores, axis=1, keepdims=True), own)
-        weight = jnp.exp(scores - largest)
-        own_weight = jnp.exp(own - largest)
-        total = jnp.sum(weight, axis=1, keepdims=True) + own_weight
-        probs.append((weight / total).astype(jnp.bfloat16))
-        own_probs.append((own_weight / total).astype(jnp.bfloat16).astype(jnp.float32))
-    sums = [jnp.zeros((pair_rows, 2 * HEAD_DIM), jnp.float32) for _ in range(pairs)]
+        scores = lax.dot_general(
+            key_buf[r], queries, contract, preferred_element_type=jnp.float32
+        )
+        past = scores if past is None else jnp.where(lane == r, scores, past)
+    past = jnp.where(position < lengths, past * scale, NEG_FILL)
+    largest = jnp.maximum(jnp.max(past, axis=0, keepdims=True), own)
+    weight = jnp.exp(past - largest)
+    own_weight = jnp.exp(own - largest)
+    inverse = 1.0 / (jnp.sum(weight, axis=0, keepdims=True) + own_weight)
+    probs = (weight * inverse).T.astype(jnp.bfloat16)
+    own_prob = (own_weight * inverse).astype(jnp.bfloat16).astype(jnp.float32)
+    own_prob = jnp.broadcast_to(own_prob, (8, total_rows)).T[:, :1]
+    own_part = own_prob * value_rows[...]
+    request = lax.broadcasted_iota(jnp.int32, (block, 1), 0) % row_count
+    sums = [own_part[g * block : (g + 1) * block] for g in range(kv_local)]
     for r in range(row_count):
         value_copies[r].wait()
-        for p in range(pairs):
-            values = value_buf[r, :, p * 2 * HEAD_DIM : (p + 1) * 2 * HEAD_DIM]
-            product = jnp.dot(probs[p], values, preferred_element_type=jnp.float32)
-            sums[p] = jnp.where(request == r, product, sums[p])
-    for p in range(pairs):
-        rows = pl.ds(p * pair_rows, pair_rows)
-        own_part = own_probs[p] * value_rows[rows, :]
-        lower = sums[p][:block, :HEAD_DIM] + own_part[:block]
-        upper = sums[p][block:, HEAD_DIM:] + own_part[block:]
-        result_rows[pl.ds(p * pair_rows, block), :] = lower
-        result_rows[pl.ds(p * pair_rows + block, block), :] = upper
+        for g in range(0, kv_local, 2):
+            product = jnp.dot(
+                probs[g * block : (g + 2) * block],
+                value_buf[r, :, g * HEAD_DIM : (g + 2) * HEAD_DIM],
+                preferred_element_type=jnp.float32,
+            )
+            sums[g] = sums[g] + jnp.where(request == r, product[:block, :HEAD_DIM], 0.0)
+            sums[g + 1] = sums[g + 1] + jnp.where(request == r, product[block:, HEAD_DIM:], 0.0)
+    for g in range(kv_local):
+        result_rows[pl.ds(g * block, block), :] = sums[g]
     width = query_hbm.shape[1]
     for head in range(kv_local * group):
-        rows = result_rows[pl.ds(head * row_count, row_count), :].astype(jnp.bfloat16)
-        for index in range(out_ref.shape[0]):
-            out_ref[index, :, head * HEAD_DIM : (head + 1) * HEAD_DIM] = rows
+        out_ref[:, head * HEAD_DIM : (head + 1) * HEAD_DIM] = result_rows[
+            pl.ds(head * row_count, row_count), :
+        ].astype(jnp.bfloat16)
     gain_row = gain_ref[...].reshape(1, -1)
     half = gain_row.shape[1] // 2
     row = lax.broadcasted_iota(jnp.int32, (row_count, half), 0)
@@ -288,19 +275,17 @@
     right = jnp.broadcast_to(gain_row[:, half:], (row_count, half))
     gain = jnp.where(row % 2 == 0, left, right)
     upper = gain.astype(jnp.bfloat16).astype(jnp.float32)
-    parts = jnp.where(row < 2, upper, gain - upper).astype(jnp.bfloat16)
-    for index in range(out_ref.shape[0]):
-        out_ref[index, :, width:] = parts
-
-
-def attend(count, queries, key_cache, value_cache, new_key, new_value, cache_length, gain):
+    out_ref[:, width:] = jnp.where(row < 2, upper, gain - upper).astype(jnp.bfloat16)
+
+
+def attend(queries, key_cache, value_cache, new_key, new_value, cache_length, gain):
     row_count, width = queries.shape
-    heads = width // HEAD_DIM
-    table = pltpu.VMEM((heads * row_count, HEAD_DIM), jnp.float32)
+    total_rows = width // HEAD_DIM * row_count
+    table = pltpu.VMEM((total_rows, HEAD_DIM), jnp.float32)
     nbytes = 2 * key_cache.size * 2
     return call(
         attend_kernel,
-        jax.ShapeDtypeStruct((count, row_count, width + gain.shape[0] // 2), jnp.bfloat16),
+        jax.ShapeDtypeStruct((row_count, width + gain.shape[0] // 2), jnp.bfloat16),
         [SMEM_SPEC] + [HBM_SPEC] * 6,
         [
             pltpu.VMEM(queries.shape, jnp.bfloat16),
@@ -309,7 +294,9 @@
             pltpu.VMEM(new_key.shape, jnp.bfloat16),
             pltpu.VMEM(new_value.shape, jnp.bfloat16),
             pltpu.VMEM(gain.shape, jnp.float32),
-            table, table, table, table,
+            pltpu.VMEM((total_rows, new_key.shape[1]), jnp.float32),
+            pltpu.VMEM((8, new_key.shape[1]), jnp.float32),
+            table, table,
             pltpu.SemaphoreType.DMA((row_count,)),
             pltpu.SemaphoreType.DMA((row_count,)),
             pltpu.SemaphoreType.DMA((4,)),
@@ -318,33 +305,58 @@
     )(cache_length, queries, key_cache, value_cache, new_key, new_value, gain)
 
 
-def project_kernel(pieces, weight_ref, out_ref, gain_ref, stack):
-    count, rows, _ = pieces.shape
+def pair_kernel(place_ref, mine_ref, other_ref, out_ref):
+    low = lax.rem(place_ref[0], 2)
+    out_ref[low] = mine_ref[...]
+    out_ref[1 - low] = other_ref[...]
+
+
+def pair_up(place, mine, other):
+    return call(
+        pair_kernel,
+        jax.ShapeDtypeStruct((2,) + mine.shape, mine.dtype),
+        [SMEM_SPEC] + [VMEM_SPEC] * 2,
+        [],
+        EXCHANGE_FLOPS, mine.size * 8, 4,
+    )(place, mine, other)
+
+
+def project_kernel(place_ref, *refs):
+    quarters, (weight_ref, out_ref, gain_ref, stack) = refs[:-4], refs[-4:]
+    _, rows, _ = quarters[0].shape
     width = weight_ref.shape[0]
-    half = gain_ref.shape[1] // 2
-    for k in range(count):
-        stack[pl.ds(k * rows, rows), :] = pieces[k, :, :width].astype(jnp.float32)
-        parts = pieces[k, :, width:].astype(jnp.float32)
-        gain_ref[pl.ds(k, 1), :half] = parts[0:1] + parts[2:3]
-        gain_ref[pl.ds(k, 1), half:] = parts[1:2] + parts[3:4]
+    half = gain_ref.shape[2] // 2
+    high = place_ref[0] // 2
+    for k, quarter in enumerate(quarters):
+        source = high ^ k
+        both = jnp.concatenate(
+            [quarter[0, :, :width].astype(jnp.float32), quarter[1, :, :width].astype(jnp.float32)],
+            axis=0,
+        )
+        stack[pl.ds(pl.multiple_of(source * 2 * rows, 2 * rows), 2 * rows), :] = both
+        for low in range(2):
+            parts = quarter[low, :, width:].astype(jnp.float32)
+            gain_ref[source * 2 + low, :, :half] = parts[0:1] + parts[2:3]
+            gain_ref[source * 2 + low, :, half:] = parts[1:2] + parts[3:4]
     out_ref[...] = jnp.dot(
         stack[...].astype(jnp.bfloat16), weight_ref[...], preferred_element_type=jnp.float32
     )
 
 
-def project(pieces, out_weight):
-    count, rows, _ = pieces.shape
+def project(place, quarters, out_weight):
+    _, rows, _ = quarters[0].shape
+    count = 2 * len(quarters)
     depth, cols = out_weight.shape
     return call(
         project_kernel,
         [
             jax.ShapeDtypeStruct((rows * count, cols), jnp.float32),
-            jax.ShapeDtypeStruct((count, cols), jnp.float32),
+            jax.ShapeDtypeStruct((count, 1, cols), jnp.float32),
         ],
-        [VMEM_SPEC, VMEM_SPEC],
+        [SMEM_SPEC] + [VMEM_SPEC] * (len(quarters) + 1),
         [pltpu.VMEM((rows * count, depth), jnp.float32)],
         2 * rows * count * out_weight.size, out_weight.size * 2, 10,
-    )(pieces, out_weight)
+    )(place, *quarters, out_weight)
 
 
 def expert_rows(routes, expert, capacity):
@@ -406,7 +418,8 @@
     )(place, mine, other, residual, routes, route_weight)
 
 
-def expert_kernel(slot_ref, pieces, gains, gate_ref, up_ref, down_ref, out_ref):
+def expert_kernel(place_ref, slot_ref, pieces, gains, gate_ref, up_ref, down_ref, keep_ref,
+                  give_ref):
     count, capacity, cols = pieces.shape
     first = second = 0.0
     for k in range(count):
@@ -421,7 +434,7 @@
     for k in range(count):
         block = slice(k * cols, (k + 1) * cols)
         wide = pieces[k].astype(jnp.float32)
-        normed = ((wide - row_mean) * inverse * gains[pl.ds(k, 1), :]).astype(jnp.bfloat16)
+        normed = ((wide - row_mean) * inverse * gains[k]).astype(jnp.bfloat16)
         gate_val = gate_val + lax.dot_general(
             gate_ref[:, block], normed, contract, preferred_element_type=jnp.float32
         )
@@ -430,29 +443,48 @@
         )
     hidden = (gate_val / (1.0 + jnp.exp(-gate_val)) * up_val).T.astype(jnp.bfloat16)
     slot_weight = slot_ref[:, :1]
-    for k in range(count):
-        block = slice(k * cols, (k + 1) * cols)
-        out_ref[k] = (
+    low = lax.rem(place_ref[0], 2)
+    for k in range(count // 2):
+        block = slice(2 * k * cols, 2 * (k + 1) * cols)
+        both = (
             jnp.dot(hidden, down_ref[:, block], preferred_element_type=jnp.float32) * slot_weight
         ).astype(jnp.bfloat16)
-
-
-def run_experts(slots, pieces, gains, gate, up, down):
+        keep_ref[k] = jnp.where(low == 0, both[:, :cols], both[:, cols:])
+        give_ref[k] = jnp.where(low == 0, both[:, cols:], both[:, :cols])
+
+
+def run_experts(place, slots, pieces, gains, gate, up, down):
+    count, capacity, cols = pieces.shape
     return call(
         expert_kernel,
-        jax.ShapeDtypeStruct(pieces.shape, jnp.bfloat16),
-        [VMEM_SPEC] * 6,
+        [jax.ShapeDtypeStruct((count // 2, capacity, cols), jnp.bfloat16)] * 2,
+        [SMEM_SPEC] + [VMEM_SPEC] * 6,
         [],
-        6 * pieces.shape[1] * gate.size, gate.size * 6, 14,
-    )(slots, pieces, gains, gate, up, down)
-
-
-def combine_kernel(cores, routes_ref, pieces, out_ref):
+        6 * capacity * gate.size, gate.size * 6, 14,
+    )(place, slots, pieces, gains, gate, up, down)
+
+
+def add_kernel(keep_ref, given_ref, out_ref):
+    out_ref[...] = (
+        keep_ref[...].astype(jnp.float32) + given_ref[...].astype(jnp.float32)
+    ).astype(jnp.bfloat16)
+
+
+def add(keep, given):
+    return call(
+        add_kernel,
+        jax.ShapeDtypeStruct(keep.shape, jnp.bfloat16),
+        [VMEM_SPEC] * 2,
+        [],
+        keep.size, keep.size * 6, 4,
+    )(keep, given)
+
+
+def combine_kernel(sharers, routes_ref, pieces, out_ref):
     count, capacity, cols = pieces.shape
-    sharers = count * cores // HELD
     routes = routes_ref[...]
     taken = [expert_rows(routes, e, capacity) for e in range(HELD)]
-    spread = [taken[k * cores // sharers] for k in range(count)]
+    spread = [taken[k // sharers] for k in range(count)]
     out_ref[...] = lax.dot_general(
         jnp.concatenate(spread, axis=0).astype(jnp.bfloat16),
         pieces[...].reshape(count * capacity, cols),
@@ -461,11 +493,11 @@
     )
 
 
-def combine(cores, routes, pieces):
+def combine(sharers, routes, pieces):
     count, capacity, cols = pieces.shape
     rows = routes.shape[1]
     return call(
-        functools.partial(combine_kernel, cores),
+        functools.partial(combine_kernel, sharers),
         jax.ShapeDtypeStruct((rows, cols), jnp.float32),
         [VMEM_SPEC] * 2,
         [],
@@ -475,6 +507,17 @@
 
 def exchange(blocks):
     return lax.all_to_all(blocks, "attn", split_axis=0, concat_axis=0, tiled=True)
+
+
+def exchange_high(blocks, count):
+    groups = [list(range(low, count, 2)) for low in range(2)]
+    return lax.all_to_all(
+        blocks, "attn", split_axis=0, concat_axis=0, axis_index_groups=groups, tiled=True
+    )
+
+
+def crossed(block, count, mask):
+    return lax.ppermute(block, "attn", [(index, index ^ mask) for index in range(count)])
 
 
 def swap(block):
@@ -504,28 +547,27 @@
     routes = routes.T
     route_weight = route_weight.T
 
-    attended = exchange(
-        attend(
-            count, queries, key_cache, value_cache, new_key, new_value, cache_length,
-            ln_gain,
-        )
-    )
-    mine, gains = project(attended, out_weight)
+    attended = attend(queries, key_cache, value_cache, new_key, new_value, cache_length, ln_gain)
+    both = pair_up(place, attended, crossed(attended, count, 1))
+    quarters = [both] + [crossed(both, count, 2 * k) for k in range(1, count // 2)]
+    mine, gains = project(place, quarters, out_weight)
     attn_stream, chosen, slots = pick(
         place, cores, count, capacity, mine, swap(mine), residual, routes, route_weight
     )
-    outgoing = run_experts(
-        slots, exchange(chosen), gains, gate_weight.T, up_weight.T, down_weight
-    )
-    combined = combine(cores, routes, exchange(outgoing))
+    keep, give = run_experts(
+        place, slots, exchange(chosen), gains, gate_weight.T, up_weight.T, down_weight
+    )
+    summed = exchange_high(add(keep, crossed(give, count, 1)), count)
+    combined = combine(count // 2 // HELD, routes, summed)
     expert_out = (combined + swap(combined)).astype(jnp.bfloat16)
     return (attn_stream, expert_out)
 
 
 def solution(mesh):
-    cols = D // mesh.shape["attn"]
+    count = mesh.shape["attn"]
+    fits = D // count % 256 == 0 and count >= 4 and count & (count - 1) == 0
     return jax.shard_map(
-        shards if cols % 256 == 0 else shards_plain,
+        shards if fits else shards_plain,
         mesh=mesh,
         in_specs=(
             P(("group", "attn"), "expert"),

time: 51.8 us -> 54.7 us (1.056)
  blocking collectives: 38 us -> 20.8 us
  waiting for transfers between devices: 2.57 us -> 12.7 us
  starting transfers between devices: 0.12 us -> 8.96 us
  local copies, waits for them, and re-layouts: 0.03 us -> 0.94 us
    all_to_all x3 -> x1, blocking collectives: 38 us -> 12.6 us  [exchange(): lax.all_to_all(blocks, 'attn', split_axis=0, concat_axis=0, tiled=True)]
    ppermute x0 -> x5, waiting for transfers between devices: none -> 10.1 us  [crossed(): lax.ppermute(block, 'attn', [(index, index ^ mask) for index in range(cou...]
    ppermute x0 -> x5, starting transfers between devices: none -> 8.88 us  [crossed(): lax.ppermute(block, 'attn', [(index, index ^ mask) for index in range(cou...]
    all_to_all x0 -> x1, blocking collectives: none -> 8.21 us  [exchange_high(): lax.all_to_all(blocks, 'attn', split_axis=0, concat_axis=0, axis_index_gr...]
    unnamed x14 -> x18, local copies, waits for them, and re-layouts: 0.03 us -> 0.94 us
    pallas_call x3 -> x5, Pallas kernels: 7.99 us -> 8.14 us  [the longest x1 5.95 us: attend(): call(attend_kernel, jax.ShapeDtypeStruct((row_count, width + gain.shape[0...]
  transfers between devices with their start and end apart: 2 -> 7, of which waited for: 2 -> 6; matrix products, arithmetic and copies ran while one was open for 0% -> 0% of each run, Pallas kernels for 0% -> 0%
where the time goes in v6:
time: 54.7 us; the launch traced here: 54.5 us
  blocking collectives  20.8 us (38%)
  waiting for transfers between devices  12.7 us (23%)
  Pallas kernels  9.74 us (18%)
  starting transfers between devices  8.96 us (16%)
  local copies, waits for them, and re-layouts  0.94 us (2%)
  between operations  0.75 us (1%)
  other arithmetic  0.63 us (1%)
    all_to_all x1, blocking collectives, exchange(): lax.all_to_all(blocks, 'attn', split_axis=0, concat_axis=0, tiled=True)  12.6 us
    ppermute x5, waiting for transfers between devices, crossed(): lax.ppermute(block, 'attn', [(index, index ^ mask) for index in range(cou...  10.1 us
    ppermute x5, starting transfers between devices, crossed(): lax.ppermute(block, 'attn', [(index, index ^ mask) for index in range(cou...  8.88 us
    all_to_all x1, blocking collectives, exchange_high(): lax.all_to_all(blocks, 'attn', split_axis=0, concat_axis=0, axis_index_gr...  8.21 us
    pallas_call x1, Pallas kernels, attend(): call(attend_kernel, jax.ShapeDtypeStruct((row_count, width + gain.shape[0...  5.95 us
    ppermute x2, waiting for transfers between devices, swap(): return lax.ppermute(block, 'expert', [(0, 1), (1, 0)])  2.58 us
    pallas_call x1, Pallas kernels, run_experts(): call(expert_kernel, [jax.ShapeDtypeStruct((count // 2, capacity, cols), j...  1.86 us
  transfers between devices with their start and end apart: 7, of which 6 were waited for; matrix products, arithmetic and copies ran while one was open for 0% of the time, Pallas kernels for 0%

profile of v6, /device:TPU:0, one launch (start us, length us, event | category | flops | bytes accessed | tf_op | source)
XLA Modules:
  0.0 54.5 jit_solution(274985245684173207)
XLA Ops:
  0.6 5.9 %shard_map.149.mine_ref = bf16[4,3456]{1,0:T(4,128)(2,1)} custom-call(s32[4]{0:T(128)} %length_ref.1, bf16[4,3072]{1,0:T(4,128)(2,1)} %query_hbm.1, bf16[4,512,512]{2,1,0:T(8,128)(2,1)} %key_hbm.1, bf16[4,512,512]{2,1,0:T(8,128)(2,1)} %value_hbm.1, bf16[4,512]{1,0:T(4,128)(2,1)} %own_key_hbm.1, bf16[4,512]{1,0:T(4,128)(2,1)} %own_value_hbm.1, f32[768]{0:T(1024)} %gain_hbm.1), custom_call_target="tpu_custom_call" | custom-call | flops 25165824 | bytes 4194304 | tf_op jit(solution)/shard_map/pallas_call | solution.py:286
  6.6 3.0 %collective-permute-start = (bf16[4,3456]{1,0:T(4,128)(2,1)}, bf16[4,3456]{1,0:T(4,128)(2,1)S(1)}, u32[]{:S(2)}, u32[]{:S(2)}) collective-permute-start(bf16[4,3456]{1,0:T(4,128)(2,1)} %shard_map.149.mine_ref), channel_id=1, source_target_pairs={{0,2},{2,0},{4,6},{6,4},{8,10},{10,8},{12,14},{14,12},{1,3},{3,1},... | collective-permute-start | bytes 82952 | tf_op jit(solution)/shard_map/ppermute | solution.py:520
  9.6 2.0 %collective-permute-done.other_ref = bf16[4,3456]{1,0:T(4,128)(2,1)S(1)} collective-permute-done((bf16[4,3456]{1,0:T(4,128)(2,1)}, bf16[4,3456]{1,0:T(4,128)(2,1)S(1)}, u32[]{:S(2)}, u32[]{:S(2)}) %collective-permute-start) | collective-permute-done | bytes 27680 | tf_op jit(solution)/shard_map/ppermute | solution.py:520
  11.7 0.0 slice-start
  11.7 0.0 copy-start.3
  11.7 0.9 %copy-done.3 = bf16[4,3456]{1,0:T(4,128)(2,1)S(1)} copy-done((bf16[4,3456]{1,0:T(4,128)(2,1)S(1)}, bf16[4,3456]{1,0:T(4,128)(2,1)}, u32[]{:S(2)}) %copy-start.3) | copy-done | bytes 27672
  12.6 0.0 slice-start.1
  12.6 0.0 copy-start.4
  12.6 0.0 copy-start.5
  12.6 0.0 copy-start.6
  12.6 4.2 %collective-permute-start.3 = (bf16[2,4,3456]{2,1,0:T(4,128)(2,1)S(1)}, bf16[2,4,3456]{2,1,0:T(4,128)(2,1)S(1)}, u32[]{:S(2)}, u32[]{:S(2)}) collective-permute-start(bf16[2,4,3456]{2,1,0:T(4,128)(2,1)S(1)} %shard_map.150.refs_0_), channel_id=1, source_target_pairs={{0,12},{2,14},{4,8},{6,10},{8,4},{10,6},{12,0},{14,2},{1,13},{3,15... | collective-permute-start | bytes 165896 | tf_op jit(solution)/shard_map/ppermute | solution.py:520
  16.8 0.0 collective-permute-start.2
  16.8 0.6 %collective-permute-start.1 = (bf16[2,4,3456]{2,1,0:T(4,128)(2,1)S(1)}, bf16[2,4,3456]{2,1,0:T(4,128)(2,1)S(1)}, u32[]{:S(2)}, u32[]{:S(2)}) collective-permute-start(bf16[2,4,3456]{2,1,0:T(4,128)(2,1)S(1)} %shard_map.150.refs_0_), channel_id=1, source_target_pairs={{0,4},{2,6},{4,0},{6,2},{8,12},{10,14},{12,8},{14,10},{1,5},{3,7},... | collective-permute-start | bytes 165896 | tf_op jit(solution)/shard_map/ppermute | solution.py:520
  17.4 1.5 %collective-permute-done.3.refs_3_ = bf16[2,4,3456]{2,1,0:T(4,128)(2,1)S(1)} collective-permute-done((bf16[2,4,3456]{2,1,0:T(4,128)(2,1)S(1)}, bf16[2,4,3456]{2,1,0:T(4,128)(2,1)S(1)}, u32[]{:S(2)}, u32[]{:S(2)}) %collective-permute-start.3) | collective-permute-done | bytes 55328 | tf_op jit(solution)/shard_map/ppermute | solution.py:520
  19.0 2.9 %collective-permute-done.2.refs_2_ = bf16[2,4,3456]{2,1,0:T(4,128)(2,1)S(1)} collective-permute-done((bf16[2,4,3456]{2,1,0:T(4,128)(2,1)S(1)}, bf16[2,4,3456]{2,1,0:T(4,128)(2,1)S(1)}, u32[]{:S(2)}, u32[]{:S(2)}) %collective-permute-start.2) | collective-permute-done | bytes 55328 | tf_op jit(solution)/shard_map/ppermute | solution.py:520
  21.8 0.0 collective-permute-done.1.refs_1_
  21.8 0.0 slice-done
  21.8 0.0 slice-done.1
  21.9 1.0 %shard_map.151 = (f32[32,768]{1,0:T(8,128)S(1)}, f32[8,1,768]{2,1,0:T(1,128)S(1)}) custom-call(s32[1]{0:T(128)} %bitcast.place_ref, bf16[2,4,3456]{2,1,0:T(4,128)(2,1)S(1)} %shard_map.150.refs_0_, bf16[2,4,3456]{2,1,0:T(4,128)(2,1)S(1)} %collective-permute-done.1.refs_1_, bf16[2,4,3456]{2,1,0:T(4,128)(2,1)S(1)} %collective-permute-done.2.refs_2_, ...), custom_call_target="tpu_custom_call" | custom-call | flops 150994944 | bytes 4718592 | tf_op jit(solution)/shard_map/pallas_call | solution.py:350
  22.8 0.0 collective-permute-start.4
  22.8 1.3 %collective-permute-done.4.other_ref = f32[32,768]{1,0:T(8,128)S(1)} collective-permute-done((f32[32,768]{1,0:T(8,128)S(1)}, f32[32,768]{1,0:T(8,128)S(1)}, u32[]{:S(2)}, u32[]{:S(2)}) %collective-permute-start.4) | collective-permute-done | bytes 98336 | tf_op jit(solution)/shard_map/ppermute | solution.py:524
  24.1 0.0 copy-done.4
  24.1 0.0 copy-done.5
  24.1 0.0 copy-done.6
  24.1 0.0 copy-start
  24.1 0.0 copy-start.1
  24.2 0.0 copy-start.2
  24.2 0.6 %shard_map.152 = (bf16[32,768]{1,0:T(8,128)(2,1)}, bf16[8,16,768]{2,1,0:T(8,128)(2,1)S(1)}, f32[16,128]{1,0:T(8,128)S(1)}) custom-call(s32[1]{0:T(128)} %bitcast.place_ref, f32[32,768]{1,0:T(8,128)S(1)} %get-tuple-element.9.mine_ref, f32[32,768]{1,0:T(8,128)S(1)} %collective-permute-done.4.other_ref, bf16[32,768]{1,0:T(8,128)(2,1)S(1)} %copy-done.5, ...), custom_call_target="tpu_custom_call" | custom-call | flops 10000000000 | bytes 294912 | tf_op jit(solution)/shard_map/pallas_call | solution.py:408
  24.8 12.6 %all_to_all.10.pieces = bf16[8,16,768]{2,1,0:T(8,128)(2,1)S(1)} all-to-all(bf16[8,16,768]{2,1,0:T(8,128)(2,1)S(1)} %get-tuple-element.12), channel_id=1, replica_groups=mesh['group'=2,'attn'=8,'expert'=2] {'attn'}, dimensions={0} | all-to-all | bytes 393216 | tf_op jit(solution)/shard_map/all_to_all | solution.py:509
  37.4 0.0 copy-done
  37.4 0.0 copy-done.1
  37.4 0.0 copy-done.2
  37.4 1.9 %shard_map.153 = (bf16[4,16,768]{2,1,0:T(8,128)(2,1)S(1)}, bf16[4,16,768]{2,1,0:T(8,128)(2,1)S(1)}) custom-call(s32[1]{0:T(128)} %bitcast.place_ref, f32[16,128]{1,0:T(8,128)S(1)} %get-tuple-element.11.slot_ref, bf16[8,16,768]{2,1,0:T(8,128)(2,1)S(1)} %all_to_all.10.pieces, f32[8,1,768]{2,1,0:T(1,128)S(1)} %get-tuple-element.13.gains, ...), custom_call_target="tpu_custom_call" | custom-call | flops 99090432 | bytes 6193152 | tf_op jit(solution)/shard_map/pallas_call | solution.py:458
  39.2 1.0 %collective-permute-start.5 = (bf16[4,16,768]{2,1,0:T(8,128)(2,1)S(1)}, bf16[4,16,768]{2,1,0:T(8,128)(2,1)S(1)}, u32[]{:S(2)}, u32[]{:S(2)}) collective-permute-start(bf16[4,16,768]{2,1,0:T(8,128)(2,1)S(1)} %get-tuple-element.15), channel_id=1, source_target_pairs={{0,2},{2,0},{4,6},{6,4},{8,10},{10,8},{12,14},{14,12},{1,3},{3,1},... | collective-permute-start | bytes 294920 | tf_op jit(solution)/shard_map/ppermute | solution.py:520
  40.3 3.6 %collective-permute-done.5.given_ref = bf16[4,16,768]{2,1,0:T(8,128)(2,1)S(1)} collective-permute-done((bf16[4,16,768]{2,1,0:T(8,128)(2,1)S(1)}, bf16[4,16,768]{2,1,0:T(8,128)(2,1)S(1)}, u32[]{:S(2)}, u32[]{:S(2)}) %collective-permute-start.5) | collective-permute-done | bytes 98336 | tf_op jit(solution)/shard_map/ppermute | solution.py:520
  43.9 8.2 %all_to_all.11.pieces = bf16[4,16,768]{2,1,0:T(8,128)(2,1)S(1)} all-to-all(bf16[4,16,768]{2,1,0:T(8,128)(2,1)S(1)} %shard_map.154), channel_id=1, replica_groups={{0,4,8,12},{2,6,10,14},{1,5,9,13},{3,7,11,15},{16,20,24,28},{18,22,26,3..., dimensions={0} | all-to-all | bytes 196608 | tf_op jit(solution)/shard_map/all_to_all | solution.py:514
  52.2 0.3 shard_map.155
  52.5 0.1 collective-permute-start.6
  52.5 1.3 %collective-permute-done.6 = f32[32,768]{1,0:T(8,128)S(1)} collective-permute-done((f32[32,768]{1,0:T(8,128)S(1)}, f32[32,768]{1,0:T(8,128)S(1)}, u32[]{:S(2)}, u32[]{:S(2)}) %collective-permute-start.6) | collective-permute-done | bytes 98336 | tf_op jit(solution)/shard_map/ppermute | solution.py:524
  53.8 0.6 %add_convert_fusion = bf16[32,768]{1,0:T(8,128)(2,1)} fusion(f32[32,768]{1,0:T(8,128)S(1)} %shard_map.155, f32[32,768]{1,0:T(8,128)S(1)} %collective-permute-done.6), kind=kLoop, calls=%fused_computation | loop fusion | flops 49152 | bytes 245760 | tf_op jit(solution)/shard_map/convert_element_type | solution.py:562
  (3 shorter events, 0.0 us)
Async XLA Ops:
  6.6 5.1 %collective-permute-start = (bf16[4,3456]{1,0:T(4,128)(2,1)}, bf16[4,3456]{1,0:T(4,128)(2,1)S(1)}, u32[]{:S(2)}, u32[]{:S(2)}) collective-permute-start(bf16[4,3456]{1,0:T(4,128)(2,1)} %shard_map.149.mine_ref), channel_id=1, source_target_pairs={{0,2},{2,0},{4,6},{6,4},{8,10},{10,8},{12,14},{14,12},{1,3},{3,1},... | collective-permute-start | bytes 82952 | tf_op jit(solution)/shard_map/ppermute | solution.py:520
  11.7 10.2 %slice-start = ((s8[4718592]{0:T(1024)(128)(4,1)}), s8[4194304]{0:T(1024)(128)(4,1)S(1)}, s32[]{:S(2)}) async-start(s8[4718592]{0:T(1024)(128)(4,1)} %bitcast.5), calls=%async_computation.2 | async-start | bytes 8388608
  11.7 0.9 %copy-start.3 = (bf16[4,3456]{1,0:T(4,128)(2,1)S(1)}, bf16[4,3456]{1,0:T(4,128)(2,1)}, u32[]{:S(2)}) copy-start(bf16[4,3456]{1,0:T(4,128)(2,1)} %shard_map.149.mine_ref) | copy-start | bytes 82948
  12.6 9.3 %slice-start.1 = ((s8[4718592]{0:T(1024)(128)(4,1)}), s8[524288]{0:T(1024)(128)(4,1)S(1)}, s32[]{:S(2)}) async-start(s8[4718592]{0:T(1024)(128)(4,1)} %bitcast.5), calls=%async_computation.3 | async-start | bytes 1048576
  12.6 11.5 %copy-start.4 = (s32[32,4]{0,1:T(4,128)S(1)}, s32[32,4]{0,1:T(4,128)}, u32[]{:S(2)}) copy-start(s32[32,4]{0,1:T(4,128)} %param.26) | copy-start | bytes 1540
  12.6 11.5 %copy-start.5 = (bf16[32,768]{1,0:T(8,128)(2,1)S(1)}, bf16[32,768]{1,0:T(8,128)(2,1)}, u32[]{:S(2)}) copy-start(bf16[32,768]{1,0:T(8,128)(2,1)} %residual_ref.1) | copy-start | bytes 147460
  12.6 11.5 %copy-start.6 = (f32[32,4]{0,1:T(4,128)S(1)}, f32[32,4]{0,1:T(4,128)}, u32[]{:S(2)}) copy-start(f32[32,4]{0,1:T(4,128)} %param.27) | copy-start | bytes 1540
  12.6 6.4 %collective-permute-start.3 = (bf16[2,4,3456]{2,1,0:T(4,128)(2,1)S(1)}, bf16[2,4,3456]{2,1,0:T(4,128)(2,1)S(1)}, u32[]{:S(2)}, u32[]{:S(2)}) collective-permute-start(bf16[2,4,3456]{2,1,0:T(4,128)(2,1)S(1)} %shard_map.150.refs_0_), channel_id=1, source_target_pairs={{0,12},{2,14},{4,8},{6,10},{8,4},{10,6},{12,0},{14,2},{1,13},{3,15... | collective-permute-start | bytes 165896 | tf_op jit(solution)/shard_map/ppermute | solution.py:520
  16.8 5.1 %collective-permute-start.2 = (bf16[2,4,3456]{2,1,0:T(4,128)(2,1)S(1)}, bf16[2,4,3456]{2,1,0:T(4,128)(2,1)S(1)}, u32[]{:S(2)}, u32[]{:S(2)}) collective-permute-start(bf16[2,4,3456]{2,1,0:T(4,128)(2,1)S(1)} %shard_map.150.refs_0_), channel_id=1, source_target_pairs={{0,8},{2,10},{4,12},{6,14},{8,0},{10,2},{12,4},{14,6},{1,9},{3,11}... | collective-permute-start | bytes 165896 | tf_op jit(solution)/shard_map/ppermute | solution.py:520
  16.8 5.1 %collective-permute-start.1 = (bf16[2,4,3456]{2,1,0:T(4,128)(2,1)S(1)}, bf16[2,4,3456]{2,1,0:T(4,128)(2,1)S(1)}, u32[]{:S(2)}, u32[]{:S(2)}) collective-permute-start(bf16[2,4,3456]{2,1,0:T(4,128)(2,1)S(1)} %shard_map.150.refs_0_), channel_id=1, source_target_pairs={{0,4},{2,6},{4,0},{6,2},{8,12},{10,14},{12,8},{14,10},{1,5},{3,7},... | collective-permute-start | bytes 165896 | tf_op jit(solution)/shard_map/ppermute | solution.py:520
  22.8 1.3 %collective-permute-start.4 = (f32[32,768]{1,0:T(8,128)S(1)}, f32[32,768]{1,0:T(8,128)S(1)}, u32[]{:S(2)}, u32[]{:S(2)}) collective-permute-start(f32[32,768]{1,0:T(8,128)S(1)} %get-tuple-element.9.mine_ref), channel_id=1, source_target_pairs={{0,1},{1,0},{2,3},{3,2},{4,5},{5,4},{6,7},{7,6},{8,9},{9,8},{10,11... | collective-permute-start | bytes 294920 | tf_op jit(solution)/shard_map/ppermute | solution.py:524
  24.1 13.2 %copy-start = (bf16[6144,168]{0,1:T(8,128)(2,1)S(1)}, bf16[6144,168]{0,1:T(8,128)(2,1)}, u32[]{:S(2)}) copy-start(bf16[6144,168]{0,1:T(8,128)(2,1)} %param.23) | copy-start | bytes 6193156
  24.1 13.2 %copy-start.1 = (bf16[6144,168]{0,1:T(8,128)(2,1)S(1)}, bf16[6144,168]{0,1:T(8,128)(2,1)}, u32[]{:S(2)}) copy-start(bf16[6144,168]{0,1:T(8,128)(2,1)} %param.24) | copy-start | bytes 6193156
  24.2 13.2 %copy-start.2 = (bf16[168,6144]{1,0:T(8,128)(2,1)S(1)}, bf16[168,6144]{1,0:T(8,128)(2,1)}, u32[]{:S(2)}) copy-start(bf16[168,6144]{1,0:T(8,128)(2,1)} %down_ref.1) | copy-start | bytes 6193156
  39.2 4.7 %collective-permute-start.5 = (bf16[4,16,768]{2,1,0:T(8,128)(2,1)S(1)}, bf16[4,16,768]{2,1,0:T(8,128)(2,1)S(1)}, u32[]{:S(2)}, u32[]{:S(2)}) collective-permute-start(bf16[4,16,768]{2,1,0:T(8,128)(2,1)S(1)} %get-tuple-element.15), channel_id=1, source_target_pairs={{0,2},{2,0},{4,6},{6,4},{8,10},{10,8},{12,14},{14,12},{1,3},{3,1},... | collective-permute-start | bytes 294920 | tf_op jit(solution)/shard_map/ppermute | solution.py:520
  52.5 1.4 %collective-permute-start.6 = (f32[32,768]{1,0:T(8,128)S(1)}, f32[32,768]{1,0:T(8,128)S(1)}, u32[]{:S(2)}, u32[]{:S(2)}) collective-permute-start(f32[32,768]{1,0:T(8,128)S(1)} %shard_map.155), channel_id=1, source_target_pairs={{0,1},{1,0},{2,3},{3,2},{4,5},{5,4},{6,7},{7,6},{8,9},{9,8},{10,11... | collective-permute-start | bytes 294920 | tf_op jit(solution)/shard_map/ppermute | solution.py:524

commit v7 on v4

--- a/solution.py
+++ b/solution.py
@@ -279,8 +279,7 @@
     width = query_hbm.shape[1]
     for head in range(kv_local * group):
         rows = result_rows[pl.ds(head * row_count, row_count), :].astype(jnp.bfloat16)
-        for index in range(out_ref.shape[0]):
-            out_ref[index, :, head * HEAD_DIM : (head + 1) * HEAD_DIM] = rows
+        out_ref[:, head * HEAD_DIM : (head + 1) * HEAD_DIM] = rows
     gain_row = gain_ref[...].reshape(1, -1)
     half = gain_row.shape[1] // 2
     row = lax.broadcasted_iota(jnp.int32, (row_count, half), 0)
@@ -289,18 +288,17 @@
     gain = jnp.where(row % 2 == 0, left, right)
     upper = gain.astype(jnp.bfloat16).astype(jnp.float32)
     parts = jnp.where(row < 2, upper, gain - upper).astype(jnp.bfloat16)
-    for index in range(out_ref.shape[0]):
-        out_ref[index, :, width:] = parts
-
-
-def attend(count, queries, key_cache, value_cache, new_key, new_value, cache_length, gain):
+    out_ref[:, width:] = parts
+
+
+def attend(queries, key_cache, value_cache, new_key, new_value, cache_length, gain):
     row_count, width = queries.shape
     heads = width // HEAD_DIM
     table = pltpu.VMEM((heads * row_count, HEAD_DIM), jnp.float32)
     nbytes = 2 * key_cache.size * 2
     return call(
         attend_kernel,
-        jax.ShapeDtypeStruct((count, row_count, width + gain.shape[0] // 2), jnp.bfloat16),
+        jax.ShapeDtypeStruct((row_count, width + gain.shape[0] // 2), jnp.bfloat16),
         [SMEM_SPEC] + [HBM_SPEC] * 6,
         [
             pltpu.VMEM(queries.shape, jnp.bfloat16),
@@ -318,33 +316,61 @@
     )(cache_length, queries, key_cache, value_cache, new_key, new_value, gain)
 
 
-def project_kernel(pieces, weight_ref, out_ref, gain_ref, stack):
-    count, rows, _ = pieces.shape
+def stack_kernel(count, place_ref, *refs):
+    out_ref = refs[-1]
+    high = place_ref[0] // 2
+    for k, block in enumerate(refs[:count]):
+        out_ref[high ^ k] = block[...]
+
+
+def stack(place, blocks, *earlier):
+    shape = (len(blocks),) + blocks[0].shape
+    return call(
+        functools.partial(stack_kernel, len(blocks)),
+        jax.ShapeDtypeStruct(shape, blocks[0].dtype),
+        [SMEM_SPEC] + [VMEM_SPEC] * (len(blocks) + len(earlier)),
+        [],
+        0, 4 * len(blocks) * blocks[0].size, 4,
+    )(place, *blocks, *earlier)
+
+
+def ordered(low, mine, other):
+    return jnp.where(low == 0, mine, other), jnp.where(low == 0, other, mine)
+
+
+def project_kernel(place_ref, mine_ref, other_ref, weight_ref, out_ref, gain_ref, rows_ref):
+    highs, rows, _ = mine_ref.shape
     width = weight_ref.shape[0]
-    half = gain_ref.shape[1] // 2
-    for k in range(count):
-        stack[pl.ds(k * rows, rows), :] = pieces[k, :, :width].astype(jnp.float32)
-        parts = pieces[k, :, width:].astype(jnp.float32)
-        gain_ref[pl.ds(k, 1), :half] = parts[0:1] + parts[2:3]
-        gain_ref[pl.ds(k, 1), half:] = parts[1:2] + parts[3:4]
+    half = gain_ref.shape[2] // 2
+    low = lax.rem(place_ref[0], 2)
+    for k in range(highs):
+        both = ordered(
+            low, mine_ref[k].astype(jnp.float32), other_ref[k].astype(jnp.float32)
+        )
+        for index, block in enumerate(both):
+            source = 2 * k + index
+            rows_ref[pl.ds(source * rows, rows), :] = block[:, :width]
+            gain_ref[source, :, :half] = block[0:1, width:] + block[2:3, width:]
+            gain_ref[source, :, half:] = block[1:2, width:] + block[3:4, width:]
     out_ref[...] = jnp.dot(
-        stack[...].astype(jnp.bfloat16), weight_ref[...], preferred_element_type=jnp.float32
-    )
-
-
-def project(pieces, out_weight):
-    count, rows, _ = pieces.shape
+        rows_ref[...].astype(jnp.bfloat16), weight_ref[...], preferred_element_type=jnp.float32
+    )
+
+
+def project(place, mine, other, out_weight):
+    highs, rows, _ = mine.shape
+    count = 2 * highs
     depth, cols = out_weight.shape
     return call(
         project_kernel,
         [
             jax.ShapeDtypeStruct((rows * count, cols), jnp.float32),
-            jax.ShapeDtypeStruct((count, cols), jnp.float32),
+            jax.ShapeDtypeStruct((count, 1, cols), jnp.float32),
         ],
-        [VMEM_SPEC, VMEM_SPEC],
+        [SMEM_SPEC] + [VMEM_SPEC] * 3,
         [pltpu.VMEM((rows * count, depth), jnp.float32)],
         2 * rows * count * out_weight.size, out_weight.size * 2, 10,
-    )(pieces, out_weight)
+    )(place, mine, other, out_weight)
 
 
 def expert_rows(routes, expert, capacity):
@@ -362,55 +388,78 @@
     return jnp.where((slot == place) & (hit > 0.5), 1.0, 0.0)
 
 
-def pick_kernel(cores, place_ref, mine_ref, other_ref, residual_ref, routes_ref, weight_ref,
-                stream_ref, out_ref, slot_ref):
-    count, capacity, _ = out_ref.shape
+def route_kernel(sharers, place_ref, routes_ref, weight_ref, taken_ref, slot_ref):
+    routes = routes_ref[...]
+    capacity = slot_ref.shape[0]
+    taken = [expert_rows(routes, e, capacity) for e in range(HELD)]
+    for e in range(HELD):
+        taken_ref[e] = taken[e]
+    first = place_ref[0] // 2 < sharers
+    expert = jnp.where(first, 0, 1)
+    row_weight = jnp.sum(
+        jnp.where(routes == expert, weight_ref[...], 0.0), axis=0, keepdims=True
+    )
+    mine = jnp.where(first, taken[0], taken[1])
+    slot_ref[...] = jnp.broadcast_to(
+        jnp.sum(mine * row_weight, axis=1, keepdims=True), slot_ref.shape
+    )
+
+
+def route(place, sharers, capacity, routes, route_weight):
+    rows = routes.shape[1]
+    return call(
+        functools.partial(route_kernel, sharers),
+        [
+            jax.ShapeDtypeStruct((HELD, capacity, rows), jnp.float32),
+            jax.ShapeDtypeStruct((capacity, 128), jnp.float32),
+        ],
+        [SMEM_SPEC] + [VMEM_SPEC] * 2,
+        [],
+        EXCHANGE_FLOPS, rows * capacity * 16, 4,
+    )(place, routes, route_weight)
+
+
+def pick_kernel(sharers, place_ref, mine_ref, other_ref, residual_ref, taken_ref, stream_ref,
+                *out_refs):
     stream = (
         residual_ref[...].astype(jnp.float32) + (mine_ref[...] + other_ref[...])
     ).astype(jnp.bfloat16)
     stream_ref[...] = stream
-    routes = routes_ref[...]
-    sharers = count * cores // HELD
-    taken = [expert_rows(routes, e, capacity) for e in range(HELD)]
     chosen = [
         jnp.dot(
-            taken[e].astype(jnp.bfloat16), stream, preferred_element_type=jnp.float32
-        ).astype(jnp.bfloat16)
+            taken_ref[e].astype(jnp.bfloat16), stream, preferred_element_type=jnp.float32
+        )
         for e in range(HELD)
     ]
-    for k in range(count):
-        out_ref[k] = chosen[k * cores // sharers]
-    first = place_ref[0] * cores < sharers
-    expert = jnp.where(first, 0, 1)
-    row_weight = jnp.sum(
-        jnp.where(routes == expert, weight_ref[...], 0.0), axis=0, keepdims=True
-    )
-    mine = jnp.where(first, taken[0], taken[1])
-    slot_ref[...] = jnp.broadcast_to(
-        jnp.sum(mine * row_weight, axis=1, keepdims=True), slot_ref.shape
-    )
-
-
-def pick(place, cores, count, capacity, mine, other, residual, routes, route_weight):
+    high = place_ref[0] // 2
+    for k, out_ref in enumerate(out_refs):
+        out_ref[...] = jnp.where((high ^ k) < sharers, chosen[0], chosen[1]).astype(jnp.bfloat16)
+
+
+def pick(place, sharers, highs, mine, other, residual, taken):
     rows, cols = mine.shape
-    return call(
-        functools.partial(pick_kernel, cores),
-        [
-            jax.ShapeDtypeStruct((rows, cols), jnp.bfloat16),
-            jax.ShapeDtypeStruct((count, capacity, cols), jnp.bfloat16),
-            jax.ShapeDtypeStruct((capacity, 128), jnp.float32),
-        ],
-        [SMEM_SPEC] + [VMEM_SPEC] * 5,
+    capacity = taken.shape[1]
+    return call(
+        functools.partial(pick_kernel, sharers),
+        [jax.ShapeDtypeStruct((rows, cols), jnp.bfloat16)]
+        + [jax.ShapeDtypeStruct((capacity, cols), jnp.bfloat16)] * highs,
+        [SMEM_SPEC] + [VMEM_SPEC] * 4,
         [],
         EXCHANGE_FLOPS, rows * cols * 12, 4,
-    )(place, mine, other, residual, routes, route_weight)
-
-
-def expert_kernel(slot_ref, pieces, gains, gate_ref, up_ref, down_ref, out_ref):
-    count, capacity, cols = pieces.shape
+    )(place, mine, other, residual, taken)
+
+
+def expert_kernel(place_ref, slot_ref, mine_ref, other_ref, gains, gate_ref, up_ref, down_ref,
+                  keep_ref, give_ref):
+    highs, capacity, cols = mine_ref.shape
+    low = lax.rem(place_ref[0], 2)
+    blocks = []
+    for k in range(highs):
+        blocks.extend(
+            ordered(low, mine_ref[k].astype(jnp.float32), other_ref[k].astype(jnp.float32))
+        )
     first = second = 0.0
-    for k in range(count):
-        wide = pieces[k].astype(jnp.float32)
+    for wide in blocks:
         first = first + wide
         second = second + wide * wide
     row_mean = jnp.sum(first, axis=1, keepdims=True) / D
@@ -418,63 +467,87 @@
     inverse = lax.rsqrt(row_var + EPSILON)
     contract = (((1,), (1,)), ((), ()))
     gate_val = up_val = 0.0
-    for k in range(count):
-        block = slice(k * cols, (k + 1) * cols)
-        wide = pieces[k].astype(jnp.float32)
-        normed = ((wide - row_mean) * inverse * gains[pl.ds(k, 1), :]).astype(jnp.bfloat16)
+    for k, wide in enumerate(blocks):
+        columns = slice(k * cols, (k + 1) * cols)
+        normed = ((wide - row_mean) * inverse * gains[k]).astype(jnp.bfloat16)
         gate_val = gate_val + lax.dot_general(
-            gate_ref[:, block], normed, contract, preferred_element_type=jnp.float32
+            gate_ref[:, columns], normed, contract, preferred_element_type=jnp.float32
         )
         up_val = up_val + lax.dot_general(
-            up_ref[:, block], normed, contract, preferred_element_type=jnp.float32
+            up_ref[:, columns], normed, contract, preferred_element_type=jnp.float32
         )
     hidden = (gate_val / (1.0 + jnp.exp(-gate_val)) * up_val).T.astype(jnp.bfloat16)
     slot_weight = slot_ref[:, :1]
-    for k in range(count):
-        block = slice(k * cols, (k + 1) * cols)
-        out_ref[k] = (
-            jnp.dot(hidden, down_ref[:, block], preferred_element_type=jnp.float32) * slot_weight
+    for k in range(highs):
+        columns = slice(2 * k * cols, 2 * (k + 1) * cols)
+        both = (
+            jnp.dot(hidden, down_ref[:, columns], preferred_element_type=jnp.float32)
+            * slot_weight
         ).astype(jnp.bfloat16)
-
-
-def run_experts(slots, pieces, gains, gate, up, down):
+        keep_ref[k], give_ref[k] = ordered(low, both[:, :cols], both[:, cols:])
+
+
+def run_experts(place, slots, mine, other, gains, gate, up, down):
     return call(
         expert_kernel,
-        jax.ShapeDtypeStruct(pieces.shape, jnp.bfloat16),
-        [VMEM_SPEC] * 6,
+        [jax.ShapeDtypeStruct(mine.shape, jnp.bfloat16)] * 2,
+        [SMEM_SPEC] + [VMEM_SPEC] * 7,
         [],
-        6 * pieces.shape[1] * gate.size, gate.size * 6, 14,
-    )(slots, pieces, gains, gate, up, down)
-
-
-def combine_kernel(cores, routes_ref, pieces, out_ref):
-    count, capacity, cols = pieces.shape
-    sharers = count * cores // HELD
-    routes = routes_ref[...]
-    taken = [expert_rows(routes, e, capacity) for e in range(HELD)]
-    spread = [taken[k * cores // sharers] for k in range(count)]
+        6 * mine.shape[1] * gate.size, gate.size * 6, 14,
+    )(place, slots, mine, other, gains, gate, up, down)
+
+
+def add_kernel(place_ref, keep_ref, given_ref, *out_refs):
+    high = place_ref[0] // 2
+    for k, out_ref in enumerate(out_refs):
+        out_ref[...] = (
+            keep_ref[high ^ k].astype(jnp.float32) + given_ref[high ^ k].astype(jnp.float32)
+        ).astype(jnp.bfloat16)
+
+
+def add(place, keep, given):
+    highs, capacity, cols = keep.shape
+    return call(
+        add_kernel,
+        [jax.ShapeDtypeStruct((capacity, cols), jnp.bfloat16)] * highs,
+        [SMEM_SPEC] + [VMEM_SPEC] * 2,
+        [],
+        keep.size, keep.size * 6, 4,
+    )(place, keep, given)
+
+
+def combine_kernel(sharers, place_ref, taken_ref, *refs):
+    pieces, out_ref = refs[:-1], refs[-1]
+    high = place_ref[0] // 2
+    spread = [
+        jnp.where((high ^ k) < sharers, taken_ref[0], taken_ref[1]) for k in range(len(pieces))
+    ]
     out_ref[...] = lax.dot_general(
         jnp.concatenate(spread, axis=0).astype(jnp.bfloat16),
-        pieces[...].reshape(count * capacity, cols),
+        jnp.concatenate([piece[...] for piece in pieces], axis=0),
         (((0,), (0,)), ((), ())),
         preferred_element_type=jnp.float32,
     )
 
 
-def combine(cores, routes, pieces):
-    count, capacity, cols = pieces.shape
-    rows = routes.shape[1]
-    return call(
-        functools.partial(combine_kernel, cores),
+def combine(place, sharers, taken, pieces):
+    capacity, cols = pieces[0].shape
+    rows = taken.shape[2]
+    return call(
+        functools.partial(combine_kernel, sharers),
         jax.ShapeDtypeStruct((rows, cols), jnp.float32),
-        [VMEM_SPEC] * 2,
+        [SMEM_SPEC] + [VMEM_SPEC] * (1 + len(pieces)),
         [],
-        2 * rows * capacity * count * cols, (count * capacity * 2 + rows * 4) * cols, 4,
-    )(routes, pieces)
-
-
-def exchange(blocks):
-    return lax.all_to_all(blocks, "attn", split_axis=0, concat_axis=0, tiled=True)
+        2 * rows * capacity * len(pieces) * cols, (len(pieces) * capacity + 2 * rows) * 2 * cols, 4,
+    )(place, taken, *pieces)
+
+
+def crossed(block, count, mask):
+    return lax.ppermute(block, "attn", [(index, index ^ mask) for index in range(count)])
+
+
+def spread_high(blocks, count):
+    return [blocks[0]] + [crossed(blocks[k], count, 2 * k) for k in range(1, count // 2)]
 
 
 def swap(block):
@@ -498,34 +571,32 @@
     route_weight,
 ):
     count = lax.axis_size("attn")
-    cores = lax.axis_size("expert")
     capacity = routes.shape[0] * TOP // EXPERTS * 2
+    highs = count // 2
+    sharers = count // HELD // 2
     place = lax.axis_index("attn").astype(jnp.int32).reshape(1)
-    routes = routes.T
-    route_weight = route_weight.T
-
-    attended = exchange(
-        attend(
-            count, queries, key_cache, value_cache, new_key, new_value, cache_length,
-            ln_gain,
-        )
-    )
-    mine, gains = project(attended, out_weight)
-    attn_stream, chosen, slots = pick(
-        place, cores, count, capacity, mine, swap(mine), residual, routes, route_weight
-    )
-    outgoing = run_experts(
-        slots, exchange(chosen), gains, gate_weight.T, up_weight.T, down_weight
-    )
-    combined = combine(cores, routes, exchange(outgoing))
+
+    attended = attend(queries, key_cache, value_cache, new_key, new_value, cache_length, ln_gain)
+    taken, slots = route(place, sharers, capacity, routes.T, route_weight.T)
+    block = stack(place, spread_high([attended] * highs, count), slots)
+    mine, gains = project(place, block, crossed(block, count, 1), out_weight)
+    attn_stream, *chosen = pick(place, sharers, highs, mine, swap(mine), residual, taken)
+    block = stack(place, spread_high(chosen, count))
+    keep, give = run_experts(
+        place, slots, block, crossed(block, count, 1), gains,
+        gate_weight.T, up_weight.T, down_weight,
+    )
+    summed = add(place, keep, crossed(give, count, 1))
+    combined = combine(place, sharers, taken, spread_high(summed, count))
     expert_out = (combined + swap(combined)).astype(jnp.bfloat16)
     return (attn_stream, expert_out)
 
 
 def solution(mesh):
-    cols = D // mesh.shape["attn"]
+    count = mesh.shape["attn"]
+    fits = D // count % 256 == 0 and count >= 4 and count & (count - 1) == 0
     return jax.shard_map(
-        shards if cols % 256 == 0 else shards_plain,
+        shards if fits else shards_plain,
         mesh=mesh,
         in_specs=(
             P(("group", "attn"), "expert"),

time: 51.8 us -> 53.6 us (1.035)
  blocking collectives: 38 us -> 0 us
  waiting for transfers between devices: 2.57 us -> 23.5 us
  starting transfers between devices: 0.12 us -> 19.4 us
    all_to_all x3 -> x0, blocking collectives: 38 us -> none  [exchange(): lax.all_to_all(blocks, 'attn', split_axis=0, concat_axis=0, tiled=True)]
    ppermute x0 -> x12, waiting for transfers between devices: none -> 20.9 us  [crossed(): lax.ppermute(block, 'attn', [(index, index ^ mask) for index in range(cou...]
    ppermute x0 -> x12, starting transfers between devices: none -> 19.4 us  [crossed(): lax.ppermute(block, 'attn', [(index, index ^ mask) for index in range(cou...]
    pallas_call x4 -> x8, Pallas kernels: 8.63 us -> 8.25 us  [the longest x1 5.3 us: attend(): call(attend_kernel, jax.ShapeDtypeStruct((row_count, width + gain.shape[0...]
  transfers between devices with their start and end apart: 2 -> 14, of which waited for: 2 -> 11; matrix products, arithmetic and copies ran while one was open for 0% -> 0% of each run, Pallas kernels for 0% -> 0%
where the time goes in v7:
time: 53.6 us; the launch traced here: 53.5 us
  waiting for transfers between devices  23.5 us (44%)
  starting transfers between devices  19.4 us (36%)
  Pallas kernels  9.15 us (17%)
  between operations  0.74 us (1%)
  other arithmetic  0.63 us (1%)
    ppermute x12, waiting for transfers between devices, crossed(): lax.ppermute(block, 'attn', [(index, index ^ mask) for index in range(cou...  20.9 us
    ppermute x12, starting transfers between devices, crossed(): lax.ppermute(block, 'attn', [(index, index ^ mask) for index in range(cou...  19.4 us
    pallas_call x1, Pallas kernels, attend(): call(attend_kernel, jax.ShapeDtypeStruct((row_count, width + gain.shape[0...  5.3 us
    ppermute x2, waiting for transfers between devices, swap(): return lax.ppermute(block, 'expert', [(0, 1), (1, 0)])  2.58 us
    pallas_call x1, Pallas kernels, run_experts(): call(expert_kernel, [jax.ShapeDtypeStruct(mine.shape, jnp.bfloat16)] * 2,...  1.86 us
  transfers between devices with their start and end apart: 14, of which 11 were waited for; matrix products, arithmetic and copies ran while one was open for 0% of the time, Pallas kernels for 0%

profile of v7, /device:TPU:0, one launch (start us, length us, event | category | flops | bytes accessed | tf_op | source)
XLA Modules:
  0.0 53.5 jit_solution(1367589868948068096)
XLA Ops:
  0.6 0.0 copy-start.6
  0.6 0.0 copy-start.5
  0.7 5.3 %shard_map.149.refs_0_ = bf16[4,3456]{1,0:T(4,128)(2,1)} custom-call(s32[4]{0:T(128)} %length_ref.1, bf16[4,3072]{1,0:T(4,128)(2,1)} %query_hbm.1, bf16[4,512,512]{2,1,0:T(8,128)(2,1)} %key_hbm.1, bf16[4,512,512]{2,1,0:T(8,128)(2,1)} %value_hbm.1, bf16[4,512]{1,0:T(4,128)(2,1)} %own_key_hbm.1, bf16[4,512]{1,0:T(4,128)(2,1)} %own_value_hbm.1, f32[768]{0:T(1024)} %gain_hbm.1), custom_call_target="tpu_custom_call" | custom-call | flops 25165824 | bytes 4194304 | tf_op jit(solution)/shard_map/pallas_call | solution.py:299
  6.0 5.1 %collective-permute-start.2 = (bf16[4,3456]{1,0:T(4,128)(2,1)}, bf16[4,3456]{1,0:T(4,128)(2,1)S(1)}, u32[]{:S(2)}, u32[]{:S(2)}) collective-permute-start(bf16[4,3456]{1,0:T(4,128)(2,1)} %shard_map.149.refs_0_), channel_id=1, source_target_pairs={{0,12},{2,14},{4,8},{6,10},{8,4},{10,6},{12,0},{14,2},{1,13},{3,15... | collective-permute-start | bytes 82952 | tf_op jit(solution)/shard_map/ppermute | solution.py:546
  11.1 0.0 collective-permute-start.1
  11.1 0.6 %collective-permute-start = (bf16[4,3456]{1,0:T(4,128)(2,1)}, bf16[4,3456]{1,0:T(4,128)(2,1)S(1)}, u32[]{:S(2)}, u32[]{:S(2)}) collective-permute-start(bf16[4,3456]{1,0:T(4,128)(2,1)} %shard_map.149.refs_0_), channel_id=1, source_target_pairs={{0,4},{2,6},{4,0},{6,2},{8,12},{10,14},{12,8},{14,10},{1,5},{3,7},... | collective-permute-start | bytes 82952 | tf_op jit(solution)/shard_map/ppermute | solution.py:546
  11.7 0.0 copy-done.6
  11.7 0.0 copy-done.5
  11.7 0.0 slice-start.1
  11.7 0.2 shard_map.150
  12.0 1.2 %collective-permute-done.2.refs_3_ = bf16[4,3456]{1,0:T(4,128)(2,1)S(1)} collective-permute-done((bf16[4,3456]{1,0:T(4,128)(2,1)}, bf16[4,3456]{1,0:T(4,128)(2,1)S(1)}, u32[]{:S(2)}, u32[]{:S(2)}) %collective-permute-start.2) | collective-permute-done | bytes 27680 | tf_op jit(solution)/shard_map/ppermute | solution.py:546
  13.1 2.9 %collective-permute-done.1.refs_2_ = bf16[4,3456]{1,0:T(4,128)(2,1)S(1)} collective-permute-done((bf16[4,3456]{1,0:T(4,128)(2,1)}, bf16[4,3456]{1,0:T(4,128)(2,1)S(1)}, u32[]{:S(2)}, u32[]{:S(2)}) %collective-permute-start.1) | collective-permute-done | bytes 27680 | tf_op jit(solution)/shard_map/ppermute | solution.py:546
  16.0 0.0 collective-permute-done.refs_1_
  16.0 0.0 copy-done.3
  16.1 0.0 copy-start.4
  16.1 1.6 %collective-permute-start.3 = (bf16[4,4,3456]{2,1,0:T(4,128)(2,1)S(1)}, bf16[4,4,3456]{2,1,0:T(4,128)(2,1)S(1)}, u32[]{:S(2)}, u32[]{:S(2)}) collective-permute-start(bf16[4,4,3456]{2,1,0:T(4,128)(2,1)S(1)} %shard_map.151.mine_ref), channel_id=1, source_target_pairs={{0,2},{2,0},{4,6},{6,4},{8,10},{10,8},{12,14},{14,12},{1,3},{3,1},... | collective-permute-start | bytes 331784 | tf_op jit(solution)/shard_map/ppermute | solution.py:546
  17.7 3.2 %collective-permute-done.3.other_ref = bf16[4,4,3456]{2,1,0:T(4,128)(2,1)S(1)} collective-permute-done((bf16[4,4,3456]{2,1,0:T(4,128)(2,1)S(1)}, bf16[4,4,3456]{2,1,0:T(4,128)(2,1)S(1)}, u32[]{:S(2)}, u32[]{:S(2)}) %collective-permute-start.3) | collective-permute-done | bytes 110624 | tf_op jit(solution)/shard_map/ppermute | solution.py:546
  20.9 0.0 slice-done
  20.9 0.0 slice-done.1
  20.9 0.9 %shard_map.152 = (f32[32,768]{1,0:T(8,128)S(1)}, f32[8,1,768]{2,1,0:T(1,128)S(1)}) custom-call(s32[1]{0:T(128)} %bitcast.place_ref, bf16[4,4,3456]{2,1,0:T(4,128)(2,1)S(1)} %shard_map.151.mine_ref, bf16[4,4,3456]{2,1,0:T(4,128)(2,1)S(1)} %collective-permute-done.3.other_ref, bf16[3072,768]{1,0:T(8,128)(2,1)S(1)} %bitcast.6), custom_call_target="tpu_custom_call" | custom-call | flops 150994944 | bytes 4718592 | tf_op jit(solution)/shard_map/pallas_call | solution.py:364
  21.8 0.0 collective-permute-start.4
  21.8 1.3 %collective-permute-done.4.other_ref = f32[32,768]{1,0:T(8,128)S(1)} collective-permute-done((f32[32,768]{1,0:T(8,128)S(1)}, f32[32,768]{1,0:T(8,128)S(1)}, u32[]{:S(2)}, u32[]{:S(2)}) %collective-permute-start.4) | collective-permute-done | bytes 98336 | tf_op jit(solution)/shard_map/ppermute | solution.py:554
  23.1 0.0 copy-done.4
  23.1 0.6 %shard_map.153 = (bf16[32,768]{1,0:T(8,128)(2,1)}, bf16[16,768]{1,0:T(8,128)(2,1)S(1)}, bf16[16,768]{1,0:T(8,128)(2,1)S(1)}, bf16[16,768]{1,0:T(8,128)(2,1)S(1)}, bf16[16,768]{1,0:T(8,128)(2,1)S(1)}) custom-call(s32[1]{0:T(128)} %bitcast.place_ref, f32[32,768]{1,0:T(8,128)S(1)} %get-tuple-element.18.mine_ref, ...), custom_call_target="tpu_custom_call" | custom-call | flops 10000000000 | bytes 294912 | tf_op jit(solution)/shard_map/pallas_call | solution.py:442
  23.8 0.0 collective-permute-start.5
  23.8 2.1 %collective-permute-start.6 = (bf16[16,768]{1,0:T(8,128)(2,1)S(1)}, bf16[16,768]{1,0:T(8,128)(2,1)S(1)}, u32[]{:S(2)}, u32[]{:S(2)}) collective-permute-start(bf16[16,768]{1,0:T(8,128)(2,1)S(1)} %get-tuple-element.23), channel_id=1, source_target_pairs={{0,8},{2,10},{4,12},{6,14},{8,0},{10,2},{12,4},{14,6},{1,9},{3,11}... | collective-permute-start | bytes 73736 | tf_op jit(solution)/shard_map/ppermute | solution.py:546
  25.8 2.3 %collective-permute-start.7 = (bf16[16,768]{1,0:T(8,128)(2,1)S(1)}, bf16[16,768]{1,0:T(8,128)(2,1)S(1)}, u32[]{:S(2)}, u32[]{:S(2)}) collective-permute-start(bf16[16,768]{1,0:T(8,128)(2,1)S(1)} %get-tuple-element.24), channel_id=1, source_target_pairs={{0,12},{2,14},{4,8},{6,10},{8,4},{10,6},{12,0},{14,2},{1,13},{3,15... | collective-permute-start | bytes 73736 | tf_op jit(solution)/shard_map/ppermute | solution.py:546
  28.2 0.0 collective-permute-done.5.refs_1_
  28.2 0.3 collective-permute-done.6.refs_2_
  28.5 3.0 %collective-permute-done.7.refs_3_ = bf16[16,768]{1,0:T(8,128)(2,1)S(1)} collective-permute-done((bf16[16,768]{1,0:T(8,128)(2,1)S(1)}, bf16[16,768]{1,0:T(8,128)(2,1)S(1)}, u32[]{:S(2)}, u32[]{:S(2)}) %collective-permute-start.7) | collective-permute-done | bytes 24608 | tf_op jit(solution)/shard_map/ppermute | solution.py:546
  31.5 1.6 %collective-permute-start.8 = (bf16[4,16,768]{2,1,0:T(8,128)(2,1)S(1)}, bf16[4,16,768]{2,1,0:T(8,128)(2,1)S(1)}, u32[]{:S(2)}, u32[]{:S(2)}) collective-permute-start(bf16[4,16,768]{2,1,0:T(8,128)(2,1)S(1)} %shard_map.154.mine_ref), channel_id=1, source_target_pairs={{0,2},{2,0},{4,6},{6,4},{8,10},{10,8},{12,14},{14,12},{1,3},{3,1},... | collective-permute-start | bytes 294920 | tf_op jit(solution)/shard_map/ppermute | solution.py:546
  33.1 3.1 %collective-permute-done.8.other_ref = bf16[4,16,768]{2,1,0:T(8,128)(2,1)S(1)} collective-permute-done((bf16[4,16,768]{2,1,0:T(8,128)(2,1)S(1)}, bf16[4,16,768]{2,1,0:T(8,128)(2,1)S(1)}, u32[]{:S(2)}, u32[]{:S(2)}) %collective-permute-start.8) | collective-permute-done | bytes 98336 | tf_op jit(solution)/shard_map/ppermute | solution.py:546
  36.2 0.0 copy-done
  36.2 0.0 copy-done.1
  36.2 0.0 copy-done.2
  36.2 1.9 %shard_map.155 = (bf16[4,16,768]{2,1,0:T(8,128)(2,1)S(1)}, bf16[4,16,768]{2,1,0:T(8,128)(2,1)S(1)}) custom-call(s32[1]{0:T(128)} %bitcast.place_ref, f32[16,128]{1,0:T(8,128)S(1)} %get-tuple-element.17.refs_4_.slot_ref, bf16[4,16,768]{2,1,0:T(8,128)(2,1)S(1)} %shard_map.154.mine_ref, bf16[4,16,768]{2,1,0:T(8,128)(2,1)S(1)} %collective-permute-done.8.other_ref, ...), custom_call_target="tpu_custom_call" | custom-call | flops 99090432 | bytes 6193152 | tf_op jit(solution)/shard_map/pallas_call | solution.py:491
  38.0 1.6 %collective-permute-start.9 = (bf16[4,16,768]{2,1,0:T(8,128)(2,1)S(1)}, bf16[4,16,768]{2,1,0:T(8,128)(2,1)S(1)}, u32[]{:S(2)}, u32[]{:S(2)}) collective-permute-start(bf16[4,16,768]{2,1,0:T(8,128)(2,1)S(1)} %get-tuple-element.27), channel_id=1, source_target_pairs={{0,2},{2,0},{4,6},{6,4},{8,10},{10,8},{12,14},{14,12},{1,3},{3,1},... | collective-permute-start | bytes 294920 | tf_op jit(solution)/shard_map/ppermute | solution.py:546
  39.6 3.1 %collective-permute-done.9.given_ref = bf16[4,16,768]{2,1,0:T(8,128)(2,1)S(1)} collective-permute-done((bf16[4,16,768]{2,1,0:T(8,128)(2,1)S(1)}, bf16[4,16,768]{2,1,0:T(8,128)(2,1)S(1)}, u32[]{:S(2)}, u32[]{:S(2)}) %collective-permute-start.9) | collective-permute-done | bytes 98336 | tf_op jit(solution)/shard_map/ppermute | solution.py:546
  42.7 0.3 collective-permute-start.10
  43.0 2.7 %collective-permute-start.11 = (bf16[16,768]{1,0:T(8,128)(2,1)S(1)}, bf16[16,768]{1,0:T(8,128)(2,1)S(1)}, u32[]{:S(2)}, u32[]{:S(2)}) collective-permute-start(bf16[16,768]{1,0:T(8,128)(2,1)S(1)} %get-tuple-element.30), channel_id=1, source_target_pairs={{0,8},{2,10},{4,12},{6,14},{8,0},{10,2},{12,4},{14,6},{1,9},{3,11}... | collective-permute-start | bytes 73736 | tf_op jit(solution)/shard_map/ppermute | solution.py:546
  45.7 1.5 %collective-permute-start.12 = (bf16[16,768]{1,0:T(8,128)(2,1)S(1)}, bf16[16,768]{1,0:T(8,128)(2,1)S(1)}, u32[]{:S(2)}, u32[]{:S(2)}) collective-permute-start(bf16[16,768]{1,0:T(8,128)(2,1)S(1)} %get-tuple-element.31), channel_id=1, source_target_pairs={{0,12},{2,14},{4,8},{6,10},{8,4},{10,6},{12,0},{14,2},{1,13},{3,15... | collective-permute-start | bytes 73736 | tf_op jit(solution)/shard_map/ppermute | solution.py:546
  47.2 0.0 collective-permute-done.10.refs_1_
  47.2 0.5 %collective-permute-done.11.refs_2_ = bf16[16,768]{1,0:T(8,128)(2,1)S(1)} collective-permute-done((bf16[16,768]{1,0:T(8,128)(2,1)S(1)}, bf16[16,768]{1,0:T(8,128)(2,1)S(1)}, u32[]{:S(2)}, u32[]{:S(2)}) %collective-permute-start.11) | collective-permute-done | bytes 24608 | tf_op jit(solution)/shard_map/ppermute | solution.py:546
  47.7 3.6 %collective-permute-done.12.refs_3_ = bf16[16,768]{1,0:T(8,128)(2,1)S(1)} collective-permute-done((bf16[16,768]{1,0:T(8,128)(2,1)S(1)}, bf16[16,768]{1,0:T(8,128)(2,1)S(1)}, u32[]{:S(2)}, u32[]{:S(2)}) %collective-permute-start.12) | collective-permute-done | bytes 24608 | tf_op jit(solution)/shard_map/ppermute | solution.py:546
  51.3 0.2 shard_map.157
  51.5 0.0 collective-permute-start.13
  51.5 1.3 %collective-permute-done.13 = f32[32,768]{1,0:T(8,128)S(1)} collective-permute-done((f32[32,768]{1,0:T(8,128)S(1)}, f32[32,768]{1,0:T(8,128)S(1)}, u32[]{:S(2)}, u32[]{:S(2)}) %collective-permute-start.13) | collective-permute-done | bytes 98336 | tf_op jit(solution)/shard_map/ppermute | solution.py:554
  52.8 0.6 %add_convert_fusion = bf16[32,768]{1,0:T(8,128)(2,1)} fusion(f32[32,768]{1,0:T(8,128)S(1)} %shard_map.157, f32[32,768]{1,0:T(8,128)S(1)} %collective-permute-done.13), kind=kLoop, calls=%fused_computation | loop fusion | flops 49152 | bytes 245760 | tf_op jit(solution)/shard_map/convert_element_type | solution.py:591
  (9 shorter events, 0.1 us)
Async XLA Ops:
  0.6 11.1 %copy-start.6 = (f32[32,4]{0,1:T(4,128)S(1)}, f32[32,4]{0,1:T(4,128)}, u32[]{:S(2)}) copy-start(f32[32,4]{0,1:T(4,128)} %param.27) | copy-start | bytes 1540
  0.6 11.1 %copy-start.5 = (s32[32,4]{0,1:T(4,128)S(1)}, s32[32,4]{0,1:T(4,128)}, u32[]{:S(2)}) copy-start(s32[32,4]{0,1:T(4,128)} %param.26) | copy-start | bytes 1540
  6.0 7.2 %collective-permute-start.2 = (bf16[4,3456]{1,0:T(4,128)(2,1)}, bf16[4,3456]{1,0:T(4,128)(2,1)S(1)}, u32[]{:S(2)}, u32[]{:S(2)}) collective-permute-start(bf16[4,3456]{1,0:T(4,128)(2,1)} %shard_map.149.refs_0_), channel_id=1, source_target_pairs={{0,12},{2,14},{4,8},{6,10},{8,4},{10,6},{12,0},{14,2},{1,13},{3,15... | collective-permute-start | bytes 82952 | tf_op jit(solution)/shard_map/ppermute | solution.py:546
  11.1 5.0 %collective-permute-start.1 = (bf16[4,3456]{1,0:T(4,128)(2,1)}, bf16[4,3456]{1,0:T(4,128)(2,1)S(1)}, u32[]{:S(2)}, u32[]{:S(2)}) collective-permute-start(bf16[4,3456]{1,0:T(4,128)(2,1)} %shard_map.149.refs_0_), channel_id=1, source_target_pairs={{0,8},{2,10},{4,12},{6,14},{8,0},{10,2},{12,4},{14,6},{1,9},{3,11}... | collective-permute-start | bytes 82952 | tf_op jit(solution)/shard_map/ppermute | solution.py:546
  11.1 5.0 %collective-permute-start = (bf16[4,3456]{1,0:T(4,128)(2,1)}, bf16[4,3456]{1,0:T(4,128)(2,1)S(1)}, u32[]{:S(2)}, u32[]{:S(2)}) collective-permute-start(bf16[4,3456]{1,0:T(4,128)(2,1)} %shard_map.149.refs_0_), channel_id=1, source_target_pairs={{0,4},{2,6},{4,0},{6,2},{8,12},{10,14},{12,8},{14,10},{1,5},{3,7},... | collective-permute-start | bytes 82952 | tf_op jit(solution)/shard_map/ppermute | solution.py:546
  11.7 9.2 %slice-start = ((s8[4718592]{0:T(1024)(128)(4,1)}), s8[4194304]{0:T(1024)(128)(4,1)S(1)}, s32[]{:S(2)}) async-start(s8[4718592]{0:T(1024)(128)(4,1)} %bitcast.5), calls=%async_computation | async-start | bytes 8388608
  11.7 4.3 %copy-start.3 = (bf16[4,3456]{1,0:T(4,128)(2,1)S(1)}, bf16[4,3456]{1,0:T(4,128)(2,1)}, u32[]{:S(2)}) copy-start(bf16[4,3456]{1,0:T(4,128)(2,1)} %shard_map.149.refs_0_) | copy-start | bytes 82948
  11.7 9.2 %slice-start.1 = ((s8[4718592]{0:T(1024)(128)(4,1)}), s8[524288]{0:T(1024)(128)(4,1)S(1)}, s32[]{:S(2)}) async-start(s8[4718592]{0:T(1024)(128)(4,1)} %bitcast.5), calls=%async_computation.1 | async-start | bytes 1048576
  16.1 7.1 %copy-start.4 = (bf16[32,768]{1,0:T(8,128)(2,1)S(1)}, bf16[32,768]{1,0:T(8,128)(2,1)}, u32[]{:S(2)}) copy-start(bf16[32,768]{1,0:T(8,128)(2,1)} %residual_ref.1) | copy-start | bytes 147460
  16.1 4.8 %collective-permute-start.3 = (bf16[4,4,3456]{2,1,0:T(4,128)(2,1)S(1)}, bf16[4,4,3456]{2,1,0:T(4,128)(2,1)S(1)}, u32[]{:S(2)}, u32[]{:S(2)}) collective-permute-start(bf16[4,4,3456]{2,1,0:T(4,128)(2,1)S(1)} %shard_map.151.mine_ref), channel_id=1, source_target_pairs={{0,2},{2,0},{4,6},{6,4},{8,10},{10,8},{12,14},{14,12},{1,3},{3,1},... | collective-permute-start | bytes 331784 | tf_op jit(solution)/shard_map/ppermute | solution.py:546
  21.8 1.3 %collective-permute-start.4 = (f32[32,768]{1,0:T(8,128)S(1)}, f32[32,768]{1,0:T(8,128)S(1)}, u32[]{:S(2)}, u32[]{:S(2)}) collective-permute-start(f32[32,768]{1,0:T(8,128)S(1)} %get-tuple-element.18.mine_ref), channel_id=1, source_target_pairs={{0,1},{1,0},{2,3},{3,2},{4,5},{5,4},{6,7},{7,6},{8,9},{9,8},{10,11... | collective-permute-start | bytes 294920 | tf_op jit(solution)/shard_map/ppermute | solution.py:554
  23.1 13.0 %copy-start = (bf16[6144,168]{0,1:T(8,128)(2,1)S(1)}, bf16[6144,168]{0,1:T(8,128)(2,1)}, u32[]{:S(2)}) copy-start(bf16[6144,168]{0,1:T(8,128)(2,1)} %param.23) | copy-start | bytes 6193156
  23.1 13.0 %copy-start.1 = (bf16[6144,168]{0,1:T(8,128)(2,1)S(1)}, bf16[6144,168]{0,1:T(8,128)(2,1)}, u32[]{:S(2)}) copy-start(bf16[6144,168]{0,1:T(8,128)(2,1)} %param.24) | copy-start | bytes 6193156
  23.1 13.0 %copy-start.2 = (bf16[168,6144]{1,0:T(8,128)(2,1)S(1)}, bf16[168,6144]{1,0:T(8,128)(2,1)}, u32[]{:S(2)}) copy-start(bf16[168,6144]{1,0:T(8,128)(2,1)} %down_ref.1) | copy-start | bytes 6193156
  23.8 4.4 %collective-permute-start.5 = (bf16[16,768]{1,0:T(8,128)(2,1)S(1)}, bf16[16,768]{1,0:T(8,128)(2,1)S(1)}, u32[]{:S(2)}, u32[]{:S(2)}) collective-permute-start(bf16[16,768]{1,0:T(8,128)(2,1)S(1)} %get-tuple-element.22), channel_id=1, source_target_pairs={{0,4},{2,6},{4,0},{6,2},{8,12},{10,14},{12,8},{14,10},{1,5},{3,7},... | collective-permute-start | bytes 73736 | tf_op jit(solution)/shard_map/ppermute | solution.py:546
  23.8 4.7 %collective-permute-start.6 = (bf16[16,768]{1,0:T(8,128)(2,1)S(1)}, bf16[16,768]{1,0:T(8,128)(2,1)S(1)}, u32[]{:S(2)}, u32[]{:S(2)}) collective-permute-start(bf16[16,768]{1,0:T(8,128)(2,1)S(1)} %get-tuple-element.23), channel_id=1, source_target_pairs={{0,8},{2,10},{4,12},{6,14},{8,0},{10,2},{12,4},{14,6},{1,9},{3,11}... | collective-permute-start | bytes 73736 | tf_op jit(solution)/shard_map/ppermute | solution.py:546
  25.8 5.6 %collective-permute-start.7 = (bf16[16,768]{1,0:T(8,128)(2,1)S(1)}, bf16[16,768]{1,0:T(8,128)(2,1)S(1)}, u32[]{:S(2)}, u32[]{:S(2)}) collective-permute-start(bf16[16,768]{1,0:T(8,128)(2,1)S(1)} %get-tuple-element.24), channel_id=1, source_target_pairs={{0,12},{2,14},{4,8},{6,10},{8,4},{10,6},{12,0},{14,2},{1,13},{3,15... | collective-permute-start | bytes 73736 | tf_op jit(solution)/shard_map/ppermute | solution.py:546
  31.5 4.7 %collective-permute-start.8 = (bf16[4,16,768]{2,1,0:T(8,128)(2,1)S(1)}, bf16[4,16,768]{2,1,0:T(8,128)(2,1)S(1)}, u32[]{:S(2)}, u32[]{:S(2)}) collective-permute-start(bf16[4,16,768]{2,1,0:T(8,128)(2,1)S(1)} %shard_map.154.mine_ref), channel_id=1, source_target_pairs={{0,2},{2,0},{4,6},{6,4},{8,10},{10,8},{12,14},{14,12},{1,3},{3,1},... | collective-permute-start | bytes 294920 | tf_op jit(solution)/shard_map/ppermute | solution.py:546
  38.0 4.7 %collective-permute-start.9 = (bf16[4,16,768]{2,1,0:T(8,128)(2,1)S(1)}, bf16[4,16,768]{2,1,0:T(8,128)(2,1)S(1)}, u32[]{:S(2)}, u32[]{:S(2)}) collective-permute-start(bf16[4,16,768]{2,1,0:T(8,128)(2,1)S(1)} %get-tuple-element.27), channel_id=1, source_target_pairs={{0,2},{2,0},{4,6},{6,4},{8,10},{10,8},{12,14},{14,12},{1,3},{3,1},... | collective-permute-start | bytes 294920 | tf_op jit(solution)/shard_map/ppermute | solution.py:546
  42.7 4.5 %collective-permute-start.10 = (bf16[16,768]{1,0:T(8,128)(2,1)S(1)}, bf16[16,768]{1,0:T(8,128)(2,1)S(1)}, u32[]{:S(2)}, u32[]{:S(2)}) collective-permute-start(bf16[16,768]{1,0:T(8,128)(2,1)S(1)} %get-tuple-element.29), channel_id=1, source_target_pairs={{0,4},{2,6},{4,0},{6,2},{8,12},{10,14},{12,8},{14,10},{1,5},{3,7},... | collective-permute-start | bytes 73736 | tf_op jit(solution)/shard_map/ppermute | solution.py:546
  43.0 4.7 %collective-permute-start.11 = (bf16[16,768]{1,0:T(8,128)(2,1)S(1)}, bf16[16,768]{1,0:T(8,128)(2,1)S(1)}, u32[]{:S(2)}, u32[]{:S(2)}) collective-permute-start(bf16[16,768]{1,0:T(8,128)(2,1)S(1)} %get-tuple-element.30), channel_id=1, source_target_pairs={{0,8},{2,10},{4,12},{6,14},{8,0},{10,2},{12,4},{14,6},{1,9},{3,11}... | collective-permute-start | bytes 73736 | tf_op jit(solution)/shard_map/ppermute | solution.py:546
  45.7 5.6 %collective-permute-start.12 = (bf16[16,768]{1,0:T(8,128)(2,1)S(1)}, bf16[16,768]{1,0:T(8,128)(2,1)S(1)}, u32[]{:S(2)}, u32[]{:S(2)}) collective-permute-start(bf16[16,768]{1,0:T(8,128)(2,1)S(1)} %get-tuple-element.31), channel_id=1, source_target_pairs={{0,12},{2,14},{4,8},{6,10},{8,4},{10,6},{12,0},{14,2},{1,13},{3,15... | collective-permute-start | bytes 73736 | tf_op jit(solution)/shard_map/ppermute | solution.py:546
  51.5 1.3 %collective-permute-start.13 = (f32[32,768]{1,0:T(8,128)S(1)}, f32[32,768]{1,0:T(8,128)S(1)}, u32[]{:S(2)}, u32[]{:S(2)}) collective-permute-start(f32[32,768]{1,0:T(8,128)S(1)} %shard_map.157), channel_id=1, source_target_pairs={{0,1},{1,0},{2,3},{3,2},{4,5},{5,4},{6,7},{7,6},{8,9},{9,8},{10,11... | collective-permute-start | bytes 294920 | tf_op jit(solution)/shard_map/ppermute | solution.py:554

commit v8 on v4

--- a/solution.py
+++ b/solution.py
@@ -181,16 +181,9 @@
     query_rows, key_rows, value_rows, result_rows, key_sem, value_sem, small_sem,
 ):
     row_count, length_max = key_hbm.shape[0], key_hbm.shape[1]
-    kv_local = own_key_ref.shape[1] // HEAD_DIM
+    kv_local = own_key_hbm.shape[1] // HEAD_DIM
     group = HEADS // KV_HEADS
-    block = group * row_count
-    key_copies = [
-        pltpu.make_async_copy(key_hbm.at[r], key_buf.at[r], key_sem.at[r]) for r in range(row_count)
-    ]
-    value_copies = [
-        pltpu.make_async_copy(value_hbm.at[r], value_buf.at[r], value_sem.at[r])
-        for r in range(row_count)
-    ]
+    heads = kv_local * group
     small_copies = [
         pltpu.make_async_copy(source, target, small_sem.at[index])
         for index, (source, target) in enumerate(
@@ -202,8 +195,23 @@
             )
         )
     ]
-    for copy in small_copies + key_copies + value_copies:
+    key_copies = [
+        pltpu.make_async_copy(key_hbm.at[r], key_buf.at[r], key_sem.at[r]) for r in range(row_count)
+    ]
+    value_copies = [
+        pltpu.make_async_copy(value_hbm.at[r], value_buf.at[r], value_sem.at[r])
+        for r in range(row_count)
+    ]
+    batches = [range(first, min(first + 2, row_count)) for first in range(0, row_count, 2)]
+    for copy in small_copies:
         copy.start()
+    for batch in batches:
+        for r in batch:
+            key_copies[r].start()
+        for r in batch:
+            value_copies[r].start()
+    head = lax.broadcasted_iota(jnp.int32, (heads, 1), 0) // group
+    position = lax.broadcasted_iota(jnp.int32, (heads, length_max), 1)
     for copy in small_copies:
         copy.wait()
     for g in range(kv_local):
@@ -211,76 +219,55 @@
         own_key = own_key_ref[:, lanes].astype(jnp.float32)
         own_value = own_value_ref[:, lanes].astype(jnp.float32)
         for i in range(group):
-            head = g * group + i
-            rows = pl.ds(g * block + i * row_count, row_count)
+            index = g * group + i
+            rows = pl.ds(index * row_count, row_count)
             query_rows[rows, :] = query_ref[
-                :, head * HEAD_DIM : (head + 1) * HEAD_DIM
+                :, index * HEAD_DIM : (index + 1) * HEAD_DIM
             ].astype(jnp.float32)
             key_rows[rows, :] = own_key
             value_rows[rows, :] = own_value
     scale = 1.0 / math.sqrt(HEAD_DIM)
-    pair_rows = 2 * block
-    request = lax.broadcasted_iota(jnp.int32, (pair_rows, 1), 0) % row_count
-    lengths = jnp.zeros((pair_rows, 1), jnp.int32)
-    for r in range(row_count):
-        lengths = jnp.where(request == r, length_ref[r], lengths)
-    position = lax.broadcasted_iota(jnp.int32, (pair_rows, length_max), 1)
-    valid = position < lengths
-    pairs = kv_local // 2
-    past = [jnp.zeros((pair_rows, length_max), jnp.float32) for _ in range(pairs)]
-    packed = []
-    for p in range(pairs):
-        rows = query_rows[pl.ds(p * pair_rows, pair_rows), :]
-        lower = rows[:block].astype(jnp.bfloat16)
-        upper = rows[block:].astype(jnp.bfloat16)
-        zero = jnp.zeros_like(lower)
-        packed.append(
-            jnp.concatenate(
-                [
-                    jnp.concatenate([lower, zero], axis=1),
-                    jnp.concatenate([zero, upper], axis=1),
-                ],
-                axis=0,
+    contract = (((1,), (1,)), ((), ()))
+    for batch in batches:
+        spread, own = {}, {}
+        for r in batch:
+            strided = pl.ds(r, heads, stride=row_count)
+            query = query_rows[strided, :]
+            own[r] = jnp.sum(query * key_rows[strided, :], axis=1, keepdims=True) * scale
+            spread[r] = jnp.concatenate(
+                [jnp.where(head == g, query, 0.0) for g in range(kv_local)], axis=1
+            ).astype(jnp.bfloat16)
+        scores = {}
+        for r in batch:
+            key_copies[r].wait()
+            scores[r] = lax.dot_general(
+                spread[r], key_buf[r], contract, preferred_element_type=jnp.float32
             )
-        )
-    for r in range(row_count):
-        key_copies[r].wait()
-        for p in range(pairs):
-            keys = key_buf[r, :, p * 2 * HEAD_DIM : (p + 1) * 2 * HEAD_DIM]
-            scores = lax.dot_general(
-                packed[p], keys, (((1,), (1,)), ((), ())), preferred_element_type=jnp.float32
-            )
-            past[p] = jnp.where(request == r, scores, past[p])
-    probs, own_probs = [], []
-    for p in range(pairs):
-        rows = pl.ds(p * pair_rows, pair_rows)
-        scores = jnp.where(valid, past[p] * scale, NEG_FILL)
-        own = jnp.sum(query_rows[rows, :] * key_rows[rows, :], axis=1, keepdims=True) * scale
-        largest = jnp.maximum(jnp.max(scores, axis=1, keepdims=True), own)
-        weight = jnp.exp(scores - largest)
-        own_weight = jnp.exp(own - largest)
-        total = jnp.sum(weight, axis=1, keepdims=True) + own_weight
-        probs.append((weight / total).astype(jnp.bfloat16))
-        own_probs.append((own_weight / total).astype(jnp.bfloat16).astype(jnp.float32))
-    sums = [jnp.zeros((pair_rows, 2 * HEAD_DIM), jnp.float32) for _ in range(pairs)]
-    for r in range(row_count):
-        value_copies[r].wait()
-        for p in range(pairs):
-            values = value_buf[r, :, p * 2 * HEAD_DIM : (p + 1) * 2 * HEAD_DIM]
-            product = jnp.dot(probs[p], values, preferred_element_type=jnp.float32)
-            sums[p] = jnp.where(request == r, product, sums[p])
-    for p in range(pairs):
-        rows = pl.ds(p * pair_rows, pair_rows)
-        own_part = own_probs[p] * value_rows[rows, :]
-        lower = sums[p][:block, :HEAD_DIM] + own_part[:block]
-        upper = sums[p][block:, HEAD_DIM:] + own_part[block:]
-        result_rows[pl.ds(p * pair_rows, block), :] = lower
-        result_rows[pl.ds(p * pair_rows + block, block), :] = upper
+        probs, own_probs = {}, {}
+        for r in batch:
+            past = jnp.where(position < length_ref[r], scores[r] * scale, NEG_FILL)
+            largest = jnp.maximum(jnp.max(past, axis=1, keepdims=True), own[r])
+            weight = jnp.exp(past - largest)
+            own_weight = jnp.exp(own[r] - largest)
+            inverse = 1.0 / (jnp.sum(weight, axis=1, keepdims=True) + own_weight)
+            probs[r] = (weight * inverse).astype(jnp.bfloat16)
+            own_probs[r] = (own_weight * inverse).astype(jnp.bfloat16).astype(jnp.float32)
+        products = {}
+        for r in batch:
+            value_copies[r].wait()
+            products[r] = jnp.dot(probs[r], value_buf[r], preferred_element_type=jnp.float32)
+        for r in batch:
+            strided = pl.ds(r, heads, stride=row_count)
+            total = own_probs[r] * value_rows[strided, :]
+            for g in range(kv_local):
+                lanes = slice(g * HEAD_DIM, (g + 1) * HEAD_DIM)
+                total = total + jnp.where(head == g, products[r][:, lanes], 0.0)
+            result_rows[strided, :] = total
     width = query_hbm.shape[1]
-    for head in range(kv_local * group):
-        rows = result_rows[pl.ds(head * row_count, row_count), :].astype(jnp.bfloat16)
-        for index in range(out_ref.shape[0]):
-            out_ref[index, :, head * HEAD_DIM : (head + 1) * HEAD_DIM] = rows
+    for index in range(heads):
+        rows = result_rows[pl.ds(index * row_count, row_count), :].astype(jnp.bfloat16)
+        for copy in range(out_ref.shape[0]):
+            out_ref[copy, :, index * HEAD_DIM : (index + 1) * HEAD_DIM] = rows
     gain_row = gain_ref[...].reshape(1, -1)
     half = gain_row.shape[1] // 2
     row = lax.broadcasted_iota(jnp.int32, (row_count, half), 0)
@@ -289,8 +276,8 @@
     gain = jnp.where(row % 2 == 0, left, right)
     upper = gain.astype(jnp.bfloat16).astype(jnp.float32)
     parts = jnp.where(row < 2, upper, gain - upper).astype(jnp.bfloat16)
-    for index in range(out_ref.shape[0]):
-        out_ref[index, :, width:] = parts
+    for copy in range(out_ref.shape[0]):
+        out_ref[copy, :, width:] = parts
 
 
 def attend(count, queries, key_cache, value_cache, new_key, new_value, cache_length, gain):
@@ -362,6 +349,10 @@
     return jnp.where((slot == place) & (hit > 0.5), 1.0, 0.0)
 
 
+def walk(count):
+    return list(range(0, count, 2)) + list(range(count - 1, 0, -2))
+
+
 def pick_kernel(cores, place_ref, mine_ref, other_ref, residual_ref, routes_ref, weight_ref,
                 stream_ref, out_ref, slot_ref):
     count, capacity, _ = out_ref.shape
@@ -378,8 +369,8 @@
         ).astype(jnp.bfloat16)
         for e in range(HELD)
     ]
-    for k in range(count):
-        out_ref[k] = chosen[k * cores // sharers]
+    for slot, k in enumerate(walk(count)):
+        out_ref[slot] = chosen[k * cores // sharers]
     first = place_ref[0] * cores < sharers
     expert = jnp.where(first, 0, 1)
     row_weight = jnp.sum(
@@ -418,9 +409,9 @@
     inverse = lax.rsqrt(row_var + EPSILON)
     contract = (((1,), (1,)), ((), ()))
     gate_val = up_val = 0.0
-    for k in range(count):
+    for slot, k in enumerate(walk(count)):
         block = slice(k * cols, (k + 1) * cols)
-        wide = pieces[k].astype(jnp.float32)
+        wide = pieces[slot].astype(jnp.float32)
         normed = ((wide - row_mean) * inverse * gains[pl.ds(k, 1), :]).astype(jnp.bfloat16)
         gate_val = gate_val + lax.dot_general(
             gate_ref[:, block], normed, contract, preferred_element_type=jnp.float32
@@ -430,9 +421,9 @@
         )
     hidden = (gate_val / (1.0 + jnp.exp(-gate_val)) * up_val).T.astype(jnp.bfloat16)
     slot_weight = slot_ref[:, :1]
-    for k in range(count):
+    for slot, k in enumerate(walk(count)):
         block = slice(k * cols, (k + 1) * cols)
-        out_ref[k] = (
+        out_ref[slot] = (
             jnp.dot(hidden, down_ref[:, block], preferred_element_type=jnp.float32) * slot_weight
         ).astype(jnp.bfloat16)
 
@@ -452,7 +443,7 @@
     sharers = count * cores // HELD
     routes = routes_ref[...]
     taken = [expert_rows(routes, e, capacity) for e in range(HELD)]
-    spread = [taken[k * cores // sharers] for k in range(count)]
+    spread = [taken[k * cores // sharers] for k in walk(count)]
     out_ref[...] = lax.dot_general(
         jnp.concatenate(spread, axis=0).astype(jnp.bfloat16),
         pieces[...].reshape(count * capacity, cols),
@@ -473,8 +464,10 @@
     )(routes, pieces)
 
 
-def exchange(blocks):
-    return lax.all_to_all(blocks, "attn", split_axis=0, concat_axis=0, tiled=True)
+def exchange(blocks, members=None):
+    return lax.all_to_all(
+        blocks, "attn", split_axis=0, concat_axis=0, axis_index_groups=members, tiled=True
+    )
 
 
 def swap(block):
@@ -515,9 +508,9 @@
         place, cores, count, capacity, mine, swap(mine), residual, routes, route_weight
     )
     outgoing = run_experts(
-        slots, exchange(chosen), gains, gate_weight.T, up_weight.T, down_weight
-    )
-    combined = combine(cores, routes, exchange(outgoing))
+        slots, exchange(chosen, [walk(count)]), gains, gate_weight.T, up_weight.T, down_weight
+    )
+    combined = combine(cores, routes, exchange(outgoing, [walk(count)]))
     expert_out = (combined + swap(combined)).astype(jnp.bfloat16)
     return (attn_stream, expert_out)
 

time: 51.8 us -> 52 us (level)
  no operation moved by 1% of the time
where the time goes in v8:
time: 52 us; the launch traced here: 51.8 us
  blocking collectives  38 us (73%)
  Pallas kernels  9.74 us (19%)
  waiting for transfers between devices  2.57 us (5%)
  between operations  0.72 us (1%)
  other arithmetic  0.63 us (1%)
    all_to_all x3, blocking collectives, exchange(): lax.all_to_all(blocks, 'attn', split_axis=0, concat_axis=0, axis_index_gr...  38 us
    pallas_call x1, Pallas kernels, attend(): call(attend_kernel, jax.ShapeDtypeStruct((count, row_count, width + gain....  6.03 us
    ppermute x2, waiting for transfers between devices, swap(): return lax.ppermute(block, 'expert', [(0, 1), (1, 0)])  2.57 us
    pallas_call x1, Pallas kernels, run_experts(): call(expert_kernel, jax.ShapeDtypeStruct(pieces.shape, jnp.bfloat16), [VM...  1.87 us
  transfers between devices with their start and end apart: 2, of which 2 were waited for; matrix products, arithmetic and copies ran while one was open for 0% of the time, Pallas kernels for 0%

profile of v8, /device:TPU:0, one launch (start us, length us, event | category | flops | bytes accessed | tf_op | source)
XLA Modules:
  0.0 51.8 jit_solution(1500039301390336425)
XLA Ops:
  0.6 0.0 copy-start
  0.6 6.0 %shard_map.149 = bf16[8,4,3456]{2,1,0:T(4,128)(2,1)} custom-call(s32[4]{0:T(128)} %length_ref.1, bf16[4,3072]{1,0:T(4,128)(2,1)} %query_hbm.1, bf16[4,512,512]{2,1,0:T(8,128)(2,1)} %key_hbm.1, bf16[4,512,512]{2,1,0:T(8,128)(2,1)} %value_hbm.1, bf16[4,512]{1,0:T(4,128)(2,1)} %own_key_hbm.1, bf16[4,512]{1,0:T(4,128)(2,1)} %own_value_hbm.1, f32[768]{0:T(1024)} %gain_hbm.1), custom_call_target="tpu_custom_call" | custom-call | flops 25165824 | bytes 4194304 | tf_op jit(solution)/shard_map/pallas_call | solution.py:288
  6.7 15.6 %all_to_all.15.pieces = bf16[8,4,3456]{2,1,0:T(4,128)(2,1)S(1)} all-to-all(bf16[8,4,3456]{2,1,0:T(4,128)(2,1)} %shard_map.149), channel_id=1, replica_groups=mesh['group'=2,'attn'=8,'expert'=2] {'attn'}, dimensions={0} | all-to-all | bytes 442368 | tf_op jit(solution)/shard_map/all_to_all | solution.py:468
  22.3 0.0 copy-done
  22.3 0.0 copy-start.4
  22.3 0.0 copy-start.5
  22.3 0.0 copy-start.6
  22.3 0.9 %shard_map.150 = (f32[32,768]{1,0:T(8,128)S(1)}, f32[8,768]{1,0:T(8,128)S(1)}) custom-call(bf16[8,4,3456]{2,1,0:T(4,128)(2,1)S(1)} %all_to_all.15.pieces, bf16[3072,768]{1,0:T(8,128)(2,1)S(1)} %copy-done), custom_call_target="tpu_custom_call" | custom-call | flops 150994944 | bytes 4718592 | tf_op jit(solution)/shard_map/pallas_call | solution.py:325
  23.2 0.0 collective-permute-start
  23.3 1.3 %collective-permute-done.other_ref = f32[32,768]{1,0:T(8,128)S(1)} collective-permute-done((f32[32,768]{1,0:T(8,128)S(1)}, f32[32,768]{1,0:T(8,128)S(1)}, u32[]{:S(2)}, u32[]{:S(2)}) %collective-permute-start) | collective-permute-done | bytes 98336 | tf_op jit(solution)/shard_map/ppermute | solution.py:474
  24.5 0.0 copy-done.4
  24.5 0.0 copy-done.5
  24.5 0.0 copy-done.6
  24.5 0.0 copy-start.1
  24.6 0.0 copy-start.2
  24.6 0.0 copy-start.3
  24.6 0.6 %shard_map.151 = (bf16[32,768]{1,0:T(8,128)(2,1)}, bf16[8,16,768]{2,1,0:T(8,128)(2,1)S(1)}, f32[16,128]{1,0:T(8,128)S(1)}) custom-call(s32[1]{0:T(128)} %bitcast.place_ref, f32[32,768]{1,0:T(8,128)S(1)} %get-tuple-element.7.mine_ref, f32[32,768]{1,0:T(8,128)S(1)} %collective-permute-done.other_ref, bf16[32,768]{1,0:T(8,128)(2,1)S(1)} %copy-done.5, ...), custom_call_target="tpu_custom_call" | custom-call | flops 10000000000 | bytes 294912 | tf_op jit(solution)/shard_map/pallas_call | solution.py:387
  25.2 11.9 %all_to_all.16.pieces = bf16[8,16,768]{2,1,0:T(8,128)(2,1)S(1)} all-to-all(bf16[8,16,768]{2,1,0:T(8,128)(2,1)S(1)} %get-tuple-element.10), channel_id=1, replica_groups={{0,4,8,12,14,10,6,2},{1,5,9,13,15,11,7,3},{16,20,24,28,30,26,22,18},{17..., dimensions={0} | all-to-all | bytes 393216 | tf_op jit(solution)/shard_map/all_to_all | solution.py:468
  37.1 0.0 copy-done.1
  37.1 0.0 copy-done.2
  37.1 0.0 copy-done.3
  37.1 1.9 %shard_map.152 = bf16[8,16,768]{2,1,0:T(8,128)(2,1)S(1)} custom-call(f32[16,128]{1,0:T(8,128)S(1)} %get-tuple-element.9.slot_ref, bf16[8,16,768]{2,1,0:T(8,128)(2,1)S(1)} %all_to_all.16.pieces, f32[8,768]{1,0:T(8,128)S(1)} %get-tuple-element.11.gains, bf16[168,6144]{1,0:T(8,128)(2,1)S(1)} %bitcast.5, bf16[168,6144]{1,0:T(8,128)(2,1)S(1)} %bitcast.6, ...), custom_call_target="tpu_custom_call" | custom-call | flops 99090432 | bytes 6193152 | tf_op jit(solution)/shard_map/pallas_call | solution.py:432
  39.0 10.5 %all_to_all.17.pieces = bf16[8,16,768]{2,1,0:T(8,128)(2,1)S(1)} all-to-all(bf16[8,16,768]{2,1,0:T(8,128)(2,1)S(1)} %shard_map.152), channel_id=1, replica_groups={{0,4,8,12,14,10,6,2},{1,5,9,13,15,11,7,3},{16,20,24,28,30,26,22,18},{17..., dimensions={0} | all-to-all | bytes 393216 | tf_op jit(solution)/shard_map/all_to_all | solution.py:468
  49.5 0.3 shard_map.153
  49.8 0.1 collective-permute-start.1
  49.8 1.3 %collective-permute-done.1 = f32[32,768]{1,0:T(8,128)S(1)} collective-permute-done((f32[32,768]{1,0:T(8,128)S(1)}, f32[32,768]{1,0:T(8,128)S(1)}, u32[]{:S(2)}, u32[]{:S(2)}) %collective-permute-start.1) | collective-permute-done | bytes 98336 | tf_op jit(solution)/shard_map/ppermute | solution.py:474
  51.1 0.6 %add_convert_fusion = bf16[32,768]{1,0:T(8,128)(2,1)} fusion(f32[32,768]{1,0:T(8,128)S(1)} %shard_map.153, f32[32,768]{1,0:T(8,128)S(1)} %collective-permute-done.1), kind=kLoop, calls=%fused_computation | loop fusion | flops 49152 | bytes 245760 | tf_op jit(solution)/shard_map/convert_element_type | solution.py:514
Async XLA Ops:
  0.6 21.7 %copy-start = (bf16[3072,768]{1,0:T(8,128)(2,1)S(1)}, bf16[3072,768]{1,0:T(8,128)(2,1)}, u32[]{:S(2)}) copy-start(bf16[3072,768]{1,0:T(8,128)(2,1)} %weight_ref.1) | copy-start | bytes 14155780
  22.3 2.2 %copy-start.4 = (s32[32,4]{0,1:T(4,128)S(1)}, s32[32,4]{0,1:T(4,128)}, u32[]{:S(2)}) copy-start(s32[32,4]{0,1:T(4,128)} %param.26) | copy-start | bytes 1540
  22.3 2.2 %copy-start.5 = (bf16[32,768]{1,0:T(8,128)(2,1)S(1)}, bf16[32,768]{1,0:T(8,128)(2,1)}, u32[]{:S(2)}) copy-start(bf16[32,768]{1,0:T(8,128)(2,1)} %residual_ref.1) | copy-start | bytes 147460
  22.3 2.2 %copy-start.6 = (f32[32,4]{0,1:T(4,128)S(1)}, f32[32,4]{0,1:T(4,128)}, u32[]{:S(2)}) copy-start(f32[32,4]{0,1:T(4,128)} %param.27) | copy-start | bytes 1540
  23.2 1.3 %collective-permute-start = (f32[32,768]{1,0:T(8,128)S(1)}, f32[32,768]{1,0:T(8,128)S(1)}, u32[]{:S(2)}, u32[]{:S(2)}) collective-permute-start(f32[32,768]{1,0:T(8,128)S(1)} %get-tuple-element.7.mine_ref), channel_id=1, source_target_pairs={{0,1},{1,0},{2,3},{3,2},{4,5},{5,4},{6,7},{7,6},{8,9},{9,8},{10,11... | collective-permute-start | bytes 294920 | tf_op jit(solution)/shard_map/ppermute | solution.py:474
  24.5 12.6 %copy-start.1 = (bf16[6144,168]{0,1:T(8,128)(2,1)S(1)}, bf16[6144,168]{0,1:T(8,128)(2,1)}, u32[]{:S(2)}) copy-start(bf16[6144,168]{0,1:T(8,128)(2,1)} %param.23) | copy-start | bytes 6193156
  24.6 12.6 %copy-start.2 = (bf16[6144,168]{0,1:T(8,128)(2,1)S(1)}, bf16[6144,168]{0,1:T(8,128)(2,1)}, u32[]{:S(2)}) copy-start(bf16[6144,168]{0,1:T(8,128)(2,1)} %param.24) | copy-start | bytes 6193156
  24.6 12.5 %copy-start.3 = (bf16[168,6144]{1,0:T(8,128)(2,1)S(1)}, bf16[168,6144]{1,0:T(8,128)(2,1)}, u32[]{:S(2)}) copy-start(bf16[168,6144]{1,0:T(8,128)(2,1)} %down_ref.1) | copy-start | bytes 6193156
  49.8 1.4 %collective-permute-start.1 = (f32[32,768]{1,0:T(8,128)S(1)}, f32[32,768]{1,0:T(8,128)S(1)}, u32[]{:S(2)}, u32[]{:S(2)}) collective-permute-start(f32[32,768]{1,0:T(8,128)S(1)} %shard_map.153), channel_id=1, source_target_pairs={{0,1},{1,0},{2,3},{3,2},{4,5},{5,4},{6,7},{7,6},{8,9},{9,8},{10,11... | collective-permute-start | bytes 294920 | tf_op jit(solution)/shard_map/ppermute | solution.py:474

commit v9 on v8

--- a/solution.py
+++ b/solution.py
@@ -155,7 +155,6 @@
 
 
 MIB = 1024 * 1024
-ATTEND_MIB = 58_000_000 / MIB
 EXCHANGE_FLOPS = 10**10
 VMEM_SPEC = pl.BlockSpec(memory_space=pltpu.VMEM)
 SMEM_SPEC = pl.BlockSpec(memory_space=pltpu.SMEM)
@@ -171,53 +170,36 @@
         out_specs=VMEM_SPEC if single else [VMEM_SPEC] * len(outs),
         scratch_shapes=scratch,
         cost_estimate=pl.CostEstimate(flops=flops, bytes_accessed=nbytes, transcendentals=0),
-        compiler_params=pltpu.CompilerParams(vmem_limit_bytes=int(vmem_mib * MIB)),
-    )
-
-
-def attend_kernel(
-    length_ref, query_hbm, key_hbm, value_hbm, own_key_hbm, own_value_hbm, gain_hbm, out_ref,
-    query_ref, key_buf, value_buf, own_key_ref, own_value_ref, gain_ref,
-    query_rows, key_rows, value_rows, result_rows, key_sem, value_sem, small_sem,
-):
-    row_count, length_max = key_hbm.shape[0], key_hbm.shape[1]
-    kv_local = own_key_hbm.shape[1] // HEAD_DIM
+        compiler_params=pltpu.CompilerParams(vmem_limit_bytes=vmem_mib * MIB),
+    )
+
+
+def order_kernel(place_ref, out_ref):
+    rows = out_ref.shape[0]
+    before = lax.broadcasted_iota(jnp.int32, (rows, rows), 0) < lax.broadcasted_iota(
+        jnp.int32, (rows, rows), 1
+    )
+    out_ref[...] = jnp.where(before & (place_ref[0] >= 0), 1.0, 0.0).astype(jnp.bfloat16)
+
+
+def order(place, rows):
+    return call(
+        order_kernel,
+        jax.ShapeDtypeStruct((rows, rows), jnp.bfloat16),
+        [SMEM_SPEC],
+        [],
+        EXCHANGE_FLOPS, rows * rows * 2, 2,
+    )(place)
+
+
+def score_kernel(length_ref, query_ref, key_ref, own_key_ref, earlier_ref, probs_ref, own_ref,
+                 query_rows, key_rows):
+    row_count, length_max, width = key_ref.shape
+    kv_local = width // HEAD_DIM
     group = HEADS // KV_HEADS
     heads = kv_local * group
-    small_copies = [
-        pltpu.make_async_copy(source, target, small_sem.at[index])
-        for index, (source, target) in enumerate(
-            (
-                (query_hbm, query_ref),
-                (own_key_hbm, own_key_ref),
-                (own_value_hbm, own_value_ref),
-                (gain_hbm, gain_ref),
-            )
-        )
-    ]
-    key_copies = [
-        pltpu.make_async_copy(key_hbm.at[r], key_buf.at[r], key_sem.at[r]) for r in range(row_count)
-    ]
-    value_copies = [
-        pltpu.make_async_copy(value_hbm.at[r], value_buf.at[r], value_sem.at[r])
-        for r in range(row_count)
-    ]
-    batches = [range(first, min(first + 2, row_count)) for first in range(0, row_count, 2)]
-    for copy in small_copies:
-        copy.start()
-    for batch in batches:
-        for r in batch:
-            key_copies[r].start()
-        for r in batch:
-            value_copies[r].start()
-    head = lax.broadcasted_iota(jnp.int32, (heads, 1), 0) // group
-    position = lax.broadcasted_iota(jnp.int32, (heads, length_max), 1)
-    for copy in small_copies:
-        copy.wait()
     for g in range(kv_local):
-        lanes = slice(g * HEAD_DIM, (g + 1) * HEAD_DIM)
-        own_key = own_key_ref[:, lanes].astype(jnp.float32)
-        own_value = own_value_ref[:, lanes].astype(jnp.float32)
+        own_key = own_key_ref[:, g * HEAD_DIM : (g + 1) * HEAD_DIM].astype(jnp.float32)
         for i in range(group):
             index = g * group + i
             rows = pl.ds(index * row_count, row_count)
@@ -225,45 +207,49 @@
                 :, index * HEAD_DIM : (index + 1) * HEAD_DIM
             ].astype(jnp.float32)
             key_rows[rows, :] = own_key
-            value_rows[rows, :] = own_value
     scale = 1.0 / math.sqrt(HEAD_DIM)
     contract = (((1,), (1,)), ((), ()))
-    for batch in batches:
-        spread, own = {}, {}
-        for r in batch:
-            strided = pl.ds(r, heads, stride=row_count)
-            query = query_rows[strided, :]
-            own[r] = jnp.sum(query * key_rows[strided, :], axis=1, keepdims=True) * scale
-            spread[r] = jnp.concatenate(
-                [jnp.where(head == g, query, 0.0) for g in range(kv_local)], axis=1
-            ).astype(jnp.bfloat16)
-        scores = {}
-        for r in batch:
-            key_copies[r].wait()
-            scores[r] = lax.dot_general(
-                spread[r], key_buf[r], contract, preferred_element_type=jnp.float32
-            )
-        probs, own_probs = {}, {}
-        for r in batch:
-            past = jnp.where(position < length_ref[r], scores[r] * scale, NEG_FILL)
-            largest = jnp.maximum(jnp.max(past, axis=1, keepdims=True), own[r])
-            weight = jnp.exp(past - largest)
-            own_weight = jnp.exp(own[r] - largest)
-            inverse = 1.0 / (jnp.sum(weight, axis=1, keepdims=True) + own_weight)
-            probs[r] = (weight * inverse).astype(jnp.bfloat16)
-            own_probs[r] = (own_weight * inverse).astype(jnp.bfloat16).astype(jnp.float32)
-        products = {}
-        for r in batch:
-            value_copies[r].wait()
-            products[r] = jnp.dot(probs[r], value_buf[r], preferred_element_type=jnp.float32)
-        for r in batch:
-            strided = pl.ds(r, heads, stride=row_count)
-            total = own_probs[r] * value_rows[strided, :]
-            for g in range(kv_local):
-                lanes = slice(g * HEAD_DIM, (g + 1) * HEAD_DIM)
-                total = total + jnp.where(head == g, products[r][:, lanes], 0.0)
-            result_rows[strided, :] = total
-    width = query_hbm.shape[1]
+    head = lax.broadcasted_iota(jnp.int32, (heads, 1), 0) // group
+    position = lax.broadcasted_iota(jnp.int32, (heads, length_max), 1)
+    for r in range(row_count):
+        strided = pl.ds(r, heads, stride=row_count)
+        query = query_rows[strided, :]
+        own = jnp.sum(query * key_rows[strided, :], axis=1, keepdims=True) * scale
+        spread = jnp.concatenate(
+            [jnp.where(head == g, query, 0.0) for g in range(kv_local)], axis=1
+        ).astype(jnp.bfloat16)
+        scores = lax.dot_general(
+            spread, key_ref[r], contract, preferred_element_type=jnp.float32
+        )
+        past = jnp.where(position < length_ref[r], scores * scale, NEG_FILL)
+        largest = jnp.maximum(jnp.max(past, axis=1, keepdims=True), own)
+        weight = jnp.exp(past - largest)
+        own_weight = jnp.exp(own - largest)
+        inverse = 1.0 / (jnp.sum(weight, axis=1, keepdims=True) + own_weight)
+        probs_ref[r] = (weight * inverse).astype(jnp.bfloat16)
+        own_prob = (own_weight * inverse).astype(jnp.bfloat16).astype(jnp.float32)
+        own_ref[r] = jnp.broadcast_to(own_prob, (heads, HEAD_DIM))
+
+
+def value_kernel(probs_ref, own_ref, value_ref, own_value_ref, gain_ref, out_ref, value_rows,
+                 result_rows):
+    row_count, length_max, width = value_ref.shape
+    kv_local = width // HEAD_DIM
+    group = HEADS // KV_HEADS
+    heads = kv_local * group
+    for g in range(kv_local):
+        own_value = own_value_ref[:, g * HEAD_DIM : (g + 1) * HEAD_DIM].astype(jnp.float32)
+        for i in range(group):
+            value_rows[pl.ds((g * group + i) * row_count, row_count), :] = own_value
+    head = lax.broadcasted_iota(jnp.int32, (heads, 1), 0) // group
+    for r in range(row_count):
+        strided = pl.ds(r, heads, stride=row_count)
+        product = jnp.dot(probs_ref[r], value_ref[r], preferred_element_type=jnp.float32)
+        total = own_ref[r] * value_rows[strided, :]
+        for g in range(kv_local):
+            lanes = slice(g * HEAD_DIM, (g + 1) * HEAD_DIM)
+            total = total + jnp.where(head == g, product[:, lanes], 0.0)
+        result_rows[strided, :] = total
     for index in range(heads):
         rows = result_rows[pl.ds(index * row_count, row_count), :].astype(jnp.bfloat16)
         for copy in range(out_ref.shape[0]):
@@ -277,32 +263,33 @@
     upper = gain.astype(jnp.bfloat16).astype(jnp.float32)
     parts = jnp.where(row < 2, upper, gain - upper).astype(jnp.bfloat16)
     for copy in range(out_ref.shape[0]):
-        out_ref[copy, :, width:] = parts
-
-
-def attend(count, queries, key_cache, value_cache, new_key, new_value, cache_length, gain):
+        out_ref[copy, :, heads * HEAD_DIM :] = parts
+
+
+def attend(
+    count, queries, key_cache, value_cache, new_key, new_value, cache_length, gain, earlier
+):
     row_count, width = queries.shape
     heads = width // HEAD_DIM
+    length_max = key_cache.shape[1]
     table = pltpu.VMEM((heads * row_count, HEAD_DIM), jnp.float32)
-    nbytes = 2 * key_cache.size * 2
+    probs, own = call(
+        score_kernel,
+        [
+            jax.ShapeDtypeStruct((row_count, heads, length_max), jnp.bfloat16),
+            jax.ShapeDtypeStruct((row_count, heads, HEAD_DIM), jnp.float32),
+        ],
+        [SMEM_SPEC] + [VMEM_SPEC] * 4,
+        [table, table],
+        2 * key_cache.size * heads, key_cache.size * 2, 8,
+    )(cache_length, queries, key_cache, new_key, earlier)
     return call(
-        attend_kernel,
+        value_kernel,
         jax.ShapeDtypeStruct((count, row_count, width + gain.shape[0] // 2), jnp.bfloat16),
-        [SMEM_SPEC] + [HBM_SPEC] * 6,
-        [
-            pltpu.VMEM(queries.shape, jnp.bfloat16),
-            pltpu.VMEM(key_cache.shape, jnp.bfloat16),
-            pltpu.VMEM(value_cache.shape, jnp.bfloat16),
-            pltpu.VMEM(new_key.shape, jnp.bfloat16),
-            pltpu.VMEM(new_value.shape, jnp.bfloat16),
-            pltpu.VMEM(gain.shape, jnp.float32),
-            table, table, table, table,
-            pltpu.SemaphoreType.DMA((row_count,)),
-            pltpu.SemaphoreType.DMA((row_count,)),
-            pltpu.SemaphoreType.DMA((4,)),
-        ],
-        4 * key_cache.size * 6, nbytes, ATTEND_MIB,
-    )(cache_length, queries, key_cache, value_cache, new_key, new_value, gain)
+        [VMEM_SPEC] * 5,
+        [table, table],
+        EXCHANGE_FLOPS, value_cache.size * 2, 8,
+    )(probs, own, value_cache, new_value, gain)
 
 
 def project_kernel(pieces, weight_ref, out_ref, gain_ref, stack):
@@ -334,15 +321,12 @@
     )(pieces, out_weight)
 
 
-def expert_rows(routes, expert, capacity):
+def expert_rows(routes, earlier, expert, capacity):
     row_count = routes.shape[1]
     hit = jnp.max((routes == expert).astype(jnp.float32), axis=0, keepdims=True)
-    earlier = lax.broadcasted_iota(jnp.int32, (row_count, row_count), 0) < lax.broadcasted_iota(
-        jnp.int32, (row_count, row_count), 1
-    )
     slot = jnp.dot(
         jnp.broadcast_to(hit, (8, row_count)).astype(jnp.bfloat16),
-        earlier.astype(jnp.bfloat16),
+        earlier,
         preferred_element_type=jnp.float32,
     )[:1]
     place = lax.broadcasted_iota(jnp.int32, (capacity, row_count), 0).astype(jnp.float32)
@@ -353,7 +337,7 @@
     return list(range(0, count, 2)) + list(range(count - 1, 0, -2))
 
 
-def pick_kernel(cores, place_ref, mine_ref, other_ref, residual_ref, routes_ref, weight_ref,
+def pick_kernel(cores, place_ref, mine_ref, other_ref, residual_ref, routes_ref, weight_ref, earlier_ref,
                 stream_ref, out_ref, slot_ref):
     count, capacity, _ = out_ref.shape
     stream = (
@@ -362,15 +346,15 @@
     stream_ref[...] = stream
     routes = routes_ref[...]
     sharers = count * cores // HELD
-    taken = [expert_rows(routes, e, capacity) for e in range(HELD)]
+    taken = [expert_rows(routes, earlier_ref[...], e, capacity) for e in range(HELD)]
     chosen = [
         jnp.dot(
             taken[e].astype(jnp.bfloat16), stream, preferred_element_type=jnp.float32
         ).astype(jnp.bfloat16)
         for e in range(HELD)
     ]
-    for slot, k in enumerate(walk(count)):
-        out_ref[slot] = chosen[k * cores // sharers]
+    for k in range(count):
+        out_ref[k] = chosen[k * cores // sharers]
     first = place_ref[0] * cores < sharers
     expert = jnp.where(first, 0, 1)
     row_weight = jnp.sum(
@@ -382,7 +366,7 @@
     )
 
 
-def pick(place, cores, count, capacity, mine, other, residual, routes, route_weight):
+def pick(place, cores, count, capacity, mine, other, residual, routes, route_weight, earlier):
     rows, cols = mine.shape
     return call(
         functools.partial(pick_kernel, cores),
@@ -391,10 +375,10 @@
             jax.ShapeDtypeStruct((count, capacity, cols), jnp.bfloat16),
             jax.ShapeDtypeStruct((capacity, 128), jnp.float32),
         ],
-        [SMEM_SPEC] + [VMEM_SPEC] * 5,
+        [SMEM_SPEC] + [VMEM_SPEC] * 6,
         [],
         EXCHANGE_FLOPS, rows * cols * 12, 4,
-    )(place, mine, other, residual, routes, route_weight)
+    )(place, mine, other, residual, routes, route_weight, earlier)
 
 
 def expert_kernel(slot_ref, pieces, gains, gate_ref, up_ref, down_ref, out_ref):
@@ -409,9 +393,9 @@
     inverse = lax.rsqrt(row_var + EPSILON)
     contract = (((1,), (1,)), ((), ()))
     gate_val = up_val = 0.0
-    for slot, k in enumerate(walk(count)):
+    for k in range(count):
         block = slice(k * cols, (k + 1) * cols)
-        wide = pieces[slot].astype(jnp.float32)
+        wide = pieces[k].astype(jnp.float32)
         normed = ((wide - row_mean) * inverse * gains[pl.ds(k, 1), :]).astype(jnp.bfloat16)
         gate_val = gate_val + lax.dot_general(
             gate_ref[:, block], normed, contract, preferred_element_type=jnp.float32
@@ -438,11 +422,11 @@
     )(slots, pieces, gains, gate, up, down)
 
 
-def combine_kernel(cores, routes_ref, pieces, out_ref):
+def combine_kernel(cores, routes_ref, earlier_ref, pieces, out_ref):
     count, capacity, cols = pieces.shape
     sharers = count * cores // HELD
     routes = routes_ref[...]
-    taken = [expert_rows(routes, e, capacity) for e in range(HELD)]
+    taken = [expert_rows(routes, earlier_ref[...], e, capacity) for e in range(HELD)]
     spread = [taken[k * cores // sharers] for k in walk(count)]
     out_ref[...] = lax.dot_general(
         jnp.concatenate(spread, axis=0).astype(jnp.bfloat16),
@@ -452,16 +436,16 @@
     )
 
 
-def combine(cores, routes, pieces):
+def combine(cores, routes, earlier, pieces):
     count, capacity, cols = pieces.shape
     rows = routes.shape[1]
     return call(
         functools.partial(combine_kernel, cores),
         jax.ShapeDtypeStruct((rows, cols), jnp.float32),
-        [VMEM_SPEC] * 2,
+        [VMEM_SPEC] * 3,
         [],
         2 * rows * capacity * count * cols, (count * capacity * 2 + rows * 4) * cols, 4,
-    )(routes, pieces)
+    )(routes, earlier, pieces)
 
 
 def exchange(blocks, members=None):
@@ -497,20 +481,21 @@
     routes = routes.T
     route_weight = route_weight.T
 
+    earlier = order(place, routes.shape[1])
     attended = exchange(
         attend(
             count, queries, key_cache, value_cache, new_key, new_value, cache_length,
-            ln_gain,
+            ln_gain, earlier,
         )
     )
     mine, gains = project(attended, out_weight)
     attn_stream, chosen, slots = pick(
-        place, cores, count, capacity, mine, swap(mine), residual, routes, route_weight
+        place, cores, count, capacity, mine, swap(mine), residual, routes, route_weight, earlier
     )
     outgoing = run_experts(
-        slots, exchange(chosen, [walk(count)]), gains, gate_weight.T, up_weight.T, down_weight
-    )
-    combined = combine(cores, routes, exchange(outgoing, [walk(count)]))
+        slots, exchange(chosen), gains, gate_weight.T, up_weight.T, down_weight
+    )
+    combined = combine(cores, routes, earlier, exchange(outgoing, [walk(count)]))
     expert_out = (combined + swap(combined)).astype(jnp.bfloat16)
     return (attn_stream, expert_out)
 

time: 52 us -> 49.6 us (0.954)
  Pallas kernels: 9.74 us -> 5.67 us
  local copies, waits for them, and re-layouts: 0.03 us -> 1.58 us
    pallas_call x1 -> x3, Pallas kernels: 6.03 us -> 1.98 us  [the longest x1 1.45 us: attend(): call(score_kernel, [jax.ShapeDtypeStruct((row_count, heads, length_max),...]
    unnamed x14 -> x30, local copies, waits for them, and re-layouts: 0.03 us -> 1.58 us
where the time goes in v9:
time: 49.6 us; the launch traced here: 49.4 us
  blocking collectives  38 us (77%)
  Pallas kernels  5.67 us (11%)
  waiting for transfers between devices  2.58 us (5%)
  local copies, waits for them, and re-layouts  1.58 us (3%)
  between operations  0.83 us (2%)
  other arithmetic  0.63 us (1%)
    all_to_all x3, blocking collectives, exchange(): lax.all_to_all(blocks, 'attn', split_axis=0, concat_axis=0, axis_index_gr...  38 us
    ppermute x2, waiting for transfers between devices, swap(): return lax.ppermute(block, 'expert', [(0, 1), (1, 0)])  2.58 us
    pallas_call x1, Pallas kernels, run_experts(): call(expert_kernel, jax.ShapeDtypeStruct(pieces.shape, jnp.bfloat16), [VM...  1.87 us
    unnamed x30, local copies, waits for them, and re-layouts  1.58 us
    pallas_call x1, Pallas kernels, attend(): call(score_kernel, [jax.ShapeDtypeStruct((row_count, heads, length_max),...  1.45 us
  transfers between devices with their start and end apart: 2, of which 2 were waited for; matrix products, arithmetic and copies ran while one was open for 0% of the time, Pallas kernels for 0%

profile of v9, /device:TPU:0, one launch (start us, length us, event | category | flops | bytes accessed | tf_op | source)
XLA Modules:
  0.0 49.4 jit_solution(4392011698325349228)
XLA Ops:
  0.6 0.0 copy-start
  0.6 0.0 copy-start.4
  0.7 0.0 copy-start.5
  0.7 0.0 copy-start.7
  0.7 0.0 copy-start.8
  0.7 0.0 copy-start.10
  0.7 0.0 copy-start.11
  0.7 1.5 %copy-done = bf16[4,512,512]{2,1,0:T(8,128)(2,1)S(1)} copy-done((bf16[4,512,512]{2,1,0:T(8,128)(2,1)S(1)}, bf16[4,512,512]{2,1,0:T(8,128)(2,1)}, u32[]{:S(2)}) %copy-start) | copy-done | bytes 2097176
  2.2 0.0 copy-done.4
  2.2 0.0 copy-done.5
  2.2 0.0 copy-done.7
  2.2 0.0 slice-start
  2.2 1.4 %shard_map.150 = (bf16[4,24,512]{2,1,0:T(8,128)(2,1)S(1)}, f32[4,24,128]{2,1,0:T(8,128)S(1)}) custom-call(s32[4]{0:T(128)S(1)} %copy-done.7, bf16[4,3072]{1,0:T(4,128)(2,1)S(1)} %copy-done.4, bf16[4,512,512]{2,1,0:T(8,128)(2,1)S(1)} %copy-done, bf16[4,512]{1,0:T(4,128)(2,1)S(1)} %copy-done.5, bf16[32,32]{1,0:T(8,128)(2,1)S(1)} %shard_map.149.earlier_ref), custom_call_target="tpu_custom_call" | custom-call | flops 50331648 | bytes 2097152 | tf_op jit(solution)/shard_map/pallas_call | solution.py:276
  3.7 0.0 copy-done.8
  3.7 0.0 copy-done.10
  3.7 0.0 copy-done.11
  3.7 0.0 slice-start.1
  3.7 0.5 %shard_map.151 = bf16[8,4,3456]{2,1,0:T(4,128)(2,1)S(1)} custom-call(bf16[4,24,512]{2,1,0:T(8,128)(2,1)S(1)} %get-tuple-element.9.probs_ref, f32[4,24,128]{2,1,0:T(8,128)S(1)} %get-tuple-element.10.own_ref, bf16[4,512,512]{2,1,0:T(8,128)(2,1)S(1)} %copy-done.8, bf16[4,512]{1,0:T(4,128)(2,1)S(1)} %copy-done.10, f32[768]{0:T(1024)S(1)} %copy-done.11), custom_call_target="tpu_custom_call" | custom-call | flops 10000000000 | bytes 2097152 | tf_op jit(solution)/shard_map/pallas_call | solution.py:286
  4.3 15.4 %all_to_all.15.pieces = bf16[8,4,3456]{2,1,0:T(4,128)(2,1)S(1)} all-to-all(bf16[8,4,3456]{2,1,0:T(4,128)(2,1)S(1)} %shard_map.151), channel_id=1, replica_groups=mesh['group'=2,'attn'=8,'expert'=2] {'attn'}, dimensions={0} | all-to-all | bytes 442368 | tf_op jit(solution)/shard_map/all_to_all | solution.py:452
  19.7 0.0 slice-done
  19.7 0.0 slice-done.1
  19.7 0.0 copy-start.6
  19.7 0.0 copy-start.9
  19.7 0.0 copy-start.12
  19.7 0.9 %shard_map.152 = (f32[32,768]{1,0:T(8,128)S(1)}, f32[8,768]{1,0:T(8,128)S(1)}) custom-call(bf16[8,4,3456]{2,1,0:T(4,128)(2,1)S(1)} %all_to_all.15.pieces, bf16[3072,768]{1,0:T(8,128)(2,1)S(1)} %bitcast.6), custom_call_target="tpu_custom_call" | custom-call | flops 150994944 | bytes 4718592 | tf_op jit(solution)/shard_map/pallas_call | solution.py:312
  20.6 0.0 collective-permute-start
  20.6 1.3 %collective-permute-done.other_ref = f32[32,768]{1,0:T(8,128)S(1)} collective-permute-done((f32[32,768]{1,0:T(8,128)S(1)}, f32[32,768]{1,0:T(8,128)S(1)}, u32[]{:S(2)}, u32[]{:S(2)}) %collective-permute-start) | collective-permute-done | bytes 98336 | tf_op jit(solution)/shard_map/ppermute | solution.py:458
  21.9 0.0 copy-done.6
  21.9 0.0 copy-done.9
  21.9 0.0 copy-done.12
  21.9 0.0 copy-start.1
  21.9 0.0 copy-start.2
  22.0 0.0 copy-start.3
  22.0 0.6 %shard_map.153 = (bf16[32,768]{1,0:T(8,128)(2,1)}, bf16[8,16,768]{2,1,0:T(8,128)(2,1)S(1)}, f32[16,128]{1,0:T(8,128)S(1)}) custom-call(s32[1]{0:T(128)} %bitcast.place_ref, f32[32,768]{1,0:T(8,128)S(1)} %get-tuple-element.11.mine_ref, f32[32,768]{1,0:T(8,128)S(1)} %collective-permute-done.other_ref, bf16[32,768]{1,0:T(8,128)(2,1)S(1)} %copy-done.9, ...), custom_call_target="tpu_custom_call" | custom-call | flops 10000000000 | bytes 294912 | tf_op jit(solution)/shard_map/pallas_call | solution.py:371
  22.6 11.6 %all_to_all.16.pieces = bf16[8,16,768]{2,1,0:T(8,128)(2,1)S(1)} all-to-all(bf16[8,16,768]{2,1,0:T(8,128)(2,1)S(1)} %get-tuple-element.14), channel_id=1, replica_groups=mesh['group'=2,'attn'=8,'expert'=2] {'attn'}, dimensions={0} | all-to-all | bytes 393216 | tf_op jit(solution)/shard_map/all_to_all | solution.py:452
  34.2 0.0 copy-done.1
  34.2 0.0 copy-done.2
  34.2 0.0 copy-done.3
  34.2 1.9 %shard_map.154 = bf16[8,16,768]{2,1,0:T(8,128)(2,1)S(1)} custom-call(f32[16,128]{1,0:T(8,128)S(1)} %get-tuple-element.13.slot_ref, bf16[8,16,768]{2,1,0:T(8,128)(2,1)S(1)} %all_to_all.16.pieces, f32[8,768]{1,0:T(8,128)S(1)} %get-tuple-element.15.gains, bf16[168,6144]{1,0:T(8,128)(2,1)S(1)} %bitcast.7, bf16[168,6144]{1,0:T(8,128)(2,1)S(1)} %bitcast.8, ...), custom_call_target="tpu_custom_call" | custom-call | flops 99090432 | bytes 6193152 | tf_op jit(solution)/shard_map/pallas_call | solution.py:416
  36.1 11.0 %all_to_all.17.pieces = bf16[8,16,768]{2,1,0:T(8,128)(2,1)S(1)} all-to-all(bf16[8,16,768]{2,1,0:T(8,128)(2,1)S(1)} %shard_map.154), channel_id=1, replica_groups={{0,4,8,12,14,10,6,2},{1,5,9,13,15,11,7,3},{16,20,24,28,30,26,22,18},{17..., dimensions={0} | all-to-all | bytes 393216 | tf_op jit(solution)/shard_map/all_to_all | solution.py:452
  47.1 0.3 shard_map.155
  47.4 0.1 collective-permute-start.1
  47.5 1.3 %collective-permute-done.1 = f32[32,768]{1,0:T(8,128)S(1)} collective-permute-done((f32[32,768]{1,0:T(8,128)S(1)}, f32[32,768]{1,0:T(8,128)S(1)}, u32[]{:S(2)}, u32[]{:S(2)}) %collective-permute-start.1) | collective-permute-done | bytes 98336 | tf_op jit(solution)/shard_map/ppermute | solution.py:458
  48.8 0.6 %add_convert_fusion = bf16[32,768]{1,0:T(8,128)(2,1)} fusion(f32[32,768]{1,0:T(8,128)S(1)} %shard_map.155, f32[32,768]{1,0:T(8,128)S(1)} %collective-permute-done.1), kind=kLoop, calls=%fused_computation | loop fusion | flops 49152 | bytes 245760 | tf_op jit(solution)/shard_map/convert_element_type | solution.py:499
  (2 shorter events, 0.0 us)
Async XLA Ops:
  0.6 1.6 %copy-start = (bf16[4,512,512]{2,1,0:T(8,128)(2,1)S(1)}, bf16[4,512,512]{2,1,0:T(8,128)(2,1)}, u32[]{:S(2)}) copy-start(bf16[4,512,512]{2,1,0:T(8,128)(2,1)} %key_ref.1) | copy-start | bytes 6291460
  0.6 1.6 %copy-start.4 = (bf16[4,3072]{1,0:T(4,128)(2,1)S(1)}, bf16[4,3072]{1,0:T(4,128)(2,1)}, u32[]{:S(2)}) copy-start(bf16[4,3072]{1,0:T(4,128)(2,1)} %query_ref.1) | copy-start | bytes 73732
  0.7 1.6 %copy-start.5 = (bf16[4,512]{1,0:T(4,128)(2,1)S(1)}, bf16[4,512]{1,0:T(4,128)(2,1)}, u32[]{:S(2)}) copy-start(bf16[4,512]{1,0:T(4,128)(2,1)} %own_key_ref.1) | copy-start | bytes 12292
  0.7 1.6 %copy-start.7 = (s32[4]{0:T(128)S(1)}, s32[4]{0:T(128)}, u32[]{:S(2)}) copy-start(s32[4]{0:T(128)} %length_ref.1) | copy-start | bytes 52
  0.7 3.0 %copy-start.8 = (bf16[4,512,512]{2,1,0:T(8,128)(2,1)S(1)}, bf16[4,512,512]{2,1,0:T(8,128)(2,1)}, u32[]{:S(2)}) copy-start(bf16[4,512,512]{2,1,0:T(8,128)(2,1)} %value_ref.1) | copy-start | bytes 6291460
  0.7 3.0 %copy-start.10 = (bf16[4,512]{1,0:T(4,128)(2,1)S(1)}, bf16[4,512]{1,0:T(4,128)(2,1)}, u32[]{:S(2)}) copy-start(bf16[4,512]{1,0:T(4,128)(2,1)} %own_value_ref.1) | copy-start | bytes 12292
  0.7 3.0 %copy-start.11 = (f32[768]{0:T(1024)S(1)}, f32[768]{0:T(1024)}, u32[]{:S(2)}) copy-start(f32[768]{0:T(1024)} %gain_ref.1) | copy-start | bytes 9220
  2.2 17.4 %slice-start = ((s8[4718592]{0:T(1024)(128)(4,1)}), s8[4194304]{0:T(1024)(128)(4,1)S(1)}, s32[]{:S(2)}) async-start(s8[4718592]{0:T(1024)(128)(4,1)} %bitcast.5), calls=%async_computation.3 | async-start | bytes 8388608
  3.7 15.9 %slice-start.1 = ((s8[4718592]{0:T(1024)(128)(4,1)}), s8[524288]{0:T(1024)(128)(4,1)S(1)}, s32[]{:S(2)}) async-start(s8[4718592]{0:T(1024)(128)(4,1)} %bitcast.5), calls=%async_computation.4 | async-start | bytes 1048576
  19.7 2.2 %copy-start.6 = (s32[32,4]{0,1:T(4,128)S(1)}, s32[32,4]{0,1:T(4,128)}, u32[]{:S(2)}) copy-start(s32[32,4]{0,1:T(4,128)} %param.26) | copy-start | bytes 1540
  19.7 2.2 %copy-start.9 = (bf16[32,768]{1,0:T(8,128)(2,1)S(1)}, bf16[32,768]{1,0:T(8,128)(2,1)}, u32[]{:S(2)}) copy-start(bf16[32,768]{1,0:T(8,128)(2,1)} %residual_ref.1) | copy-start | bytes 147460
  19.7 2.2 %copy-start.12 = (f32[32,4]{0,1:T(4,128)S(1)}, f32[32,4]{0,1:T(4,128)}, u32[]{:S(2)}) copy-start(f32[32,4]{0,1:T(4,128)} %param.27) | copy-start | bytes 1540
  20.6 1.3 %collective-permute-start = (f32[32,768]{1,0:T(8,128)S(1)}, f32[32,768]{1,0:T(8,128)S(1)}, u32[]{:S(2)}, u32[]{:S(2)}) collective-permute-start(f32[32,768]{1,0:T(8,128)S(1)} %get-tuple-element.11.mine_ref), channel_id=1, source_target_pairs={{0,1},{1,0},{2,3},{3,2},{4,5},{5,4},{6,7},{7,6},{8,9},{9,8},{10,11... | collective-permute-start | bytes 294920 | tf_op jit(solution)/shard_map/ppermute | solution.py:458
  21.9 12.3 %copy-start.1 = (bf16[6144,168]{0,1:T(8,128)(2,1)S(1)}, bf16[6144,168]{0,1:T(8,128)(2,1)}, u32[]{:S(2)}) copy-start(bf16[6144,168]{0,1:T(8,128)(2,1)} %param.23) | copy-start | bytes 6193156
  21.9 12.3 %copy-start.2 = (bf16[6144,168]{0,1:T(8,128)(2,1)S(1)}, bf16[6144,168]{0,1:T(8,128)(2,1)}, u32[]{:S(2)}) copy-start(bf16[6144,168]{0,1:T(8,128)(2,1)} %param.24) | copy-start | bytes 6193156
  22.0 12.3 %copy-start.3 = (bf16[168,6144]{1,0:T(8,128)(2,1)S(1)}, bf16[168,6144]{1,0:T(8,128)(2,1)}, u32[]{:S(2)}) copy-start(bf16[168,6144]{1,0:T(8,128)(2,1)} %down_ref.1) | copy-start | bytes 6193156
  47.4 1.4 %collective-permute-start.1 = (f32[32,768]{1,0:T(8,128)S(1)}, f32[32,768]{1,0:T(8,128)S(1)}, u32[]{:S(2)}, u32[]{:S(2)}) collective-permute-start(f32[32,768]{1,0:T(8,128)S(1)} %shard_map.155), channel_id=1, source_target_pairs={{0,1},{1,0},{2,3},{3,2},{4,5},{5,4},{6,7},{7,6},{8,9},{9,8},{10,11... | collective-permute-start | bytes 294920 | tf_op jit(solution)/shard_map/ppermute | solution.py:458

commit v10 on v9

--- a/solution.py
+++ b/solution.py
@@ -192,10 +192,22 @@
     )(place)
 
 
-def score_kernel(length_ref, query_ref, key_ref, own_key_ref, earlier_ref, probs_ref, own_ref,
-                 query_rows, key_rows):
-    row_count, length_max, width = key_ref.shape
-    kv_local = width // HEAD_DIM
+def expert_rows(routes, earlier, expert, capacity):
+    row_count = routes.shape[1]
+    hit = jnp.max((routes == expert).astype(jnp.float32), axis=0, keepdims=True)
+    slot = jnp.dot(
+        jnp.broadcast_to(hit, (8, row_count)).astype(jnp.bfloat16),
+        earlier,
+        preferred_element_type=jnp.float32,
+    )[:1]
+    place = lax.broadcasted_iota(jnp.int32, (capacity, row_count), 0).astype(jnp.float32)
+    return jnp.where((slot == place) & (hit > 0.5), 1.0, 0.0)
+
+
+def prepare_kernel(sharers, place_ref, earlier_ref, routes_ref, weight_ref, query_ref, own_key_ref,
+                   spread_ref, own_ref, taken_ref, slot_ref, query_rows, key_rows):
+    row_count = query_ref.shape[0]
+    kv_local = own_key_ref.shape[1] // HEAD_DIM
     group = HEADS // KV_HEADS
     heads = kv_local * group
     for g in range(kv_local):
@@ -208,27 +220,67 @@
             ].astype(jnp.float32)
             key_rows[rows, :] = own_key
     scale = 1.0 / math.sqrt(HEAD_DIM)
-    contract = (((1,), (1,)), ((), ()))
     head = lax.broadcasted_iota(jnp.int32, (heads, 1), 0) // group
-    position = lax.broadcasted_iota(jnp.int32, (heads, length_max), 1)
     for r in range(row_count):
         strided = pl.ds(r, heads, stride=row_count)
         query = query_rows[strided, :]
         own = jnp.sum(query * key_rows[strided, :], axis=1, keepdims=True) * scale
-        spread = jnp.concatenate(
+        own_ref[r] = jnp.broadcast_to(own, (heads, HEAD_DIM))
+        spread_ref[r] = jnp.concatenate(
             [jnp.where(head == g, query, 0.0) for g in range(kv_local)], axis=1
         ).astype(jnp.bfloat16)
+    routes = routes_ref[...]
+    capacity = slot_ref.shape[0]
+    taken = [expert_rows(routes, earlier_ref[...], e, capacity) for e in range(HELD)]
+    for e in range(HELD):
+        taken_ref[e] = taken[e]
+    first = place_ref[0] < sharers
+    expert = jnp.where(first, 0, 1)
+    row_weight = jnp.sum(
+        jnp.where(routes == expert, weight_ref[...], 0.0), axis=0, keepdims=True
+    )
+    mine = jnp.where(first, taken[0], taken[1])
+    slot_ref[...] = jnp.broadcast_to(
+        jnp.sum(mine * row_weight, axis=1, keepdims=True), slot_ref.shape
+    )
+
+
+def prepare(place, sharers, capacity, earlier, routes, route_weight, queries, new_key):
+    row_count, width = queries.shape
+    heads = width // HEAD_DIM
+    table = pltpu.VMEM((heads * row_count, HEAD_DIM), jnp.float32)
+    return call(
+        functools.partial(prepare_kernel, sharers),
+        [
+            jax.ShapeDtypeStruct((row_count, heads, new_key.shape[1]), jnp.bfloat16),
+            jax.ShapeDtypeStruct((row_count, heads, HEAD_DIM), jnp.float32),
+            jax.ShapeDtypeStruct((HELD, capacity, routes.shape[1]), jnp.float32),
+            jax.ShapeDtypeStruct((capacity, HEAD_DIM), jnp.float32),
+        ],
+        [SMEM_SPEC] + [VMEM_SPEC] * 5,
+        [table, table],
+        queries.size * 8, queries.size * 16, 4,
+    )(place, earlier, routes, route_weight, queries, new_key)
+
+
+def score_kernel(length_ref, spread_ref, own_ref, key_ref, probs_ref, own_probs_ref):
+    row_count, heads, length_max = probs_ref.shape
+    scale = 1.0 / math.sqrt(HEAD_DIM)
+    contract = (((1,), (1,)), ((), ()))
+    position = lax.broadcasted_iota(jnp.int32, (heads, length_max), 1)
+    for r in range(row_count):
         scores = lax.dot_general(
-            spread, key_ref[r], contract, preferred_element_type=jnp.float32
+            spread_ref[r], key_ref[r], contract, preferred_element_type=jnp.float32
         )
         past = jnp.where(position < length_ref[r], scores * scale, NEG_FILL)
+        own = own_ref[r, :, :1]
         largest = jnp.maximum(jnp.max(past, axis=1, keepdims=True), own)
         weight = jnp.exp(past - largest)
         own_weight = jnp.exp(own - largest)
         inverse = 1.0 / (jnp.sum(weight, axis=1, keepdims=True) + own_weight)
         probs_ref[r] = (weight * inverse).astype(jnp.bfloat16)
         own_prob = (own_weight * inverse).astype(jnp.bfloat16).astype(jnp.float32)
-        own_ref[r] = jnp.broadcast_to(own_prob, (heads, HEAD_DIM))
+        own_probs_ref[r] = jnp.broadcast_to(own_prob, own_probs_ref.shape[1:])
 
 
 def value_kernel(probs_ref, own_ref, value_ref, own_value_ref, gain_ref, out_ref, value_rows,
@@ -266,30 +318,28 @@
         out_ref[copy, :, heads * HEAD_DIM :] = parts
 
 
-def attend(
-    count, queries, key_cache, value_cache, new_key, new_value, cache_length, gain, earlier
-):
-    row_count, width = queries.shape
-    heads = width // HEAD_DIM
+def attend(count, spread, own, key_cache, value_cache, new_value, cache_length, gain):
+    row_count, heads, _ = spread.shape
     length_max = key_cache.shape[1]
     table = pltpu.VMEM((heads * row_count, HEAD_DIM), jnp.float32)
-    probs, own = call(
+    probs, own_probs = call(
         score_kernel,
         [
             jax.ShapeDtypeStruct((row_count, heads, length_max), jnp.bfloat16),
             jax.ShapeDtypeStruct((row_count, heads, HEAD_DIM), jnp.float32),
         ],
-        [SMEM_SPEC] + [VMEM_SPEC] * 4,
-        [table, table],
+        [SMEM_SPEC] + [VMEM_SPEC] * 3,
+        [],
         2 * key_cache.size * heads, key_cache.size * 2, 8,
-    )(cache_length, queries, key_cache, new_key, earlier)
+    )(cache_length, spread, own, key_cache)
+    width = heads * HEAD_DIM + gain.shape[0] // 2
     return call(
         value_kernel,
-        jax.ShapeDtypeStruct((count, row_count, width + gain.shape[0] // 2), jnp.bfloat16),
+        jax.ShapeDtypeStruct((count, row_count, width), jnp.bfloat16),
         [VMEM_SPEC] * 5,
         [table, table],
         EXCHANGE_FLOPS, value_cache.size * 2, 8,
-    )(probs, own, value_cache, new_value, gain)
+    )(probs, own_probs, value_cache, new_value, gain)
 
 
 def project_kernel(pieces, weight_ref, out_ref, gain_ref, stack):
@@ -321,64 +371,33 @@
     )(pieces, out_weight)
 
 
-def expert_rows(routes, earlier, expert, capacity):
-    row_count = routes.shape[1]
-    hit = jnp.max((routes == expert).astype(jnp.float32), axis=0, keepdims=True)
-    slot = jnp.dot(
-        jnp.broadcast_to(hit, (8, row_count)).astype(jnp.bfloat16),
-        earlier,
-        preferred_element_type=jnp.float32,
-    )[:1]
-    place = lax.broadcasted_iota(jnp.int32, (capacity, row_count), 0).astype(jnp.float32)
-    return jnp.where((slot == place) & (hit > 0.5), 1.0, 0.0)
-
-
-def walk(count):
-    return list(range(0, count, 2)) + list(range(count - 1, 0, -2))
-
-
-def pick_kernel(cores, place_ref, mine_ref, other_ref, residual_ref, routes_ref, weight_ref, earlier_ref,
-                stream_ref, out_ref, slot_ref):
-    count, capacity, _ = out_ref.shape
+def pick_kernel(sharers, mine_ref, other_ref, residual_ref, taken_ref, stream_ref, out_ref):
     stream = (
         residual_ref[...].astype(jnp.float32) + (mine_ref[...] + other_ref[...])
     ).astype(jnp.bfloat16)
     stream_ref[...] = stream
-    routes = routes_ref[...]
-    sharers = count * cores // HELD
-    taken = [expert_rows(routes, earlier_ref[...], e, capacity) for e in range(HELD)]
     chosen = [
         jnp.dot(
-            taken[e].astype(jnp.bfloat16), stream, preferred_element_type=jnp.float32
+            taken_ref[e].astype(jnp.bfloat16), stream, preferred_element_type=jnp.float32
         ).astype(jnp.bfloat16)
         for e in range(HELD)
     ]
-    for k in range(count):
-        out_ref[k] = chosen[k * cores // sharers]
-    first = place_ref[0] * cores < sharers
-    expert = jnp.where(first, 0, 1)
-    row_weight = jnp.sum(
-        jnp.where(routes == expert, weight_ref[...], 0.0), axis=0, keepdims=True
-    )
-    mine = jnp.where(first, taken[0], taken[1])
-    slot_ref[...] = jnp.broadcast_to(
-        jnp.sum(mine * row_weight, axis=1, keepdims=True), slot_ref.shape
-    )
-
-
-def pick(place, cores, count, capacity, mine, other, residual, routes, route_weight, earlier):
+    for k in range(out_ref.shape[0]):
+        out_ref[k] = chosen[k // sharers]
+
+
+def pick(sharers, count, mine, other, residual, taken):
     rows, cols = mine.shape
     return call(
-        functools.partial(pick_kernel, cores),
+        functools.partial(pick_kernel, sharers),
         [
             jax.ShapeDtypeStruct((rows, cols), jnp.bfloat16),
-            jax.ShapeDtypeStruct((count, capacity, cols), jnp.bfloat16),
-            jax.ShapeDtypeStruct((capacity, 128), jnp.float32),
+            jax.ShapeDtypeStruct((count, taken.shape[1], cols), jnp.bfloat16),
         ],
-        [SMEM_SPEC] + [VMEM_SPEC] * 6,
+        [VMEM_SPEC] * 4,
         [],
         EXCHANGE_FLOPS, rows * cols * 12, 4,
-    )(place, mine, other, residual, routes, route_weight, earlier)
+    )(mine, other, residual, taken)
 
 
 def expert_kernel(slot_ref, pieces, gains, gate_ref, up_ref, down_ref, out_ref):
@@ -405,9 +424,9 @@
         )
     hidden = (gate_val / (1.0 + jnp.exp(-gate_val)) * up_val).T.astype(jnp.bfloat16)
     slot_weight = slot_ref[:, :1]
-    for slot, k in enumerate(walk(count)):
+    for k in range(count):
         block = slice(k * cols, (k + 1) * cols)
-        out_ref[slot] = (
+        out_ref[k] = (
             jnp.dot(hidden, down_ref[:, block], preferred_element_type=jnp.float32) * slot_weight
         ).astype(jnp.bfloat16)
 
@@ -422,12 +441,9 @@
     )(slots, pieces, gains, gate, up, down)
 
 
-def combine_kernel(cores, routes_ref, earlier_ref, pieces, out_ref):
+def combine_kernel(sharers, taken_ref, pieces, out_ref):
     count, capacity, cols = pieces.shape
-    sharers = count * cores // HELD
-    routes = routes_ref[...]
-    taken = [expert_rows(routes, earlier_ref[...], e, capacity) for e in range(HELD)]
-    spread = [taken[k * cores // sharers] for k in walk(count)]
+    spread = [taken_ref[k // sharers] for k in range(count)]
     out_ref[...] = lax.dot_general(
         jnp.concatenate(spread, axis=0).astype(jnp.bfloat16),
         pieces[...].reshape(count * capacity, cols),
@@ -436,22 +452,35 @@
     )
 
 
-def combine(cores, routes, earlier, pieces):
+def combine(sharers, taken, pieces):
     count, capacity, cols = pieces.shape
-    rows = routes.shape[1]
-    return call(
-        functools.partial(combine_kernel, cores),
+    rows = taken.shape[2]
+    return call(
+        functools.partial(combine_kernel, sharers),
         jax.ShapeDtypeStruct((rows, cols), jnp.float32),
+        [VMEM_SPEC] * 2,
+        [],
+        2 * rows * capacity * count * cols, (count * capacity * 2 + rows * 4) * cols, 4,
+    )(taken, pieces)
+
+
+def finish_kernel(stream_ref, mine_ref, other_ref, stream_out_ref, out_ref):
+    stream_out_ref[...] = stream_ref[...]
+    out_ref[...] = (mine_ref[...] + other_ref[...]).astype(jnp.bfloat16)
+
+
+def finish(stream, mine, other):
+    return call(
+        finish_kernel,
+        [jax.ShapeDtypeStruct(stream.shape, jnp.bfloat16)] * 2,
         [VMEM_SPEC] * 3,
         [],
-        2 * rows * capacity * count * cols, (count * capacity * 2 + rows * 4) * cols, 4,
-    )(routes, earlier, pieces)
-
-
-def exchange(blocks, members=None):
-    return lax.all_to_all(
-        blocks, "attn", split_axis=0, concat_axis=0, axis_index_groups=members, tiled=True
-    )
+        mine.size, mine.size * 14, 4,
+    )(stream, mine, other)
+
+
+def exchange(blocks):
+    return lax.all_to_all(blocks, "attn", split_axis=0, concat_axis=0, tiled=True)
 
 
 def swap(block):
@@ -475,35 +504,32 @@
     route_weight,
 ):
     count = lax.axis_size("attn")
-    cores = lax.axis_size("expert")
+    sharers = count // HELD
     capacity = routes.shape[0] * TOP // EXPERTS * 2
     place = lax.axis_index("attn").astype(jnp.int32).reshape(1)
-    routes = routes.T
-    route_weight = route_weight.T
-
-    earlier = order(place, routes.shape[1])
+
+    earlier = order(place, routes.shape[0])
+    spread, own, taken, slots = prepare(
+        place, sharers, capacity, earlier, routes.T, route_weight.T, queries, new_key
+    )
     attended = exchange(
-        attend(
-            count, queries, key_cache, value_cache, new_key, new_value, cache_length,
-            ln_gain, earlier,
-        )
+        attend(count, spread, own, key_cache, value_cache, new_value, cache_length, ln_gain)
     )
     mine, gains = project(attended, out_weight)
-    attn_stream, chosen, slots = pick(
-        place, cores, count, capacity, mine, swap(mine), residual, routes, route_weight, earlier
-    )
+    stream, chosen = pick(sharers, count, mine, swap(mine), residual, taken)
     outgoing = run_experts(
         slots, exchange(chosen), gains, gate_weight.T, up_weight.T, down_weight
     )
-    combined = combine(cores, routes, earlier, exchange(outgoing, [walk(count)]))
-    expert_out = (combined + swap(combined)).astype(jnp.bfloat16)
+    combined = combine(sharers, taken, exchange(outgoing))
+    attn_stream, expert_out = finish(stream, combined, swap(combined))
     return (attn_stream, expert_out)
 
 
 def solution(mesh):
-    cols = D // mesh.shape["attn"]
+    count = mesh.shape["attn"]
+    fits = D // count % 256 == 0 and count % HELD == 0 and mesh.shape["expert"] == 2
     return jax.shard_map(
-        shards if cols % 256 == 0 else shards_plain,
+        shards if fits else shards_plain,
         mesh=mesh,
         in_specs=(
             P(("group", "attn"), "expert"),

time: 49.6 us -> 49 us (0.988)
  other arithmetic: 0.63 us -> 0.01 us
    convert_element_type x1 -> x0, other arithmetic: 0.63 us -> none  [shards(): expert_out = (combined + swap(combined)).astype(jnp.bfloat16)]
    pallas_call x3 -> x5, Pallas kernels: 1.47 us -> 1.7 us  [the longest x1 0.65 us: finish(): call(finish_kernel, [jax.ShapeDtypeStruct(stream.shape, jnp.bfloat16)] *...]
where the time goes in v10:
time: 49 us; the launch traced here: 48.8 us
  blocking collectives  37.7 us (77%)
  Pallas kernels  6.16 us (13%)
  waiting for transfers between devices  2.6 us (5%)
  local copies, waits for them, and re-layouts  1.39 us (3%)
  between operations  0.81 us (2%)
    all_to_all x3, blocking collectives, exchange(): lax.all_to_all(blocks, 'attn', split_axis=0, concat_axis=0, tiled=True)  37.7 us
    ppermute x2, waiting for transfers between devices, swap(): return lax.ppermute(block, 'expert', [(0, 1), (1, 0)])  2.6 us
    pallas_call x1, Pallas kernels, run_experts(): call(expert_kernel, jax.ShapeDtypeStruct(pieces.shape, jnp.bfloat16), [VM...  1.87 us
    pallas_call x1, Pallas kernels, attend(): call(score_kernel, [jax.ShapeDtypeStruct((row_count, heads, length_max),...  1.71 us
    unnamed x30, local copies, waits for them, and re-layouts  1.39 us
  transfers between devices with their start and end apart: 2, of which 2 were waited for; matrix products, arithmetic and copies ran while one was open for 0% of the time, Pallas kernels for 0%

profile of v10, /device:TPU:0, one launch (start us, length us, event | category | flops | bytes accessed | tf_op | source)
XLA Modules:
  0.0 48.8 jit_solution(12222323865752067307)
XLA Ops:
  0.6 0.0 copy-start.4
  0.6 0.0 copy-start.5
  0.7 0.0 copy-start.6
  0.7 0.0 copy-start.7
  0.7 0.0 copy-start
  0.7 0.0 copy-start.8
  0.7 0.0 copy-start.9
  0.7 0.0 copy-start.11
  0.7 0.0 copy-start.12
  0.8 0.6 %copy-done.4 = bf16[4,3072]{1,0:T(4,128)(2,1)S(1)} copy-done((bf16[4,3072]{1,0:T(4,128)(2,1)S(1)}, bf16[4,3072]{1,0:T(4,128)(2,1)}, u32[]{:S(2)}) %copy-start.4) | copy-done | bytes 24600
  1.4 0.0 copy-done.5
  1.4 0.0 copy-done.6
  1.4 0.0 copy-done.7
  1.4 0.2 shard_map.150
  1.6 0.7 %copy-done = bf16[4,512,512]{2,1,0:T(8,128)(2,1)S(1)} copy-done((bf16[4,512,512]{2,1,0:T(8,128)(2,1)S(1)}, bf16[4,512,512]{2,1,0:T(8,128)(2,1)}, u32[]{:S(2)}) %copy-start) | copy-done | bytes 2097176
  2.3 0.0 copy-done.8
  2.3 0.0 slice-start
  2.3 1.7 %shard_map.151 = (bf16[4,24,512]{2,1,0:T(8,128)(2,1)S(1)}, f32[4,24,128]{2,1,0:T(8,128)S(1)}) custom-call(s32[4]{0:T(128)S(1)} %copy-done.8, bf16[4,24,512]{2,1,0:T(8,128)(2,1)S(1)} %get-tuple-element.12.spread_ref, f32[4,24,128]{2,1,0:T(8,128)S(1)} %get-tuple-element.13.own_ref, bf16[4,512,512]{2,1,0:T(8,128)(2,1)S(1)} %copy-done), custom_call_target="tpu_custom_call" | custom-call | flops 50331648 | bytes 2097152 | tf_op jit(solution)/shard_map/pallas_call | solution.py:325
  4.0 0.0 copy-done.9
  4.0 0.0 copy-done.11
  4.0 0.0 copy-done.12
  4.0 0.0 slice-start.1
  4.1 0.5 %shard_map.152 = bf16[8,4,3456]{2,1,0:T(4,128)(2,1)S(1)} custom-call(bf16[4,24,512]{2,1,0:T(8,128)(2,1)S(1)} %get-tuple-element.14.probs_ref, f32[4,24,128]{2,1,0:T(8,128)S(1)} %get-tuple-element.15.own_ref, bf16[4,512,512]{2,1,0:T(8,128)(2,1)S(1)} %copy-done.9, bf16[4,512]{1,0:T(4,128)(2,1)S(1)} %copy-done.11, f32[768]{0:T(1024)S(1)} %copy-done.12), custom_call_target="tpu_custom_call" | custom-call | flops 10000000000 | bytes 2097152 | tf_op jit(solution)/shard_map/pallas_call | solution.py:336
  4.6 15.4 %all_to_all.15.pieces = bf16[8,4,3456]{2,1,0:T(4,128)(2,1)S(1)} all-to-all(bf16[8,4,3456]{2,1,0:T(4,128)(2,1)S(1)} %shard_map.152), channel_id=1, replica_groups=mesh['group'=2,'attn'=8,'expert'=2] {'attn'}, dimensions={0} | all-to-all | bytes 442368 | tf_op jit(solution)/shard_map/all_to_all | solution.py:483
  20.0 0.0 slice-done
  20.0 0.0 slice-done.1
  20.0 0.0 copy-start.10
  20.0 0.9 %shard_map.153 = (f32[32,768]{1,0:T(8,128)S(1)}, f32[8,768]{1,0:T(8,128)S(1)}) custom-call(bf16[8,4,3456]{2,1,0:T(4,128)(2,1)S(1)} %all_to_all.15.pieces, bf16[3072,768]{1,0:T(8,128)(2,1)S(1)} %bitcast.6), custom_call_target="tpu_custom_call" | custom-call | flops 150994944 | bytes 4718592 | tf_op jit(solution)/shard_map/pallas_call | solution.py:362
  20.9 0.0 collective-permute-start
  20.9 1.3 %collective-permute-done.other_ref = f32[32,768]{1,0:T(8,128)S(1)} collective-permute-done((f32[32,768]{1,0:T(8,128)S(1)}, f32[32,768]{1,0:T(8,128)S(1)}, u32[]{:S(2)}, u32[]{:S(2)}) %collective-permute-start) | collective-permute-done | bytes 98336 | tf_op jit(solution)/shard_map/ppermute | solution.py:487
  22.2 0.0 copy-done.10
  22.2 0.0 copy-start.1
  22.2 0.0 copy-start.2
  22.2 0.0 copy-start.3
  22.2 0.1 shard_map.154
  22.4 11.6 %all_to_all.16.pieces = bf16[8,16,768]{2,1,0:T(8,128)(2,1)S(1)} all-to-all(bf16[8,16,768]{2,1,0:T(8,128)(2,1)S(1)} %get-tuple-element.20), channel_id=1, replica_groups=mesh['group'=2,'attn'=8,'expert'=2] {'attn'}, dimensions={0} | all-to-all | bytes 393216 | tf_op jit(solution)/shard_map/all_to_all | solution.py:483
  34.0 0.0 copy-done.1
  34.0 0.0 copy-done.2
  34.0 0.0 copy-done.3
  34.0 1.9 %shard_map.155 = bf16[8,16,768]{2,1,0:T(8,128)(2,1)S(1)} custom-call(f32[16,128]{1,0:T(8,128)S(1)} %get-tuple-element.19.slot_ref, bf16[8,16,768]{2,1,0:T(8,128)(2,1)S(1)} %all_to_all.16.pieces, f32[8,768]{1,0:T(8,128)S(1)} %get-tuple-element.21.gains, bf16[168,6144]{1,0:T(8,128)(2,1)S(1)} %bitcast.7, bf16[168,6144]{1,0:T(8,128)(2,1)S(1)} %bitcast.8, ...), custom_call_target="tpu_custom_call" | custom-call | flops 99090432 | bytes 6193152 | tf_op jit(solution)/shard_map/pallas_call | solution.py:435
  35.9 10.7 %all_to_all.17.pieces = bf16[8,16,768]{2,1,0:T(8,128)(2,1)S(1)} all-to-all(bf16[8,16,768]{2,1,0:T(8,128)(2,1)S(1)} %shard_map.155), channel_id=1, replica_groups=mesh['group'=2,'attn'=8,'expert'=2] {'attn'}, dimensions={0} | all-to-all | bytes 393216 | tf_op jit(solution)/shard_map/all_to_all | solution.py:483
  46.6 0.2 shard_map.156.mine_ref
  46.8 0.0 collective-permute-start.1
  46.8 1.3 %collective-permute-done.1.other_ref = f32[32,768]{1,0:T(8,128)S(1)} collective-permute-done((f32[32,768]{1,0:T(8,128)S(1)}, f32[32,768]{1,0:T(8,128)S(1)}, u32[]{:S(2)}, u32[]{:S(2)}) %collective-permute-start.1) | collective-permute-done | bytes 98336 | tf_op jit(solution)/shard_map/ppermute | solution.py:487
  48.1 0.6 %shard_map.157 = (bf16[32,768]{1,0:T(8,128)(2,1)}, bf16[32,768]{1,0:T(8,128)(2,1)}) custom-call(bf16[32,768]{1,0:T(8,128)(2,1)S(1)} %get-tuple-element.18.stream_ref, f32[32,768]{1,0:T(8,128)S(1)} %shard_map.156.mine_ref, f32[32,768]{1,0:T(8,128)S(1)} %collective-permute-done.1.other_ref), custom_call_target="tpu_custom_call" | custom-call | flops 24576 | bytes 344064 | tf_op jit(solution)/shard_map/pallas_call | solution.py:473
  (2 shorter events, 0.0 us)
Async XLA Ops:
  0.6 0.7 %copy-start.4 = (bf16[4,3072]{1,0:T(4,128)(2,1)S(1)}, bf16[4,3072]{1,0:T(4,128)(2,1)}, u32[]{:S(2)}) copy-start(bf16[4,3072]{1,0:T(4,128)(2,1)} %query_ref.1) | copy-start | bytes 73732
  0.6 0.7 %copy-start.5 = (bf16[4,512]{1,0:T(4,128)(2,1)S(1)}, bf16[4,512]{1,0:T(4,128)(2,1)}, u32[]{:S(2)}) copy-start(bf16[4,512]{1,0:T(4,128)(2,1)} %own_key_ref.1) | copy-start | bytes 12292
  0.7 0.7 %copy-start.6 = (s32[32,4]{0,1:T(4,128)S(1)}, s32[32,4]{0,1:T(4,128)}, u32[]{:S(2)}) copy-start(s32[32,4]{0,1:T(4,128)} %param.26) | copy-start | bytes 1540
  0.7 0.7 %copy-start.7 = (f32[32,4]{0,1:T(4,128)S(1)}, f32[32,4]{0,1:T(4,128)}, u32[]{:S(2)}) copy-start(f32[32,4]{0,1:T(4,128)} %param.27) | copy-start | bytes 1540
  0.7 1.6 %copy-start = (bf16[4,512,512]{2,1,0:T(8,128)(2,1)S(1)}, bf16[4,512,512]{2,1,0:T(8,128)(2,1)}, u32[]{:S(2)}) copy-start(bf16[4,512,512]{2,1,0:T(8,128)(2,1)} %key_ref.1) | copy-start | bytes 6291460
  0.7 1.6 %copy-start.8 = (s32[4]{0:T(128)S(1)}, s32[4]{0:T(128)}, u32[]{:S(2)}) copy-start(s32[4]{0:T(128)} %length_ref.1) | copy-start | bytes 52
  0.7 3.3 %copy-start.9 = (bf16[4,512,512]{2,1,0:T(8,128)(2,1)S(1)}, bf16[4,512,512]{2,1,0:T(8,128)(2,1)}, u32[]{:S(2)}) copy-start(bf16[4,512,512]{2,1,0:T(8,128)(2,1)} %value_ref.1) | copy-start | bytes 6291460
  0.7 3.3 %copy-start.11 = (bf16[4,512]{1,0:T(4,128)(2,1)S(1)}, bf16[4,512]{1,0:T(4,128)(2,1)}, u32[]{:S(2)}) copy-start(bf16[4,512]{1,0:T(4,128)(2,1)} %own_value_ref.1) | copy-start | bytes 12292
  0.7 3.3 %copy-start.12 = (f32[768]{0:T(1024)S(1)}, f32[768]{0:T(1024)}, u32[]{:S(2)}) copy-start(f32[768]{0:T(1024)} %gain_ref.1) | copy-start | bytes 9220
  2.3 17.7 %slice-start = ((s8[4718592]{0:T(1024)(128)(4,1)}), s8[4194304]{0:T(1024)(128)(4,1)S(1)}, s32[]{:S(2)}) async-start(s8[4718592]{0:T(1024)(128)(4,1)} %bitcast.5), calls=%async_computation.3 | async-start | bytes 8388608
  4.0 15.9 %slice-start.1 = ((s8[4718592]{0:T(1024)(128)(4,1)}), s8[524288]{0:T(1024)(128)(4,1)S(1)}, s32[]{:S(2)}) async-start(s8[4718592]{0:T(1024)(128)(4,1)} %bitcast.5), calls=%async_computation.4 | async-start | bytes 1048576
  20.0 2.2 %copy-start.10 = (bf16[32,768]{1,0:T(8,128)(2,1)S(1)}, bf16[32,768]{1,0:T(8,128)(2,1)}, u32[]{:S(2)}) copy-start(bf16[32,768]{1,0:T(8,128)(2,1)} %residual_ref.1) | copy-start | bytes 147460
  20.9 1.3 %collective-permute-start = (f32[32,768]{1,0:T(8,128)S(1)}, f32[32,768]{1,0:T(8,128)S(1)}, u32[]{:S(2)}, u32[]{:S(2)}) collective-permute-start(f32[32,768]{1,0:T(8,128)S(1)} %get-tuple-element.16.mine_ref), channel_id=1, source_target_pairs={{0,1},{1,0},{2,3},{3,2},{4,5},{5,4},{6,7},{7,6},{8,9},{9,8},{10,11... | collective-permute-start | bytes 294920 | tf_op jit(solution)/shard_map/ppermute | solution.py:487
  22.2 11.8 %copy-start.1 = (bf16[6144,168]{0,1:T(8,128)(2,1)S(1)}, bf16[6144,168]{0,1:T(8,128)(2,1)}, u32[]{:S(2)}) copy-start(bf16[6144,168]{0,1:T(8,128)(2,1)} %param.23) | copy-start | bytes 6193156
  22.2 11.8 %copy-start.2 = (bf16[6144,168]{0,1:T(8,128)(2,1)S(1)}, bf16[6144,168]{0,1:T(8,128)(2,1)}, u32[]{:S(2)}) copy-start(bf16[6144,168]{0,1:T(8,128)(2,1)} %param.24) | copy-start | bytes 6193156
  22.2 11.8 %copy-start.3 = (bf16[168,6144]{1,0:T(8,128)(2,1)S(1)}, bf16[168,6144]{1,0:T(8,128)(2,1)}, u32[]{:S(2)}) copy-start(bf16[168,6144]{1,0:T(8,128)(2,1)} %down_ref.1) | copy-start | bytes 6193156
  46.8 1.3 %collective-permute-start.1 = (f32[32,768]{1,0:T(8,128)S(1)}, f32[32,768]{1,0:T(8,128)S(1)}, u32[]{:S(2)}, u32[]{:S(2)}) collective-permute-start(f32[32,768]{1,0:T(8,128)S(1)} %shard_map.156.mine_ref), channel_id=1, source_target_pairs={{0,1},{1,0},{2,3},{3,2},{4,5},{5,4},{6,7},{7,6},{8,9},{9,8},{10,11... | collective-permute-start | bytes 294920 | tf_op jit(solution)/shard_map/ppermute | solution.py:487

commit v11 on v10

--- a/solution.py
+++ b/solution.py
@@ -204,8 +204,9 @@
     return jnp.where((slot == place) & (hit > 0.5), 1.0, 0.0)
 
 
-def prepare_kernel(sharers, place_ref, earlier_ref, routes_ref, weight_ref, query_ref, own_key_ref,
-                   spread_ref, own_ref, taken_ref, slot_ref, query_rows, key_rows):
+def prepare_kernel(sharers, place_ref, length_ref, earlier_ref, routes_ref, weight_ref, query_ref,
+                   own_key_ref, spread_ref, own_ref, limit_ref, taken_ref, slot_ref, query_rows,
+                   key_rows):
     row_count = query_ref.shape[0]
     kv_local = own_key_ref.shape[1] // HEAD_DIM
     group = HEADS // KV_HEADS
@@ -226,6 +227,7 @@
         query = query_rows[strided, :]
         own = jnp.sum(query * key_rows[strided, :], axis=1, keepdims=True) * scale
         own_ref[r] = jnp.broadcast_to(own, (heads, HEAD_DIM))
+        limit_ref[r] = jnp.full((heads, HEAD_DIM), length_ref[r], jnp.int32)
         spread_ref[r] = jnp.concatenate(
             [jnp.where(head == g, query, 0.0) for g in range(kv_local)], axis=1
         ).astype(jnp.bfloat16)
@@ -234,7 +236,7 @@
     taken = [expert_rows(routes, earlier_ref[...], e, capacity) for e in range(HELD)]
     for e in range(HELD):
         taken_ref[e] = taken[e]
-    first = place_ref[0] < sharers
+    first = place_ref[0] // 4 < sharers
     expert = jnp.where(first, 0, 1)
     row_weight = jnp.sum(
         jnp.where(routes == expert, weight_ref[...], 0.0), axis=0, keepdims=True
@@ -245,7 +247,9 @@
     )
 
 
-def prepare(place, sharers, capacity, earlier, routes, route_weight, queries, new_key):
+def prepare(
+    place, sharers, capacity, cache_length, earlier, routes, route_weight, queries, new_key
+):
     row_count, width = queries.shape
     heads = width // HEAD_DIM
     table = pltpu.VMEM((heads * row_count, HEAD_DIM), jnp.float32)
@@ -254,16 +258,17 @@
         [
             jax.ShapeDtypeStruct((row_count, heads, new_key.shape[1]), jnp.bfloat16),
             jax.ShapeDtypeStruct((row_count, heads, HEAD_DIM), jnp.float32),
+            jax.ShapeDtypeStruct((row_count, heads, HEAD_DIM), jnp.int32),
             jax.ShapeDtypeStruct((HELD, capacity, routes.shape[1]), jnp.float32),
             jax.ShapeDtypeStruct((capacity, HEAD_DIM), jnp.float32),
         ],
-        [SMEM_SPEC] + [VMEM_SPEC] * 5,
+        [SMEM_SPEC] * 2 + [VMEM_SPEC] * 5,
         [table, table],
         queries.size * 8, queries.size * 16, 4,
-    )(place, earlier, routes, route_weight, queries, new_key)
-
-
-def score_kernel(length_ref, spread_ref, own_ref, key_ref, probs_ref, own_probs_ref):
+    )(place, cache_length, earlier, routes, route_weight, queries, new_key)
+
+
+def score_kernel(spread_ref, own_ref, limit_ref, key_ref, probs_ref, own_probs_ref):
     row_count, heads, length_max = probs_ref.shape
     scale = 1.0 / math.sqrt(HEAD_DIM)
     contract = (((1,), (1,)), ((), ()))
@@ -272,7 +277,7 @@
         scores = lax.dot_general(
             spread_ref[r], key_ref[r], contract, preferred_element_type=jnp.float32
         )
-        past = jnp.where(position < length_ref[r], scores * scale, NEG_FILL)
+        past = jnp.where(position < limit_ref[r, :, :1], scores * scale, NEG_FILL)
         own = own_ref[r, :, :1]
         largest = jnp.maximum(jnp.max(past, axis=1, keepdims=True), own)
         weight = jnp.exp(past - largest)
@@ -318,7 +323,7 @@
         out_ref[copy, :, heads * HEAD_DIM :] = parts
 
 
-def attend(count, spread, own, key_cache, value_cache, new_value, cache_length, gain):
+def attend(count, spread, own, limit, key_cache, value_cache, new_value, gain):
     row_count, heads, _ = spread.shape
     length_max = key_cache.shape[1]
     table = pltpu.VMEM((heads * row_count, HEAD_DIM), jnp.float32)
@@ -328,10 +333,10 @@
             jax.ShapeDtypeStruct((row_count, heads, length_max), jnp.bfloat16),
             jax.ShapeDtypeStruct((row_count, heads, HEAD_DIM), jnp.float32),
         ],
-        [SMEM_SPEC] + [VMEM_SPEC] * 3,
+        [VMEM_SPEC] * 4,
         [],
         2 * key_cache.size * heads, key_cache.size * 2, 8,
-    )(cache_length, spread, own, key_cache)
+    )(spread, own, limit, key_cache)
     width = heads * HEAD_DIM + gain.shape[0] // 2
     return call(
         value_kernel,
@@ -367,11 +372,12 @@
         ],
         [VMEM_SPEC, VMEM_SPEC],
         [pltpu.VMEM((rows * count, depth), jnp.float32)],
-        2 * rows * count * out_weight.size, out_weight.size * 2, 10,
+        EXCHANGE_FLOPS, out_weight.size * 2, 10,
     )(pieces, out_weight)
 
 
-def pick_kernel(sharers, mine_ref, other_ref, residual_ref, taken_ref, stream_ref, out_ref):
+def pick_kernel(sharers, place_ref, mine_ref, other_ref, residual_ref, taken_ref, stream_ref,
+                *out_refs):
     stream = (
         residual_ref[...].astype(jnp.float32) + (mine_ref[...] + other_ref[...])
     ).astype(jnp.bfloat16)
@@ -379,32 +385,59 @@
     chosen = [
         jnp.dot(
             taken_ref[e].astype(jnp.bfloat16), stream, preferred_element_type=jnp.float32
-        ).astype(jnp.bfloat16)
+        )
         for e in range(HELD)
     ]
-    for k in range(out_ref.shape[0]):
-        out_ref[k] = chosen[k // sharers]
-
-
-def pick(sharers, count, mine, other, residual, taken):
+    high = place_ref[0] // 4
+    for k, out_ref in enumerate(out_refs):
+        out_ref[...] = jnp.where((high ^ k) < sharers, chosen[0], chosen[1]).astype(jnp.bfloat16)
+
+
+def pick(place, sharers, highs, mine, other, residual, taken):
     rows, cols = mine.shape
     return call(
         functools.partial(pick_kernel, sharers),
-        [
-            jax.ShapeDtypeStruct((rows, cols), jnp.bfloat16),
-            jax.ShapeDtypeStruct((count, taken.shape[1], cols), jnp.bfloat16),
-        ],
-        [VMEM_SPEC] * 4,
-        [],
-        EXCHANGE_FLOPS, rows * cols * 12, 4,
-    )(mine, other, residual, taken)
-
-
-def expert_kernel(slot_ref, pieces, gains, gate_ref, up_ref, down_ref, out_ref):
-    count, capacity, cols = pieces.shape
+        [jax.ShapeDtypeStruct((rows, cols), jnp.bfloat16)]
+        + [jax.ShapeDtypeStruct((taken.shape[1], cols), jnp.bfloat16)] * highs,
+        [SMEM_SPEC] + [VMEM_SPEC] * 4,
+        [],
+        2 * HELD * taken.shape[1] * rows * cols, rows * cols * 12, 4,
+    )(place, mine, other, residual, taken)
+
+
+def stack_kernel(place_ref, *refs):
+    out_ref = refs[-1]
+    high = place_ref[0] // 4
+    for k, block in enumerate(refs[:-1]):
+        out_ref[high ^ k] = block[...]
+
+
+def stack(place, blocks):
+    return call(
+        stack_kernel,
+        jax.ShapeDtypeStruct((len(blocks),) + blocks[0].shape, blocks[0].dtype),
+        [SMEM_SPEC] + [VMEM_SPEC] * len(blocks),
+        [],
+        0, 4 * len(blocks) * blocks[0].size, 4,
+    )(place, *blocks)
+
+
+def ordered(low, mine, other):
+    return jnp.where(low == 0, mine, other), jnp.where(low == 0, other, mine)
+
+
+def expert_kernel(place_ref, slot_ref, mine_ref, other_ref, mine_given_ref, other_given_ref, gains,
+                  gate_ref, up_ref, down_ref, keep_ref, give_ref):
+    highs, capacity, cols = mine_ref.shape
+    core = place_ref[0] % 2
+    low = place_ref[0] // 2 % 2
+    blocks = []
+    for k in range(highs):
+        mine = jnp.where(core == 1, mine_ref[k], mine_given_ref[k])
+        other = jnp.where(core == 1, other_ref[k], other_given_ref[k])
+        blocks.extend(ordered(low, mine.astype(jnp.float32), other.astype(jnp.float32)))
     first = second = 0.0
-    for k in range(count):
-        wide = pieces[k].astype(jnp.float32)
+    for wide in blocks:
         first = first + wide
         second = second + wide * wide
     row_mean = jnp.sum(first, axis=1, keepdims=True) / D
@@ -412,75 +445,130 @@
     inverse = lax.rsqrt(row_var + EPSILON)
     contract = (((1,), (1,)), ((), ()))
     gate_val = up_val = 0.0
-    for k in range(count):
-        block = slice(k * cols, (k + 1) * cols)
-        wide = pieces[k].astype(jnp.float32)
+    for k, wide in enumerate(blocks):
+        columns = slice(k * cols, (k + 1) * cols)
         normed = ((wide - row_mean) * inverse * gains[pl.ds(k, 1), :]).astype(jnp.bfloat16)
         gate_val = gate_val + lax.dot_general(
-            gate_ref[:, block], normed, contract, preferred_element_type=jnp.float32
+            gate_ref[:, columns], normed, contract, preferred_element_type=jnp.float32
         )
         up_val = up_val + lax.dot_general(
-            up_ref[:, block], normed, contract, preferred_element_type=jnp.float32
+            up_ref[:, columns], normed, contract, preferred_element_type=jnp.float32
         )
     hidden = (gate_val / (1.0 + jnp.exp(-gate_val)) * up_val).T.astype(jnp.bfloat16)
     slot_weight = slot_ref[:, :1]
-    for k in range(count):
-        block = slice(k * cols, (k + 1) * cols)
-        out_ref[k] = (
-            jnp.dot(hidden, down_ref[:, block], preferred_element_type=jnp.float32) * slot_weight
+    for k in range(highs):
+        columns = slice(2 * k * cols, 2 * (k + 1) * cols)
+        both = (
+            jnp.dot(hidden, down_ref[:, columns], preferred_element_type=jnp.float32)
+            * slot_weight
         ).astype(jnp.bfloat16)
-
-
-def run_experts(slots, pieces, gains, gate, up, down):
+        keep_ref[k], give_ref[k] = ordered(low, both[:, :cols], both[:, cols:])
+
+
+def run_experts(place, slots, blocks, gains, gate, up, down):
     return call(
         expert_kernel,
-        jax.ShapeDtypeStruct(pieces.shape, jnp.bfloat16),
-        [VMEM_SPEC] * 6,
-        [],
-        6 * pieces.shape[1] * gate.size, gate.size * 6, 14,
-    )(slots, pieces, gains, gate, up, down)
-
-
-def combine_kernel(sharers, taken_ref, pieces, out_ref):
-    count, capacity, cols = pieces.shape
-    spread = [taken_ref[k // sharers] for k in range(count)]
+        [jax.ShapeDtypeStruct(blocks[0].shape, jnp.bfloat16)] * 2,
+        [SMEM_SPEC] + [VMEM_SPEC] * (5 + len(blocks)),
+        [],
+        6 * blocks[0].shape[1] * gate.size, gate.size * 6, 14,
+    )(place, slots, *blocks, gains, gate, up, down)
+
+
+def add_kernel(mine_ref, given_ref, out_ref):
+    out_ref[...] = (
+        mine_ref[...].astype(jnp.float32) + given_ref[...].astype(jnp.float32)
+    ).astype(jnp.bfloat16)
+
+
+def add(mine, given):
+    return call(
+        add_kernel,
+        jax.ShapeDtypeStruct(mine.shape, jnp.bfloat16),
+        [VMEM_SPEC] * 2,
+        [],
+        mine.size, mine.size * 6, 4,
+    )(mine, given)
+
+
+def send_kernel(place_ref, *refs):
+    highs = refs[0].shape[0]
+    terms, out_refs = refs[:-highs], refs[-highs:]
+    high = place_ref[0] // 4
+    for k, out_ref in enumerate(out_refs):
+        total = 0.0
+        for term in terms:
+            total = total + term[high ^ k].astype(jnp.float32)
+        out_ref[...] = total.astype(jnp.bfloat16)
+
+
+def send_blocks(place, *terms):
+    highs, capacity, cols = terms[0].shape
+    return call(
+        send_kernel,
+        [jax.ShapeDtypeStruct((capacity, cols), jnp.bfloat16)] * highs,
+        [SMEM_SPEC] + [VMEM_SPEC] * len(terms),
+        [],
+        terms[0].size, terms[0].size * 8, 4,
+    )(place, *terms)
+
+
+def combine_kernel(sharers, place_ref, taken_ref, *refs):
+    pieces, out_ref = refs[:-1], refs[-1]
+    high = place_ref[0] // 4
+    spread = [
+        jnp.where((high ^ k) < sharers, taken_ref[0], taken_ref[1]) for k in range(len(pieces))
+    ]
     out_ref[...] = lax.dot_general(
         jnp.concatenate(spread, axis=0).astype(jnp.bfloat16),
-        pieces[...].reshape(count * capacity, cols),
+        jnp.concatenate([piece[...] for piece in pieces], axis=0),
         (((0,), (0,)), ((), ())),
         preferred_element_type=jnp.float32,
-    )
-
-
-def combine(sharers, taken, pieces):
-    count, capacity, cols = pieces.shape
+    ).astype(jnp.bfloat16)
+
+
+def combine(place, sharers, taken, pieces):
+    capacity, cols = pieces[0].shape
     rows = taken.shape[2]
     return call(
         functools.partial(combine_kernel, sharers),
-        jax.ShapeDtypeStruct((rows, cols), jnp.float32),
-        [VMEM_SPEC] * 2,
-        [],
-        2 * rows * capacity * count * cols, (count * capacity * 2 + rows * 4) * cols, 4,
-    )(taken, pieces)
-
-
-def finish_kernel(stream_ref, mine_ref, other_ref, stream_out_ref, out_ref):
+        jax.ShapeDtypeStruct((rows, cols), jnp.bfloat16),
+        [SMEM_SPEC] + [VMEM_SPEC] * (1 + len(pieces)),
+        [],
+        2 * rows * capacity * len(pieces) * cols, (len(pieces) * capacity + rows) * 2 * cols, 4,
+    )(place, taken, *pieces)
+
+
+def finish_kernel(place_ref, stream_ref, mine_ref, given_ref, stream_out_ref, out_ref):
     stream_out_ref[...] = stream_ref[...]
-    out_ref[...] = (mine_ref[...] + other_ref[...]).astype(jnp.bfloat16)
-
-
-def finish(stream, mine, other):
+    out_ref[...] = jnp.where(place_ref[0] % 2 == 1, mine_ref[...], given_ref[...])
+
+
+def finish(place, stream, mine, given):
     return call(
         finish_kernel,
         [jax.ShapeDtypeStruct(stream.shape, jnp.bfloat16)] * 2,
-        [VMEM_SPEC] * 3,
-        [],
-        mine.size, mine.size * 14, 4,
-    )(stream, mine, other)
+        [SMEM_SPEC] + [VMEM_SPEC] * 3,
+        [],
+        mine.size, mine.size * 10, 4,
+    )(place, stream, mine, given)
 
 
 def exchange(blocks):
     return lax.all_to_all(blocks, "attn", split_axis=0, concat_axis=0, tiled=True)
+
+
+def crossed(block, count, mask):
+    pairs = [(2 * index + 1, 2 * (index ^ mask) + 1) for index in range(count)]
+    return lax.ppermute(block, ("attn", "expert"), pairs)
+
+
+def spread_high(blocks, count):
+    return [blocks[0]] + [crossed(blocks[k], count, 2 * k) for k in range(1, count // 2)]
+
+
+def hand(block, source):
+    return lax.ppermute(block, "expert", [(source, 1 - source)])
 
 
 def swap(block):
@@ -504,30 +592,38 @@
     route_weight,
 ):
     count = lax.axis_size("attn")
-    sharers = count // HELD
+    highs = count // 2
+    sharers = highs // HELD
     capacity = routes.shape[0] * TOP // EXPERTS * 2
-    place = lax.axis_index("attn").astype(jnp.int32).reshape(1)
+    place = lax.axis_index(("attn", "expert")).astype(jnp.int32).reshape(1)
 
     earlier = order(place, routes.shape[0])
-    spread, own, taken, slots = prepare(
-        place, sharers, capacity, earlier, routes.T, route_weight.T, queries, new_key
+    spread, own, limit, taken, slots = prepare(
+        place, sharers, capacity, cache_length, earlier, routes.T, route_weight.T, queries, new_key
     )
     attended = exchange(
-        attend(count, spread, own, key_cache, value_cache, new_value, cache_length, ln_gain)
+        attend(count, spread, own, limit, key_cache, value_cache, new_value, ln_gain)
     )
     mine, gains = project(attended, out_weight)
-    stream, chosen = pick(sharers, count, mine, swap(mine), residual, taken)
-    outgoing = run_experts(
-        slots, exchange(chosen), gains, gate_weight.T, up_weight.T, down_weight
-    )
-    combined = combine(sharers, taken, exchange(outgoing))
-    attn_stream, expert_out = finish(stream, combined, swap(combined))
+    stream, *chosen = pick(place, sharers, highs, mine, swap(mine), residual, taken)
+    block = stack(place, spread_high(chosen, count))
+    other = crossed(block, count, 1)
+    keep, give = run_experts(
+        place, slots, (block, other, hand(block, 1), hand(other, 1)), gains,
+        gate_weight.T, up_weight.T, down_weight,
+    )
+    keep_given = hand(keep, 0)
+    arrived = crossed(add(give, hand(give, 0)), count, 1)
+    outgoing = send_blocks(place, keep, keep_given, arrived)
+    combined = combine(place, sharers, taken, spread_high(outgoing, count))
+    attn_stream, expert_out = finish(place, stream, combined, hand(combined, 1))
     return (attn_stream, expert_out)
 
 
 def solution(mesh):
     count = mesh.shape["attn"]
-    fits = D // count % 256 == 0 and count % HELD == 0 and mesh.shape["expert"] == 2
+    fits = D // count % 256 == 0 and count % (2 * HELD) == 0 and count & (count - 1) == 0
+    fits = fits and mesh.shape["expert"] == 2
     return jax.shard_map(
         shards if fits else shards_plain,
         mesh=mesh,

time: 49 us -> 67.6 us (1.38)
  waiting for transfers between devices: 2.6 us -> 31.1 us
  blocking collectives: 37.7 us -> 15.4 us
  starting transfers between devices: 0.05 us -> 12.6 us
    ppermute x0 -> x13, waiting for transfers between devices: none -> 29.8 us  [the longest x5 29.8 us: hand(): return lax.ppermute(block, 'expert', [(source, 1 - source)])]
    all_to_all x3 -> x1, blocking collectives: 37.7 us -> 15.4 us  [exchange(): lax.all_to_all(blocks, 'attn', split_axis=0, concat_axis=0, tiled=True)]
    ppermute x0 -> x13, starting transfers between devices: none -> 12.5 us  [the longest x5 7.22 us: hand(): return lax.ppermute(block, 'expert', [(source, 1 - source)])]
    ppermute x2 -> x1, waiting for transfers between devices: 2.6 us -> 1.29 us  [swap(): return lax.ppermute(block, 'expert', [(0, 1), (1, 0)])]
    pallas_call x1 -> x4, Pallas kernels: 1.87 us -> 1.98 us  [the longest x1 1.89 us: run_experts(): call(expert_kernel, [jax.ShapeDtypeStruct(blocks[0].shape, jnp.bfloat16)]...]
  transfers between devices with their start and end apart: 2 -> 14, of which waited for: 2 -> 5; matrix products, arithmetic and copies ran while one was open for 0% -> 0% of each run, Pallas kernels for 0% -> 0%
where the time goes in v11:
time: 67.6 us; the launch traced here: 67.2 us
  waiting for transfers between devices  31.1 us (46%)
  blocking collectives  15.4 us (23%)
  starting transfers between devices  12.6 us (19%)
  Pallas kernels  6.27 us (9%)
  between operations  1 us (1%)
  local copies, waits for them, and re-layouts  0.87 us (1%)
    ppermute x5, waiting for transfers between devices, hand(): return lax.ppermute(block, 'expert', [(source, 1 - source)])  29.8 us
    all_to_all x1, blocking collectives, exchange(): lax.all_to_all(blocks, 'attn', split_axis=0, concat_axis=0, tiled=True)  15.4 us
    ppermute x5, starting transfers between devices, hand(): return lax.ppermute(block, 'expert', [(source, 1 - source)])  7.22 us
    ppermute x8, starting transfers between devices, crossed(): return lax.ppermute(block, ('attn', 'expert'), pairs)  5.31 us
    pallas_call x1, Pallas kernels, run_experts(): call(expert_kernel, [jax.ShapeDtypeStruct(blocks[0].shape, jnp.bfloat16)]...  1.89 us
  transfers between devices with their start and end apart: 14, of which 5 were waited for; matrix products, arithmetic and copies ran while one was open for 0% of the time, Pallas kernels for 0%

profile of v11, /device:TPU:0, one launch (start us, length us, event | category | flops | bytes accessed | tf_op | source)
XLA Modules:
  0.0 67.2 jit_solution(8502100462657172790)
XLA Ops:
  0.7 0.0 copy-start.10
  0.7 0.0 copy-start.11
  0.7 0.0 copy-start.12
  0.8 0.6 copy-done.5
  1.4 0.0 copy-done.6
  1.4 0.0 copy-done.8
  1.4 0.7 %shard_map.150 = (bf16[4,24,512]{2,1,0:T(8,128)(2,1)S(1)}, f32[4,24,128]{2,1,0:T(8,128)S(1)}, s32[4,24,128]{2,1,0:T(8,128)S(1)}, f32[2,16,32]{2,1,0:T(8,128)S(1)}, f32[16,128]{1,0:T(8,128)S(1)}) custom-call(s32[1]{0:T(128)} %bitcast.place_ref, s32[4]{0:T(128)S(1)} %copy-done.9, bf16[32,32]{1,0:T(8,128)(2,1)S(1)} %shard_map.149.earlier_ref, ...), custom_call_target="tpu_custom_call" | custom-call | flops 98304 | bytes 196608 | tf_op jit(solution)/shard_map/pallas_call | solution.py:256
  2.1 0.2 copy-done
  2.3 1.2 %shard_map.151 = (bf16[4,24,512]{2,1,0:T(8,128)(2,1)S(1)}, f32[4,24,128]{2,1,0:T(8,128)S(1)}) custom-call(bf16[4,24,512]{2,1,0:T(8,128)(2,1)S(1)} %get-tuple-element.22.spread_ref, f32[4,24,128]{2,1,0:T(8,128)S(1)} %get-tuple-element.23.own_ref, s32[4,24,128]{2,1,0:T(8,128)S(1)} %get-tuple-element.24.limit_ref, bf16[4,512,512]{2,1,0:T(8,128)(2,1)S(1)} %copy-done), custom_call_target="tpu_custom_call" | custom-call | flops 50331648 | bytes 2097152 | tf_op jit(solution)/shard_map/pallas_call | solution.py:330
  3.5 0.0 slice-start.1
  3.5 0.5 shard_map.152
  4.0 15.4 %all_to_all.5.pieces = bf16[8,4,3456]{2,1,0:T(4,128)(2,1)S(1)} all-to-all(bf16[8,4,3456]{2,1,0:T(4,128)(2,1)S(1)} %shard_map.152), channel_id=1, replica_groups=mesh['group'=2,'attn'=8,'expert'=2] {'attn'}, dimensions={0} | all-to-all | bytes 442368 | tf_op jit(solution)/shard_map/all_to_all | solution.py:558
  19.4 0.0 copy-start.1
  19.5 0.0 copy-start.2
  19.5 0.0 copy-start.3
  19.5 0.9 %shard_map.153 = (f32[32,768]{1,0:T(8,128)S(1)}, f32[8,768]{1,0:T(8,128)S(1)}) custom-call(bf16[8,4,3456]{2,1,0:T(4,128)(2,1)S(1)} %all_to_all.5.pieces, bf16[3072,768]{1,0:T(8,128)(2,1)S(1)} %bitcast.10), custom_call_target="tpu_custom_call" | custom-call | flops 10000000000 | bytes 4718592 | tf_op jit(solution)/shard_map/pallas_call | solution.py:367
  20.4 0.0 collective-permute-start
  20.4 1.3 %collective-permute-done.other_ref = f32[32,768]{1,0:T(8,128)S(1)} collective-permute-done((f32[32,768]{1,0:T(8,128)S(1)}, f32[32,768]{1,0:T(8,128)S(1)}, u32[]{:S(2)}, u32[]{:S(2)}) %collective-permute-start) | collective-permute-done | bytes 98336 | tf_op jit(solution)/shard_map/ppermute | solution.py:575
  21.7 0.1 shard_map.154
  21.9 0.7 collective-permute-start.1
  22.5 0.7 collective-permute-start.2
  23.2 0.7 collective-permute-start.3
  23.9 0.0 collective-permute-done.1.refs_1_
  23.9 0.0 collective-permute-done.2.refs_2_
  23.9 0.0 collective-permute-done.3.refs_3_
  23.9 0.7 collective-permute-start.4
  24.6 1.3 %collective-permute-start.5 = (bf16[4,16,768]{2,1,0:T(8,128)(2,1)S(1)}, bf16[4,16,768]{2,1,0:T(8,128)(2,1)S(1)}, u32[]{:S(2)}, u32[]{:S(2)}) collective-permute-start(bf16[4,16,768]{2,1,0:T(8,128)(2,1)S(1)} %shard_map.155.mine_ref), channel_id=1, source_target_pairs={{1,0},{3,2},{5,4},{7,6},{9,8},{11,10},{13,12},{15,14},{17,16},{19,... | collective-permute-start | bytes 294920 | tf_op jit(solution)/shard_map/ppermute | solution.py:571
  25.9 0.0 collective-permute-done.4.other_ref
  25.9 1.3 %collective-permute-start.6 = (bf16[4,16,768]{2,1,0:T(8,128)(2,1)S(1)}, bf16[4,16,768]{2,1,0:T(8,128)(2,1)S(1)}, u32[]{:S(2)}, u32[]{:S(2)}) collective-permute-start(bf16[4,16,768]{2,1,0:T(8,128)(2,1)S(1)} %collective-permute-done.4.other_ref), channel_id=1, source_target_pairs={{1,0},{3,2},{5,4},{7,6},{9,8},{11,10},{13,12},{15,14},{17,16},{19,... | collective-permute-start | bytes 294920 | tf_op jit(solution)/shard_map/ppermute | solution.py:571
  27.2 11.3 %collective-permute-done.5.mine_given_ref = bf16[4,16,768]{2,1,0:T(8,128)(2,1)S(1)} collective-permute-done((bf16[4,16,768]{2,1,0:T(8,128)(2,1)S(1)}, bf16[4,16,768]{2,1,0:T(8,128)(2,1)S(1)}, u32[]{:S(2)}, u32[]{:S(2)}) %collective-permute-start.5) | collective-permute-done | bytes 98336 | tf_op jit(solution)/shard_map/ppermute | solution.py:571
  38.5 2.0 %collective-permute-done.6.other_given_ref = bf16[4,16,768]{2,1,0:T(8,128)(2,1)S(1)} collective-permute-done((bf16[4,16,768]{2,1,0:T(8,128)(2,1)S(1)}, bf16[4,16,768]{2,1,0:T(8,128)(2,1)S(1)}, u32[]{:S(2)}, u32[]{:S(2)}) %collective-permute-start.6) | collective-permute-done | bytes 98336 | tf_op jit(solution)/shard_map/ppermute | solution.py:571
  40.5 1.9 %shard_map.156 = (bf16[4,16,768]{2,1,0:T(8,128)(2,1)S(1)}, bf16[4,16,768]{2,1,0:T(8,128)(2,1)S(1)}) custom-call(s32[1]{0:T(128)} %bitcast.place_ref, f32[16,128]{1,0:T(8,128)S(1)} %get-tuple-element.30.slot_ref, bf16[4,16,768]{2,1,0:T(8,128)(2,1)S(1)} %shard_map.155.mine_ref, bf16[4,16,768]{2,1,0:T(8,128)(2,1)S(1)} %collective-permute-done.4.other_ref, ...), custom_call_target="tpu_custom_call" | custom-call | flops 99090432 | bytes 6193152 | tf_op jit(solution)/shard_map/pallas_call | solution.py:469
  42.4 2.0 %collective-permute-start.8 = (bf16[4,16,768]{2,1,0:T(8,128)(2,1)S(1)}, bf16[4,16,768]{2,1,0:T(8,128)(2,1)S(1)}, u32[]{:S(2)}, u32[]{:S(2)}) collective-permute-start(bf16[4,16,768]{2,1,0:T(8,128)(2,1)S(1)} %get-tuple-element.37.mine_ref), channel_id=1, source_target_pairs={{0,1},{2,3},{4,5},{6,7},{8,9},{10,11},{12,13},{14,15},{16,17},{18,... | collective-permute-start | bytes 294920 | tf_op jit(solution)/shard_map/ppermute | solution.py:571
  44.5 1.3 %collective-permute-start.7 = (bf16[4,16,768]{2,1,0:T(8,128)(2,1)S(1)}, bf16[4,16,768]{2,1,0:T(8,128)(2,1)S(1)}, u32[]{:S(2)}, u32[]{:S(2)}) collective-permute-start(bf16[4,16,768]{2,1,0:T(8,128)(2,1)S(1)} %get-tuple-element.36.refs_0_), channel_id=1, source_target_pairs={{0,1},{2,3},{4,5},{6,7},{8,9},{10,11},{12,13},{14,15},{16,17},{18,... | collective-permute-start | bytes 294920 | tf_op jit(solution)/shard_map/ppermute | solution.py:571
  45.8 0.0 collective-permute-done.8.given_ref
  45.8 0.7 collective-permute-start.9
  46.5 0.2 collective-permute-done.7.refs_1_
  46.7 0.0 collective-permute-done.9.refs_2_
  46.8 0.7 collective-permute-start.10
  47.4 0.7 collective-permute-start.11
  48.1 0.7 collective-permute-start.12
  48.8 0.0 collective-permute-done.10.refs_1_
  48.8 0.0 collective-permute-done.11.refs_2_
  48.8 0.0 collective-permute-done.12.refs_3_
  48.8 0.2 shard_map.159.mine_ref
  49.0 1.3 %collective-permute-start.13 = (bf16[32,768]{1,0:T(8,128)(2,1)S(1)}, bf16[32,768]{1,0:T(8,128)(2,1)S(1)}, u32[]{:S(2)}, u32[]{:S(2)}) collective-permute-start(bf16[32,768]{1,0:T(8,128)(2,1)S(1)} %shard_map.159.mine_ref), channel_id=1, source_target_pairs={{1,0},{3,2},{5,4},{7,6},{9,8},{11,10},{13,12},{15,14},{17,16},{19,... | collective-permute-start | bytes 147464 | tf_op jit(solution)/shard_map/ppermute | solution.py:571
  50.3 16.3 %collective-permute-done.13.given_ref = bf16[32,768]{1,0:T(8,128)(2,1)S(1)} collective-permute-done((bf16[32,768]{1,0:T(8,128)(2,1)S(1)}, bf16[32,768]{1,0:T(8,128)(2,1)S(1)}, u32[]{:S(2)}, u32[]{:S(2)}) %collective-permute-start.13) | collective-permute-done | bytes 49184 | tf_op jit(solution)/shard_map/ppermute | solution.py:571
  66.5 0.6 shard_map.160
  (24 shorter events, 0.1 us)
Async XLA Ops:
  0.6 0.7 %copy-start.5 = (bf16[4,3072]{1,0:T(4,128)(2,1)S(1)}, bf16[4,3072]{1,0:T(4,128)(2,1)}, u32[]{:S(2)}) copy-start(bf16[4,3072]{1,0:T(4,128)(2,1)} %query_ref.1) | copy-start | bytes 73732
  0.6 0.7 %copy-start.6 = (bf16[4,512]{1,0:T(4,128)(2,1)S(1)}, bf16[4,512]{1,0:T(4,128)(2,1)}, u32[]{:S(2)}) copy-start(bf16[4,512]{1,0:T(4,128)(2,1)} %own_key_ref.1) | copy-start | bytes 12292
  0.7 0.7 %copy-start.7 = (s32[32,4]{0,1:T(4,128)S(1)}, s32[32,4]{0,1:T(4,128)}, u32[]{:S(2)}) copy-start(s32[32,4]{0,1:T(4,128)} %param.26) | copy-start | bytes 1540
  0.7 0.7 %copy-start.8 = (f32[32,4]{0,1:T(4,128)S(1)}, f32[32,4]{0,1:T(4,128)}, u32[]{:S(2)}) copy-start(f32[32,4]{0,1:T(4,128)} %param.27) | copy-start | bytes 1540
  0.7 0.7 %copy-start.9 = (s32[4]{0:T(128)S(1)}, s32[4]{0:T(128)}, u32[]{:S(2)}) copy-start(s32[4]{0:T(128)} %length_ref.1) | copy-start | bytes 52
  0.7 1.6 %copy-start = (bf16[4,512,512]{2,1,0:T(8,128)(2,1)S(1)}, bf16[4,512,512]{2,1,0:T(8,128)(2,1)}, u32[]{:S(2)}) copy-start(bf16[4,512,512]{2,1,0:T(8,128)(2,1)} %key_ref.1) | copy-start | bytes 6291460
  0.7 2.8 %copy-start.10 = (bf16[4,512,512]{2,1,0:T(8,128)(2,1)S(1)}, bf16[4,512,512]{2,1,0:T(8,128)(2,1)}, u32[]{:S(2)}) copy-start(bf16[4,512,512]{2,1,0:T(8,128)(2,1)} %value_ref.1) | copy-start | bytes 6291460
  0.7 2.8 %copy-start.11 = (bf16[4,512]{1,0:T(4,128)(2,1)S(1)}, bf16[4,512]{1,0:T(4,128)(2,1)}, u32[]{:S(2)}) copy-start(bf16[4,512]{1,0:T(4,128)(2,1)} %own_value_ref.1) | copy-start | bytes 12292
  0.7 2.8 %copy-start.12 = (f32[768]{0:T(1024)S(1)}, f32[768]{0:T(1024)}, u32[]{:S(2)}) copy-start(f32[768]{0:T(1024)} %gain_ref.1) | copy-start | bytes 9220
  2.3 17.1 %slice-start = ((s8[4718592]{0:T(1024)(128)(4,1)}), s8[4194304]{0:T(1024)(128)(4,1)S(1)}, s32[]{:S(2)}) async-start(s8[4718592]{0:T(1024)(128)(4,1)} %bitcast.9), calls=%async_computation.1 | async-start | bytes 8388608
  3.5 15.9 %slice-start.1 = ((s8[4718592]{0:T(1024)(128)(4,1)}), s8[524288]{0:T(1024)(128)(4,1)S(1)}, s32[]{:S(2)}) async-start(s8[4718592]{0:T(1024)(128)(4,1)} %bitcast.9), calls=%async_computation.2 | async-start | bytes 1048576
  19.4 2.3 %copy-start.4 = (bf16[32,768]{1,0:T(8,128)(2,1)S(1)}, bf16[32,768]{1,0:T(8,128)(2,1)}, u32[]{:S(2)}) copy-start(bf16[32,768]{1,0:T(8,128)(2,1)} %residual_ref.1) | copy-start | bytes 147460
  19.4 21.1 %copy-start.1 = (bf16[6144,168]{0,1:T(8,128)(2,1)S(1)}, bf16[6144,168]{0,1:T(8,128)(2,1)}, u32[]{:S(2)}) copy-start(bf16[6144,168]{0,1:T(8,128)(2,1)} %param.23) | copy-start | bytes 6193156
  19.5 21.1 %copy-start.2 = (bf16[6144,168]{0,1:T(8,128)(2,1)S(1)}, bf16[6144,168]{0,1:T(8,128)(2,1)}, u32[]{:S(2)}) copy-start(bf16[6144,168]{0,1:T(8,128)(2,1)} %param.24) | copy-start | bytes 6193156
  19.5 21.1 %copy-start.3 = (bf16[168,6144]{1,0:T(8,128)(2,1)S(1)}, bf16[168,6144]{1,0:T(8,128)(2,1)}, u32[]{:S(2)}) copy-start(bf16[168,6144]{1,0:T(8,128)(2,1)} %down_ref.1) | copy-start | bytes 6193156
  20.4 1.3 %collective-permute-start = (f32[32,768]{1,0:T(8,128)S(1)}, f32[32,768]{1,0:T(8,128)S(1)}, u32[]{:S(2)}, u32[]{:S(2)}) collective-permute-start(f32[32,768]{1,0:T(8,128)S(1)} %get-tuple-element.27.mine_ref), channel_id=1, source_target_pairs={{0,1},{1,0},{2,3},{3,2},{4,5},{5,4},{6,7},{7,6},{8,9},{9,8},{10,11... | collective-permute-start | bytes 294920 | tf_op jit(solution)/shard_map/ppermute | solution.py:575
  21.9 2.0 %collective-permute-start.1 = (bf16[16,768]{1,0:T(8,128)(2,1)S(1)}, bf16[16,768]{1,0:T(8,128)(2,1)S(1)}, u32[]{:S(2)}, u32[]{:S(2)}) collective-permute-start(bf16[16,768]{1,0:T(8,128)(2,1)S(1)} %get-tuple-element.32), channel_id=1, source_target_pairs={{1,5},{3,7},{5,1},{7,3},{9,13},{11,15},{13,9},{15,11},{17,21},{19,... | collective-permute-start | bytes 73736 | tf_op jit(solution)/shard_map/ppermute | solution.py:563
  22.5 1.4 %collective-permute-start.2 = (bf16[16,768]{1,0:T(8,128)(2,1)S(1)}, bf16[16,768]{1,0:T(8,128)(2,1)S(1)}, u32[]{:S(2)}, u32[]{:S(2)}) collective-permute-start(bf16[16,768]{1,0:T(8,128)(2,1)S(1)} %get-tuple-element.33), channel_id=1, source_target_pairs={{1,9},{3,11},{5,13},{7,15},{9,1},{11,3},{13,5},{15,7},{17,25},{19,... | collective-permute-start | bytes 73736 | tf_op jit(solution)/shard_map/ppermute | solution.py:563
  23.2 0.7 %collective-permute-start.3 = (bf16[16,768]{1,0:T(8,128)(2,1)S(1)}, bf16[16,768]{1,0:T(8,128)(2,1)S(1)}, u32[]{:S(2)}, u32[]{:S(2)}) collective-permute-start(bf16[16,768]{1,0:T(8,128)(2,1)S(1)} %get-tuple-element.34), channel_id=1, source_target_pairs={{1,13},{3,15},{5,9},{7,11},{9,5},{11,7},{13,1},{15,3},{17,29},{19,... | collective-permute-start | bytes 73736 | tf_op jit(solution)/shard_map/ppermute | solution.py:563
  23.9 2.0 %collective-permute-start.4 = (bf16[4,16,768]{2,1,0:T(8,128)(2,1)S(1)}, bf16[4,16,768]{2,1,0:T(8,128)(2,1)S(1)}, u32[]{:S(2)}, u32[]{:S(2)}) collective-permute-start(bf16[4,16,768]{2,1,0:T(8,128)(2,1)S(1)} %shard_map.155.mine_ref), channel_id=1, source_target_pairs={{1,3},{3,1},{5,7},{7,5},{9,11},{11,9},{13,15},{15,13},{17,19},{19,... | collective-permute-start | bytes 294920 | tf_op jit(solution)/shard_map/ppermute | solution.py:563
  24.6 13.9 %collective-permute-start.5 = (bf16[4,16,768]{2,1,0:T(8,128)(2,1)S(1)}, bf16[4,16,768]{2,1,0:T(8,128)(2,1)S(1)}, u32[]{:S(2)}, u32[]{:S(2)}) collective-permute-start(bf16[4,16,768]{2,1,0:T(8,128)(2,1)S(1)} %shard_map.155.mine_ref), channel_id=1, source_target_pairs={{1,0},{3,2},{5,4},{7,6},{9,8},{11,10},{13,12},{15,14},{17,16},{19,... | collective-permute-start | bytes 294920 | tf_op jit(solution)/shard_map/ppermute | solution.py:571
  25.9 14.6 %collective-permute-start.6 = (bf16[4,16,768]{2,1,0:T(8,128)(2,1)S(1)}, bf16[4,16,768]{2,1,0:T(8,128)(2,1)S(1)}, u32[]{:S(2)}, u32[]{:S(2)}) collective-permute-start(bf16[4,16,768]{2,1,0:T(8,128)(2,1)S(1)} %collective-permute-done.4.other_ref), channel_id=1, source_target_pairs={{1,0},{3,2},{5,4},{7,6},{9,8},{11,10},{13,12},{15,14},{17,16},{19,... | collective-permute-start | bytes 294920 | tf_op jit(solution)/shard_map/ppermute | solution.py:571
  42.4 3.4 %collective-permute-start.8 = (bf16[4,16,768]{2,1,0:T(8,128)(2,1)S(1)}, bf16[4,16,768]{2,1,0:T(8,128)(2,1)S(1)}, u32[]{:S(2)}, u32[]{:S(2)}) collective-permute-start(bf16[4,16,768]{2,1,0:T(8,128)(2,1)S(1)} %get-tuple-element.37.mine_ref), channel_id=1, source_target_pairs={{0,1},{2,3},{4,5},{6,7},{8,9},{10,11},{12,13},{14,15},{16,17},{18,... | collective-permute-start | bytes 294920 | tf_op jit(solution)/shard_map/ppermute | solution.py:571
  44.5 2.2 %collective-permute-start.7 = (bf16[4,16,768]{2,1,0:T(8,128)(2,1)S(1)}, bf16[4,16,768]{2,1,0:T(8,128)(2,1)S(1)}, u32[]{:S(2)}, u32[]{:S(2)}) collective-permute-start(bf16[4,16,768]{2,1,0:T(8,128)(2,1)S(1)} %get-tuple-element.36.refs_0_), channel_id=1, source_target_pairs={{0,1},{2,3},{4,5},{6,7},{8,9},{10,11},{12,13},{14,15},{16,17},{18,... | collective-permute-start | bytes 294920 | tf_op jit(solution)/shard_map/ppermute | solution.py:571
  45.8 0.9 %collective-permute-start.9 = (bf16[4,16,768]{2,1,0:T(8,128)(2,1)S(1)}, bf16[4,16,768]{2,1,0:T(8,128)(2,1)S(1)}, u32[]{:S(2)}, u32[]{:S(2)}) collective-permute-start(bf16[4,16,768]{2,1,0:T(8,128)(2,1)S(1)} %shard_map.157), channel_id=1, source_target_pairs={{1,3},{3,1},{5,7},{7,5},{9,11},{11,9},{13,15},{15,13},{17,19},{19,... | collective-permute-start | bytes 294920 | tf_op jit(solution)/shard_map/ppermute | solution.py:563
  46.8 2.0 %collective-permute-start.10 = (bf16[16,768]{1,0:T(8,128)(2,1)S(1)}, bf16[16,768]{1,0:T(8,128)(2,1)S(1)}, u32[]{:S(2)}, u32[]{:S(2)}) collective-permute-start(bf16[16,768]{1,0:T(8,128)(2,1)S(1)} %get-tuple-element.39), channel_id=1, source_target_pairs={{1,5},{3,7},{5,1},{7,3},{9,13},{11,15},{13,9},{15,11},{17,21},{19,... | collective-permute-start | bytes 73736 | tf_op jit(solution)/shard_map/ppermute | solution.py:563
  47.4 1.4 %collective-permute-start.11 = (bf16[16,768]{1,0:T(8,128)(2,1)S(1)}, bf16[16,768]{1,0:T(8,128)(2,1)S(1)}, u32[]{:S(2)}, u32[]{:S(2)}) collective-permute-start(bf16[16,768]{1,0:T(8,128)(2,1)S(1)} %get-tuple-element.40), channel_id=1, source_target_pairs={{1,9},{3,11},{5,13},{7,15},{9,1},{11,3},{13,5},{15,7},{17,25},{19,... | collective-permute-start | bytes 73736 | tf_op jit(solution)/shard_map/ppermute | solution.py:563
  48.1 0.7 %collective-permute-start.12 = (bf16[16,768]{1,0:T(8,128)(2,1)S(1)}, bf16[16,768]{1,0:T(8,128)(2,1)S(1)}, u32[]{:S(2)}, u32[]{:S(2)}) collective-permute-start(bf16[16,768]{1,0:T(8,128)(2,1)S(1)} %get-tuple-element.41), channel_id=1, source_target_pairs={{1,13},{3,15},{5,9},{7,11},{9,5},{11,7},{13,1},{15,3},{17,29},{19,... | collective-permute-start | bytes 73736 | tf_op jit(solution)/shard_map/ppermute | solution.py:563
  49.0 17.6 %collective-permute-start.13 = (bf16[32,768]{1,0:T(8,128)(2,1)S(1)}, bf16[32,768]{1,0:T(8,128)(2,1)S(1)}, u32[]{:S(2)}, u32[]{:S(2)}) collective-permute-start(bf16[32,768]{1,0:T(8,128)(2,1)S(1)} %shard_map.159.mine_ref), channel_id=1, source_target_pairs={{1,0},{3,2},{5,4},{7,6},{9,8},{11,10},{13,12},{15,14},{17,16},{19,... | collective-permute-start | bytes 147464 | tf_op jit(solution)/shard_map/ppermute | solution.py:571

commit v12 on v10

--- a/solution.py
+++ b/solution.py
@@ -204,8 +204,9 @@
     return jnp.where((slot == place) & (hit > 0.5), 1.0, 0.0)
 
 
-def prepare_kernel(sharers, place_ref, earlier_ref, routes_ref, weight_ref, query_ref, own_key_ref,
-                   spread_ref, own_ref, taken_ref, slot_ref, query_rows, key_rows):
+def prepare_kernel(sharers, place_ref, length_ref, earlier_ref, routes_ref, weight_ref, query_ref,
+                   own_key_ref, spread_ref, own_ref, limit_ref, taken_ref, slot_ref, query_rows,
+                   key_rows):
     row_count = query_ref.shape[0]
     kv_local = own_key_ref.shape[1] // HEAD_DIM
     group = HEADS // KV_HEADS
@@ -226,6 +227,7 @@
         query = query_rows[strided, :]
         own = jnp.sum(query * key_rows[strided, :], axis=1, keepdims=True) * scale
         own_ref[r] = jnp.broadcast_to(own, (heads, HEAD_DIM))
+        limit_ref[r] = jnp.full((heads, HEAD_DIM), length_ref[r], jnp.int32)
         spread_ref[r] = jnp.concatenate(
             [jnp.where(head == g, query, 0.0) for g in range(kv_local)], axis=1
         ).astype(jnp.bfloat16)
@@ -245,7 +247,9 @@
     )
 
 
-def prepare(place, sharers, capacity, earlier, routes, route_weight, queries, new_key):
+def prepare(
+    place, sharers, capacity, cache_length, earlier, routes, route_weight, queries, new_key
+):
     row_count, width = queries.shape
     heads = width // HEAD_DIM
     table = pltpu.VMEM((heads * row_count, HEAD_DIM), jnp.float32)
@@ -254,16 +258,17 @@
         [
             jax.ShapeDtypeStruct((row_count, heads, new_key.shape[1]), jnp.bfloat16),
             jax.ShapeDtypeStruct((row_count, heads, HEAD_DIM), jnp.float32),
+            jax.ShapeDtypeStruct((row_count, heads, HEAD_DIM), jnp.int32),
             jax.ShapeDtypeStruct((HELD, capacity, routes.shape[1]), jnp.float32),
             jax.ShapeDtypeStruct((capacity, HEAD_DIM), jnp.float32),
         ],
-        [SMEM_SPEC] + [VMEM_SPEC] * 5,
+        [SMEM_SPEC] * 2 + [VMEM_SPEC] * 5,
         [table, table],
         queries.size * 8, queries.size * 16, 4,
-    )(place, earlier, routes, route_weight, queries, new_key)
-
-
-def score_kernel(length_ref, spread_ref, own_ref, key_ref, probs_ref, own_probs_ref):
+    )(place, cache_length, earlier, routes, route_weight, queries, new_key)
+
+
+def score_kernel(spread_ref, own_ref, limit_ref, key_ref, probs_ref, own_probs_ref):
     row_count, heads, length_max = probs_ref.shape
     scale = 1.0 / math.sqrt(HEAD_DIM)
     contract = (((1,), (1,)), ((), ()))
@@ -272,7 +277,7 @@
         scores = lax.dot_general(
             spread_ref[r], key_ref[r], contract, preferred_element_type=jnp.float32
         )
-        past = jnp.where(position < length_ref[r], scores * scale, NEG_FILL)
+        past = jnp.where(position < limit_ref[r, :, :1], scores * scale, NEG_FILL)
         own = own_ref[r, :, :1]
         largest = jnp.maximum(jnp.max(past, axis=1, keepdims=True), own)
         weight = jnp.exp(past - largest)
@@ -318,7 +323,7 @@
         out_ref[copy, :, heads * HEAD_DIM :] = parts
 
 
-def attend(count, spread, own, key_cache, value_cache, new_value, cache_length, gain):
+def attend(count, spread, own, limit, key_cache, value_cache, new_value, gain):
     row_count, heads, _ = spread.shape
     length_max = key_cache.shape[1]
     table = pltpu.VMEM((heads * row_count, HEAD_DIM), jnp.float32)
@@ -328,10 +333,10 @@
             jax.ShapeDtypeStruct((row_count, heads, length_max), jnp.bfloat16),
             jax.ShapeDtypeStruct((row_count, heads, HEAD_DIM), jnp.float32),
         ],
-        [SMEM_SPEC] + [VMEM_SPEC] * 3,
+        [VMEM_SPEC] * 4,
         [],
         2 * key_cache.size * heads, key_cache.size * 2, 8,
-    )(cache_length, spread, own, key_cache)
+    )(spread, own, limit, key_cache)
     width = heads * HEAD_DIM + gain.shape[0] // 2
     return call(
         value_kernel,
@@ -367,7 +372,7 @@
         ],
         [VMEM_SPEC, VMEM_SPEC],
         [pltpu.VMEM((rows * count, depth), jnp.float32)],
-        2 * rows * count * out_weight.size, out_weight.size * 2, 10,
+        EXCHANGE_FLOPS, out_weight.size * 2, 10,
     )(pieces, out_weight)
 
 
@@ -396,7 +401,7 @@
         ],
         [VMEM_SPEC] * 4,
         [],
-        EXCHANGE_FLOPS, rows * cols * 12, 4,
+        2 * HELD * taken.shape[1] * rows * cols, rows * cols * 12, 4,
     )(mine, other, residual, taken)
 
 
@@ -509,11 +514,11 @@
     place = lax.axis_index("attn").astype(jnp.int32).reshape(1)
 
     earlier = order(place, routes.shape[0])
-    spread, own, taken, slots = prepare(
-        place, sharers, capacity, earlier, routes.T, route_weight.T, queries, new_key
+    spread, own, limit, taken, slots = prepare(
+        place, sharers, capacity, cache_length, earlier, routes.T, route_weight.T, queries, new_key
     )
     attended = exchange(
-        attend(count, spread, own, key_cache, value_cache, new_value, cache_length, ln_gain)
+        attend(count, spread, own, limit, key_cache, value_cache, new_value, ln_gain)
     )
     mine, gains = project(attended, out_weight)
     stream, chosen = pick(sharers, count, mine, swap(mine), residual, taken)

time: 49 us -> 48.2 us (0.984)
  local copies, waits for them, and re-layouts: 1.39 us -> 0.87 us
    pallas_call x1, Pallas kernels: 1.71 us -> 1.15 us  [attend(): call(score_kernel, [jax.ShapeDtypeStruct((row_count, heads, length_max),...]
    pallas_call x1, Pallas kernels: 0.21 us -> 0.75 us  [prepare(): call(functools.partial(prepare_kernel, sharers), [jax.ShapeDtypeStruct((r...]
    unnamed x30, local copies, waits for them, and re-layouts: 1.39 us -> 0.87 us
where the time goes in v12:
time: 48.2 us; the launch traced here: 48 us
  blocking collectives  37.5 us (78%)
  Pallas kernels  6.15 us (13%)
  waiting for transfers between devices  2.6 us (5%)
  local copies, waits for them, and re-layouts  0.87 us (2%)
  between operations  0.82 us (2%)
    all_to_all x3, blocking collectives, exchange(): lax.all_to_all(blocks, 'attn', split_axis=0, concat_axis=0, tiled=True)  37.5 us
    ppermute x2, waiting for transfers between devices, swap(): return lax.ppermute(block, 'expert', [(0, 1), (1, 0)])  2.6 us
    pallas_call x1, Pallas kernels, run_experts(): call(expert_kernel, jax.ShapeDtypeStruct(pieces.shape, jnp.bfloat16), [VM...  1.87 us
    pallas_call x1, Pallas kernels, attend(): call(score_kernel, [jax.ShapeDtypeStruct((row_count, heads, length_max),...  1.15 us
  transfers between devices with their start and end apart: 2, of which 2 were waited for; matrix products, arithmetic and copies ran while one was open for 0% of the time, Pallas kernels for 0%

profile of v12, /device:TPU:0, one launch (start us, length us, event | category | flops | bytes accessed | tf_op | source)
XLA Modules:
  0.0 48.0 jit_solution(2977245925194871761)
XLA Ops:
  0.6 0.0 copy-start.5
  0.6 0.0 copy-start.6
  0.7 0.0 copy-start.7
  0.7 0.0 copy-start.8
  0.7 0.0 copy-start.9
  0.7 0.0 copy-start
  0.7 0.0 copy-start.10
  0.7 0.0 copy-start.11
  0.7 0.0 copy-start.12
  0.8 0.6 %copy-done.5 = bf16[4,3072]{1,0:T(4,128)(2,1)S(1)} copy-done((bf16[4,3072]{1,0:T(4,128)(2,1)S(1)}, bf16[4,3072]{1,0:T(4,128)(2,1)}, u32[]{:S(2)}) %copy-start.5) | copy-done | bytes 24600
  1.4 0.0 copy-done.6
  1.4 0.0 copy-done.7
  1.4 0.0 copy-done.8
  1.4 0.0 copy-done.9
  1.4 0.7 %shard_map.150 = (bf16[4,24,512]{2,1,0:T(8,128)(2,1)S(1)}, f32[4,24,128]{2,1,0:T(8,128)S(1)}, s32[4,24,128]{2,1,0:T(8,128)S(1)}, f32[2,16,32]{2,1,0:T(8,128)S(1)}, f32[16,128]{1,0:T(8,128)S(1)}) custom-call(s32[1]{0:T(128)} %bitcast.place_ref, s32[4]{0:T(128)S(1)} %copy-done.9, bf16[32,32]{1,0:T(8,128)(2,1)S(1)} %shard_map.149.earlier_ref, ...), custom_call_target="tpu_custom_call" | custom-call | flops 98304 | bytes 196608 | tf_op jit(solution)/shard_map/pallas_call | solution.py:256
  2.1 0.2 copy-done
  2.3 0.0 slice-start
  2.3 1.1 %shard_map.151 = (bf16[4,24,512]{2,1,0:T(8,128)(2,1)S(1)}, f32[4,24,128]{2,1,0:T(8,128)S(1)}) custom-call(bf16[4,24,512]{2,1,0:T(8,128)(2,1)S(1)} %get-tuple-element.13.spread_ref, f32[4,24,128]{2,1,0:T(8,128)S(1)} %get-tuple-element.14.own_ref, s32[4,24,128]{2,1,0:T(8,128)S(1)} %get-tuple-element.15.limit_ref, bf16[4,512,512]{2,1,0:T(8,128)(2,1)S(1)} %copy-done), custom_call_target="tpu_custom_call" | custom-call | flops 50331648 | bytes 2097152 | tf_op jit(solution)/shard_map/pallas_call | solution.py:330
  3.5 0.0 copy-done.10
  3.5 0.0 copy-done.11
  3.5 0.0 copy-done.12
  3.5 0.0 slice-start.1
  3.5 0.5 %shard_map.152 = bf16[8,4,3456]{2,1,0:T(4,128)(2,1)S(1)} custom-call(bf16[4,24,512]{2,1,0:T(8,128)(2,1)S(1)} %get-tuple-element.16.probs_ref, f32[4,24,128]{2,1,0:T(8,128)S(1)} %get-tuple-element.17.own_ref, bf16[4,512,512]{2,1,0:T(8,128)(2,1)S(1)} %copy-done.10, bf16[4,512]{1,0:T(4,128)(2,1)S(1)} %copy-done.11, f32[768]{0:T(1024)S(1)} %copy-done.12), custom_call_target="tpu_custom_call" | custom-call | flops 10000000000 | bytes 2097152 | tf_op jit(solution)/shard_map/pallas_call | solution.py:341
  4.0 15.4 %all_to_all.15.pieces = bf16[8,4,3456]{2,1,0:T(4,128)(2,1)S(1)} all-to-all(bf16[8,4,3456]{2,1,0:T(4,128)(2,1)S(1)} %shard_map.152), channel_id=1, replica_groups=mesh['group'=2,'attn'=8,'expert'=2] {'attn'}, dimensions={0} | all-to-all | bytes 442368 | tf_op jit(solution)/shard_map/all_to_all | solution.py:488
  19.4 0.0 slice-done
  19.4 0.0 slice-done.1
  19.4 0.0 copy-start.4
  19.4 0.0 copy-start.1
  19.5 0.0 copy-start.2
  19.5 0.0 copy-start.3
  19.5 0.9 %shard_map.153 = (f32[32,768]{1,0:T(8,128)S(1)}, f32[8,768]{1,0:T(8,128)S(1)}) custom-call(bf16[8,4,3456]{2,1,0:T(4,128)(2,1)S(1)} %all_to_all.15.pieces, bf16[3072,768]{1,0:T(8,128)(2,1)S(1)} %bitcast.10), custom_call_target="tpu_custom_call" | custom-call | flops 10000000000 | bytes 4718592 | tf_op jit(solution)/shard_map/pallas_call | solution.py:367
  20.4 0.0 collective-permute-start
  20.4 1.3 %collective-permute-done.other_ref = f32[32,768]{1,0:T(8,128)S(1)} collective-permute-done((f32[32,768]{1,0:T(8,128)S(1)}, f32[32,768]{1,0:T(8,128)S(1)}, u32[]{:S(2)}, u32[]{:S(2)}) %collective-permute-start) | collective-permute-done | bytes 98336 | tf_op jit(solution)/shard_map/ppermute | solution.py:492
  21.7 0.0 copy-done.4
  21.7 0.1 shard_map.154
  21.9 11.4 %all_to_all.16.pieces = bf16[8,16,768]{2,1,0:T(8,128)(2,1)S(1)} all-to-all(bf16[8,16,768]{2,1,0:T(8,128)(2,1)S(1)} %get-tuple-element.22), channel_id=1, replica_groups=mesh['group'=2,'attn'=8,'expert'=2] {'attn'}, dimensions={0} | all-to-all | bytes 393216 | tf_op jit(solution)/shard_map/all_to_all | solution.py:488
  33.2 0.0 copy-done.1
  33.2 0.0 copy-done.2
  33.2 0.0 copy-done.3
  33.2 1.9 %shard_map.155 = bf16[8,16,768]{2,1,0:T(8,128)(2,1)S(1)} custom-call(f32[16,128]{1,0:T(8,128)S(1)} %get-tuple-element.21.slot_ref, bf16[8,16,768]{2,1,0:T(8,128)(2,1)S(1)} %all_to_all.16.pieces, f32[8,768]{1,0:T(8,128)S(1)} %get-tuple-element.23.gains, bf16[168,6144]{1,0:T(8,128)(2,1)S(1)} %bitcast.5, bf16[168,6144]{1,0:T(8,128)(2,1)S(1)} %bitcast.6, ...), custom_call_target="tpu_custom_call" | custom-call | flops 99090432 | bytes 6193152 | tf_op jit(solution)/shard_map/pallas_call | solution.py:440
  35.1 10.7 %all_to_all.17.pieces = bf16[8,16,768]{2,1,0:T(8,128)(2,1)S(1)} all-to-all(bf16[8,16,768]{2,1,0:T(8,128)(2,1)S(1)} %shard_map.155), channel_id=1, replica_groups=mesh['group'=2,'attn'=8,'expert'=2] {'attn'}, dimensions={0} | all-to-all | bytes 393216 | tf_op jit(solution)/shard_map/all_to_all | solution.py:488
  45.8 0.2 shard_map.156.mine_ref
  46.0 0.0 collective-permute-start.1
  46.0 1.3 %collective-permute-done.1.other_ref = f32[32,768]{1,0:T(8,128)S(1)} collective-permute-done((f32[32,768]{1,0:T(8,128)S(1)}, f32[32,768]{1,0:T(8,128)S(1)}, u32[]{:S(2)}, u32[]{:S(2)}) %collective-permute-start.1) | collective-permute-done | bytes 98336 | tf_op jit(solution)/shard_map/ppermute | solution.py:492
  47.3 0.6 %shard_map.157 = (bf16[32,768]{1,0:T(8,128)(2,1)}, bf16[32,768]{1,0:T(8,128)(2,1)}) custom-call(bf16[32,768]{1,0:T(8,128)(2,1)S(1)} %get-tuple-element.20.stream_ref, f32[32,768]{1,0:T(8,128)S(1)} %shard_map.156.mine_ref, f32[32,768]{1,0:T(8,128)S(1)} %collective-permute-done.1.other_ref), custom_call_target="tpu_custom_call" | custom-call | flops 24576 | bytes 344064 | tf_op jit(solution)/shard_map/pallas_call | solution.py:478
  (2 shorter events, 0.0 us)
Async XLA Ops:
  0.6 0.7 %copy-start.5 = (bf16[4,3072]{1,0:T(4,128)(2,1)S(1)}, bf16[4,3072]{1,0:T(4,128)(2,1)}, u32[]{:S(2)}) copy-start(bf16[4,3072]{1,0:T(4,128)(2,1)} %query_ref.1) | copy-start | bytes 73732
  0.6 0.7 %copy-start.6 = (bf16[4,512]{1,0:T(4,128)(2,1)S(1)}, bf16[4,512]{1,0:T(4,128)(2,1)}, u32[]{:S(2)}) copy-start(bf16[4,512]{1,0:T(4,128)(2,1)} %own_key_ref.1) | copy-start | bytes 12292
  0.7 0.7 %copy-start.7 = (s32[32,4]{0,1:T(4,128)S(1)}, s32[32,4]{0,1:T(4,128)}, u32[]{:S(2)}) copy-start(s32[32,4]{0,1:T(4,128)} %param.26) | copy-start | bytes 1540
  0.7 0.7 %copy-start.8 = (f32[32,4]{0,1:T(4,128)S(1)}, f32[32,4]{0,1:T(4,128)}, u32[]{:S(2)}) copy-start(f32[32,4]{0,1:T(4,128)} %param.27) | copy-start | bytes 1540
  0.7 0.7 %copy-start.9 = (s32[4]{0:T(128)S(1)}, s32[4]{0:T(128)}, u32[]{:S(2)}) copy-start(s32[4]{0:T(128)} %length_ref.1) | copy-start | bytes 52
  0.7 1.6 %copy-start = (bf16[4,512,512]{2,1,0:T(8,128)(2,1)S(1)}, bf16[4,512,512]{2,1,0:T(8,128)(2,1)}, u32[]{:S(2)}) copy-start(bf16[4,512,512]{2,1,0:T(8,128)(2,1)} %key_ref.1) | copy-start | bytes 6291460
  0.7 2.7 %copy-start.10 = (bf16[4,512,512]{2,1,0:T(8,128)(2,1)S(1)}, bf16[4,512,512]{2,1,0:T(8,128)(2,1)}, u32[]{:S(2)}) copy-start(bf16[4,512,512]{2,1,0:T(8,128)(2,1)} %value_ref.1) | copy-start | bytes 6291460
  0.7 2.7 %copy-start.11 = (bf16[4,512]{1,0:T(4,128)(2,1)S(1)}, bf16[4,512]{1,0:T(4,128)(2,1)}, u32[]{:S(2)}) copy-start(bf16[4,512]{1,0:T(4,128)(2,1)} %own_value_ref.1) | copy-start | bytes 12292
  0.7 2.7 %copy-start.12 = (f32[768]{0:T(1024)S(1)}, f32[768]{0:T(1024)}, u32[]{:S(2)}) copy-start(f32[768]{0:T(1024)} %gain_ref.1) | copy-start | bytes 9220
  2.3 17.1 %slice-start = ((s8[4718592]{0:T(1024)(128)(4,1)}), s8[4194304]{0:T(1024)(128)(4,1)S(1)}, s32[]{:S(2)}) async-start(s8[4718592]{0:T(1024)(128)(4,1)} %bitcast.9), calls=%async_computation.3 | async-start | bytes 8388608
  3.5 15.9 %slice-start.1 = ((s8[4718592]{0:T(1024)(128)(4,1)}), s8[524288]{0:T(1024)(128)(4,1)S(1)}, s32[]{:S(2)}) async-start(s8[4718592]{0:T(1024)(128)(4,1)} %bitcast.9), calls=%async_computation.4 | async-start | bytes 1048576
  19.4 2.3 %copy-start.4 = (bf16[32,768]{1,0:T(8,128)(2,1)S(1)}, bf16[32,768]{1,0:T(8,128)(2,1)}, u32[]{:S(2)}) copy-start(bf16[32,768]{1,0:T(8,128)(2,1)} %residual_ref.1) | copy-start | bytes 147460
  19.4 13.8 %copy-start.1 = (bf16[6144,168]{0,1:T(8,128)(2,1)S(1)}, bf16[6144,168]{0,1:T(8,128)(2,1)}, u32[]{:S(2)}) copy-start(bf16[6144,168]{0,1:T(8,128)(2,1)} %param.23) | copy-start | bytes 6193156
  19.5 13.8 %copy-start.2 = (bf16[6144,168]{0,1:T(8,128)(2,1)S(1)}, bf16[6144,168]{0,1:T(8,128)(2,1)}, u32[]{:S(2)}) copy-start(bf16[6144,168]{0,1:T(8,128)(2,1)} %param.24) | copy-start | bytes 6193156
  19.5 13.8 %copy-start.3 = (bf16[168,6144]{1,0:T(8,128)(2,1)S(1)}, bf16[168,6144]{1,0:T(8,128)(2,1)}, u32[]{:S(2)}) copy-start(bf16[168,6144]{1,0:T(8,128)(2,1)} %down_ref.1) | copy-start | bytes 6193156
  20.4 1.3 %collective-permute-start = (f32[32,768]{1,0:T(8,128)S(1)}, f32[32,768]{1,0:T(8,128)S(1)}, u32[]{:S(2)}, u32[]{:S(2)}) collective-permute-start(f32[32,768]{1,0:T(8,128)S(1)} %get-tuple-element.18.mine_ref), channel_id=1, source_target_pairs={{0,1},{1,0},{2,3},{3,2},{4,5},{5,4},{6,7},{7,6},{8,9},{9,8},{10,11... | collective-permute-start | bytes 294920 | tf_op jit(solution)/shard_map/ppermute | solution.py:492
  46.0 1.3 %collective-permute-start.1 = (f32[32,768]{1,0:T(8,128)S(1)}, f32[32,768]{1,0:T(8,128)S(1)}, u32[]{:S(2)}, u32[]{:S(2)}) collective-permute-start(f32[32,768]{1,0:T(8,128)S(1)} %shard_map.156.mine_ref), channel_id=1, source_target_pairs={{0,1},{1,0},{2,3},{3,2},{4,5},{5,4},{6,7},{7,6},{8,9},{9,8},{10,11... | collective-permute-start | bytes 294920 | tf_op jit(solution)/shard_map/ppermute | solution.py:492

commit v13 on v12

--- a/solution.py
+++ b/solution.py
@@ -272,20 +272,29 @@
     row_count, heads, length_max = probs_ref.shape
     scale = 1.0 / math.sqrt(HEAD_DIM)
     contract = (((1,), (1,)), ((), ()))
-    position = lax.broadcasted_iota(jnp.int32, (heads, length_max), 1)
+    scores = jnp.concatenate(
+        [
+            lax.dot_general(
+                spread_ref[r], key_ref[r], contract, preferred_element_type=jnp.float32
+            )
+            for r in range(row_count)
+        ],
+        axis=0,
+    )
+    position = lax.broadcasted_iota(jnp.int32, scores.shape, 1)
+    limit = jnp.concatenate([limit_ref[r, :, :1] for r in range(row_count)], axis=0)
+    own = jnp.concatenate([own_ref[r, :, :1] for r in range(row_count)], axis=0)
+    past = jnp.where(position < limit, scores * scale, NEG_FILL)
+    largest = jnp.maximum(jnp.max(past, axis=1, keepdims=True), own)
+    weight = jnp.exp(past - largest)
+    own_weight = jnp.exp(own - largest)
+    inverse = 1.0 / (jnp.sum(weight, axis=1, keepdims=True) + own_weight)
+    probs = weight * inverse
+    own_prob = (own_weight * inverse).astype(jnp.bfloat16).astype(jnp.float32)
     for r in range(row_count):
-        scores = lax.dot_general(
-            spread_ref[r], key_ref[r], contract, preferred_element_type=jnp.float32
-        )
-        past = jnp.where(position < limit_ref[r, :, :1], scores * scale, NEG_FILL)
-        own = own_ref[r, :, :1]
-        largest = jnp.maximum(jnp.max(past, axis=1, keepdims=True), own)
-        weight = jnp.exp(past - largest)
-        own_weight = jnp.exp(own - largest)
-        inverse = 1.0 / (jnp.sum(weight, axis=1, keepdims=True) + own_weight)
-        probs_ref[r] = (weight * inverse).astype(jnp.bfloat16)
-        own_prob = (own_weight * inverse).astype(jnp.bfloat16).astype(jnp.float32)
-        own_probs_ref[r] = jnp.broadcast_to(own_prob, own_probs_ref.shape[1:])
+        rows = slice(r * heads, (r + 1) * heads)
+        probs_ref[r] = probs[rows].astype(jnp.bfloat16)
+        own_probs_ref[r] = jnp.broadcast_to(own_prob[rows], own_probs_ref.shape[1:])
 
 
 def value_kernel(probs_ref, own_ref, value_ref, own_value_ref, gain_ref, out_ref, value_rows,
@@ -422,12 +431,12 @@
         wide = pieces[k].astype(jnp.float32)
         normed = ((wide - row_mean) * inverse * gains[pl.ds(k, 1), :]).astype(jnp.bfloat16)
         gate_val = gate_val + lax.dot_general(
-            gate_ref[:, block], normed, contract, preferred_element_type=jnp.float32
+            normed, gate_ref[:, block], contract, preferred_element_type=jnp.float32
         )
         up_val = up_val + lax.dot_general(
-            up_ref[:, block], normed, contract, preferred_element_type=jnp.float32
+            normed, up_ref[:, block], contract, preferred_element_type=jnp.float32
         )
-    hidden = (gate_val / (1.0 + jnp.exp(-gate_val)) * up_val).T.astype(jnp.bfloat16)
+    hidden = (gate_val / (1.0 + jnp.exp(-gate_val)) * up_val).astype(jnp.bfloat16)
     slot_weight = slot_ref[:, :1]
     for k in range(count):
         block = slice(k * cols, (k + 1) * cols)

time: 48.2 us -> 48 us (level)
  no operation moved by 1% of the time
where the time goes in v13:
time: 48 us; the launch traced here: 47.7 us
  blocking collectives  37.5 us (78%)
  Pallas kernels  5.9 us (12%)
  waiting for transfers between devices  2.6 us (5%)
  local copies, waits for them, and re-layouts  0.87 us (2%)
  between operations  0.82 us (2%)
    all_to_all x3, blocking collectives, exchange(): lax.all_to_all(blocks, 'attn', split_axis=0, concat_axis=0, tiled=True)  37.5 us
    ppermute x2, waiting for transfers between devices, swap(): return lax.ppermute(block, 'expert', [(0, 1), (1, 0)])  2.6 us
    pallas_call x1, Pallas kernels, run_experts(): call(expert_kernel, jax.ShapeDtypeStruct(pieces.shape, jnp.bfloat16), [VM...  1.74 us
    pallas_call x1, Pallas kernels, attend(): call(score_kernel, [jax.ShapeDtypeStruct((row_count, heads, length_max),...  1.02 us
  transfers between devices with their start and end apart: 2, of which 2 were waited for; matrix products, arithmetic and copies ran while one was open for 0% of the time, Pallas kernels for 0%

profile of v13, /device:TPU:0, one launch (start us, length us, event | category | flops | bytes accessed | tf_op | source)
XLA Modules:
  0.0 47.7 jit_solution(2765709681653573841)
XLA Ops:
  0.6 0.0 copy-start.5
  0.6 0.0 copy-start.6
  0.7 0.0 copy-start.7
  0.7 0.0 copy-start.8
  0.7 0.0 copy-start.9
  0.7 0.0 copy-start
  0.7 0.0 copy-start.10
  0.7 0.0 copy-start.11
  0.7 0.0 copy-start.12
  0.8 0.6 %copy-done.5 = bf16[4,3072]{1,0:T(4,128)(2,1)S(1)} copy-done((bf16[4,3072]{1,0:T(4,128)(2,1)S(1)}, bf16[4,3072]{1,0:T(4,128)(2,1)}, u32[]{:S(2)}) %copy-start.5) | copy-done | bytes 24600
  1.4 0.0 copy-done.6
  1.4 0.0 copy-done.7
  1.4 0.0 copy-done.8
  1.4 0.0 copy-done.9
  1.4 0.7 %shard_map.150 = (bf16[4,24,512]{2,1,0:T(8,128)(2,1)S(1)}, f32[4,24,128]{2,1,0:T(8,128)S(1)}, s32[4,24,128]{2,1,0:T(8,128)S(1)}, f32[2,16,32]{2,1,0:T(8,128)S(1)}, f32[16,128]{1,0:T(8,128)S(1)}) custom-call(s32[1]{0:T(128)} %bitcast.place_ref, s32[4]{0:T(128)S(1)} %copy-done.9, bf16[32,32]{1,0:T(8,128)(2,1)S(1)} %shard_map.149.earlier_ref, ...), custom_call_target="tpu_custom_call" | custom-call | flops 98304 | bytes 196608 | tf_op jit(solution)/shard_map/pallas_call | solution.py:256
  2.1 0.2 copy-done
  2.3 0.0 slice-start
  2.3 1.0 %shard_map.151 = (bf16[4,24,512]{2,1,0:T(8,128)(2,1)S(1)}, f32[4,24,128]{2,1,0:T(8,128)S(1)}) custom-call(bf16[4,24,512]{2,1,0:T(8,128)(2,1)S(1)} %get-tuple-element.13.spread_ref, f32[4,24,128]{2,1,0:T(8,128)S(1)} %get-tuple-element.14.own_ref, s32[4,24,128]{2,1,0:T(8,128)S(1)} %get-tuple-element.15.limit_ref, bf16[4,512,512]{2,1,0:T(8,128)(2,1)S(1)} %copy-done), custom_call_target="tpu_custom_call" | custom-call | flops 50331648 | bytes 2097152 | tf_op jit(solution)/shard_map/pallas_call | solution.py:339
  3.3 0.0 copy-done.10
  3.3 0.0 copy-done.11
  3.4 0.0 copy-done.12
  3.4 0.0 slice-start.1
  3.4 0.5 %shard_map.152 = bf16[8,4,3456]{2,1,0:T(4,128)(2,1)S(1)} custom-call(bf16[4,24,512]{2,1,0:T(8,128)(2,1)S(1)} %get-tuple-element.16.probs_ref, f32[4,24,128]{2,1,0:T(8,128)S(1)} %get-tuple-element.17.own_ref, bf16[4,512,512]{2,1,0:T(8,128)(2,1)S(1)} %copy-done.10, bf16[4,512]{1,0:T(4,128)(2,1)S(1)} %copy-done.11, f32[768]{0:T(1024)S(1)} %copy-done.12), custom_call_target="tpu_custom_call" | custom-call | flops 10000000000 | bytes 2097152 | tf_op jit(solution)/shard_map/pallas_call | solution.py:350
  3.9 15.4 %all_to_all.15.pieces = bf16[8,4,3456]{2,1,0:T(4,128)(2,1)S(1)} all-to-all(bf16[8,4,3456]{2,1,0:T(4,128)(2,1)S(1)} %shard_map.152), channel_id=1, replica_groups=mesh['group'=2,'attn'=8,'expert'=2] {'attn'}, dimensions={0} | all-to-all | bytes 442368 | tf_op jit(solution)/shard_map/all_to_all | solution.py:497
  19.3 0.0 slice-done
  19.3 0.0 slice-done.1
  19.3 0.0 copy-start.4
  19.3 0.0 copy-start.1
  19.3 0.0 copy-start.2
  19.3 0.0 copy-start.3
  19.4 0.9 %shard_map.153 = (f32[32,768]{1,0:T(8,128)S(1)}, f32[8,768]{1,0:T(8,128)S(1)}) custom-call(bf16[8,4,3456]{2,1,0:T(4,128)(2,1)S(1)} %all_to_all.15.pieces, bf16[3072,768]{1,0:T(8,128)(2,1)S(1)} %bitcast.10), custom_call_target="tpu_custom_call" | custom-call | flops 10000000000 | bytes 4718592 | tf_op jit(solution)/shard_map/pallas_call | solution.py:376
  20.2 0.0 collective-permute-start
  20.3 1.3 %collective-permute-done.other_ref = f32[32,768]{1,0:T(8,128)S(1)} collective-permute-done((f32[32,768]{1,0:T(8,128)S(1)}, f32[32,768]{1,0:T(8,128)S(1)}, u32[]{:S(2)}, u32[]{:S(2)}) %collective-permute-start) | collective-permute-done | bytes 98336 | tf_op jit(solution)/shard_map/ppermute | solution.py:501
  21.6 0.0 copy-done.4
  21.6 0.1 shard_map.154
  21.7 11.4 %all_to_all.16.pieces = bf16[8,16,768]{2,1,0:T(8,128)(2,1)S(1)} all-to-all(bf16[8,16,768]{2,1,0:T(8,128)(2,1)S(1)} %get-tuple-element.22), channel_id=1, replica_groups=mesh['group'=2,'attn'=8,'expert'=2] {'attn'}, dimensions={0} | all-to-all | bytes 393216 | tf_op jit(solution)/shard_map/all_to_all | solution.py:497
  33.1 0.0 copy-done.1
  33.1 0.0 copy-done.2
  33.1 0.0 copy-done.3
  33.1 1.7 %shard_map.155 = bf16[8,16,768]{2,1,0:T(8,128)(2,1)S(1)} custom-call(f32[16,128]{1,0:T(8,128)S(1)} %get-tuple-element.21.slot_ref, bf16[8,16,768]{2,1,0:T(8,128)(2,1)S(1)} %all_to_all.16.pieces, f32[8,768]{1,0:T(8,128)S(1)} %get-tuple-element.23.gains, bf16[168,6144]{1,0:T(8,128)(2,1)S(1)} %bitcast.5, bf16[168,6144]{1,0:T(8,128)(2,1)S(1)} %bitcast.6, ...), custom_call_target="tpu_custom_call" | custom-call | flops 99090432 | bytes 6193152 | tf_op jit(solution)/shard_map/pallas_call | solution.py:449
  34.9 10.7 %all_to_all.17.pieces = bf16[8,16,768]{2,1,0:T(8,128)(2,1)S(1)} all-to-all(bf16[8,16,768]{2,1,0:T(8,128)(2,1)S(1)} %shard_map.155), channel_id=1, replica_groups=mesh['group'=2,'attn'=8,'expert'=2] {'attn'}, dimensions={0} | all-to-all | bytes 393216 | tf_op jit(solution)/shard_map/all_to_all | solution.py:497
  45.6 0.2 shard_map.156.mine_ref
  45.8 0.0 collective-permute-start.1
  45.8 1.3 %collective-permute-done.1.other_ref = f32[32,768]{1,0:T(8,128)S(1)} collective-permute-done((f32[32,768]{1,0:T(8,128)S(1)}, f32[32,768]{1,0:T(8,128)S(1)}, u32[]{:S(2)}, u32[]{:S(2)}) %collective-permute-start.1) | collective-permute-done | bytes 98336 | tf_op jit(solution)/shard_map/ppermute | solution.py:501
  47.1 0.6 %shard_map.157 = (bf16[32,768]{1,0:T(8,128)(2,1)}, bf16[32,768]{1,0:T(8,128)(2,1)}) custom-call(bf16[32,768]{1,0:T(8,128)(2,1)S(1)} %get-tuple-element.20.stream_ref, f32[32,768]{1,0:T(8,128)S(1)} %shard_map.156.mine_ref, f32[32,768]{1,0:T(8,128)S(1)} %collective-permute-done.1.other_ref), custom_call_target="tpu_custom_call" | custom-call | flops 24576 | bytes 344064 | tf_op jit(solution)/shard_map/pallas_call | solution.py:487
  (2 shorter events, 0.0 us)
Async XLA Ops:
  0.6 0.7 %copy-start.5 = (bf16[4,3072]{1,0:T(4,128)(2,1)S(1)}, bf16[4,3072]{1,0:T(4,128)(2,1)}, u32[]{:S(2)}) copy-start(bf16[4,3072]{1,0:T(4,128)(2,1)} %query_ref.1) | copy-start | bytes 73732
  0.6 0.7 %copy-start.6 = (bf16[4,512]{1,0:T(4,128)(2,1)S(1)}, bf16[4,512]{1,0:T(4,128)(2,1)}, u32[]{:S(2)}) copy-start(bf16[4,512]{1,0:T(4,128)(2,1)} %own_key_ref.1) | copy-start | bytes 12292
  0.7 0.7 %copy-start.7 = (s32[32,4]{0,1:T(4,128)S(1)}, s32[32,4]{0,1:T(4,128)}, u32[]{:S(2)}) copy-start(s32[32,4]{0,1:T(4,128)} %param.26) | copy-start | bytes 1540
  0.7 0.7 %copy-start.8 = (f32[32,4]{0,1:T(4,128)S(1)}, f32[32,4]{0,1:T(4,128)}, u32[]{:S(2)}) copy-start(f32[32,4]{0,1:T(4,128)} %param.27) | copy-start | bytes 1540
  0.7 0.7 %copy-start.9 = (s32[4]{0:T(128)S(1)}, s32[4]{0:T(128)}, u32[]{:S(2)}) copy-start(s32[4]{0:T(128)} %length_ref.1) | copy-start | bytes 52
  0.7 1.6 %copy-start = (bf16[4,512,512]{2,1,0:T(8,128)(2,1)S(1)}, bf16[4,512,512]{2,1,0:T(8,128)(2,1)}, u32[]{:S(2)}) copy-start(bf16[4,512,512]{2,1,0:T(8,128)(2,1)} %key_ref.1) | copy-start | bytes 6291460
  0.7 2.6 %copy-start.10 = (bf16[4,512,512]{2,1,0:T(8,128)(2,1)S(1)}, bf16[4,512,512]{2,1,0:T(8,128)(2,1)}, u32[]{:S(2)}) copy-start(bf16[4,512,512]{2,1,0:T(8,128)(2,1)} %value_ref.1) | copy-start | bytes 6291460
  0.7 2.6 %copy-start.11 = (bf16[4,512]{1,0:T(4,128)(2,1)S(1)}, bf16[4,512]{1,0:T(4,128)(2,1)}, u32[]{:S(2)}) copy-start(bf16[4,512]{1,0:T(4,128)(2,1)} %own_value_ref.1) | copy-start | bytes 12292
  0.7 2.6 %copy-start.12 = (f32[768]{0:T(1024)S(1)}, f32[768]{0:T(1024)}, u32[]{:S(2)}) copy-start(f32[768]{0:T(1024)} %gain_ref.1) | copy-start | bytes 9220
  2.3 17.0 %slice-start = ((s8[4718592]{0:T(1024)(128)(4,1)}), s8[4194304]{0:T(1024)(128)(4,1)S(1)}, s32[]{:S(2)}) async-start(s8[4718592]{0:T(1024)(128)(4,1)} %bitcast.9), calls=%async_computation.3 | async-start | bytes 8388608
  3.4 15.9 %slice-start.1 = ((s8[4718592]{0:T(1024)(128)(4,1)}), s8[524288]{0:T(1024)(128)(4,1)S(1)}, s32[]{:S(2)}) async-start(s8[4718592]{0:T(1024)(128)(4,1)} %bitcast.9), calls=%async_computation.4 | async-start | bytes 1048576
  19.3 2.3 %copy-start.4 = (bf16[32,768]{1,0:T(8,128)(2,1)S(1)}, bf16[32,768]{1,0:T(8,128)(2,1)}, u32[]{:S(2)}) copy-start(bf16[32,768]{1,0:T(8,128)(2,1)} %residual_ref.1) | copy-start | bytes 147460
  19.3 13.8 %copy-start.1 = (bf16[6144,168]{0,1:T(8,128)(2,1)S(1)}, bf16[6144,168]{0,1:T(8,128)(2,1)}, u32[]{:S(2)}) copy-start(bf16[6144,168]{0,1:T(8,128)(2,1)} %param.23) | copy-start | bytes 6193156
  19.3 13.8 %copy-start.2 = (bf16[6144,168]{0,1:T(8,128)(2,1)S(1)}, bf16[6144,168]{0,1:T(8,128)(2,1)}, u32[]{:S(2)}) copy-start(bf16[6144,168]{0,1:T(8,128)(2,1)} %param.24) | copy-start | bytes 6193156
  19.3 13.8 %copy-start.3 = (bf16[168,6144]{1,0:T(8,128)(2,1)S(1)}, bf16[168,6144]{1,0:T(8,128)(2,1)}, u32[]{:S(2)}) copy-start(bf16[168,6144]{1,0:T(8,128)(2,1)} %down_ref.1) | copy-start | bytes 6193156
  20.2 1.3 %collective-permute-start = (f32[32,768]{1,0:T(8,128)S(1)}, f32[32,768]{1,0:T(8,128)S(1)}, u32[]{:S(2)}, u32[]{:S(2)}) collective-permute-start(f32[32,768]{1,0:T(8,128)S(1)} %get-tuple-element.18.mine_ref), channel_id=1, source_target_pairs={{0,1},{1,0},{2,3},{3,2},{4,5},{5,4},{6,7},{7,6},{8,9},{9,8},{10,11... | collective-permute-start | bytes 294920 | tf_op jit(solution)/shard_map/ppermute | solution.py:501
  45.8 1.3 %collective-permute-start.1 = (f32[32,768]{1,0:T(8,128)S(1)}, f32[32,768]{1,0:T(8,128)S(1)}, u32[]{:S(2)}, u32[]{:S(2)}) collective-permute-start(f32[32,768]{1,0:T(8,128)S(1)} %shard_map.156.mine_ref), channel_id=1, source_target_pairs={{0,1},{1,0},{2,3},{3,2},{4,5},{5,4},{6,7},{7,6},{8,9},{9,8},{10,11... | collective-permute-start | bytes 294920 | tf_op jit(solution)/shard_map/ppermute | solution.py:501

commit v14 on v13

--- a/solution.py
+++ b/solution.py
@@ -233,10 +233,13 @@
         ).astype(jnp.bfloat16)
     routes = routes_ref[...]
     capacity = slot_ref.shape[0]
-    taken = [expert_rows(routes, earlier_ref[...], e, capacity) for e in range(HELD)]
+    core = place_ref[0] % 2
+    taken = []
     for e in range(HELD):
+        both = expert_rows(routes, earlier_ref[...], e, 2 * capacity)
+        taken.append(jnp.where(core == 0, both[:capacity], both[capacity:]))
         taken_ref[e] = taken[e]
-    first = place_ref[0] < sharers
+    first = place_ref[0] // 2 < sharers
     expert = jnp.where(first, 0, 1)
     row_weight = jnp.sum(
         jnp.where(routes == expert, weight_ref[...], 0.0), axis=0, keepdims=True
@@ -414,7 +417,8 @@
     )(mine, other, residual, taken)
 
 
-def expert_kernel(slot_ref, pieces, gains, gate_ref, up_ref, down_ref, out_ref):
+def expert_kernel(slot_ref, pieces, gains, *refs):
+    weights, out_ref = (refs[:3], refs[3:6]), refs[6]
     count, capacity, cols = pieces.shape
     first = second = 0.0
     for k in range(count):
@@ -425,42 +429,49 @@
     row_var = jnp.sum(second, axis=1, keepdims=True) / D - row_mean * row_mean
     inverse = lax.rsqrt(row_var + EPSILON)
     contract = (((1,), (1,)), ((), ()))
-    gate_val = up_val = 0.0
+    gate_val, up_val = [0.0, 0.0], [0.0, 0.0]
     for k in range(count):
         block = slice(k * cols, (k + 1) * cols)
         wide = pieces[k].astype(jnp.float32)
         normed = ((wide - row_mean) * inverse * gains[pl.ds(k, 1), :]).astype(jnp.bfloat16)
-        gate_val = gate_val + lax.dot_general(
-            normed, gate_ref[:, block], contract, preferred_element_type=jnp.float32
-        )
-        up_val = up_val + lax.dot_general(
-            normed, up_ref[:, block], contract, preferred_element_type=jnp.float32
-        )
-    hidden = (gate_val / (1.0 + jnp.exp(-gate_val)) * up_val).astype(jnp.bfloat16)
+        for index, (gate_ref, up_ref, _) in enumerate(weights):
+            gate_val[index] = gate_val[index] + lax.dot_general(
+                normed, gate_ref[:, block], contract, preferred_element_type=jnp.float32
+            )
+            up_val[index] = up_val[index] + lax.dot_general(
+                normed, up_ref[:, block], contract, preferred_element_type=jnp.float32
+            )
+    hidden = [
+        (gate / (1.0 + jnp.exp(-gate)) * up).astype(jnp.bfloat16)
+        for gate, up in zip(gate_val, up_val)
+    ]
     slot_weight = slot_ref[:, :1]
     for k in range(count):
         block = slice(k * cols, (k + 1) * cols)
-        out_ref[k] = (
-            jnp.dot(hidden, down_ref[:, block], preferred_element_type=jnp.float32) * slot_weight
-        ).astype(jnp.bfloat16)
-
-
-def run_experts(slots, pieces, gains, gate, up, down):
+        piece = sum(
+            jnp.dot(part, refs_of[2][:, block], preferred_element_type=jnp.float32)
+            for part, refs_of in zip(hidden, weights)
+        )
+        out_ref[k] = (piece * slot_weight).astype(jnp.bfloat16)
+
+
+def run_experts(slots, pieces, gains, own, other):
     return call(
         expert_kernel,
         jax.ShapeDtypeStruct(pieces.shape, jnp.bfloat16),
-        [VMEM_SPEC] * 6,
+        [VMEM_SPEC] * 9,
         [],
-        6 * pieces.shape[1] * gate.size, gate.size * 6, 14,
-    )(slots, pieces, gains, gate, up, down)
+        12 * pieces.shape[1] * own[0].size, own[0].size * 12, 20,
+    )(slots, pieces, gains, *own, *other)
 
 
 def combine_kernel(sharers, taken_ref, pieces, out_ref):
     count, capacity, cols = pieces.shape
     spread = [taken_ref[k // sharers] for k in range(count)]
+    rows = [pieces[k].astype(jnp.float32) for k in range(count)]
     out_ref[...] = lax.dot_general(
         jnp.concatenate(spread, axis=0).astype(jnp.bfloat16),
-        pieces[...].reshape(count * capacity, cols),
+        jnp.concatenate(rows, axis=0).astype(jnp.bfloat16),
         (((0,), (0,)), ((), ())),
         preferred_element_type=jnp.float32,
     )
@@ -519,10 +530,12 @@
 ):
     count = lax.axis_size("attn")
     sharers = count // HELD
-    capacity = routes.shape[0] * TOP // EXPERTS * 2
-    place = lax.axis_index("attn").astype(jnp.int32).reshape(1)
+    capacity = routes.shape[0] * TOP // EXPERTS
+    place = lax.axis_index(("attn", "expert")).astype(jnp.int32).reshape(1)
 
     earlier = order(place, routes.shape[0])
+    weights = (gate_weight.T, up_weight.T, down_weight)
+    other_weights = [swap(block) for block in weights]
     spread, own, limit, taken, slots = prepare(
         place, sharers, capacity, cache_length, earlier, routes.T, route_weight.T, queries, new_key
     )
@@ -531,9 +544,7 @@
     )
     mine, gains = project(attended, out_weight)
     stream, chosen = pick(sharers, count, mine, swap(mine), residual, taken)
-    outgoing = run_experts(
-        slots, exchange(chosen), gains, gate_weight.T, up_weight.T, down_weight
-    )
+    outgoing = run_experts(slots, exchange(chosen), gains, weights, other_weights)
     combined = combine(sharers, taken, exchange(outgoing))
     attn_stream, expert_out = finish(stream, combined, swap(combined))
     return (attn_stream, expert_out)

time: 48 us -> 50.5 us (1.052)
  Pallas kernels: 5.9 us -> 9.44 us
  blocking collectives: 37.5 us -> 35.4 us
  starting transfers between devices: 0.05 us -> 1.08 us
    pallas_call x1, Pallas kernels: 1.74 us -> 5.3 us  [run_experts(): call(expert_kernel, jax.ShapeDtypeStruct(pieces.shape, jnp.bfloat16), [VM...]
    all_to_all x3, blocking collectives: 37.5 us -> 35.4 us  [exchange(): lax.all_to_all(blocks, 'attn', split_axis=0, concat_axis=0, tiled=True)]
    ppermute x2 -> x5, starting transfers between devices: 0.05 us -> 1.08 us  [swap(): return lax.ppermute(block, 'expert', [(0, 1), (1, 0)])]
    ppermute x2 -> x5, waiting for transfers between devices: 2.6 us -> 2.59 us  [swap(): return lax.ppermute(block, 'expert', [(0, 1), (1, 0)])]
  transfers between devices with their start and end apart: 2 -> 5, of which waited for: 2 -> 2; matrix products, arithmetic and copies ran while one was open for 0% -> 0% of each run, Pallas kernels for 0% -> 7%
where the time goes in v14:
time: 50.5 us; the launch traced here: 50.2 us
  blocking collectives  35.4 us (70%)
  Pallas kernels  9.44 us (19%)
  waiting for transfers between devices  2.59 us (5%)
  starting transfers between devices  1.08 us (2%)
  local copies, waits for them, and re-layouts  0.9 us (2%)
  between operations  0.81 us (2%)
    all_to_all x3, blocking collectives, exchange(): lax.all_to_all(blocks, 'attn', split_axis=0, concat_axis=0, tiled=True)  35.4 us
    pallas_call x1, Pallas kernels, run_experts(): call(expert_kernel, jax.ShapeDtypeStruct(pieces.shape, jnp.bfloat16), [VM...  5.3 us
    ppermute x5, waiting for transfers between devices, swap(): return lax.ppermute(block, 'expert', [(0, 1), (1, 0)])  2.59 us
    ppermute x5, starting transfers between devices, swap(): return lax.ppermute(block, 'expert', [(0, 1), (1, 0)])  1.08 us
    pallas_call x1, Pallas kernels, attend(): call(score_kernel, [jax.ShapeDtypeStruct((row_count, heads, length_max),...  1.03 us
  transfers between devices with their start and end apart: 5, of which 2 were waited for; matrix products, arithmetic and copies ran while one was open for 0% of the time, Pallas kernels for 7%

profile of v14, /device:TPU:0, one launch (start us, length us, event | category | flops | bytes accessed | tf_op | source)
XLA Modules:
  0.0 50.2 jit_solution(15005551597151037969)
XLA Ops:
  0.6 0.5 %collective-permute-start.1 = (bf16[168,6144]{1,0:T(8,128)(2,1)}, bf16[168,6144]{1,0:T(8,128)(2,1)S(1)}, u32[]{:S(2)}, u32[]{:S(2)}) collective-permute-start(bf16[168,6144]{1,0:T(8,128)(2,1)} %bitcast.5), channel_id=1, source_target_pairs={{0,1},{1,0},{2,3},{3,2},{4,5},{5,4},{6,7},{7,6},{8,9},{9,8},{10,11... | collective-permute-start | bytes 6193160 | tf_op jit(solution)/shard_map/ppermute | solution.py:512
  1.1 0.1 collective-permute-start.2
  1.2 0.4 collective-permute-start.3
  1.7 0.0 copy-start.5
  1.7 0.0 copy-start.6
  1.7 0.0 copy-start.8
  1.7 0.0 copy-start.9
  1.7 0.0 copy-start
  1.7 0.0 copy-start.10
  1.7 0.0 copy-start.11
  1.7 0.0 copy-start.12
  1.7 0.7 %copy-done.5 = bf16[4,3072]{1,0:T(4,128)(2,1)S(1)} copy-done((bf16[4,3072]{1,0:T(4,128)(2,1)S(1)}, bf16[4,3072]{1,0:T(4,128)(2,1)}, u32[]{:S(2)}) %copy-start.5) | copy-done | bytes 24600
  2.4 0.0 copy-done.6
  2.4 0.0 copy-done.7
  2.4 0.0 copy-done.8
  2.4 0.0 copy-done.9
  2.4 0.7 %shard_map.150 = (bf16[4,24,512]{2,1,0:T(8,128)(2,1)S(1)}, f32[4,24,128]{2,1,0:T(8,128)S(1)}, s32[4,24,128]{2,1,0:T(8,128)S(1)}, f32[2,8,32]{2,1,0:T(8,128)S(1)}, f32[8,128]{1,0:T(8,128)S(1)}) custom-call(s32[1]{0:T(128)} %bitcast.place_ref, s32[4]{0:T(128)S(1)} %copy-done.9, bf16[32,32]{1,0:T(8,128)(2,1)S(1)} %shard_map.149.earlier_ref, ...), custom_call_target="tpu_custom_call" | custom-call | flops 98304 | bytes 196608 | tf_op jit(solution)/shard_map/pallas_call | solution.py:259
  3.2 0.2 copy-done
  3.3 1.0 %shard_map.151 = (bf16[4,24,512]{2,1,0:T(8,128)(2,1)S(1)}, f32[4,24,128]{2,1,0:T(8,128)S(1)}) custom-call(bf16[4,24,512]{2,1,0:T(8,128)(2,1)S(1)} %get-tuple-element.13.spread_ref, f32[4,24,128]{2,1,0:T(8,128)S(1)} %get-tuple-element.14.own_ref, s32[4,24,128]{2,1,0:T(8,128)S(1)} %get-tuple-element.15.limit_ref, bf16[4,512,512]{2,1,0:T(8,128)(2,1)S(1)} %copy-done), custom_call_target="tpu_custom_call" | custom-call | flops 50331648 | bytes 2097152 | tf_op jit(solution)/shard_map/pallas_call | solution.py:342
  4.4 0.0 copy-done.10
  4.4 0.0 copy-done.11
  4.4 0.0 copy-done.12
  4.4 0.0 slice-start.1
  4.4 0.5 %shard_map.152 = bf16[8,4,3456]{2,1,0:T(4,128)(2,1)S(1)} custom-call(bf16[4,24,512]{2,1,0:T(8,128)(2,1)S(1)} %get-tuple-element.16.probs_ref, f32[4,24,128]{2,1,0:T(8,128)S(1)} %get-tuple-element.17.own_ref, bf16[4,512,512]{2,1,0:T(8,128)(2,1)S(1)} %copy-done.10, bf16[4,512]{1,0:T(4,128)(2,1)S(1)} %copy-done.11, f32[768]{0:T(1024)S(1)} %copy-done.12), custom_call_target="tpu_custom_call" | custom-call | flops 10000000000 | bytes 2097152 | tf_op jit(solution)/shard_map/pallas_call | solution.py:353
  4.9 15.6 %all_to_all.15.pieces = bf16[8,4,3456]{2,1,0:T(4,128)(2,1)S(1)} all-to-all(bf16[8,4,3456]{2,1,0:T(4,128)(2,1)S(1)} %shard_map.152), channel_id=1, replica_groups=mesh['group'=2,'attn'=8,'expert'=2] {'attn'}, dimensions={0} | all-to-all | bytes 442368 | tf_op jit(solution)/shard_map/all_to_all | solution.py:508
  20.6 0.0 slice-done
  20.6 0.0 slice-done.1
  20.6 0.0 copy-start.1
  20.6 0.0 copy-start.2
  20.6 0.0 copy-start.3
  20.6 0.9 %shard_map.153 = (f32[32,768]{1,0:T(8,128)S(1)}, f32[8,768]{1,0:T(8,128)S(1)}) custom-call(bf16[8,4,3456]{2,1,0:T(4,128)(2,1)S(1)} %all_to_all.15.pieces, bf16[3072,768]{1,0:T(8,128)(2,1)S(1)} %bitcast.12), custom_call_target="tpu_custom_call" | custom-call | flops 10000000000 | bytes 4718592 | tf_op jit(solution)/shard_map/pallas_call | solution.py:379
  21.5 0.0 collective-permute-start
  21.5 1.3 %collective-permute-done.other_ref = f32[32,768]{1,0:T(8,128)S(1)} collective-permute-done((f32[32,768]{1,0:T(8,128)S(1)}, f32[32,768]{1,0:T(8,128)S(1)}, u32[]{:S(2)}, u32[]{:S(2)}) %collective-permute-start) | collective-permute-done | bytes 98336 | tf_op jit(solution)/shard_map/ppermute | solution.py:512
  22.8 0.0 copy-done.4
  22.8 0.1 shard_map.154
  23.0 10.2 %all_to_all.16.pieces = bf16[8,8,768]{2,1,0:T(8,128)(2,1)S(1)} all-to-all(bf16[8,8,768]{2,1,0:T(8,128)(2,1)S(1)} %get-tuple-element.22), channel_id=1, replica_groups=mesh['group'=2,'attn'=8,'expert'=2] {'attn'}, dimensions={0} | all-to-all | bytes 196608 | tf_op jit(solution)/shard_map/all_to_all | solution.py:508
  33.2 0.0 collective-permute-done.1.refs_3_
  33.2 0.0 collective-permute-done.2.refs_4_
  33.2 0.0 collective-permute-done.3.refs_5_
  33.2 0.0 copy-done.1
  33.2 0.0 copy-done.2
  33.2 0.0 copy-done.3
  33.3 5.3 %shard_map.155 = bf16[8,8,768]{2,1,0:T(8,128)(2,1)S(1)} custom-call(f32[8,128]{1,0:T(8,128)S(1)} %get-tuple-element.21.slot_ref, bf16[8,8,768]{2,1,0:T(8,128)(2,1)S(1)} %all_to_all.16.pieces, f32[8,768]{1,0:T(8,128)S(1)} %get-tuple-element.23.gains, bf16[168,6144]{1,0:T(8,128)(2,1)S(1)} %bitcast.6, bf16[168,6144]{1,0:T(8,128)(2,1)S(1)} %bitcast.8, ...), custom_call_target="tpu_custom_call" | custom-call | flops 99090432 | bytes 12386304 | tf_op jit(solution)/shard_map/pallas_call | solution.py:459
  38.6 9.5 %all_to_all.17.pieces = bf16[8,8,768]{2,1,0:T(8,128)(2,1)S(1)} all-to-all(bf16[8,8,768]{2,1,0:T(8,128)(2,1)S(1)} %shard_map.155), channel_id=1, replica_groups=mesh['group'=2,'attn'=8,'expert'=2] {'attn'}, dimensions={0} | all-to-all | bytes 196608 | tf_op jit(solution)/shard_map/all_to_all | solution.py:508
  48.1 0.2 shard_map.156.mine_ref
  48.2 0.0 collective-permute-start.4
  48.3 1.3 %collective-permute-done.4.other_ref = f32[32,768]{1,0:T(8,128)S(1)} collective-permute-done((f32[32,768]{1,0:T(8,128)S(1)}, f32[32,768]{1,0:T(8,128)S(1)}, u32[]{:S(2)}, u32[]{:S(2)}) %collective-permute-start.4) | collective-permute-done | bytes 98336 | tf_op jit(solution)/shard_map/ppermute | solution.py:512
  49.5 0.6 %shard_map.157 = (bf16[32,768]{1,0:T(8,128)(2,1)}, bf16[32,768]{1,0:T(8,128)(2,1)}) custom-call(bf16[32,768]{1,0:T(8,128)(2,1)S(1)} %get-tuple-element.20.stream_ref, f32[32,768]{1,0:T(8,128)S(1)} %shard_map.156.mine_ref, f32[32,768]{1,0:T(8,128)S(1)} %collective-permute-done.4.other_ref), custom_call_target="tpu_custom_call" | custom-call | flops 24576 | bytes 344064 | tf_op jit(solution)/shard_map/pallas_call | solution.py:498
  (5 shorter events, 0.0 us)
Async XLA Ops:
  0.6 32.6 %collective-permute-start.1 = (bf16[168,6144]{1,0:T(8,128)(2,1)}, bf16[168,6144]{1,0:T(8,128)(2,1)S(1)}, u32[]{:S(2)}, u32[]{:S(2)}) collective-permute-start(bf16[168,6144]{1,0:T(8,128)(2,1)} %bitcast.5), channel_id=1, source_target_pairs={{0,1},{1,0},{2,3},{3,2},{4,5},{5,4},{6,7},{7,6},{8,9},{9,8},{10,11... | collective-permute-start | bytes 6193160 | tf_op jit(solution)/shard_map/ppermute | solution.py:512
  1.1 32.1 %collective-permute-start.2 = (bf16[168,6144]{1,0:T(8,128)(2,1)}, bf16[168,6144]{1,0:T(8,128)(2,1)}, u32[]{:S(2)}, u32[]{:S(2)}) collective-permute-start(bf16[168,6144]{1,0:T(8,128)(2,1)} %bitcast.7), channel_id=1, source_target_pairs={{0,1},{1,0},{2,3},{3,2},{4,5},{5,4},{6,7},{7,6},{8,9},{9,8},{10,11... | collective-permute-start | bytes 6193160 | tf_op jit(solution)/shard_map/ppermute | solution.py:512
  1.2 32.0 %collective-permute-start.3 = (bf16[168,6144]{1,0:T(8,128)(2,1)}, bf16[168,6144]{1,0:T(8,128)(2,1)}, u32[]{:S(2)}, u32[]{:S(2)}) collective-permute-start(bf16[168,6144]{1,0:T(8,128)(2,1)} %refs_2_.1), channel_id=1, source_target_pairs={{0,1},{1,0},{2,3},{3,2},{4,5},{5,4},{6,7},{7,6},{8,9},{9,8},{10,11... | collective-permute-start | bytes 6193160 | tf_op jit(solution)/shard_map/ppermute | solution.py:512
  1.7 0.7 %copy-start.5 = (bf16[4,3072]{1,0:T(4,128)(2,1)S(1)}, bf16[4,3072]{1,0:T(4,128)(2,1)}, u32[]{:S(2)}) copy-start(bf16[4,3072]{1,0:T(4,128)(2,1)} %query_ref.1) | copy-start | bytes 73732
  1.7 0.7 %copy-start.6 = (bf16[4,512]{1,0:T(4,128)(2,1)S(1)}, bf16[4,512]{1,0:T(4,128)(2,1)}, u32[]{:S(2)}) copy-start(bf16[4,512]{1,0:T(4,128)(2,1)} %own_key_ref.1) | copy-start | bytes 12292
  1.7 0.7 %copy-start.7 = (s32[32,4]{0,1:T(4,128)S(1)}, s32[32,4]{0,1:T(4,128)}, u32[]{:S(2)}) copy-start(s32[32,4]{0,1:T(4,128)} %param.26) | copy-start | bytes 1540
  1.7 0.7 %copy-start.8 = (f32[32,4]{0,1:T(4,128)S(1)}, f32[32,4]{0,1:T(4,128)}, u32[]{:S(2)}) copy-start(f32[32,4]{0,1:T(4,128)} %param.27) | copy-start | bytes 1540
  1.7 0.7 %copy-start.9 = (s32[4]{0:T(128)S(1)}, s32[4]{0:T(128)}, u32[]{:S(2)}) copy-start(s32[4]{0:T(128)} %length_ref.1) | copy-start | bytes 52
  1.7 1.7 %copy-start = (bf16[4,512,512]{2,1,0:T(8,128)(2,1)S(1)}, bf16[4,512,512]{2,1,0:T(8,128)(2,1)}, u32[]{:S(2)}) copy-start(bf16[4,512,512]{2,1,0:T(8,128)(2,1)} %key_ref.1) | copy-start | bytes 6291460
  1.7 2.7 %copy-start.10 = (bf16[4,512,512]{2,1,0:T(8,128)(2,1)S(1)}, bf16[4,512,512]{2,1,0:T(8,128)(2,1)}, u32[]{:S(2)}) copy-start(bf16[4,512,512]{2,1,0:T(8,128)(2,1)} %value_ref.1) | copy-start | bytes 6291460
  1.7 2.7 %copy-start.11 = (bf16[4,512]{1,0:T(4,128)(2,1)S(1)}, bf16[4,512]{1,0:T(4,128)(2,1)}, u32[]{:S(2)}) copy-start(bf16[4,512]{1,0:T(4,128)(2,1)} %own_value_ref.1) | copy-start | bytes 12292
  1.7 2.7 %copy-start.12 = (f32[768]{0:T(1024)S(1)}, f32[768]{0:T(1024)}, u32[]{:S(2)}) copy-start(f32[768]{0:T(1024)} %gain_ref.1) | copy-start | bytes 9220
  3.3 17.2 %slice-start = ((s8[4718592]{0:T(1024)(128)(4,1)}), s8[4194304]{0:T(1024)(128)(4,1)S(1)}, s32[]{:S(2)}) async-start(s8[4718592]{0:T(1024)(128)(4,1)} %bitcast.11), calls=%async_computation.3 | async-start | bytes 8388608
  4.4 16.2 %slice-start.1 = ((s8[4718592]{0:T(1024)(128)(4,1)}), s8[524288]{0:T(1024)(128)(4,1)S(1)}, s32[]{:S(2)}) async-start(s8[4718592]{0:T(1024)(128)(4,1)} %bitcast.11), calls=%async_computation.4 | async-start | bytes 1048576
  20.6 2.3 %copy-start.4 = (bf16[32,768]{1,0:T(8,128)(2,1)S(1)}, bf16[32,768]{1,0:T(8,128)(2,1)}, u32[]{:S(2)}) copy-start(bf16[32,768]{1,0:T(8,128)(2,1)} %residual_ref.1) | copy-start | bytes 147460
  20.6 12.6 %copy-start.1 = (bf16[6144,168]{0,1:T(8,128)(2,1)S(1)}, bf16[6144,168]{0,1:T(8,128)(2,1)}, u32[]{:S(2)}) copy-start(bf16[6144,168]{0,1:T(8,128)(2,1)} %param.23) | copy-start | bytes 6193156
  20.6 12.6 %copy-start.2 = (bf16[6144,168]{0,1:T(8,128)(2,1)S(1)}, bf16[6144,168]{0,1:T(8,128)(2,1)}, u32[]{:S(2)}) copy-start(bf16[6144,168]{0,1:T(8,128)(2,1)} %param.24) | copy-start | bytes 6193156
  20.6 12.6 %copy-start.3 = (bf16[168,6144]{1,0:T(8,128)(2,1)S(1)}, bf16[168,6144]{1,0:T(8,128)(2,1)}, u32[]{:S(2)}) copy-start(bf16[168,6144]{1,0:T(8,128)(2,1)} %refs_2_.1) | copy-start | bytes 6193156
  21.5 1.3 %collective-permute-start = (f32[32,768]{1,0:T(8,128)S(1)}, f32[32,768]{1,0:T(8,128)S(1)}, u32[]{:S(2)}, u32[]{:S(2)}) collective-permute-start(f32[32,768]{1,0:T(8,128)S(1)} %get-tuple-element.18.mine_ref), channel_id=1, source_target_pairs={{0,1},{1,0},{2,3},{3,2},{4,5},{5,4},{6,7},{7,6},{8,9},{9,8},{10,11... | collective-permute-start | bytes 294920 | tf_op jit(solution)/shard_map/ppermute | solution.py:512
  48.2 1.3 %collective-permute-start.4 = (f32[32,768]{1,0:T(8,128)S(1)}, f32[32,768]{1,0:T(8,128)S(1)}, u32[]{:S(2)}, u32[]{:S(2)}) collective-permute-start(f32[32,768]{1,0:T(8,128)S(1)} %shard_map.156.mine_ref), channel_id=1, source_target_pairs={{0,1},{1,0},{2,3},{3,2},{4,5},{5,4},{6,7},{7,6},{8,9},{9,8},{10,11... | collective-permute-start | bytes 294920 | tf_op jit(solution)/shard_map/ppermute | solution.py:512

commit v15 on v14

--- a/solution.py
+++ b/solution.py
@@ -174,22 +174,22 @@
     )
 
 
-def order_kernel(place_ref, out_ref):
+def order_kernel(out_ref):
     rows = out_ref.shape[0]
     before = lax.broadcasted_iota(jnp.int32, (rows, rows), 0) < lax.broadcasted_iota(
         jnp.int32, (rows, rows), 1
     )
-    out_ref[...] = jnp.where(before & (place_ref[0] >= 0), 1.0, 0.0).astype(jnp.bfloat16)
-
-
-def order(place, rows):
+    out_ref[...] = jnp.where(before, 1.0, 0.0).astype(jnp.bfloat16)
+
+
+def order(rows):
     return call(
         order_kernel,
         jax.ShapeDtypeStruct((rows, rows), jnp.bfloat16),
-        [SMEM_SPEC],
+        [],
         [],
         EXCHANGE_FLOPS, rows * rows * 2, 2,
-    )(place)
+    )()
 
 
 def expert_rows(routes, earlier, expert, capacity):
@@ -204,7 +204,7 @@
     return jnp.where((slot == place) & (hit > 0.5), 1.0, 0.0)
 
 
-def prepare_kernel(sharers, place_ref, length_ref, earlier_ref, routes_ref, weight_ref, query_ref,
+def prepare_kernel(sharers, length_ref, earlier_ref, routes_ref, weight_ref, query_ref,
                    own_key_ref, spread_ref, own_ref, limit_ref, taken_ref, slot_ref, query_rows,
                    key_rows):
     row_count = query_ref.shape[0]
@@ -233,13 +233,13 @@
         ).astype(jnp.bfloat16)
     routes = routes_ref[...]
     capacity = slot_ref.shape[0]
-    core = place_ref[0] % 2
+    core = lax.axis_index("expert")
     taken = []
     for e in range(HELD):
         both = expert_rows(routes, earlier_ref[...], e, 2 * capacity)
         taken.append(jnp.where(core == 0, both[:capacity], both[capacity:]))
         taken_ref[e] = taken[e]
-    first = place_ref[0] // 2 < sharers
+    first = lax.axis_index("attn") < sharers
     expert = jnp.where(first, 0, 1)
     row_weight = jnp.sum(
         jnp.where(routes == expert, weight_ref[...], 0.0), axis=0, keepdims=True
@@ -251,7 +251,7 @@
 
 
 def prepare(
-    place, sharers, capacity, cache_length, earlier, routes, route_weight, queries, new_key
+    sharers, capacity, cache_length, earlier, routes, route_weight, queries, new_key
 ):
     row_count, width = queries.shape
     heads = width // HEAD_DIM
@@ -265,10 +265,10 @@
             jax.ShapeDtypeStruct((HELD, capacity, routes.shape[1]), jnp.float32),
             jax.ShapeDtypeStruct((capacity, HEAD_DIM), jnp.float32),
         ],
-        [SMEM_SPEC] * 2 + [VMEM_SPEC] * 5,
+        [SMEM_SPEC] + [VMEM_SPEC] * 5,
         [table, table],
         queries.size * 8, queries.size * 16, 4,
-    )(place, cache_length, earlier, routes, route_weight, queries, new_key)
+    )(cache_length, earlier, routes, route_weight, queries, new_key)
 
 
 def score_kernel(spread_ref, own_ref, limit_ref, key_ref, probs_ref, own_probs_ref):
@@ -531,13 +531,12 @@
     count = lax.axis_size("attn")
     sharers = count // HELD
     capacity = routes.shape[0] * TOP // EXPERTS
-    place = lax.axis_index(("attn", "expert")).astype(jnp.int32).reshape(1)
-
-    earlier = order(place, routes.shape[0])
+
+    earlier = order(routes.shape[0])
     weights = (gate_weight.T, up_weight.T, down_weight)
     other_weights = [swap(block) for block in weights]
     spread, own, limit, taken, slots = prepare(
-        place, sharers, capacity, cache_length, earlier, routes.T, route_weight.T, queries, new_key
+        sharers, capacity, cache_length, earlier, routes.T, route_weight.T, queries, new_key
     )
     attended = exchange(
         attend(count, spread, own, limit, key_cache, value_cache, new_value, ln_gain)

time: 50.5 us -> 47.8 us (0.947)
  Pallas kernels: 9.44 us -> 7.24 us
  local copies, waits for them, and re-layouts: 0.9 us -> 0.34 us
    pallas_call x1, Pallas kernels: 5.3 us -> 3.08 us  [run_experts(): call(expert_kernel, jax.ShapeDtypeStruct(pieces.shape, jnp.bfloat16), [VM...]
    unnamed x30, local copies, waits for them, and re-layouts: 0.9 us -> 0.34 us
where the time goes in v15:
time: 47.8 us; the launch traced here: 47.6 us
  blocking collectives  35.5 us (74%)
  Pallas kernels  7.24 us (15%)
  waiting for transfers between devices  2.59 us (5%)
  starting transfers between devices  1.14 us (2%)
  between operations  0.8 us (2%)
    all_to_all x3, blocking collectives, exchange(): lax.all_to_all(blocks, 'attn', split_axis=0, concat_axis=0, tiled=True)  35.5 us
    pallas_call x1, Pallas kernels, run_experts(): call(expert_kernel, jax.ShapeDtypeStruct(pieces.shape, jnp.bfloat16), [VM...  3.08 us
    ppermute x5, waiting for transfers between devices, swap(): return lax.ppermute(block, 'expert', [(0, 1), (1, 0)])  2.59 us
    ppermute x5, starting transfers between devices, swap(): return lax.ppermute(block, 'expert', [(0, 1), (1, 0)])  1.14 us
    pallas_call x1, Pallas kernels, attend(): call(score_kernel, [jax.ShapeDtypeStruct((row_count, heads, length_max),...  1.03 us
  transfers between devices with their start and end apart: 5, of which 2 were waited for; matrix products, arithmetic and copies ran while one was open for 0% of the time, Pallas kernels for 7%

profile of v15, /device:TPU:0, one launch (start us, length us, event | category | flops | bytes accessed | tf_op | source)
XLA Modules:
  0.0 47.6 jit_solution(2183298300995111231)
XLA Ops:
  0.6 0.5 %collective-permute-start.1 = (bf16[168,6144]{1,0:T(8,128)(2,1)}, bf16[168,6144]{1,0:T(8,128)(2,1)S(1)}, u32[]{:S(2)}, u32[]{:S(2)}) collective-permute-start(bf16[168,6144]{1,0:T(8,128)(2,1)} %bitcast.4), channel_id=1, source_target_pairs={{0,1},{1,0},{2,3},{3,2},{4,5},{5,4},{6,7},{7,6},{8,9},{9,8},{10,11... | collective-permute-start | bytes 6193160 | tf_op jit(solution)/shard_map/ppermute | solution.py:512
  1.1 0.0 copy-start.5
  1.2 0.0 copy-start.6
  1.2 0.0 copy-start.7
  1.2 0.0 copy-start.8
  1.2 0.0 copy-start.9
  1.2 0.0 copy-start
  1.2 0.1 collective-permute-start.2
  1.3 0.5 collective-permute-start.3
  1.8 0.0 copy-start.10
  1.8 0.0 copy-start.12
  1.8 0.1 copy-done.5
  1.9 0.0 copy-done.6
  1.9 0.0 copy-done.7
  1.9 0.0 copy-done.8
  1.9 0.0 copy-done.9
  1.9 0.7 %shard_map.150 = (bf16[4,24,512]{2,1,0:T(8,128)(2,1)S(1)}, f32[4,24,128]{2,1,0:T(8,128)S(1)}, s32[4,24,128]{2,1,0:T(8,128)S(1)}, f32[2,8,32]{2,1,0:T(8,128)S(1)}, f32[8,128]{1,0:T(8,128)S(1)}) custom-call(s32[4]{0:T(128)S(1)} %copy-done.9, bf16[32,32]{1,0:T(8,128)(2,1)S(1)} %shard_map.149.earlier_ref, s32[4,32]{1,0:T(4,128)S(1)} %bitcast.8, ...), custom_call_target="tpu_custom_call" | custom-call | flops 98304 | bytes 196608 | tf_op jit(solution)/shard_map/pallas_call | solution.py:259
  2.6 0.2 copy-done
  2.8 1.0 %shard_map.151 = (bf16[4,24,512]{2,1,0:T(8,128)(2,1)S(1)}, f32[4,24,128]{2,1,0:T(8,128)S(1)}) custom-call(bf16[4,24,512]{2,1,0:T(8,128)(2,1)S(1)} %get-tuple-element.13.spread_ref, f32[4,24,128]{2,1,0:T(8,128)S(1)} %get-tuple-element.14.own_ref, s32[4,24,128]{2,1,0:T(8,128)S(1)} %get-tuple-element.15.limit_ref, bf16[4,512,512]{2,1,0:T(8,128)(2,1)S(1)} %copy-done), custom_call_target="tpu_custom_call" | custom-call | flops 50331648 | bytes 2097152 | tf_op jit(solution)/shard_map/pallas_call | solution.py:342
  3.9 0.0 copy-done.10
  3.9 0.0 copy-done.11
  3.9 0.0 copy-done.12
  3.9 0.0 slice-start.1
  3.9 0.5 %shard_map.152 = bf16[8,4,3456]{2,1,0:T(4,128)(2,1)S(1)} custom-call(bf16[4,24,512]{2,1,0:T(8,128)(2,1)S(1)} %get-tuple-element.16.probs_ref, f32[4,24,128]{2,1,0:T(8,128)S(1)} %get-tuple-element.17.own_ref, bf16[4,512,512]{2,1,0:T(8,128)(2,1)S(1)} %copy-done.10, bf16[4,512]{1,0:T(4,128)(2,1)S(1)} %copy-done.11, f32[768]{0:T(1024)S(1)} %copy-done.12), custom_call_target="tpu_custom_call" | custom-call | flops 10000000000 | bytes 2097152 | tf_op jit(solution)/shard_map/pallas_call | solution.py:353
  4.4 15.7 %all_to_all.15.pieces = bf16[8,4,3456]{2,1,0:T(4,128)(2,1)S(1)} all-to-all(bf16[8,4,3456]{2,1,0:T(4,128)(2,1)S(1)} %shard_map.152), channel_id=1, replica_groups=mesh['group'=2,'attn'=8,'expert'=2] {'attn'}, dimensions={0} | all-to-all | bytes 442368 | tf_op jit(solution)/shard_map/all_to_all | solution.py:508
  20.2 0.0 slice-done
  20.2 0.0 slice-done.1
  20.2 0.0 copy-start.1
  20.2 0.0 copy-start.2
  20.2 0.0 copy-start.3
  20.2 0.9 %shard_map.153 = (f32[32,768]{1,0:T(8,128)S(1)}, f32[8,768]{1,0:T(8,128)S(1)}) custom-call(bf16[8,4,3456]{2,1,0:T(4,128)(2,1)S(1)} %all_to_all.15.pieces, bf16[3072,768]{1,0:T(8,128)(2,1)S(1)} %bitcast.11), custom_call_target="tpu_custom_call" | custom-call | flops 10000000000 | bytes 4718592 | tf_op jit(solution)/shard_map/pallas_call | solution.py:379
  21.1 0.0 collective-permute-start
  21.2 1.3 %collective-permute-done.other_ref = f32[32,768]{1,0:T(8,128)S(1)} collective-permute-done((f32[32,768]{1,0:T(8,128)S(1)}, f32[32,768]{1,0:T(8,128)S(1)}, u32[]{:S(2)}, u32[]{:S(2)}) %collective-permute-start) | collective-permute-done | bytes 98336 | tf_op jit(solution)/shard_map/ppermute | solution.py:512
  22.5 0.0 copy-done.4
  22.5 0.1 shard_map.154
  22.6 10.2 %all_to_all.16.pieces = bf16[8,8,768]{2,1,0:T(8,128)(2,1)S(1)} all-to-all(bf16[8,8,768]{2,1,0:T(8,128)(2,1)S(1)} %get-tuple-element.22), channel_id=1, replica_groups=mesh['group'=2,'attn'=8,'expert'=2] {'attn'}, dimensions={0} | all-to-all | bytes 196608 | tf_op jit(solution)/shard_map/all_to_all | solution.py:508
  32.8 0.0 collective-permute-done.1.refs_3_
  32.8 0.0 collective-permute-done.2.refs_4_
  32.8 0.0 collective-permute-done.3.refs_5_
  32.8 0.0 copy-done.1
  32.9 0.0 copy-done.2
  32.9 0.0 copy-done.3
  32.9 3.1 %shard_map.155 = bf16[8,8,768]{2,1,0:T(8,128)(2,1)S(1)} custom-call(f32[8,128]{1,0:T(8,128)S(1)} %get-tuple-element.21.slot_ref, bf16[8,8,768]{2,1,0:T(8,128)(2,1)S(1)} %all_to_all.16.pieces, f32[8,768]{1,0:T(8,128)S(1)} %get-tuple-element.23.gains, bf16[168,6144]{1,0:T(8,128)(2,1)S(1)} %bitcast.5, bf16[168,6144]{1,0:T(8,128)(2,1)S(1)} %bitcast.7, ...), custom_call_target="tpu_custom_call" | custom-call | flops 99090432 | bytes 12386304 | tf_op jit(solution)/shard_map/pallas_call | solution.py:459
  36.0 9.5 %all_to_all.17.pieces = bf16[8,8,768]{2,1,0:T(8,128)(2,1)S(1)} all-to-all(bf16[8,8,768]{2,1,0:T(8,128)(2,1)S(1)} %shard_map.155), channel_id=1, replica_groups=mesh['group'=2,'attn'=8,'expert'=2] {'attn'}, dimensions={0} | all-to-all | bytes 196608 | tf_op jit(solution)/shard_map/all_to_all | solution.py:508
  45.5 0.2 shard_map.156.mine_ref
  45.6 0.0 collective-permute-start.4
  45.7 1.3 %collective-permute-done.4.other_ref = f32[32,768]{1,0:T(8,128)S(1)} collective-permute-done((f32[32,768]{1,0:T(8,128)S(1)}, f32[32,768]{1,0:T(8,128)S(1)}, u32[]{:S(2)}, u32[]{:S(2)}) %collective-permute-start.4) | collective-permute-done | bytes 98336 | tf_op jit(solution)/shard_map/ppermute | solution.py:512
  47.0 0.6 %shard_map.157 = (bf16[32,768]{1,0:T(8,128)(2,1)}, bf16[32,768]{1,0:T(8,128)(2,1)}) custom-call(bf16[32,768]{1,0:T(8,128)(2,1)S(1)} %get-tuple-element.20.stream_ref, f32[32,768]{1,0:T(8,128)S(1)} %shard_map.156.mine_ref, f32[32,768]{1,0:T(8,128)S(1)} %collective-permute-done.4.other_ref), custom_call_target="tpu_custom_call" | custom-call | flops 24576 | bytes 344064 | tf_op jit(solution)/shard_map/pallas_call | solution.py:498
  (5 shorter events, 0.0 us)
Async XLA Ops:
  0.6 32.2 %collective-permute-start.1 = (bf16[168,6144]{1,0:T(8,128)(2,1)}, bf16[168,6144]{1,0:T(8,128)(2,1)S(1)}, u32[]{:S(2)}, u32[]{:S(2)}) collective-permute-start(bf16[168,6144]{1,0:T(8,128)(2,1)} %bitcast.4), channel_id=1, source_target_pairs={{0,1},{1,0},{2,3},{3,2},{4,5},{5,4},{6,7},{7,6},{8,9},{9,8},{10,11... | collective-permute-start | bytes 6193160 | tf_op jit(solution)/shard_map/ppermute | solution.py:512
  1.1 0.7 %copy-start.5 = (bf16[4,3072]{1,0:T(4,128)(2,1)S(1)}, bf16[4,3072]{1,0:T(4,128)(2,1)}, u32[]{:S(2)}) copy-start(bf16[4,3072]{1,0:T(4,128)(2,1)} %query_ref.1) | copy-start | bytes 73732
  1.2 0.7 %copy-start.6 = (bf16[4,512]{1,0:T(4,128)(2,1)S(1)}, bf16[4,512]{1,0:T(4,128)(2,1)}, u32[]{:S(2)}) copy-start(bf16[4,512]{1,0:T(4,128)(2,1)} %own_key_ref.1) | copy-start | bytes 12292
  1.2 0.7 %copy-start.7 = (s32[32,4]{0,1:T(4,128)S(1)}, s32[32,4]{0,1:T(4,128)}, u32[]{:S(2)}) copy-start(s32[32,4]{0,1:T(4,128)} %param.26) | copy-start | bytes 1540
  1.2 0.7 %copy-start.8 = (f32[32,4]{0,1:T(4,128)S(1)}, f32[32,4]{0,1:T(4,128)}, u32[]{:S(2)}) copy-start(f32[32,4]{0,1:T(4,128)} %param.27) | copy-start | bytes 1540
  1.2 0.7 %copy-start.9 = (s32[4]{0:T(128)S(1)}, s32[4]{0:T(128)}, u32[]{:S(2)}) copy-start(s32[4]{0:T(128)} %length_ref.1) | copy-start | bytes 52
  1.2 1.7 %copy-start = (bf16[4,512,512]{2,1,0:T(8,128)(2,1)S(1)}, bf16[4,512,512]{2,1,0:T(8,128)(2,1)}, u32[]{:S(2)}) copy-start(bf16[4,512,512]{2,1,0:T(8,128)(2,1)} %key_ref.1) | copy-start | bytes 6291460
  1.2 31.7 %collective-permute-start.2 = (bf16[168,6144]{1,0:T(8,128)(2,1)}, bf16[168,6144]{1,0:T(8,128)(2,1)S(1)}, u32[]{:S(2)}, u32[]{:S(2)}) collective-permute-start(bf16[168,6144]{1,0:T(8,128)(2,1)} %bitcast.6), channel_id=1, source_target_pairs={{0,1},{1,0},{2,3},{3,2},{4,5},{5,4},{6,7},{7,6},{8,9},{9,8},{10,11... | collective-permute-start | bytes 6193160 | tf_op jit(solution)/shard_map/ppermute | solution.py:512
  1.3 31.5 %collective-permute-start.3 = (bf16[168,6144]{1,0:T(8,128)(2,1)}, bf16[168,6144]{1,0:T(8,128)(2,1)S(1)}, u32[]{:S(2)}, u32[]{:S(2)}) collective-permute-start(bf16[168,6144]{1,0:T(8,128)(2,1)} %refs_2_.1), channel_id=1, source_target_pairs={{0,1},{1,0},{2,3},{3,2},{4,5},{5,4},{6,7},{7,6},{8,9},{9,8},{10,11... | collective-permute-start | bytes 6193160 | tf_op jit(solution)/shard_map/ppermute | solution.py:512
  1.8 2.1 %copy-start.10 = (bf16[4,512,512]{2,1,0:T(8,128)(2,1)S(1)}, bf16[4,512,512]{2,1,0:T(8,128)(2,1)}, u32[]{:S(2)}) copy-start(bf16[4,512,512]{2,1,0:T(8,128)(2,1)} %value_ref.1) | copy-start | bytes 6291460
  1.8 2.1 %copy-start.11 = (bf16[4,512]{1,0:T(4,128)(2,1)S(1)}, bf16[4,512]{1,0:T(4,128)(2,1)}, u32[]{:S(2)}) copy-start(bf16[4,512]{1,0:T(4,128)(2,1)} %own_value_ref.1) | copy-start | bytes 12292
  1.8 2.1 %copy-start.12 = (f32[768]{0:T(1024)S(1)}, f32[768]{0:T(1024)}, u32[]{:S(2)}) copy-start(f32[768]{0:T(1024)} %gain_ref.1) | copy-start | bytes 9220
  2.8 17.4 %slice-start = ((s8[4718592]{0:T(1024)(128)(4,1)}), s8[524288]{0:T(1024)(128)(4,1)S(1)}, s32[]{:S(2)}) async-start(s8[4718592]{0:T(1024)(128)(4,1)} %bitcast.10), calls=%async_computation.3 | async-start | bytes 1048576
  3.9 16.3 %slice-start.1 = ((s8[4718592]{0:T(1024)(128)(4,1)}), s8[4194304]{0:T(1024)(128)(4,1)S(1)}, s32[]{:S(2)}) async-start(s8[4718592]{0:T(1024)(128)(4,1)} %bitcast.10), calls=%async_computation.4 | async-start | bytes 8388608
  20.2 2.3 %copy-start.4 = (bf16[32,768]{1,0:T(8,128)(2,1)S(1)}, bf16[32,768]{1,0:T(8,128)(2,1)}, u32[]{:S(2)}) copy-start(bf16[32,768]{1,0:T(8,128)(2,1)} %residual_ref.1) | copy-start | bytes 147460
  20.2 12.7 %copy-start.1 = (bf16[6144,168]{0,1:T(8,128)(2,1)S(1)}, bf16[6144,168]{0,1:T(8,128)(2,1)}, u32[]{:S(2)}) copy-start(bf16[6144,168]{0,1:T(8,128)(2,1)} %param.23) | copy-start | bytes 6193156
  20.2 12.7 %copy-start.2 = (bf16[6144,168]{0,1:T(8,128)(2,1)S(1)}, bf16[6144,168]{0,1:T(8,128)(2,1)}, u32[]{:S(2)}) copy-start(bf16[6144,168]{0,1:T(8,128)(2,1)} %param.24) | copy-start | bytes 6193156
  20.2 12.7 %copy-start.3 = (bf16[168,6144]{1,0:T(8,128)(2,1)S(1)}, bf16[168,6144]{1,0:T(8,128)(2,1)}, u32[]{:S(2)}) copy-start(bf16[168,6144]{1,0:T(8,128)(2,1)} %refs_2_.1) | copy-start | bytes 6193156
  21.1 1.3 %collective-permute-start = (f32[32,768]{1,0:T(8,128)S(1)}, f32[32,768]{1,0:T(8,128)S(1)}, u32[]{:S(2)}, u32[]{:S(2)}) collective-permute-start(f32[32,768]{1,0:T(8,128)S(1)} %get-tuple-element.18.mine_ref), channel_id=1, source_target_pairs={{0,1},{1,0},{2,3},{3,2},{4,5},{5,4},{6,7},{7,6},{8,9},{9,8},{10,11... | collective-permute-start | bytes 294920 | tf_op jit(solution)/shard_map/ppermute | solution.py:512
  45.6 1.3 %collective-permute-start.4 = (f32[32,768]{1,0:T(8,128)S(1)}, f32[32,768]{1,0:T(8,128)S(1)}, u32[]{:S(2)}, u32[]{:S(2)}) collective-permute-start(f32[32,768]{1,0:T(8,128)S(1)} %shard_map.156.mine_ref), channel_id=1, source_target_pairs={{0,1},{1,0},{2,3},{3,2},{4,5},{5,4},{6,7},{7,6},{8,9},{9,8},{10,11... | collective-permute-start | bytes 294920 | tf_op jit(solution)/shard_map/ppermute | solution.py:512

commit v16 on v15

--- a/solution.py
+++ b/solution.py
@@ -221,13 +221,14 @@
             ].astype(jnp.float32)
             key_rows[rows, :] = own_key
     scale = 1.0 / math.sqrt(HEAD_DIM)
+    lengths = length_ref[...].reshape(1, -1)
     head = lax.broadcasted_iota(jnp.int32, (heads, 1), 0) // group
     for r in range(row_count):
         strided = pl.ds(r, heads, stride=row_count)
         query = query_rows[strided, :]
         own = jnp.sum(query * key_rows[strided, :], axis=1, keepdims=True) * scale
         own_ref[r] = jnp.broadcast_to(own, (heads, HEAD_DIM))
-        limit_ref[r] = jnp.full((heads, HEAD_DIM), length_ref[r], jnp.int32)
+        limit_ref[r] = jnp.broadcast_to(lengths[:, r : r + 1], (heads, HEAD_DIM))
         spread_ref[r] = jnp.concatenate(
             [jnp.where(head == g, query, 0.0) for g in range(kv_local)], axis=1
         ).astype(jnp.bfloat16)
@@ -265,7 +266,7 @@
             jax.ShapeDtypeStruct((HELD, capacity, routes.shape[1]), jnp.float32),
             jax.ShapeDtypeStruct((capacity, HEAD_DIM), jnp.float32),
         ],
-        [SMEM_SPEC] + [VMEM_SPEC] * 5,
+        [VMEM_SPEC] * 6,
         [table, table],
         queries.size * 8, queries.size * 16, 4,
     )(cache_length, earlier, routes, route_weight, queries, new_key)
@@ -418,7 +419,7 @@
 
 
 def expert_kernel(slot_ref, pieces, gains, *refs):
-    weights, out_ref = (refs[:3], refs[3:6]), refs[6]
+    weights, out_ref, rows_ref = (refs[:3], refs[3:6]), refs[6], refs[7]
     count, capacity, cols = pieces.shape
     first = second = 0.0
     for k in range(count):
@@ -428,23 +429,17 @@
     row_mean = jnp.sum(first, axis=1, keepdims=True) / D
     row_var = jnp.sum(second, axis=1, keepdims=True) / D - row_mean * row_mean
     inverse = lax.rsqrt(row_var + EPSILON)
+    for k in range(count):
+        wide = pieces[k].astype(jnp.float32)
+        normed = (wide - row_mean) * inverse * gains[pl.ds(k, 1), :]
+        rows_ref[:, k * cols : (k + 1) * cols] = normed.astype(jnp.bfloat16)
+    rows = rows_ref[...]
     contract = (((1,), (1,)), ((), ()))
-    gate_val, up_val = [0.0, 0.0], [0.0, 0.0]
-    for k in range(count):
-        block = slice(k * cols, (k + 1) * cols)
-        wide = pieces[k].astype(jnp.float32)
-        normed = ((wide - row_mean) * inverse * gains[pl.ds(k, 1), :]).astype(jnp.bfloat16)
-        for index, (gate_ref, up_ref, _) in enumerate(weights):
-            gate_val[index] = gate_val[index] + lax.dot_general(
-                normed, gate_ref[:, block], contract, preferred_element_type=jnp.float32
-            )
-            up_val[index] = up_val[index] + lax.dot_general(
-                normed, up_ref[:, block], contract, preferred_element_type=jnp.float32
-            )
-    hidden = [
-        (gate / (1.0 + jnp.exp(-gate)) * up).astype(jnp.bfloat16)
-        for gate, up in zip(gate_val, up_val)
-    ]
+    hidden = []
+    for gate_ref, up_ref, _ in weights:
+        gate = lax.dot_general(rows, gate_ref[...], contract, preferred_element_type=jnp.float32)
+        up = lax.dot_general(rows, up_ref[...], contract, preferred_element_type=jnp.float32)
+        hidden.append((gate / (1.0 + jnp.exp(-gate)) * up).astype(jnp.bfloat16))
     slot_weight = slot_ref[:, :1]
     for k in range(count):
         block = slice(k * cols, (k + 1) * cols)
@@ -456,12 +451,13 @@
 
 
 def run_experts(slots, pieces, gains, own, other):
+    count, capacity, cols = pieces.shape
     return call(
         expert_kernel,
         jax.ShapeDtypeStruct(pieces.shape, jnp.bfloat16),
         [VMEM_SPEC] * 9,
-        [],
-        12 * pieces.shape[1] * own[0].size, own[0].size * 12, 20,
+        [pltpu.VMEM((capacity, count * cols), jnp.bfloat16)],
+        12 * capacity * own[0].size, own[0].size * 12, 20,
     )(slots, pieces, gains, *own, *other)
 
 
@@ -534,10 +530,10 @@
 
     earlier = order(routes.shape[0])
     weights = (gate_weight.T, up_weight.T, down_weight)
-    other_weights = [swap(block) for block in weights]
     spread, own, limit, taken, slots = prepare(
         sharers, capacity, cache_length, earlier, routes.T, route_weight.T, queries, new_key
     )
+    other_weights = [swap(block) for block in weights]
     attended = exchange(
         attend(count, spread, own, limit, key_cache, value_cache, new_value, ln_gain)
     )

time: 47.8 us -> 47.8 us (level)
  Pallas kernels: 7.24 us -> 6.71 us
  local copies, waits for them, and re-layouts: 0.34 us -> 0.87 us
    pallas_call x1, Pallas kernels: 0.75 us -> 0.22 us  [prepare(): call(functools.partial(prepare_kernel, sharers), [jax.ShapeDtypeStruct((r...]
    unnamed x30, local copies, waits for them, and re-layouts: 0.34 us -> 0.87 us
  transfers between devices with their start and end apart: 5 -> 5, of which waited for: 2 -> 2; matrix products, arithmetic and copies ran while one was open for 0% -> 0% of each run, Pallas kernels for 7% -> 6%
where the time goes in v16:
time: 47.8 us; the launch traced here: 47.6 us
  blocking collectives  35.5 us (74%)
  Pallas kernels  6.71 us (14%)
  waiting for transfers between devices  2.59 us (5%)
  starting transfers between devices  1.14 us (2%)
  local copies, waits for them, and re-layouts  0.87 us (2%)
  between operations  0.8 us (2%)
    all_to_all x3, blocking collectives, exchange(): lax.all_to_all(blocks, 'attn', split_axis=0, concat_axis=0, tiled=True)  35.5 us
    pallas_call x1, Pallas kernels, run_experts(): call(expert_kernel, jax.ShapeDtypeStruct(pieces.shape, jnp.bfloat16), [VM...  3.08 us
    ppermute x5, waiting for transfers between devices, swap(): return lax.ppermute(block, 'expert', [(0, 1), (1, 0)])  2.59 us
    ppermute x5, starting transfers between devices, swap(): return lax.ppermute(block, 'expert', [(0, 1), (1, 0)])  1.14 us
    pallas_call x1, Pallas kernels, attend(): call(score_kernel, [jax.ShapeDtypeStruct((row_count, heads, length_max),...  1.03 us
  transfers between devices with their start and end apart: 5, of which 2 were waited for; matrix products, arithmetic and copies ran while one was open for 0% of the time, Pallas kernels for 6%

profile of v16, /device:TPU:0, one launch (start us, length us, event | category | flops | bytes accessed | tf_op | source)
XLA Modules:
  0.0 47.6 jit_solution(1874661908637488576)
XLA Ops:
  0.6 0.5 %collective-permute-start.1 = (bf16[168,6144]{1,0:T(8,128)(2,1)}, bf16[168,6144]{1,0:T(8,128)(2,1)S(1)}, u32[]{:S(2)}, u32[]{:S(2)}) collective-permute-start(bf16[168,6144]{1,0:T(8,128)(2,1)} %bitcast.4), channel_id=1, source_target_pairs={{0,1},{1,0},{2,3},{3,2},{4,5},{5,4},{6,7},{7,6},{8,9},{9,8},{10,11... | collective-permute-start | bytes 6193160 | tf_op jit(solution)/shard_map/ppermute | solution.py:508
  1.1 0.0 copy-start.5
  1.2 0.0 copy-start.6
  1.2 0.0 copy-start.7
  1.2 0.0 copy-start.8
  1.2 0.0 copy-start.9
  1.2 0.0 copy-start
  1.2 0.1 collective-permute-start.2
  1.3 0.5 collective-permute-start.3
  1.8 0.0 copy-start.10
  1.8 0.0 copy-start.12
  1.8 0.1 copy-done.5
  1.9 0.0 copy-done.6
  1.9 0.0 copy-done.7
  1.9 0.0 copy-done.8
  1.9 0.0 copy-done.9
  1.9 0.2 shard_map.150
  2.1 0.7 %copy-done = bf16[4,512,512]{2,1,0:T(8,128)(2,1)S(1)} copy-done((bf16[4,512,512]{2,1,0:T(8,128)(2,1)S(1)}, bf16[4,512,512]{2,1,0:T(8,128)(2,1)}, u32[]{:S(2)}) %copy-start) | copy-done | bytes 2097176
  2.8 1.0 %shard_map.151 = (bf16[4,24,512]{2,1,0:T(8,128)(2,1)S(1)}, f32[4,24,128]{2,1,0:T(8,128)S(1)}) custom-call(bf16[4,24,512]{2,1,0:T(8,128)(2,1)S(1)} %get-tuple-element.13.spread_ref, f32[4,24,128]{2,1,0:T(8,128)S(1)} %get-tuple-element.14.own_ref, s32[4,24,128]{2,1,0:T(8,128)S(1)} %get-tuple-element.15.limit_ref, bf16[4,512,512]{2,1,0:T(8,128)(2,1)S(1)} %copy-done), custom_call_target="tpu_custom_call" | custom-call | flops 50331648 | bytes 2097152 | tf_op jit(solution)/shard_map/pallas_call | solution.py:343
  3.9 0.0 copy-done.10
  3.9 0.0 copy-done.11
  3.9 0.0 copy-done.12
  3.9 0.0 slice-start.1
  3.9 0.5 %shard_map.152 = bf16[8,4,3456]{2,1,0:T(4,128)(2,1)S(1)} custom-call(bf16[4,24,512]{2,1,0:T(8,128)(2,1)S(1)} %get-tuple-element.16.probs_ref, f32[4,24,128]{2,1,0:T(8,128)S(1)} %get-tuple-element.17.own_ref, bf16[4,512,512]{2,1,0:T(8,128)(2,1)S(1)} %copy-done.10, bf16[4,512]{1,0:T(4,128)(2,1)S(1)} %copy-done.11, f32[768]{0:T(1024)S(1)} %copy-done.12), custom_call_target="tpu_custom_call" | custom-call | flops 10000000000 | bytes 2097152 | tf_op jit(solution)/shard_map/pallas_call | solution.py:354
  4.4 15.7 %all_to_all.15.pieces = bf16[8,4,3456]{2,1,0:T(4,128)(2,1)S(1)} all-to-all(bf16[8,4,3456]{2,1,0:T(4,128)(2,1)S(1)} %shard_map.152), channel_id=1, replica_groups=mesh['group'=2,'attn'=8,'expert'=2] {'attn'}, dimensions={0} | all-to-all | bytes 442368 | tf_op jit(solution)/shard_map/all_to_all | solution.py:504
  20.2 0.0 slice-done
  20.2 0.0 slice-done.1
  20.2 0.0 copy-start.1
  20.2 0.0 copy-start.2
  20.2 0.0 copy-start.3
  20.2 0.9 %shard_map.153 = (f32[32,768]{1,0:T(8,128)S(1)}, f32[8,768]{1,0:T(8,128)S(1)}) custom-call(bf16[8,4,3456]{2,1,0:T(4,128)(2,1)S(1)} %all_to_all.15.pieces, bf16[3072,768]{1,0:T(8,128)(2,1)S(1)} %bitcast.11), custom_call_target="tpu_custom_call" | custom-call | flops 10000000000 | bytes 4718592 | tf_op jit(solution)/shard_map/pallas_call | solution.py:380
  21.1 0.0 collective-permute-start
  21.2 1.3 %collective-permute-done.other_ref = f32[32,768]{1,0:T(8,128)S(1)} collective-permute-done((f32[32,768]{1,0:T(8,128)S(1)}, f32[32,768]{1,0:T(8,128)S(1)}, u32[]{:S(2)}, u32[]{:S(2)}) %collective-permute-start) | collective-permute-done | bytes 98336 | tf_op jit(solution)/shard_map/ppermute | solution.py:508
  22.5 0.0 copy-done.4
  22.5 0.1 shard_map.154
  22.6 10.2 %all_to_all.16.pieces = bf16[8,8,768]{2,1,0:T(8,128)(2,1)S(1)} all-to-all(bf16[8,8,768]{2,1,0:T(8,128)(2,1)S(1)} %get-tuple-element.22), channel_id=1, replica_groups=mesh['group'=2,'attn'=8,'expert'=2] {'attn'}, dimensions={0} | all-to-all | bytes 196608 | tf_op jit(solution)/shard_map/all_to_all | solution.py:504
  32.8 0.0 collective-permute-done.1.refs_3_
  32.8 0.0 collective-permute-done.2.refs_4_
  32.8 0.0 collective-permute-done.3.refs_5_
  32.8 0.0 copy-done.1
  32.9 0.0 copy-done.2
  32.9 0.0 copy-done.3
  32.9 3.1 %shard_map.155 = bf16[8,8,768]{2,1,0:T(8,128)(2,1)S(1)} custom-call(f32[8,128]{1,0:T(8,128)S(1)} %get-tuple-element.21.slot_ref, bf16[8,8,768]{2,1,0:T(8,128)(2,1)S(1)} %all_to_all.16.pieces, f32[8,768]{1,0:T(8,128)S(1)} %get-tuple-element.23.gains, bf16[168,6144]{1,0:T(8,128)(2,1)S(1)} %bitcast.5, bf16[168,6144]{1,0:T(8,128)(2,1)S(1)} %bitcast.7, ...), custom_call_target="tpu_custom_call" | custom-call | flops 99090432 | bytes 12386304 | tf_op jit(solution)/shard_map/pallas_call | solution.py:455
  36.0 9.5 %all_to_all.17.pieces = bf16[8,8,768]{2,1,0:T(8,128)(2,1)S(1)} all-to-all(bf16[8,8,768]{2,1,0:T(8,128)(2,1)S(1)} %shard_map.155), channel_id=1, replica_groups=mesh['group'=2,'attn'=8,'expert'=2] {'attn'}, dimensions={0} | all-to-all | bytes 196608 | tf_op jit(solution)/shard_map/all_to_all | solution.py:504
  45.5 0.2 shard_map.156.mine_ref
  45.6 0.0 collective-permute-start.4
  45.7 1.3 %collective-permute-done.4.other_ref = f32[32,768]{1,0:T(8,128)S(1)} collective-permute-done((f32[32,768]{1,0:T(8,128)S(1)}, f32[32,768]{1,0:T(8,128)S(1)}, u32[]{:S(2)}, u32[]{:S(2)}) %collective-permute-start.4) | collective-permute-done | bytes 98336 | tf_op jit(solution)/shard_map/ppermute | solution.py:508
  47.0 0.6 %shard_map.157 = (bf16[32,768]{1,0:T(8,128)(2,1)}, bf16[32,768]{1,0:T(8,128)(2,1)}) custom-call(bf16[32,768]{1,0:T(8,128)(2,1)S(1)} %get-tuple-element.20.stream_ref, f32[32,768]{1,0:T(8,128)S(1)} %shard_map.156.mine_ref, f32[32,768]{1,0:T(8,128)S(1)} %collective-permute-done.4.other_ref), custom_call_target="tpu_custom_call" | custom-call | flops 24576 | bytes 344064 | tf_op jit(solution)/shard_map/pallas_call | solution.py:494
  (5 shorter events, 0.0 us)
Async XLA Ops:
  0.6 32.2 %collective-permute-start.1 = (bf16[168,6144]{1,0:T(8,128)(2,1)}, bf16[168,6144]{1,0:T(8,128)(2,1)S(1)}, u32[]{:S(2)}, u32[]{:S(2)}) collective-permute-start(bf16[168,6144]{1,0:T(8,128)(2,1)} %bitcast.4), channel_id=1, source_target_pairs={{0,1},{1,0},{2,3},{3,2},{4,5},{5,4},{6,7},{7,6},{8,9},{9,8},{10,11... | collective-permute-start | bytes 6193160 | tf_op jit(solution)/shard_map/ppermute | solution.py:508
  1.1 0.7 %copy-start.5 = (bf16[4,3072]{1,0:T(4,128)(2,1)S(1)}, bf16[4,3072]{1,0:T(4,128)(2,1)}, u32[]{:S(2)}) copy-start(bf16[4,3072]{1,0:T(4,128)(2,1)} %query_ref.1) | copy-start | bytes 73732
  1.2 0.7 %copy-start.6 = (bf16[4,512]{1,0:T(4,128)(2,1)S(1)}, bf16[4,512]{1,0:T(4,128)(2,1)}, u32[]{:S(2)}) copy-start(bf16[4,512]{1,0:T(4,128)(2,1)} %own_key_ref.1) | copy-start | bytes 12292
  1.2 0.7 %copy-start.7 = (s32[32,4]{0,1:T(4,128)S(1)}, s32[32,4]{0,1:T(4,128)}, u32[]{:S(2)}) copy-start(s32[32,4]{0,1:T(4,128)} %param.26) | copy-start | bytes 1540
  1.2 0.7 %copy-start.8 = (f32[32,4]{0,1:T(4,128)S(1)}, f32[32,4]{0,1:T(4,128)}, u32[]{:S(2)}) copy-start(f32[32,4]{0,1:T(4,128)} %param.27) | copy-start | bytes 1540
  1.2 0.7 %copy-start.9 = (s32[4]{0:T(128)S(1)}, s32[4]{0:T(128)}, u32[]{:S(2)}) copy-start(s32[4]{0:T(128)} %length_ref.1) | copy-start | bytes 52
  1.2 1.7 %copy-start = (bf16[4,512,512]{2,1,0:T(8,128)(2,1)S(1)}, bf16[4,512,512]{2,1,0:T(8,128)(2,1)}, u32[]{:S(2)}) copy-start(bf16[4,512,512]{2,1,0:T(8,128)(2,1)} %key_ref.1) | copy-start | bytes 6291460
  1.2 31.7 %collective-permute-start.2 = (bf16[168,6144]{1,0:T(8,128)(2,1)}, bf16[168,6144]{1,0:T(8,128)(2,1)S(1)}, u32[]{:S(2)}, u32[]{:S(2)}) collective-permute-start(bf16[168,6144]{1,0:T(8,128)(2,1)} %bitcast.6), channel_id=1, source_target_pairs={{0,1},{1,0},{2,3},{3,2},{4,5},{5,4},{6,7},{7,6},{8,9},{9,8},{10,11... | collective-permute-start | bytes 6193160 | tf_op jit(solution)/shard_map/ppermute | solution.py:508
  1.3 31.5 %collective-permute-start.3 = (bf16[168,6144]{1,0:T(8,128)(2,1)}, bf16[168,6144]{1,0:T(8,128)(2,1)S(1)}, u32[]{:S(2)}, u32[]{:S(2)}) collective-permute-start(bf16[168,6144]{1,0:T(8,128)(2,1)} %refs_2_.1), channel_id=1, source_target_pairs={{0,1},{1,0},{2,3},{3,2},{4,5},{5,4},{6,7},{7,6},{8,9},{9,8},{10,11... | collective-permute-start | bytes 6193160 | tf_op jit(solution)/shard_map/ppermute | solution.py:508
  1.8 2.1 %copy-start.10 = (bf16[4,512,512]{2,1,0:T(8,128)(2,1)S(1)}, bf16[4,512,512]{2,1,0:T(8,128)(2,1)}, u32[]{:S(2)}) copy-start(bf16[4,512,512]{2,1,0:T(8,128)(2,1)} %value_ref.1) | copy-start | bytes 6291460
  1.8 2.1 %copy-start.11 = (bf16[4,512]{1,0:T(4,128)(2,1)S(1)}, bf16[4,512]{1,0:T(4,128)(2,1)}, u32[]{:S(2)}) copy-start(bf16[4,512]{1,0:T(4,128)(2,1)} %own_value_ref.1) | copy-start | bytes 12292
  1.8 2.1 %copy-start.12 = (f32[768]{0:T(1024)S(1)}, f32[768]{0:T(1024)}, u32[]{:S(2)}) copy-start(f32[768]{0:T(1024)} %gain_ref.1) | copy-start | bytes 9220
  2.8 17.4 %slice-start = ((s8[4718592]{0:T(1024)(128)(4,1)}), s8[524288]{0:T(1024)(128)(4,1)S(1)}, s32[]{:S(2)}) async-start(s8[4718592]{0:T(1024)(128)(4,1)} %bitcast.10), calls=%async_computation.3 | async-start | bytes 1048576
  3.9 16.3 %slice-start.1 = ((s8[4718592]{0:T(1024)(128)(4,1)}), s8[4194304]{0:T(1024)(128)(4,1)S(1)}, s32[]{:S(2)}) async-start(s8[4718592]{0:T(1024)(128)(4,1)} %bitcast.10), calls=%async_computation.4 | async-start | bytes 8388608
  20.2 2.3 %copy-start.4 = (bf16[32,768]{1,0:T(8,128)(2,1)S(1)}, bf16[32,768]{1,0:T(8,128)(2,1)}, u32[]{:S(2)}) copy-start(bf16[32,768]{1,0:T(8,128)(2,1)} %residual_ref.1) | copy-start | bytes 147460
  20.2 12.7 %copy-start.1 = (bf16[6144,168]{0,1:T(8,128)(2,1)S(1)}, bf16[6144,168]{0,1:T(8,128)(2,1)}, u32[]{:S(2)}) copy-start(bf16[6144,168]{0,1:T(8,128)(2,1)} %param.23) | copy-start | bytes 6193156
  20.2 12.7 %copy-start.2 = (bf16[6144,168]{0,1:T(8,128)(2,1)S(1)}, bf16[6144,168]{0,1:T(8,128)(2,1)}, u32[]{:S(2)}) copy-start(bf16[6144,168]{0,1:T(8,128)(2,1)} %param.24) | copy-start | bytes 6193156
  20.2 12.7 %copy-start.3 = (bf16[168,6144]{1,0:T(8,128)(2,1)S(1)}, bf16[168,6144]{1,0:T(8,128)(2,1)}, u32[]{:S(2)}) copy-start(bf16[168,6144]{1,0:T(8,128)(2,1)} %refs_2_.1) | copy-start | bytes 6193156
  21.1 1.3 %collective-permute-start = (f32[32,768]{1,0:T(8,128)S(1)}, f32[32,768]{1,0:T(8,128)S(1)}, u32[]{:S(2)}, u32[]{:S(2)}) collective-permute-start(f32[32,768]{1,0:T(8,128)S(1)} %get-tuple-element.18.mine_ref), channel_id=1, source_target_pairs={{0,1},{1,0},{2,3},{3,2},{4,5},{5,4},{6,7},{7,6},{8,9},{9,8},{10,11... | collective-permute-start | bytes 294920 | tf_op jit(solution)/shard_map/ppermute | solution.py:508
  45.6 1.3 %collective-permute-start.4 = (f32[32,768]{1,0:T(8,128)S(1)}, f32[32,768]{1,0:T(8,128)S(1)}, u32[]{:S(2)}, u32[]{:S(2)}) collective-permute-start(f32[32,768]{1,0:T(8,128)S(1)} %shard_map.156.mine_ref), channel_id=1, source_target_pairs={{0,1},{1,0},{2,3},{3,2},{4,5},{5,4},{6,7},{7,6},{8,9},{9,8},{10,11... | collective-permute-start | bytes 294920 | tf_op jit(solution)/shard_map/ppermute | solution.py:508

commit v17 on v16

--- a/solution.py
+++ b/solution.py
@@ -438,7 +438,7 @@
     hidden = []
     for gate_ref, up_ref, _ in weights:
         gate = lax.dot_general(rows, gate_ref[...], contract, preferred_element_type=jnp.float32)
-        up = lax.dot_general(rows, up_ref[...], contract, preferred_element_type=jnp.float32)
+        up = lax.dot_general(up_ref[...], rows, contract, preferred_element_type=jnp.float32).T
         hidden.append((gate / (1.0 + jnp.exp(-gate)) * up).astype(jnp.bfloat16))
     slot_weight = slot_ref[:, :1]
     for k in range(count):

time: 47.8 us -> 47.9 us (level)
  no operation moved by 1% of the time
where the time goes in v17:
time: 47.9 us; the launch traced here: 47.7 us
  blocking collectives  35.5 us (74%)
  Pallas kernels  6.79 us (14%)
  waiting for transfers between devices  2.59 us (5%)
  starting transfers between devices  1.14 us (2%)
  local copies, waits for them, and re-layouts  0.87 us (2%)
  between operations  0.8 us (2%)
    all_to_all x3, blocking collectives, exchange(): lax.all_to_all(blocks, 'attn', split_axis=0, concat_axis=0, tiled=True)  35.5 us
    pallas_call x1, Pallas kernels, run_experts(): call(expert_kernel, jax.ShapeDtypeStruct(pieces.shape, jnp.bfloat16), [VM...  3.16 us
    ppermute x5, waiting for transfers between devices, swap(): return lax.ppermute(block, 'expert', [(0, 1), (1, 0)])  2.59 us
    ppermute x5, starting transfers between devices, swap(): return lax.ppermute(block, 'expert', [(0, 1), (1, 0)])  1.14 us
    pallas_call x1, Pallas kernels, attend(): call(score_kernel, [jax.ShapeDtypeStruct((row_count, heads, length_max),...  1.03 us
  transfers between devices with their start and end apart: 5, of which 2 were waited for; matrix products, arithmetic and copies ran while one was open for 0% of the time, Pallas kernels for 6%

profile of v17, /device:TPU:0, one launch (start us, length us, event | category | flops | bytes accessed | tf_op | source)
XLA Modules:
  0.0 47.7 jit_solution(7249264469268705666)
XLA Ops:
  0.6 0.5 %collective-permute-start.1 = (bf16[168,6144]{1,0:T(8,128)(2,1)}, bf16[168,6144]{1,0:T(8,128)(2,1)S(1)}, u32[]{:S(2)}, u32[]{:S(2)}) collective-permute-start(bf16[168,6144]{1,0:T(8,128)(2,1)} %bitcast.4), channel_id=1, source_target_pairs={{0,1},{1,0},{2,3},{3,2},{4,5},{5,4},{6,7},{7,6},{8,9},{9,8},{10,11... | collective-permute-start | bytes 6193160 | tf_op jit(solution)/shard_map/ppermute | solution.py:508
  1.1 0.0 copy-start.5
  1.2 0.0 copy-start.6
  1.2 0.0 copy-start.7
  1.2 0.0 copy-start.8
  1.2 0.0 copy-start.9
  1.2 0.0 copy-start
  1.2 0.1 collective-permute-start.2
  1.3 0.5 collective-permute-start.3
  1.8 0.0 copy-start.10
  1.8 0.0 copy-start.12
  1.8 0.1 copy-done.5
  1.9 0.0 copy-done.6
  1.9 0.0 copy-done.7
  1.9 0.0 copy-done.8
  1.9 0.0 copy-done.9
  1.9 0.2 shard_map.150
  2.1 0.7 %copy-done = bf16[4,512,512]{2,1,0:T(8,128)(2,1)S(1)} copy-done((bf16[4,512,512]{2,1,0:T(8,128)(2,1)S(1)}, bf16[4,512,512]{2,1,0:T(8,128)(2,1)}, u32[]{:S(2)}) %copy-start) | copy-done | bytes 2097176
  2.8 1.0 %shard_map.151 = (bf16[4,24,512]{2,1,0:T(8,128)(2,1)S(1)}, f32[4,24,128]{2,1,0:T(8,128)S(1)}) custom-call(bf16[4,24,512]{2,1,0:T(8,128)(2,1)S(1)} %get-tuple-element.13.spread_ref, f32[4,24,128]{2,1,0:T(8,128)S(1)} %get-tuple-element.14.own_ref, s32[4,24,128]{2,1,0:T(8,128)S(1)} %get-tuple-element.15.limit_ref, bf16[4,512,512]{2,1,0:T(8,128)(2,1)S(1)} %copy-done), custom_call_target="tpu_custom_call" | custom-call | flops 50331648 | bytes 2097152 | tf_op jit(solution)/shard_map/pallas_call | solution.py:343
  3.9 0.0 copy-done.10
  3.9 0.0 copy-done.11
  3.9 0.0 copy-done.12
  3.9 0.0 slice-start.1
  3.9 0.5 %shard_map.152 = bf16[8,4,3456]{2,1,0:T(4,128)(2,1)S(1)} custom-call(bf16[4,24,512]{2,1,0:T(8,128)(2,1)S(1)} %get-tuple-element.16.probs_ref, f32[4,24,128]{2,1,0:T(8,128)S(1)} %get-tuple-element.17.own_ref, bf16[4,512,512]{2,1,0:T(8,128)(2,1)S(1)} %copy-done.10, bf16[4,512]{1,0:T(4,128)(2,1)S(1)} %copy-done.11, f32[768]{0:T(1024)S(1)} %copy-done.12), custom_call_target="tpu_custom_call" | custom-call | flops 10000000000 | bytes 2097152 | tf_op jit(solution)/shard_map/pallas_call | solution.py:354
  4.4 15.7 %all_to_all.15.pieces = bf16[8,4,3456]{2,1,0:T(4,128)(2,1)S(1)} all-to-all(bf16[8,4,3456]{2,1,0:T(4,128)(2,1)S(1)} %shard_map.152), channel_id=1, replica_groups=mesh['group'=2,'attn'=8,'expert'=2] {'attn'}, dimensions={0} | all-to-all | bytes 442368 | tf_op jit(solution)/shard_map/all_to_all | solution.py:504
  20.2 0.0 slice-done
  20.2 0.0 slice-done.1
  20.2 0.0 copy-start.1
  20.2 0.0 copy-start.2
  20.2 0.0 copy-start.3
  20.2 0.9 %shard_map.153 = (f32[32,768]{1,0:T(8,128)S(1)}, f32[8,768]{1,0:T(8,128)S(1)}) custom-call(bf16[8,4,3456]{2,1,0:T(4,128)(2,1)S(1)} %all_to_all.15.pieces, bf16[3072,768]{1,0:T(8,128)(2,1)S(1)} %bitcast.11), custom_call_target="tpu_custom_call" | custom-call | flops 10000000000 | bytes 4718592 | tf_op jit(solution)/shard_map/pallas_call | solution.py:380
  21.1 0.0 collective-permute-start
  21.2 1.3 %collective-permute-done.other_ref = f32[32,768]{1,0:T(8,128)S(1)} collective-permute-done((f32[32,768]{1,0:T(8,128)S(1)}, f32[32,768]{1,0:T(8,128)S(1)}, u32[]{:S(2)}, u32[]{:S(2)}) %collective-permute-start) | collective-permute-done | bytes 98336 | tf_op jit(solution)/shard_map/ppermute | solution.py:508
  22.5 0.0 copy-done.4
  22.5 0.1 shard_map.154
  22.6 10.2 %all_to_all.16.pieces = bf16[8,8,768]{2,1,0:T(8,128)(2,1)S(1)} all-to-all(bf16[8,8,768]{2,1,0:T(8,128)(2,1)S(1)} %get-tuple-element.22), channel_id=1, replica_groups=mesh['group'=2,'attn'=8,'expert'=2] {'attn'}, dimensions={0} | all-to-all | bytes 196608 | tf_op jit(solution)/shard_map/all_to_all | solution.py:504
  32.8 0.0 collective-permute-done.1.refs_3_
  32.8 0.0 collective-permute-done.2.refs_4_
  32.8 0.0 collective-permute-done.3.refs_5_
  32.8 0.0 copy-done.1
  32.9 0.0 copy-done.2
  32.9 0.0 copy-done.3
  32.9 3.2 %shard_map.155 = bf16[8,8,768]{2,1,0:T(8,128)(2,1)S(1)} custom-call(f32[8,128]{1,0:T(8,128)S(1)} %get-tuple-element.21.slot_ref, bf16[8,8,768]{2,1,0:T(8,128)(2,1)S(1)} %all_to_all.16.pieces, f32[8,768]{1,0:T(8,128)S(1)} %get-tuple-element.23.gains, bf16[168,6144]{1,0:T(8,128)(2,1)S(1)} %bitcast.5, bf16[168,6144]{1,0:T(8,128)(2,1)S(1)} %bitcast.7, ...), custom_call_target="tpu_custom_call" | custom-call | flops 99090432 | bytes 12386304 | tf_op jit(solution)/shard_map/pallas_call | solution.py:455
  36.0 9.5 %all_to_all.17.pieces = bf16[8,8,768]{2,1,0:T(8,128)(2,1)S(1)} all-to-all(bf16[8,8,768]{2,1,0:T(8,128)(2,1)S(1)} %shard_map.155), channel_id=1, replica_groups=mesh['group'=2,'attn'=8,'expert'=2] {'attn'}, dimensions={0} | all-to-all | bytes 196608 | tf_op jit(solution)/shard_map/all_to_all | solution.py:504
  45.5 0.2 shard_map.156.mine_ref
  45.7 0.0 collective-permute-start.4
  45.7 1.3 %collective-permute-done.4.other_ref = f32[32,768]{1,0:T(8,128)S(1)} collective-permute-done((f32[32,768]{1,0:T(8,128)S(1)}, f32[32,768]{1,0:T(8,128)S(1)}, u32[]{:S(2)}, u32[]{:S(2)}) %collective-permute-start.4) | collective-permute-done | bytes 98336 | tf_op jit(solution)/shard_map/ppermute | solution.py:508
  47.0 0.6 %shard_map.157 = (bf16[32,768]{1,0:T(8,128)(2,1)}, bf16[32,768]{1,0:T(8,128)(2,1)}) custom-call(bf16[32,768]{1,0:T(8,128)(2,1)S(1)} %get-tuple-element.20.stream_ref, f32[32,768]{1,0:T(8,128)S(1)} %shard_map.156.mine_ref, f32[32,768]{1,0:T(8,128)S(1)} %collective-permute-done.4.other_ref), custom_call_target="tpu_custom_call" | custom-call | flops 24576 | bytes 344064 | tf_op jit(solution)/shard_map/pallas_call | solution.py:494
  (5 shorter events, 0.0 us)
Async XLA Ops:
  0.6 32.2 %collective-permute-start.1 = (bf16[168,6144]{1,0:T(8,128)(2,1)}, bf16[168,6144]{1,0:T(8,128)(2,1)S(1)}, u32[]{:S(2)}, u32[]{:S(2)}) collective-permute-start(bf16[168,6144]{1,0:T(8,128)(2,1)} %bitcast.4), channel_id=1, source_target_pairs={{0,1},{1,0},{2,3},{3,2},{4,5},{5,4},{6,7},{7,6},{8,9},{9,8},{10,11... | collective-permute-start | bytes 6193160 | tf_op jit(solution)/shard_map/ppermute | solution.py:508
  1.1 0.7 %copy-start.5 = (bf16[4,3072]{1,0:T(4,128)(2,1)S(1)}, bf16[4,3072]{1,0:T(4,128)(2,1)}, u32[]{:S(2)}) copy-start(bf16[4,3072]{1,0:T(4,128)(2,1)} %query_ref.1) | copy-start | bytes 73732
  1.2 0.7 %copy-start.6 = (bf16[4,512]{1,0:T(4,128)(2,1)S(1)}, bf16[4,512]{1,0:T(4,128)(2,1)}, u32[]{:S(2)}) copy-start(bf16[4,512]{1,0:T(4,128)(2,1)} %own_key_ref.1) | copy-start | bytes 12292
  1.2 0.7 %copy-start.7 = (s32[32,4]{0,1:T(4,128)S(1)}, s32[32,4]{0,1:T(4,128)}, u32[]{:S(2)}) copy-start(s32[32,4]{0,1:T(4,128)} %param.26) | copy-start | bytes 1540
  1.2 0.7 %copy-start.8 = (f32[32,4]{0,1:T(4,128)S(1)}, f32[32,4]{0,1:T(4,128)}, u32[]{:S(2)}) copy-start(f32[32,4]{0,1:T(4,128)} %param.27) | copy-start | bytes 1540
  1.2 0.7 %copy-start.9 = (s32[4]{0:T(128)S(1)}, s32[4]{0:T(128)}, u32[]{:S(2)}) copy-start(s32[4]{0:T(128)} %length_ref.1) | copy-start | bytes 52
  1.2 1.7 %copy-start = (bf16[4,512,512]{2,1,0:T(8,128)(2,1)S(1)}, bf16[4,512,512]{2,1,0:T(8,128)(2,1)}, u32[]{:S(2)}) copy-start(bf16[4,512,512]{2,1,0:T(8,128)(2,1)} %key_ref.1) | copy-start | bytes 6291460
  1.2 31.7 %collective-permute-start.2 = (bf16[168,6144]{1,0:T(8,128)(2,1)}, bf16[168,6144]{1,0:T(8,128)(2,1)S(1)}, u32[]{:S(2)}, u32[]{:S(2)}) collective-permute-start(bf16[168,6144]{1,0:T(8,128)(2,1)} %bitcast.6), channel_id=1, source_target_pairs={{0,1},{1,0},{2,3},{3,2},{4,5},{5,4},{6,7},{7,6},{8,9},{9,8},{10,11... | collective-permute-start | bytes 6193160 | tf_op jit(solution)/shard_map/ppermute | solution.py:508
  1.3 31.5 %collective-permute-start.3 = (bf16[168,6144]{1,0:T(8,128)(2,1)}, bf16[168,6144]{1,0:T(8,128)(2,1)S(1)}, u32[]{:S(2)}, u32[]{:S(2)}) collective-permute-start(bf16[168,6144]{1,0:T(8,128)(2,1)} %refs_2_.1), channel_id=1, source_target_pairs={{0,1},{1,0},{2,3},{3,2},{4,5},{5,4},{6,7},{7,6},{8,9},{9,8},{10,11... | collective-permute-start | bytes 6193160 | tf_op jit(solution)/shard_map/ppermute | solution.py:508
  1.8 2.1 %copy-start.10 = (bf16[4,512,512]{2,1,0:T(8,128)(2,1)S(1)}, bf16[4,512,512]{2,1,0:T(8,128)(2,1)}, u32[]{:S(2)}) copy-start(bf16[4,512,512]{2,1,0:T(8,128)(2,1)} %value_ref.1) | copy-start | bytes 6291460
  1.8 2.1 %copy-start.11 = (bf16[4,512]{1,0:T(4,128)(2,1)S(1)}, bf16[4,512]{1,0:T(4,128)(2,1)}, u32[]{:S(2)}) copy-start(bf16[4,512]{1,0:T(4,128)(2,1)} %own_value_ref.1) | copy-start | bytes 12292
  1.8 2.1 %copy-start.12 = (f32[768]{0:T(1024)S(1)}, f32[768]{0:T(1024)}, u32[]{:S(2)}) copy-start(f32[768]{0:T(1024)} %gain_ref.1) | copy-start | bytes 9220
  2.8 17.4 %slice-start = ((s8[4718592]{0:T(1024)(128)(4,1)}), s8[524288]{0:T(1024)(128)(4,1)S(1)}, s32[]{:S(2)}) async-start(s8[4718592]{0:T(1024)(128)(4,1)} %bitcast.10), calls=%async_computation.3 | async-start | bytes 1048576
  3.9 16.3 %slice-start.1 = ((s8[4718592]{0:T(1024)(128)(4,1)}), s8[4194304]{0:T(1024)(128)(4,1)S(1)}, s32[]{:S(2)}) async-start(s8[4718592]{0:T(1024)(128)(4,1)} %bitcast.10), calls=%async_computation.4 | async-start | bytes 8388608
  20.2 2.3 %copy-start.4 = (bf16[32,768]{1,0:T(8,128)(2,1)S(1)}, bf16[32,768]{1,0:T(8,128)(2,1)}, u32[]{:S(2)}) copy-start(bf16[32,768]{1,0:T(8,128)(2,1)} %residual_ref.1) | copy-start | bytes 147460
  20.2 12.7 %copy-start.1 = (bf16[6144,168]{0,1:T(8,128)(2,1)S(1)}, bf16[6144,168]{0,1:T(8,128)(2,1)}, u32[]{:S(2)}) copy-start(bf16[6144,168]{0,1:T(8,128)(2,1)} %param.23) | copy-start | bytes 6193156
  20.2 12.7 %copy-start.2 = (bf16[6144,168]{0,1:T(8,128)(2,1)S(1)}, bf16[6144,168]{0,1:T(8,128)(2,1)}, u32[]{:S(2)}) copy-start(bf16[6144,168]{0,1:T(8,128)(2,1)} %param.24) | copy-start | bytes 6193156
  20.2 12.7 %copy-start.3 = (bf16[168,6144]{1,0:T(8,128)(2,1)S(1)}, bf16[168,6144]{1,0:T(8,128)(2,1)}, u32[]{:S(2)}) copy-start(bf16[168,6144]{1,0:T(8,128)(2,1)} %refs_2_.1) | copy-start | bytes 6193156
  21.1 1.3 %collective-permute-start = (f32[32,768]{1,0:T(8,128)S(1)}, f32[32,768]{1,0:T(8,128)S(1)}, u32[]{:S(2)}, u32[]{:S(2)}) collective-permute-start(f32[32,768]{1,0:T(8,128)S(1)} %get-tuple-element.18.mine_ref), channel_id=1, source_target_pairs={{0,1},{1,0},{2,3},{3,2},{4,5},{5,4},{6,7},{7,6},{8,9},{9,8},{10,11... | collective-permute-start | bytes 294920 | tf_op jit(solution)/shard_map/ppermute | solution.py:508
  45.7 1.3 %collective-permute-start.4 = (f32[32,768]{1,0:T(8,128)S(1)}, f32[32,768]{1,0:T(8,128)S(1)}, u32[]{:S(2)}, u32[]{:S(2)}) collective-permute-start(f32[32,768]{1,0:T(8,128)S(1)} %shard_map.156.mine_ref), channel_id=1, source_target_pairs={{0,1},{1,0},{2,3},{3,2},{4,5},{5,4},{6,7},{7,6},{8,9},{9,8},{10,11... | collective-permute-start | bytes 294920 | tf_op jit(solution)/shard_map/ppermute | solution.py:508

commit v18 on v16

--- a/solution.py
+++ b/solution.py
@@ -533,7 +533,7 @@
     spread, own, limit, taken, slots = prepare(
         sharers, capacity, cache_length, earlier, routes.T, route_weight.T, queries, new_key
     )
-    other_weights = [swap(block) for block in weights]
+    other_weights = [swap(block) for block in lax.optimization_barrier(weights)]
     attended = exchange(
         attend(count, spread, own, limit, key_cache, value_cache, new_value, ln_gain)
     )

time: 47.8 us -> 47.4 us (level)
  no operation moved by 1% of the time
where the time goes in v18:
time: 47.4 us; the launch traced here: 47.1 us
  blocking collectives  35.4 us (75%)
  Pallas kernels  6.71 us (14%)
  waiting for transfers between devices  2.59 us (5%)
  starting transfers between devices  1.08 us (2%)
  between operations  0.83 us (2%)
  local copies, waits for them, and re-layouts  0.48 us (1%)
    all_to_all x3, blocking collectives, exchange(): lax.all_to_all(blocks, 'attn', split_axis=0, concat_axis=0, tiled=True)  35.4 us
    pallas_call x1, Pallas kernels, run_experts(): call(expert_kernel, jax.ShapeDtypeStruct(pieces.shape, jnp.bfloat16), [VM...  3.08 us
    ppermute x5, waiting for transfers between devices, swap(): return lax.ppermute(block, 'expert', [(0, 1), (1, 0)])  2.59 us
    ppermute x5, starting transfers between devices, swap(): return lax.ppermute(block, 'expert', [(0, 1), (1, 0)])  1.08 us
    pallas_call x1, Pallas kernels, attend(): call(score_kernel, [jax.ShapeDtypeStruct((row_count, heads, length_max),...  1.03 us
  transfers between devices with their start and end apart: 5, of which 2 were waited for; matrix products, arithmetic and copies ran while one was open for 0% of the time, Pallas kernels for 6%

profile of v18, /device:TPU:0, one launch (start us, length us, event | category | flops | bytes accessed | tf_op | source)
XLA Modules:
  0.0 47.1 jit_solution(2776730192487023018)
XLA Ops:
  0.6 0.0 copy-start.5
  0.6 0.0 copy-start.6
  0.7 0.0 copy-start.7
  0.7 0.0 copy-start.8
  0.7 0.0 copy-start.9
  0.7 0.0 copy-start
  0.7 0.5 %collective-permute-start.1 = (bf16[168,6144]{1,0:T(8,128)(2,1)}, bf16[168,6144]{1,0:T(8,128)(2,1)S(1)}, u32[]{:S(2)}, u32[]{:S(2)}) collective-permute-start(bf16[168,6144]{1,0:T(8,128)(2,1)} %bitcast.4), channel_id=1, source_target_pairs={{0,1},{1,0},{2,3},{3,2},{4,5},{5,4},{6,7},{7,6},{8,9},{9,8},{10,11... | collective-permute-start | bytes 6193160 | tf_op jit(solution)/shard_map/ppermute | solution.py:508
  1.2 0.1 collective-permute-start.2
  1.3 0.4 collective-permute-start.3
  1.7 0.0 copy-start.10
  1.7 0.0 copy-start.11
  1.7 0.0 copy-start.12
  1.7 0.0 copy-done.5
  1.8 0.0 copy-done.6
  1.8 0.0 copy-done.7
  1.8 0.0 copy-done.8
  1.8 0.0 copy-done.9
  1.8 0.2 shard_map.150
  2.0 0.3 copy-done
  2.3 1.0 %shard_map.151 = (bf16[4,24,512]{2,1,0:T(8,128)(2,1)S(1)}, f32[4,24,128]{2,1,0:T(8,128)S(1)}) custom-call(bf16[4,24,512]{2,1,0:T(8,128)(2,1)S(1)} %get-tuple-element.16.spread_ref, f32[4,24,128]{2,1,0:T(8,128)S(1)} %get-tuple-element.17.own_ref, s32[4,24,128]{2,1,0:T(8,128)S(1)} %get-tuple-element.18.limit_ref, bf16[4,512,512]{2,1,0:T(8,128)(2,1)S(1)} %copy-done), custom_call_target="tpu_custom_call" | custom-call | flops 50331648 | bytes 2097152 | tf_op jit(solution)/shard_map/pallas_call | solution.py:343
  3.3 0.1 copy-done.10
  3.5 0.0 copy-done.11
  3.5 0.0 copy-done.12
  3.5 0.5 %shard_map.152 = bf16[8,4,3456]{2,1,0:T(4,128)(2,1)S(1)} custom-call(bf16[4,24,512]{2,1,0:T(8,128)(2,1)S(1)} %get-tuple-element.19.probs_ref, f32[4,24,128]{2,1,0:T(8,128)S(1)} %get-tuple-element.20.own_ref, bf16[4,512,512]{2,1,0:T(8,128)(2,1)S(1)} %copy-done.10, bf16[4,512]{1,0:T(4,128)(2,1)S(1)} %copy-done.11, f32[768]{0:T(1024)S(1)} %copy-done.12), custom_call_target="tpu_custom_call" | custom-call | flops 10000000000 | bytes 2097152 | tf_op jit(solution)/shard_map/pallas_call | solution.py:354
  4.0 15.7 %all_to_all.15.pieces = bf16[8,4,3456]{2,1,0:T(4,128)(2,1)S(1)} all-to-all(bf16[8,4,3456]{2,1,0:T(4,128)(2,1)S(1)} %shard_map.152), channel_id=1, replica_groups=mesh['group'=2,'attn'=8,'expert'=2] {'attn'}, dimensions={0} | all-to-all | bytes 442368 | tf_op jit(solution)/shard_map/all_to_all | solution.py:504
  19.7 0.0 slice-done
  19.7 0.0 slice-done.1
  19.7 0.0 copy-start.1
  19.7 0.0 copy-start.2
  19.7 0.0 copy-start.3
  19.7 0.9 %shard_map.153 = (f32[32,768]{1,0:T(8,128)S(1)}, f32[8,768]{1,0:T(8,128)S(1)}) custom-call(bf16[8,4,3456]{2,1,0:T(4,128)(2,1)S(1)} %all_to_all.15.pieces, bf16[3072,768]{1,0:T(8,128)(2,1)S(1)} %bitcast.11), custom_call_target="tpu_custom_call" | custom-call | flops 10000000000 | bytes 4718592 | tf_op jit(solution)/shard_map/pallas_call | solution.py:380
  20.6 0.0 collective-permute-start
  20.7 1.3 %collective-permute-done.other_ref = f32[32,768]{1,0:T(8,128)S(1)} collective-permute-done((f32[32,768]{1,0:T(8,128)S(1)}, f32[32,768]{1,0:T(8,128)S(1)}, u32[]{:S(2)}, u32[]{:S(2)}) %collective-permute-start) | collective-permute-done | bytes 98336 | tf_op jit(solution)/shard_map/ppermute | solution.py:508
  22.0 0.0 copy-done.4
  22.0 0.1 shard_map.154
  22.1 10.2 %all_to_all.16.pieces = bf16[8,8,768]{2,1,0:T(8,128)(2,1)S(1)} all-to-all(bf16[8,8,768]{2,1,0:T(8,128)(2,1)S(1)} %get-tuple-element.25), channel_id=1, replica_groups=mesh['group'=2,'attn'=8,'expert'=2] {'attn'}, dimensions={0} | all-to-all | bytes 196608 | tf_op jit(solution)/shard_map/all_to_all | solution.py:504
  32.4 0.0 collective-permute-done.1.refs_3_
  32.4 0.0 collective-permute-done.2.refs_4_
  32.4 0.0 collective-permute-done.3.refs_5_
  32.4 0.0 copy-done.1
  32.4 0.0 copy-done.2
  32.4 0.0 copy-done.3
  32.4 3.1 %shard_map.155 = bf16[8,8,768]{2,1,0:T(8,128)(2,1)S(1)} custom-call(f32[8,128]{1,0:T(8,128)S(1)} %get-tuple-element.24.slot_ref, bf16[8,8,768]{2,1,0:T(8,128)(2,1)S(1)} %all_to_all.16.pieces, f32[8,768]{1,0:T(8,128)S(1)} %get-tuple-element.26.gains, bf16[168,6144]{1,0:T(8,128)(2,1)S(1)} %bitcast.5, bf16[168,6144]{1,0:T(8,128)(2,1)S(1)} %bitcast.7, ...), custom_call_target="tpu_custom_call" | custom-call | flops 99090432 | bytes 12386304 | tf_op jit(solution)/shard_map/pallas_call | solution.py:455
  35.5 9.5 %all_to_all.17.pieces = bf16[8,8,768]{2,1,0:T(8,128)(2,1)S(1)} all-to-all(bf16[8,8,768]{2,1,0:T(8,128)(2,1)S(1)} %shard_map.155), channel_id=1, replica_groups=mesh['group'=2,'attn'=8,'expert'=2] {'attn'}, dimensions={0} | all-to-all | bytes 196608 | tf_op jit(solution)/shard_map/all_to_all | solution.py:504
  45.0 0.2 shard_map.156.mine_ref
  45.2 0.0 collective-permute-start.4
  45.2 1.3 %collective-permute-done.4.other_ref = f32[32,768]{1,0:T(8,128)S(1)} collective-permute-done((f32[32,768]{1,0:T(8,128)S(1)}, f32[32,768]{1,0:T(8,128)S(1)}, u32[]{:S(2)}, u32[]{:S(2)}) %collective-permute-start.4) | collective-permute-done | bytes 98336 | tf_op jit(solution)/shard_map/ppermute | solution.py:508
  46.5 0.6 %shard_map.157 = (bf16[32,768]{1,0:T(8,128)(2,1)}, bf16[32,768]{1,0:T(8,128)(2,1)}) custom-call(bf16[32,768]{1,0:T(8,128)(2,1)S(1)} %get-tuple-element.23.stream_ref, f32[32,768]{1,0:T(8,128)S(1)} %shard_map.156.mine_ref, f32[32,768]{1,0:T(8,128)S(1)} %collective-permute-done.4.other_ref), custom_call_target="tpu_custom_call" | custom-call | flops 24576 | bytes 344064 | tf_op jit(solution)/shard_map/pallas_call | solution.py:494
  (5 shorter events, 0.0 us)
Async XLA Ops:
  0.6 1.1 %copy-start.5 = (bf16[4,3072]{1,0:T(4,128)(2,1)S(1)}, bf16[4,3072]{1,0:T(4,128)(2,1)}, u32[]{:S(2)}) copy-start(bf16[4,3072]{1,0:T(4,128)(2,1)} %query_ref.1) | copy-start | bytes 73732
  0.6 1.1 %copy-start.6 = (bf16[4,512]{1,0:T(4,128)(2,1)S(1)}, bf16[4,512]{1,0:T(4,128)(2,1)}, u32[]{:S(2)}) copy-start(bf16[4,512]{1,0:T(4,128)(2,1)} %own_key_ref.1) | copy-start | bytes 12292
  0.7 1.1 %copy-start.7 = (s32[32,4]{0,1:T(4,128)S(1)}, s32[32,4]{0,1:T(4,128)}, u32[]{:S(2)}) copy-start(s32[32,4]{0,1:T(4,128)} %param.26) | copy-start | bytes 1540
  0.7 1.1 %copy-start.8 = (f32[32,4]{0,1:T(4,128)S(1)}, f32[32,4]{0,1:T(4,128)}, u32[]{:S(2)}) copy-start(f32[32,4]{0,1:T(4,128)} %param.27) | copy-start | bytes 1540
  0.7 1.1 %copy-start.9 = (s32[4]{0:T(128)S(1)}, s32[4]{0:T(128)}, u32[]{:S(2)}) copy-start(s32[4]{0:T(128)} %length_ref.1) | copy-start | bytes 52
  0.7 1.6 %copy-start = (bf16[4,512,512]{2,1,0:T(8,128)(2,1)S(1)}, bf16[4,512,512]{2,1,0:T(8,128)(2,1)}, u32[]{:S(2)}) copy-start(bf16[4,512,512]{2,1,0:T(8,128)(2,1)} %key_ref.1) | copy-start | bytes 6291460
  0.7 31.7 %collective-permute-start.1 = (bf16[168,6144]{1,0:T(8,128)(2,1)}, bf16[168,6144]{1,0:T(8,128)(2,1)S(1)}, u32[]{:S(2)}, u32[]{:S(2)}) collective-permute-start(bf16[168,6144]{1,0:T(8,128)(2,1)} %bitcast.4), channel_id=1, source_target_pairs={{0,1},{1,0},{2,3},{3,2},{4,5},{5,4},{6,7},{7,6},{8,9},{9,8},{10,11... | collective-permute-start | bytes 6193160 | tf_op jit(solution)/shard_map/ppermute | solution.py:508
  1.2 31.2 %collective-permute-start.2 = (bf16[168,6144]{1,0:T(8,128)(2,1)}, bf16[168,6144]{1,0:T(8,128)(2,1)S(1)}, u32[]{:S(2)}, u32[]{:S(2)}) collective-permute-start(bf16[168,6144]{1,0:T(8,128)(2,1)} %bitcast.6), channel_id=1, source_target_pairs={{0,1},{1,0},{2,3},{3,2},{4,5},{5,4},{6,7},{7,6},{8,9},{9,8},{10,11... | collective-permute-start | bytes 6193160 | tf_op jit(solution)/shard_map/ppermute | solution.py:508
  1.3 31.1 %collective-permute-start.3 = (bf16[168,6144]{1,0:T(8,128)(2,1)}, bf16[168,6144]{1,0:T(8,128)(2,1)S(1)}, u32[]{:S(2)}, u32[]{:S(2)}) collective-permute-start(bf16[168,6144]{1,0:T(8,128)(2,1)} %refs_2_.1), channel_id=1, source_target_pairs={{0,1},{1,0},{2,3},{3,2},{4,5},{5,4},{6,7},{7,6},{8,9},{9,8},{10,11... | collective-permute-start | bytes 6193160 | tf_op jit(solution)/shard_map/ppermute | solution.py:508
  1.7 1.7 %copy-start.10 = (bf16[4,512,512]{2,1,0:T(8,128)(2,1)S(1)}, bf16[4,512,512]{2,1,0:T(8,128)(2,1)}, u32[]{:S(2)}) copy-start(bf16[4,512,512]{2,1,0:T(8,128)(2,1)} %value_ref.1) | copy-start | bytes 6291460
  1.7 1.7 %copy-start.11 = (bf16[4,512]{1,0:T(4,128)(2,1)S(1)}, bf16[4,512]{1,0:T(4,128)(2,1)}, u32[]{:S(2)}) copy-start(bf16[4,512]{1,0:T(4,128)(2,1)} %own_value_ref.1) | copy-start | bytes 12292
  1.7 1.7 %copy-start.12 = (f32[768]{0:T(1024)S(1)}, f32[768]{0:T(1024)}, u32[]{:S(2)}) copy-start(f32[768]{0:T(1024)} %gain_ref.1) | copy-start | bytes 9220
  2.3 17.4 %slice-start = ((s8[4718592]{0:T(1024)(128)(4,1)}), s8[524288]{0:T(1024)(128)(4,1)S(1)}, s32[]{:S(2)}) async-start(s8[4718592]{0:T(1024)(128)(4,1)} %bitcast.10), calls=%async_computation.3 | async-start | bytes 1048576
  3.5 16.2 %slice-start.1 = ((s8[4718592]{0:T(1024)(128)(4,1)}), s8[4194304]{0:T(1024)(128)(4,1)S(1)}, s32[]{:S(2)}) async-start(s8[4718592]{0:T(1024)(128)(4,1)} %bitcast.10), calls=%async_computation.4 | async-start | bytes 8388608
  19.7 2.3 %copy-start.4 = (bf16[32,768]{1,0:T(8,128)(2,1)S(1)}, bf16[32,768]{1,0:T(8,128)(2,1)}, u32[]{:S(2)}) copy-start(bf16[32,768]{1,0:T(8,128)(2,1)} %residual_ref.1) | copy-start | bytes 147460
  19.7 12.7 %copy-start.1 = (bf16[6144,168]{0,1:T(8,128)(2,1)S(1)}, bf16[6144,168]{0,1:T(8,128)(2,1)}, u32[]{:S(2)}) copy-start(bf16[6144,168]{0,1:T(8,128)(2,1)} %param.23) | copy-start | bytes 6193156
  19.7 12.7 %copy-start.2 = (bf16[6144,168]{0,1:T(8,128)(2,1)S(1)}, bf16[6144,168]{0,1:T(8,128)(2,1)}, u32[]{:S(2)}) copy-start(bf16[6144,168]{0,1:T(8,128)(2,1)} %param.24) | copy-start | bytes 6193156
  19.7 12.7 %copy-start.3 = (bf16[168,6144]{1,0:T(8,128)(2,1)S(1)}, bf16[168,6144]{1,0:T(8,128)(2,1)}, u32[]{:S(2)}) copy-start(bf16[168,6144]{1,0:T(8,128)(2,1)} %refs_2_.1) | copy-start | bytes 6193156
  20.6 1.3 %collective-permute-start = (f32[32,768]{1,0:T(8,128)S(1)}, f32[32,768]{1,0:T(8,128)S(1)}, u32[]{:S(2)}, u32[]{:S(2)}) collective-permute-start(f32[32,768]{1,0:T(8,128)S(1)} %get-tuple-element.21.mine_ref), channel_id=1, source_target_pairs={{0,1},{1,0},{2,3},{3,2},{4,5},{5,4},{6,7},{7,6},{8,9},{9,8},{10,11... | collective-permute-start | bytes 294920 | tf_op jit(solution)/shard_map/ppermute | solution.py:508
  45.2 1.3 %collective-permute-start.4 = (f32[32,768]{1,0:T(8,128)S(1)}, f32[32,768]{1,0:T(8,128)S(1)}, u32[]{:S(2)}, u32[]{:S(2)}) collective-permute-start(f32[32,768]{1,0:T(8,128)S(1)} %shard_map.156.mine_ref), channel_id=1, source_target_pairs={{0,1},{1,0},{2,3},{3,2},{4,5},{5,4},{6,7},{7,6},{8,9},{9,8},{10,11... | collective-permute-start | bytes 294920 | tf_op jit(solution)/shard_map/ppermute | solution.py:508

commit v19 on v18

--- a/solution.py
+++ b/solution.py
@@ -418,6 +418,23 @@
     )(mine, other, residual, taken)
 
 
+def packed_rows(height, number):
+    whole = height // 16 * 16
+    ranges, groups, room = [], [[]], 256
+    for n in range(number):
+        ranges.append((n, 0, whole))
+    ranges += [(n, whole, height) for n in range(number) if whole < height]
+    for n, low, high in ranges:
+        while low < high:
+            if room == 0:
+                groups.append([])
+                room = 256
+            step = min(room, high - low)
+            groups[-1].append((n, low, low + step))
+            low, room = low + step, room - step
+    return groups
+
+
 def expert_kernel(slot_ref, pieces, gains, *refs):
     weights, out_ref, rows_ref = (refs[:3], refs[3:6]), refs[6], refs[7]
     count, capacity, cols = pieces.shape
@@ -433,13 +450,32 @@
         wide = pieces[k].astype(jnp.float32)
         normed = (wide - row_mean) * inverse * gains[pl.ds(k, 1), :]
         rows_ref[:, k * cols : (k + 1) * cols] = normed.astype(jnp.bfloat16)
-    rows = rows_ref[...]
     contract = (((1,), (1,)), ((), ()))
-    hidden = []
-    for gate_ref, up_ref, _ in weights:
-        gate = lax.dot_general(rows, gate_ref[...], contract, preferred_element_type=jnp.float32)
-        up = lax.dot_general(rows, up_ref[...], contract, preferred_element_type=jnp.float32)
-        hidden.append((gate / (1.0 + jnp.exp(-gate)) * up).astype(jnp.bfloat16))
+    blocks = [ref for refs_of in weights for ref in refs_of[:2]]
+    groups = packed_rows(blocks[0].shape[0], len(blocks))
+    sums = [0.0] * len(groups)
+    for k in range(count):
+        columns = slice(k * cols, (k + 1) * cols)
+        rows = rows_ref[:, columns]
+        for index, group in enumerate(groups):
+            tile = jnp.concatenate([blocks[n][low:high, columns] for n, low, high in group], axis=0)
+            sums[index] = sums[index] + lax.dot_general(
+                rows, tile, contract, preferred_element_type=jnp.float32
+            )
+    parts = [[] for _ in blocks]
+    for group, total in zip(groups, sums):
+        start = 0
+        for n, low, high in group:
+            parts[n].append((low, total[:, start : start + high - low]))
+            start += high - low
+    values = [
+        jnp.concatenate([part for _, part in sorted(pieces_of, key=lambda item: item[0])], axis=1)
+        for pieces_of in parts
+    ]
+    hidden = [
+        (gate / (1.0 + jnp.exp(-gate)) * up).astype(jnp.bfloat16)
+        for gate, up in (values[:2], values[2:])
+    ]
     slot_weight = slot_ref[:, :1]
     for k in range(count):
         block = slice(k * cols, (k + 1) * cols)

time: 47.4 us -> 48.3 us (1.019)
  Pallas kernels: 6.71 us -> 7.68 us
    pallas_call x1, Pallas kernels: 3.08 us -> 4.04 us  [run_experts(): call(expert_kernel, jax.ShapeDtypeStruct(pieces.shape, jnp.bfloat16), [VM...]
where the time goes in v19:
time: 48.3 us; the launch traced here: 48.1 us
  blocking collectives  35.4 us (73%)
  Pallas kernels  7.68 us (16%)
  waiting for transfers between devices  2.59 us (5%)
  starting transfers between devices  1.08 us (2%)
  between operations  0.83 us (2%)
    all_to_all x3, blocking collectives, exchange(): lax.all_to_all(blocks, 'attn', split_axis=0, concat_axis=0, tiled=True)  35.4 us
    pallas_call x1, Pallas kernels, run_experts(): call(expert_kernel, jax.ShapeDtypeStruct(pieces.shape, jnp.bfloat16), [VM...  4.04 us
    ppermute x5, waiting for transfers between devices, swap(): return lax.ppermute(block, 'expert', [(0, 1), (1, 0)])  2.59 us
    ppermute x5, starting transfers between devices, swap(): return lax.ppermute(block, 'expert', [(0, 1), (1, 0)])  1.08 us
    pallas_call x1, Pallas kernels, attend(): call(score_kernel, [jax.ShapeDtypeStruct((row_count, heads, length_max),...  1.03 us
  transfers between devices with their start and end apart: 5, of which 2 were waited for; matrix products, arithmetic and copies ran while one was open for 0% of the time, Pallas kernels for 6%

profile of v19, /device:TPU:0, one launch (start us, length us, event | category | flops | bytes accessed | tf_op | source)
XLA Modules:
  0.0 48.1 jit_solution(16986103245706021882)
XLA Ops:
  0.6 0.0 copy-start.5
  0.6 0.0 copy-start.6
  0.7 0.0 copy-start.7
  0.7 0.0 copy-start.8
  0.7 0.0 copy-start.9
  0.7 0.0 copy-start
  0.7 0.5 %collective-permute-start.1 = (bf16[168,6144]{1,0:T(8,128)(2,1)}, bf16[168,6144]{1,0:T(8,128)(2,1)S(1)}, u32[]{:S(2)}, u32[]{:S(2)}) collective-permute-start(bf16[168,6144]{1,0:T(8,128)(2,1)} %bitcast.4), channel_id=1, source_target_pairs={{0,1},{1,0},{2,3},{3,2},{4,5},{5,4},{6,7},{7,6},{8,9},{9,8},{10,11... | collective-permute-start | bytes 6193160 | tf_op jit(solution)/shard_map/ppermute | solution.py:544
  1.2 0.1 collective-permute-start.2
  1.3 0.4 collective-permute-start.3
  1.7 0.0 copy-start.10
  1.7 0.0 copy-start.11
  1.7 0.0 copy-start.12
  1.7 0.0 copy-done.5
  1.8 0.0 copy-done.6
  1.8 0.0 copy-done.7
  1.8 0.0 copy-done.8
  1.8 0.0 copy-done.9
  1.8 0.2 shard_map.150
  2.0 0.3 copy-done
  2.3 1.0 %shard_map.151 = (bf16[4,24,512]{2,1,0:T(8,128)(2,1)S(1)}, f32[4,24,128]{2,1,0:T(8,128)S(1)}) custom-call(bf16[4,24,512]{2,1,0:T(8,128)(2,1)S(1)} %get-tuple-element.16.spread_ref, f32[4,24,128]{2,1,0:T(8,128)S(1)} %get-tuple-element.17.own_ref, s32[4,24,128]{2,1,0:T(8,128)S(1)} %get-tuple-element.18.limit_ref, bf16[4,512,512]{2,1,0:T(8,128)(2,1)S(1)} %copy-done), custom_call_target="tpu_custom_call" | custom-call | flops 50331648 | bytes 2097152 | tf_op jit(solution)/shard_map/pallas_call | solution.py:343
  3.3 0.1 copy-done.10
  3.5 0.0 copy-done.11
  3.5 0.0 copy-done.12
  3.5 0.5 %shard_map.152 = bf16[8,4,3456]{2,1,0:T(4,128)(2,1)S(1)} custom-call(bf16[4,24,512]{2,1,0:T(8,128)(2,1)S(1)} %get-tuple-element.19.probs_ref, f32[4,24,128]{2,1,0:T(8,128)S(1)} %get-tuple-element.20.own_ref, bf16[4,512,512]{2,1,0:T(8,128)(2,1)S(1)} %copy-done.10, bf16[4,512]{1,0:T(4,128)(2,1)S(1)} %copy-done.11, f32[768]{0:T(1024)S(1)} %copy-done.12), custom_call_target="tpu_custom_call" | custom-call | flops 10000000000 | bytes 2097152 | tf_op jit(solution)/shard_map/pallas_call | solution.py:354
  4.0 15.7 %all_to_all.15.pieces = bf16[8,4,3456]{2,1,0:T(4,128)(2,1)S(1)} all-to-all(bf16[8,4,3456]{2,1,0:T(4,128)(2,1)S(1)} %shard_map.152), channel_id=1, replica_groups=mesh['group'=2,'attn'=8,'expert'=2] {'attn'}, dimensions={0} | all-to-all | bytes 442368 | tf_op jit(solution)/shard_map/all_to_all | solution.py:540
  19.7 0.0 slice-done
  19.7 0.0 slice-done.1
  19.7 0.0 copy-start.1
  19.7 0.0 copy-start.2
  19.7 0.0 copy-start.3
  19.7 0.9 %shard_map.153 = (f32[32,768]{1,0:T(8,128)S(1)}, f32[8,768]{1,0:T(8,128)S(1)}) custom-call(bf16[8,4,3456]{2,1,0:T(4,128)(2,1)S(1)} %all_to_all.15.pieces, bf16[3072,768]{1,0:T(8,128)(2,1)S(1)} %bitcast.11), custom_call_target="tpu_custom_call" | custom-call | flops 10000000000 | bytes 4718592 | tf_op jit(solution)/shard_map/pallas_call | solution.py:380
  20.6 0.0 collective-permute-start
  20.7 1.3 %collective-permute-done.other_ref = f32[32,768]{1,0:T(8,128)S(1)} collective-permute-done((f32[32,768]{1,0:T(8,128)S(1)}, f32[32,768]{1,0:T(8,128)S(1)}, u32[]{:S(2)}, u32[]{:S(2)}) %collective-permute-start) | collective-permute-done | bytes 98336 | tf_op jit(solution)/shard_map/ppermute | solution.py:544
  22.0 0.0 copy-done.4
  22.0 0.1 shard_map.154
  22.1 10.2 %all_to_all.16.pieces = bf16[8,8,768]{2,1,0:T(8,128)(2,1)S(1)} all-to-all(bf16[8,8,768]{2,1,0:T(8,128)(2,1)S(1)} %get-tuple-element.25), channel_id=1, replica_groups=mesh['group'=2,'attn'=8,'expert'=2] {'attn'}, dimensions={0} | all-to-all | bytes 196608 | tf_op jit(solution)/shard_map/all_to_all | solution.py:540
  32.4 0.0 collective-permute-done.1.refs_3_
  32.4 0.0 collective-permute-done.2.refs_4_
  32.4 0.0 collective-permute-done.3.refs_5_
  32.4 0.0 copy-done.1
  32.4 0.0 copy-done.2
  32.4 0.0 copy-done.3
  32.4 4.0 %shard_map.155 = bf16[8,8,768]{2,1,0:T(8,128)(2,1)S(1)} custom-call(f32[8,128]{1,0:T(8,128)S(1)} %get-tuple-element.24.slot_ref, bf16[8,8,768]{2,1,0:T(8,128)(2,1)S(1)} %all_to_all.16.pieces, f32[8,768]{1,0:T(8,128)S(1)} %get-tuple-element.26.gains, bf16[168,6144]{1,0:T(8,128)(2,1)S(1)} %bitcast.5, bf16[168,6144]{1,0:T(8,128)(2,1)S(1)} %bitcast.7, ...), custom_call_target="tpu_custom_call" | custom-call | flops 99090432 | bytes 12386304 | tf_op jit(solution)/shard_map/pallas_call | solution.py:491
  36.4 9.5 %all_to_all.17.pieces = bf16[8,8,768]{2,1,0:T(8,128)(2,1)S(1)} all-to-all(bf16[8,8,768]{2,1,0:T(8,128)(2,1)S(1)} %shard_map.155), channel_id=1, replica_groups=mesh['group'=2,'attn'=8,'expert'=2] {'attn'}, dimensions={0} | all-to-all | bytes 196608 | tf_op jit(solution)/shard_map/all_to_all | solution.py:540
  46.0 0.2 shard_map.156.mine_ref
  46.1 0.0 collective-permute-start.4
  46.1 1.3 %collective-permute-done.4.other_ref = f32[32,768]{1,0:T(8,128)S(1)} collective-permute-done((f32[32,768]{1,0:T(8,128)S(1)}, f32[32,768]{1,0:T(8,128)S(1)}, u32[]{:S(2)}, u32[]{:S(2)}) %collective-permute-start.4) | collective-permute-done | bytes 98336 | tf_op jit(solution)/shard_map/ppermute | solution.py:544
  47.4 0.6 %shard_map.157 = (bf16[32,768]{1,0:T(8,128)(2,1)}, bf16[32,768]{1,0:T(8,128)(2,1)}) custom-call(bf16[32,768]{1,0:T(8,128)(2,1)S(1)} %get-tuple-element.23.stream_ref, f32[32,768]{1,0:T(8,128)S(1)} %shard_map.156.mine_ref, f32[32,768]{1,0:T(8,128)S(1)} %collective-permute-done.4.other_ref), custom_call_target="tpu_custom_call" | custom-call | flops 24576 | bytes 344064 | tf_op jit(solution)/shard_map/pallas_call | solution.py:530
  (5 shorter events, 0.0 us)
Async XLA Ops:
  0.6 1.1 %copy-start.5 = (bf16[4,3072]{1,0:T(4,128)(2,1)S(1)}, bf16[4,3072]{1,0:T(4,128)(2,1)}, u32[]{:S(2)}) copy-start(bf16[4,3072]{1,0:T(4,128)(2,1)} %query_ref.1) | copy-start | bytes 73732
  0.6 1.1 %copy-start.6 = (bf16[4,512]{1,0:T(4,128)(2,1)S(1)}, bf16[4,512]{1,0:T(4,128)(2,1)}, u32[]{:S(2)}) copy-start(bf16[4,512]{1,0:T(4,128)(2,1)} %own_key_ref.1) | copy-start | bytes 12292
  0.7 1.1 %copy-start.7 = (s32[32,4]{0,1:T(4,128)S(1)}, s32[32,4]{0,1:T(4,128)}, u32[]{:S(2)}) copy-start(s32[32,4]{0,1:T(4,128)} %param.26) | copy-start | bytes 1540
  0.7 1.1 %copy-start.8 = (f32[32,4]{0,1:T(4,128)S(1)}, f32[32,4]{0,1:T(4,128)}, u32[]{:S(2)}) copy-start(f32[32,4]{0,1:T(4,128)} %param.27) | copy-start | bytes 1540
  0.7 1.1 %copy-start.9 = (s32[4]{0:T(128)S(1)}, s32[4]{0:T(128)}, u32[]{:S(2)}) copy-start(s32[4]{0:T(128)} %length_ref.1) | copy-start | bytes 52
  0.7 1.6 %copy-start = (bf16[4,512,512]{2,1,0:T(8,128)(2,1)S(1)}, bf16[4,512,512]{2,1,0:T(8,128)(2,1)}, u32[]{:S(2)}) copy-start(bf16[4,512,512]{2,1,0:T(8,128)(2,1)} %key_ref.1) | copy-start | bytes 6291460
  0.7 31.7 %collective-permute-start.1 = (bf16[168,6144]{1,0:T(8,128)(2,1)}, bf16[168,6144]{1,0:T(8,128)(2,1)S(1)}, u32[]{:S(2)}, u32[]{:S(2)}) collective-permute-start(bf16[168,6144]{1,0:T(8,128)(2,1)} %bitcast.4), channel_id=1, source_target_pairs={{0,1},{1,0},{2,3},{3,2},{4,5},{5,4},{6,7},{7,6},{8,9},{9,8},{10,11... | collective-permute-start | bytes 6193160 | tf_op jit(solution)/shard_map/ppermute | solution.py:544
  1.2 31.2 %collective-permute-start.2 = (bf16[168,6144]{1,0:T(8,128)(2,1)}, bf16[168,6144]{1,0:T(8,128)(2,1)S(1)}, u32[]{:S(2)}, u32[]{:S(2)}) collective-permute-start(bf16[168,6144]{1,0:T(8,128)(2,1)} %bitcast.6), channel_id=1, source_target_pairs={{0,1},{1,0},{2,3},{3,2},{4,5},{5,4},{6,7},{7,6},{8,9},{9,8},{10,11... | collective-permute-start | bytes 6193160 | tf_op jit(solution)/shard_map/ppermute | solution.py:544
  1.3 31.1 %collective-permute-start.3 = (bf16[168,6144]{1,0:T(8,128)(2,1)}, bf16[168,6144]{1,0:T(8,128)(2,1)S(1)}, u32[]{:S(2)}, u32[]{:S(2)}) collective-permute-start(bf16[168,6144]{1,0:T(8,128)(2,1)} %refs_2_.1), channel_id=1, source_target_pairs={{0,1},{1,0},{2,3},{3,2},{4,5},{5,4},{6,7},{7,6},{8,9},{9,8},{10,11... | collective-permute-start | bytes 6193160 | tf_op jit(solution)/shard_map/ppermute | solution.py:544
  1.7 1.7 %copy-start.10 = (bf16[4,512,512]{2,1,0:T(8,128)(2,1)S(1)}, bf16[4,512,512]{2,1,0:T(8,128)(2,1)}, u32[]{:S(2)}) copy-start(bf16[4,512,512]{2,1,0:T(8,128)(2,1)} %value_ref.1) | copy-start | bytes 6291460
  1.7 1.7 %copy-start.11 = (bf16[4,512]{1,0:T(4,128)(2,1)S(1)}, bf16[4,512]{1,0:T(4,128)(2,1)}, u32[]{:S(2)}) copy-start(bf16[4,512]{1,0:T(4,128)(2,1)} %own_value_ref.1) | copy-start | bytes 12292
  1.7 1.7 %copy-start.12 = (f32[768]{0:T(1024)S(1)}, f32[768]{0:T(1024)}, u32[]{:S(2)}) copy-start(f32[768]{0:T(1024)} %gain_ref.1) | copy-start | bytes 9220
  2.3 17.4 %slice-start = ((s8[4718592]{0:T(1024)(128)(4,1)}), s8[524288]{0:T(1024)(128)(4,1)S(1)}, s32[]{:S(2)}) async-start(s8[4718592]{0:T(1024)(128)(4,1)} %bitcast.10), calls=%async_computation.3 | async-start | bytes 1048576
  3.5 16.2 %slice-start.1 = ((s8[4718592]{0:T(1024)(128)(4,1)}), s8[4194304]{0:T(1024)(128)(4,1)S(1)}, s32[]{:S(2)}) async-start(s8[4718592]{0:T(1024)(128)(4,1)} %bitcast.10), calls=%async_computation.4 | async-start | bytes 8388608
  19.7 2.3 %copy-start.4 = (bf16[32,768]{1,0:T(8,128)(2,1)S(1)}, bf16[32,768]{1,0:T(8,128)(2,1)}, u32[]{:S(2)}) copy-start(bf16[32,768]{1,0:T(8,128)(2,1)} %residual_ref.1) | copy-start | bytes 147460
  19.7 12.7 %copy-start.1 = (bf16[6144,168]{0,1:T(8,128)(2,1)S(1)}, bf16[6144,168]{0,1:T(8,128)(2,1)}, u32[]{:S(2)}) copy-start(bf16[6144,168]{0,1:T(8,128)(2,1)} %param.23) | copy-start | bytes 6193156
  19.7 12.7 %copy-start.2 = (bf16[6144,168]{0,1:T(8,128)(2,1)S(1)}, bf16[6144,168]{0,1:T(8,128)(2,1)}, u32[]{:S(2)}) copy-start(bf16[6144,168]{0,1:T(8,128)(2,1)} %param.24) | copy-start | bytes 6193156
  19.7 12.7 %copy-start.3 = (bf16[168,6144]{1,0:T(8,128)(2,1)S(1)}, bf16[168,6144]{1,0:T(8,128)(2,1)}, u32[]{:S(2)}) copy-start(bf16[168,6144]{1,0:T(8,128)(2,1)} %refs_2_.1) | copy-start | bytes 6193156
  20.6 1.3 %collective-permute-start = (f32[32,768]{1,0:T(8,128)S(1)}, f32[32,768]{1,0:T(8,128)S(1)}, u32[]{:S(2)}, u32[]{:S(2)}) collective-permute-start(f32[32,768]{1,0:T(8,128)S(1)} %get-tuple-element.21.mine_ref), channel_id=1, source_target_pairs={{0,1},{1,0},{2,3},{3,2},{4,5},{5,4},{6,7},{7,6},{8,9},{9,8},{10,11... | collective-permute-start | bytes 294920 | tf_op jit(solution)/shard_map/ppermute | solution.py:544
  46.1 1.3 %collective-permute-start.4 = (f32[32,768]{1,0:T(8,128)S(1)}, f32[32,768]{1,0:T(8,128)S(1)}, u32[]{:S(2)}, u32[]{:S(2)}) collective-permute-start(f32[32,768]{1,0:T(8,128)S(1)} %shard_map.156.mine_ref), channel_id=1, source_target_pairs={{0,1},{1,0},{2,3},{3,2},{4,5},{5,4},{6,7},{7,6},{8,9},{9,8},{10,11... | collective-permute-start | bytes 294920 | tf_op jit(solution)/shard_map/ppermute | solution.py:544

commit v20 on v18

--- a/solution.py
+++ b/solution.py
@@ -276,29 +276,27 @@
     row_count, heads, length_max = probs_ref.shape
     scale = 1.0 / math.sqrt(HEAD_DIM)
     contract = (((1,), (1,)), ((), ()))
-    scores = jnp.concatenate(
-        [
-            lax.dot_general(
-                spread_ref[r], key_ref[r], contract, preferred_element_type=jnp.float32
-            )
-            for r in range(row_count)
-        ],
-        axis=0,
-    )
-    position = lax.broadcasted_iota(jnp.int32, scores.shape, 1)
-    limit = jnp.concatenate([limit_ref[r, :, :1] for r in range(row_count)], axis=0)
-    own = jnp.concatenate([own_ref[r, :, :1] for r in range(row_count)], axis=0)
-    past = jnp.where(position < limit, scores * scale, NEG_FILL)
-    largest = jnp.maximum(jnp.max(past, axis=1, keepdims=True), own)
-    weight = jnp.exp(past - largest)
-    own_weight = jnp.exp(own - largest)
-    inverse = 1.0 / (jnp.sum(weight, axis=1, keepdims=True) + own_weight)
-    probs = weight * inverse
-    own_prob = (own_weight * inverse).astype(jnp.bfloat16).astype(jnp.float32)
-    for r in range(row_count):
-        rows = slice(r * heads, (r + 1) * heads)
-        probs_ref[r] = probs[rows].astype(jnp.bfloat16)
-        own_probs_ref[r] = jnp.broadcast_to(own_prob[rows], own_probs_ref.shape[1:])
+    products = [
+        lax.dot_general(spread_ref[r], key_ref[r], contract, preferred_element_type=jnp.float32)
+        for r in range(row_count)
+    ]
+    for first in range(0, row_count, 2):
+        batch = range(first, min(first + 2, row_count))
+        scores = jnp.concatenate([products[r] for r in batch], axis=0)
+        position = lax.broadcasted_iota(jnp.int32, scores.shape, 1)
+        limit = jnp.concatenate([limit_ref[r, :, :1] for r in batch], axis=0)
+        own = jnp.concatenate([own_ref[r, :, :1] for r in batch], axis=0)
+        past = jnp.where(position < limit, scores * scale, NEG_FILL)
+        largest = jnp.maximum(jnp.max(past, axis=1, keepdims=True), own)
+        weight = jnp.exp(past - largest)
+        own_weight = jnp.exp(own - largest)
+        inverse = 1.0 / (jnp.sum(weight, axis=1, keepdims=True) + own_weight)
+        probs = weight * inverse
+        own_prob = (own_weight * inverse).astype(jnp.bfloat16).astype(jnp.float32)
+        for index, r in enumerate(batch):
+            rows = slice(index * heads, (index + 1) * heads)
+            probs_ref[r] = probs[rows].astype(jnp.bfloat16)
+            own_probs_ref[r] = jnp.broadcast_to(own_prob[rows], own_probs_ref.shape[1:])
 
 
 def value_kernel(probs_ref, own_ref, value_ref, own_value_ref, gain_ref, out_ref, value_rows,
@@ -365,13 +363,21 @@
     width = weight_ref.shape[0]
     half = gain_ref.shape[1] // 2
     for k in range(count):
-        stack[pl.ds(k * rows, rows), :] = pieces[k, :, :width].astype(jnp.float32)
         parts = pieces[k, :, width:].astype(jnp.float32)
         gain_ref[pl.ds(k, 1), :half] = parts[0:1] + parts[2:3]
         gain_ref[pl.ds(k, 1), half:] = parts[1:2] + parts[3:4]
-    out_ref[...] = jnp.dot(
-        stack[...].astype(jnp.bfloat16), weight_ref[...], preferred_element_type=jnp.float32
-    )
+    total = 0.0
+    step = width // 4
+    for start in range(0, width, step):
+        part = slice(start, start + step)
+        for k in range(count):
+            stack[pl.ds(k * rows, rows), part] = pieces[k, :, part].astype(jnp.float32)
+        total = total + jnp.dot(
+            stack[:, part].astype(jnp.bfloat16),
+            weight_ref[part, :],
+            preferred_element_type=jnp.float32,
+        )
+    out_ref[...] = total
 
 
 def project(pieces, out_weight):

time: 47.4 us -> 47.4 us (level)
  no operation moved by 1% of the time
where the time goes in v20:
time: 47.4 us; the launch traced here: 47.2 us
  blocking collectives  35.4 us (75%)
  Pallas kernels  6.73 us (14%)
  waiting for transfers between devices  2.59 us (5%)
  starting transfers between devices  1.09 us (2%)
  between operations  0.83 us (2%)
  local copies, waits for them, and re-layouts  0.48 us (1%)
    all_to_all x3, blocking collectives, exchange(): lax.all_to_all(blocks, 'attn', split_axis=0, concat_axis=0, tiled=True)  35.4 us
    pallas_call x1, Pallas kernels, run_experts(): call(expert_kernel, jax.ShapeDtypeStruct(pieces.shape, jnp.bfloat16), [VM...  3.08 us
    ppermute x5, waiting for transfers between devices, swap(): return lax.ppermute(block, 'expert', [(0, 1), (1, 0)])  2.59 us
    ppermute x5, starting transfers between devices, swap(): return lax.ppermute(block, 'expert', [(0, 1), (1, 0)])  1.09 us
    pallas_call x1, Pallas kernels, attend(): call(score_kernel, [jax.ShapeDtypeStruct((row_count, heads, length_max),...  1.03 us
  transfers between devices with their start and end apart: 5, of which 2 were waited for; matrix products, arithmetic and copies ran while one was open for 0% of the time, Pallas kernels for 6%

profile of v20, /device:TPU:0, one launch (start us, length us, event | category | flops | bytes accessed | tf_op | source)
XLA Modules:
  0.0 47.2 jit_solution(9203762695777352928)
XLA Ops:
  0.6 0.0 copy-start.5
  0.6 0.0 copy-start.6
  0.7 0.0 copy-start.7
  0.7 0.0 copy-start.8
  0.7 0.0 copy-start.9
  0.7 0.0 copy-start
  0.7 0.5 %collective-permute-start.1 = (bf16[168,6144]{1,0:T(8,128)(2,1)}, bf16[168,6144]{1,0:T(8,128)(2,1)S(1)}, u32[]{:S(2)}, u32[]{:S(2)}) collective-permute-start(bf16[168,6144]{1,0:T(8,128)(2,1)} %bitcast.4), channel_id=1, source_target_pairs={{0,1},{1,0},{2,3},{3,2},{4,5},{5,4},{6,7},{7,6},{8,9},{9,8},{10,11... | collective-permute-start | bytes 6193160 | tf_op jit(solution)/shard_map/ppermute | solution.py:514
  1.2 0.1 collective-permute-start.2
  1.3 0.4 collective-permute-start.3
  1.7 0.0 copy-start.10
  1.7 0.0 copy-start.11
  1.7 0.0 copy-start.12
  1.7 0.0 copy-done.5
  1.8 0.0 copy-done.6
  1.8 0.0 copy-done.7
  1.8 0.0 copy-done.8
  1.8 0.0 copy-done.9
  1.8 0.2 shard_map.150
  2.0 0.3 copy-done
  2.3 1.0 %shard_map.151 = (bf16[4,24,512]{2,1,0:T(8,128)(2,1)S(1)}, f32[4,24,128]{2,1,0:T(8,128)S(1)}) custom-call(bf16[4,24,512]{2,1,0:T(8,128)(2,1)S(1)} %get-tuple-element.16.spread_ref, f32[4,24,128]{2,1,0:T(8,128)S(1)} %get-tuple-element.17.own_ref, s32[4,24,128]{2,1,0:T(8,128)S(1)} %get-tuple-element.18.limit_ref, bf16[4,512,512]{2,1,0:T(8,128)(2,1)S(1)} %copy-done), custom_call_target="tpu_custom_call" | custom-call | flops 50331648 | bytes 2097152 | tf_op jit(solution)/shard_map/pallas_call | solution.py:341
  3.3 0.1 copy-done.10
  3.5 0.0 copy-done.11
  3.5 0.0 copy-done.12
  3.5 0.5 %shard_map.152 = bf16[8,4,3456]{2,1,0:T(4,128)(2,1)S(1)} custom-call(bf16[4,24,512]{2,1,0:T(8,128)(2,1)S(1)} %get-tuple-element.19.probs_ref, f32[4,24,128]{2,1,0:T(8,128)S(1)} %get-tuple-element.20.own_ref, bf16[4,512,512]{2,1,0:T(8,128)(2,1)S(1)} %copy-done.10, bf16[4,512]{1,0:T(4,128)(2,1)S(1)} %copy-done.11, f32[768]{0:T(1024)S(1)} %copy-done.12), custom_call_target="tpu_custom_call" | custom-call | flops 10000000000 | bytes 2097152 | tf_op jit(solution)/shard_map/pallas_call | solution.py:352
  4.0 15.7 %all_to_all.15.pieces = bf16[8,4,3456]{2,1,0:T(4,128)(2,1)S(1)} all-to-all(bf16[8,4,3456]{2,1,0:T(4,128)(2,1)S(1)} %shard_map.152), channel_id=1, replica_groups=mesh['group'=2,'attn'=8,'expert'=2] {'attn'}, dimensions={0} | all-to-all | bytes 442368 | tf_op jit(solution)/shard_map/all_to_all | solution.py:510
  19.7 0.0 slice-done
  19.7 0.0 slice-done.1
  19.7 0.0 copy-start.1
  19.7 0.0 copy-start.2
  19.7 0.0 copy-start.3
  19.7 0.9 %shard_map.153 = (f32[32,768]{1,0:T(8,128)S(1)}, f32[8,768]{1,0:T(8,128)S(1)}) custom-call(bf16[8,4,3456]{2,1,0:T(4,128)(2,1)S(1)} %all_to_all.15.pieces, bf16[3072,768]{1,0:T(8,128)(2,1)S(1)} %bitcast.11), custom_call_target="tpu_custom_call" | custom-call | flops 10000000000 | bytes 4718592 | tf_op jit(solution)/shard_map/pallas_call | solution.py:386
  20.6 0.1 collective-permute-start
  20.7 1.3 %collective-permute-done.other_ref = f32[32,768]{1,0:T(8,128)S(1)} collective-permute-done((f32[32,768]{1,0:T(8,128)S(1)}, f32[32,768]{1,0:T(8,128)S(1)}, u32[]{:S(2)}, u32[]{:S(2)}) %collective-permute-start) | collective-permute-done | bytes 98336 | tf_op jit(solution)/shard_map/ppermute | solution.py:514
  22.0 0.0 copy-done.4
  22.0 0.1 shard_map.154
  22.2 10.2 %all_to_all.16.pieces = bf16[8,8,768]{2,1,0:T(8,128)(2,1)S(1)} all-to-all(bf16[8,8,768]{2,1,0:T(8,128)(2,1)S(1)} %get-tuple-element.25), channel_id=1, replica_groups=mesh['group'=2,'attn'=8,'expert'=2] {'attn'}, dimensions={0} | all-to-all | bytes 196608 | tf_op jit(solution)/shard_map/all_to_all | solution.py:510
  32.4 0.0 collective-permute-done.1.refs_3_
  32.4 0.0 collective-permute-done.2.refs_4_
  32.4 0.0 collective-permute-done.3.refs_5_
  32.4 0.0 copy-done.1
  32.4 0.0 copy-done.2
  32.4 0.0 copy-done.3
  32.4 3.1 %shard_map.155 = bf16[8,8,768]{2,1,0:T(8,128)(2,1)S(1)} custom-call(f32[8,128]{1,0:T(8,128)S(1)} %get-tuple-element.24.slot_ref, bf16[8,8,768]{2,1,0:T(8,128)(2,1)S(1)} %all_to_all.16.pieces, f32[8,768]{1,0:T(8,128)S(1)} %get-tuple-element.26.gains, bf16[168,6144]{1,0:T(8,128)(2,1)S(1)} %bitcast.5, bf16[168,6144]{1,0:T(8,128)(2,1)S(1)} %bitcast.7, ...), custom_call_target="tpu_custom_call" | custom-call | flops 99090432 | bytes 12386304 | tf_op jit(solution)/shard_map/pallas_call | solution.py:461
  35.5 9.5 %all_to_all.17.pieces = bf16[8,8,768]{2,1,0:T(8,128)(2,1)S(1)} all-to-all(bf16[8,8,768]{2,1,0:T(8,128)(2,1)S(1)} %shard_map.155), channel_id=1, replica_groups=mesh['group'=2,'attn'=8,'expert'=2] {'attn'}, dimensions={0} | all-to-all | bytes 196608 | tf_op jit(solution)/shard_map/all_to_all | solution.py:510
  45.0 0.2 shard_map.156.mine_ref
  45.2 0.0 collective-permute-start.4
  45.2 1.3 %collective-permute-done.4.other_ref = f32[32,768]{1,0:T(8,128)S(1)} collective-permute-done((f32[32,768]{1,0:T(8,128)S(1)}, f32[32,768]{1,0:T(8,128)S(1)}, u32[]{:S(2)}, u32[]{:S(2)}) %collective-permute-start.4) | collective-permute-done | bytes 98336 | tf_op jit(solution)/shard_map/ppermute | solution.py:514
  46.5 0.6 %shard_map.157 = (bf16[32,768]{1,0:T(8,128)(2,1)}, bf16[32,768]{1,0:T(8,128)(2,1)}) custom-call(bf16[32,768]{1,0:T(8,128)(2,1)S(1)} %get-tuple-element.23.stream_ref, f32[32,768]{1,0:T(8,128)S(1)} %shard_map.156.mine_ref, f32[32,768]{1,0:T(8,128)S(1)} %collective-permute-done.4.other_ref), custom_call_target="tpu_custom_call" | custom-call | flops 24576 | bytes 344064 | tf_op jit(solution)/shard_map/pallas_call | solution.py:500
  (5 shorter events, 0.0 us)
Async XLA Ops:
  0.6 1.1 %copy-start.5 = (bf16[4,3072]{1,0:T(4,128)(2,1)S(1)}, bf16[4,3072]{1,0:T(4,128)(2,1)}, u32[]{:S(2)}) copy-start(bf16[4,3072]{1,0:T(4,128)(2,1)} %query_ref.1) | copy-start | bytes 73732
  0.6 1.1 %copy-start.6 = (bf16[4,512]{1,0:T(4,128)(2,1)S(1)}, bf16[4,512]{1,0:T(4,128)(2,1)}, u32[]{:S(2)}) copy-start(bf16[4,512]{1,0:T(4,128)(2,1)} %own_key_ref.1) | copy-start | bytes 12292
  0.7 1.1 %copy-start.7 = (s32[32,4]{0,1:T(4,128)S(1)}, s32[32,4]{0,1:T(4,128)}, u32[]{:S(2)}) copy-start(s32[32,4]{0,1:T(4,128)} %param.26) | copy-start | bytes 1540
  0.7 1.1 %copy-start.8 = (f32[32,4]{0,1:T(4,128)S(1)}, f32[32,4]{0,1:T(4,128)}, u32[]{:S(2)}) copy-start(f32[32,4]{0,1:T(4,128)} %param.27) | copy-start | bytes 1540
  0.7 1.1 %copy-start.9 = (s32[4]{0:T(128)S(1)}, s32[4]{0:T(128)}, u32[]{:S(2)}) copy-start(s32[4]{0:T(128)} %length_ref.1) | copy-start | bytes 52
  0.7 1.6 %copy-start = (bf16[4,512,512]{2,1,0:T(8,128)(2,1)S(1)}, bf16[4,512,512]{2,1,0:T(8,128)(2,1)}, u32[]{:S(2)}) copy-start(bf16[4,512,512]{2,1,0:T(8,128)(2,1)} %key_ref.1) | copy-start | bytes 6291460
  0.7 31.7 %collective-permute-start.1 = (bf16[168,6144]{1,0:T(8,128)(2,1)}, bf16[168,6144]{1,0:T(8,128)(2,1)S(1)}, u32[]{:S(2)}, u32[]{:S(2)}) collective-permute-start(bf16[168,6144]{1,0:T(8,128)(2,1)} %bitcast.4), channel_id=1, source_target_pairs={{0,1},{1,0},{2,3},{3,2},{4,5},{5,4},{6,7},{7,6},{8,9},{9,8},{10,11... | collective-permute-start | bytes 6193160 | tf_op jit(solution)/shard_map/ppermute | solution.py:514
  1.2 31.2 %collective-permute-start.2 = (bf16[168,6144]{1,0:T(8,128)(2,1)}, bf16[168,6144]{1,0:T(8,128)(2,1)S(1)}, u32[]{:S(2)}, u32[]{:S(2)}) collective-permute-start(bf16[168,6144]{1,0:T(8,128)(2,1)} %bitcast.6), channel_id=1, source_target_pairs={{0,1},{1,0},{2,3},{3,2},{4,5},{5,4},{6,7},{7,6},{8,9},{9,8},{10,11... | collective-permute-start | bytes 6193160 | tf_op jit(solution)/shard_map/ppermute | solution.py:514
  1.3 31.1 %collective-permute-start.3 = (bf16[168,6144]{1,0:T(8,128)(2,1)}, bf16[168,6144]{1,0:T(8,128)(2,1)S(1)}, u32[]{:S(2)}, u32[]{:S(2)}) collective-permute-start(bf16[168,6144]{1,0:T(8,128)(2,1)} %refs_2_.1), channel_id=1, source_target_pairs={{0,1},{1,0},{2,3},{3,2},{4,5},{5,4},{6,7},{7,6},{8,9},{9,8},{10,11... | collective-permute-start | bytes 6193160 | tf_op jit(solution)/shard_map/ppermute | solution.py:514
  1.7 1.7 %copy-start.10 = (bf16[4,512,512]{2,1,0:T(8,128)(2,1)S(1)}, bf16[4,512,512]{2,1,0:T(8,128)(2,1)}, u32[]{:S(2)}) copy-start(bf16[4,512,512]{2,1,0:T(8,128)(2,1)} %value_ref.1) | copy-start | bytes 6291460
  1.7 1.7 %copy-start.11 = (bf16[4,512]{1,0:T(4,128)(2,1)S(1)}, bf16[4,512]{1,0:T(4,128)(2,1)}, u32[]{:S(2)}) copy-start(bf16[4,512]{1,0:T(4,128)(2,1)} %own_value_ref.1) | copy-start | bytes 12292
  1.7 1.7 %copy-start.12 = (f32[768]{0:T(1024)S(1)}, f32[768]{0:T(1024)}, u32[]{:S(2)}) copy-start(f32[768]{0:T(1024)} %gain_ref.1) | copy-start | bytes 9220
  2.3 17.4 %slice-start = ((s8[4718592]{0:T(1024)(128)(4,1)}), s8[524288]{0:T(1024)(128)(4,1)S(1)}, s32[]{:S(2)}) async-start(s8[4718592]{0:T(1024)(128)(4,1)} %bitcast.10), calls=%async_computation.3 | async-start | bytes 1048576
  3.5 16.2 %slice-start.1 = ((s8[4718592]{0:T(1024)(128)(4,1)}), s8[4194304]{0:T(1024)(128)(4,1)S(1)}, s32[]{:S(2)}) async-start(s8[4718592]{0:T(1024)(128)(4,1)} %bitcast.10), calls=%async_computation.4 | async-start | bytes 8388608
  19.7 2.3 %copy-start.4 = (bf16[32,768]{1,0:T(8,128)(2,1)S(1)}, bf16[32,768]{1,0:T(8,128)(2,1)}, u32[]{:S(2)}) copy-start(bf16[32,768]{1,0:T(8,128)(2,1)} %residual_ref.1) | copy-start | bytes 147460
  19.7 12.7 %copy-start.1 = (bf16[6144,168]{0,1:T(8,128)(2,1)S(1)}, bf16[6144,168]{0,1:T(8,128)(2,1)}, u32[]{:S(2)}) copy-start(bf16[6144,168]{0,1:T(8,128)(2,1)} %param.23) | copy-start | bytes 6193156
  19.7 12.7 %copy-start.2 = (bf16[6144,168]{0,1:T(8,128)(2,1)S(1)}, bf16[6144,168]{0,1:T(8,128)(2,1)}, u32[]{:S(2)}) copy-start(bf16[6144,168]{0,1:T(8,128)(2,1)} %param.24) | copy-start | bytes 6193156
  19.7 12.7 %copy-start.3 = (bf16[168,6144]{1,0:T(8,128)(2,1)S(1)}, bf16[168,6144]{1,0:T(8,128)(2,1)}, u32[]{:S(2)}) copy-start(bf16[168,6144]{1,0:T(8,128)(2,1)} %refs_2_.1) | copy-start | bytes 6193156
  20.6 1.4 %collective-permute-start = (f32[32,768]{1,0:T(8,128)S(1)}, f32[32,768]{1,0:T(8,128)S(1)}, u32[]{:S(2)}, u32[]{:S(2)}) collective-permute-start(f32[32,768]{1,0:T(8,128)S(1)} %get-tuple-element.21.mine_ref), channel_id=1, source_target_pairs={{0,1},{1,0},{2,3},{3,2},{4,5},{5,4},{6,7},{7,6},{8,9},{9,8},{10,11... | collective-permute-start | bytes 294920 | tf_op jit(solution)/shard_map/ppermute | solution.py:514
  45.2 1.3 %collective-permute-start.4 = (f32[32,768]{1,0:T(8,128)S(1)}, f32[32,768]{1,0:T(8,128)S(1)}, u32[]{:S(2)}, u32[]{:S(2)}) collective-permute-start(f32[32,768]{1,0:T(8,128)S(1)} %shard_map.156.mine_ref), channel_id=1, source_target_pairs={{0,1},{1,0},{2,3},{3,2},{4,5},{5,4},{6,7},{7,6},{8,9},{9,8},{10,11... | collective-permute-start | bytes 294920 | tf_op jit(solution)/shard_map/ppermute | solution.py:514

commit v21 on v20

--- a/solution.py
+++ b/solution.py
@@ -391,7 +391,7 @@
         ],
         [VMEM_SPEC, VMEM_SPEC],
         [pltpu.VMEM((rows * count, depth), jnp.float32)],
-        EXCHANGE_FLOPS, out_weight.size * 2, 10,
+        2 * rows * count * out_weight.size, out_weight.size * 2, 10,
     )(pieces, out_weight)
 
 

time: 47.4 us -> 47.4 us (level)
  no operation moved by 1% of the time
where the time goes in v21:
time: 47.4 us; the launch traced here: 47.1 us
  blocking collectives  35.4 us (75%)
  Pallas kernels  6.72 us (14%)
  waiting for transfers between devices  2.59 us (5%)
  starting transfers between devices  1.09 us (2%)
  between operations  0.83 us (2%)
  local copies, waits for them, and re-layouts  0.48 us (1%)
    all_to_all x3, blocking collectives, exchange(): lax.all_to_all(blocks, 'attn', split_axis=0, concat_axis=0, tiled=True)  35.4 us
    pallas_call x1, Pallas kernels, run_experts(): call(expert_kernel, jax.ShapeDtypeStruct(pieces.shape, jnp.bfloat16), [VM...  3.08 us
    ppermute x5, waiting for transfers between devices, swap(): return lax.ppermute(block, 'expert', [(0, 1), (1, 0)])  2.59 us
    ppermute x5, starting transfers between devices, swap(): return lax.ppermute(block, 'expert', [(0, 1), (1, 0)])  1.09 us
    pallas_call x1, Pallas kernels, attend(): call(score_kernel, [jax.ShapeDtypeStruct((row_count, heads, length_max),...  1.03 us
  transfers between devices with their start and end apart: 5, of which 2 were waited for; matrix products, arithmetic and copies ran while one was open for 0% of the time, Pallas kernels for 6%

profile of v21, /device:TPU:0, one launch (start us, length us, event | category | flops | bytes accessed | tf_op | source)
XLA Modules:
  0.0 47.1 jit_solution(11256847521156294851)
XLA Ops:
  0.6 0.0 copy-start.5
  0.6 0.0 copy-start.6
  0.7 0.0 copy-start.7
  0.7 0.0 copy-start.8
  0.7 0.0 copy-start.9
  0.7 0.0 copy-start
  0.7 0.5 %collective-permute-start.1 = (bf16[168,6144]{1,0:T(8,128)(2,1)}, bf16[168,6144]{1,0:T(8,128)(2,1)S(1)}, u32[]{:S(2)}, u32[]{:S(2)}) collective-permute-start(bf16[168,6144]{1,0:T(8,128)(2,1)} %bitcast.6), channel_id=1, source_target_pairs={{0,1},{1,0},{2,3},{3,2},{4,5},{5,4},{6,7},{7,6},{8,9},{9,8},{10,11... | collective-permute-start | bytes 6193160 | tf_op jit(solution)/shard_map/ppermute | solution.py:514
  1.2 0.1 collective-permute-start.2
  1.3 0.4 collective-permute-start.3
  1.7 0.0 copy-start.10
  1.7 0.0 copy-start.11
  1.7 0.0 copy-start.12
  1.7 0.0 copy-done.5
  1.8 0.0 copy-done.6
  1.8 0.0 copy-done.7
  1.8 0.0 copy-done.8
  1.8 0.0 copy-done.9
  1.8 0.2 shard_map.150
  2.0 0.3 copy-done
  2.3 0.0 slice-start
  2.3 1.0 %shard_map.151 = (bf16[4,24,512]{2,1,0:T(8,128)(2,1)S(1)}, f32[4,24,128]{2,1,0:T(8,128)S(1)}) custom-call(bf16[4,24,512]{2,1,0:T(8,128)(2,1)S(1)} %get-tuple-element.16.spread_ref, f32[4,24,128]{2,1,0:T(8,128)S(1)} %get-tuple-element.17.own_ref, s32[4,24,128]{2,1,0:T(8,128)S(1)} %get-tuple-element.18.limit_ref, bf16[4,512,512]{2,1,0:T(8,128)(2,1)S(1)} %copy-done), custom_call_target="tpu_custom_call" | custom-call | flops 50331648 | bytes 2097152 | tf_op jit(solution)/shard_map/pallas_call | solution.py:341
  3.3 0.1 copy-done.10
  3.5 0.0 copy-done.11
  3.5 0.0 copy-done.12
  3.5 0.5 %shard_map.152 = bf16[8,4,3456]{2,1,0:T(4,128)(2,1)S(1)} custom-call(bf16[4,24,512]{2,1,0:T(8,128)(2,1)S(1)} %get-tuple-element.19.probs_ref, f32[4,24,128]{2,1,0:T(8,128)S(1)} %get-tuple-element.20.own_ref, bf16[4,512,512]{2,1,0:T(8,128)(2,1)S(1)} %copy-done.10, bf16[4,512]{1,0:T(4,128)(2,1)S(1)} %copy-done.11, f32[768]{0:T(1024)S(1)} %copy-done.12), custom_call_target="tpu_custom_call" | custom-call | flops 10000000000 | bytes 2097152 | tf_op jit(solution)/shard_map/pallas_call | solution.py:352
  4.0 15.7 %all_to_all.15.pieces = bf16[8,4,3456]{2,1,0:T(4,128)(2,1)S(1)} all-to-all(bf16[8,4,3456]{2,1,0:T(4,128)(2,1)S(1)} %shard_map.152), channel_id=1, replica_groups=mesh['group'=2,'attn'=8,'expert'=2] {'attn'}, dimensions={0} | all-to-all | bytes 442368 | tf_op jit(solution)/shard_map/all_to_all | solution.py:510
  19.7 0.0 slice-done
  19.7 0.0 slice-done.1
  19.7 0.0 copy-start.1
  19.7 0.0 copy-start.2
  19.7 0.9 %shard_map.153 = (f32[32,768]{1,0:T(8,128)S(1)}, f32[8,768]{1,0:T(8,128)S(1)}) custom-call(bf16[8,4,3456]{2,1,0:T(4,128)(2,1)S(1)} %all_to_all.15.pieces, bf16[3072,768]{1,0:T(8,128)(2,1)S(1)} %bitcast.5), custom_call_target="tpu_custom_call" | custom-call | flops 150994944 | bytes 4718592 | tf_op jit(solution)/shard_map/pallas_call | solution.py:386
  20.6 0.1 collective-permute-start
  20.7 1.3 %collective-permute-done.other_ref = f32[32,768]{1,0:T(8,128)S(1)} collective-permute-done((f32[32,768]{1,0:T(8,128)S(1)}, f32[32,768]{1,0:T(8,128)S(1)}, u32[]{:S(2)}, u32[]{:S(2)}) %collective-permute-start) | collective-permute-done | bytes 98336 | tf_op jit(solution)/shard_map/ppermute | solution.py:514
  22.0 0.0 copy-done.4
  22.0 0.1 shard_map.154
  22.1 10.2 %all_to_all.16.pieces = bf16[8,8,768]{2,1,0:T(8,128)(2,1)S(1)} all-to-all(bf16[8,8,768]{2,1,0:T(8,128)(2,1)S(1)} %get-tuple-element.25), channel_id=1, replica_groups=mesh['group'=2,'attn'=8,'expert'=2] {'attn'}, dimensions={0} | all-to-all | bytes 196608 | tf_op jit(solution)/shard_map/all_to_all | solution.py:510
  32.4 0.0 collective-permute-done.1.refs_3_
  32.4 0.0 collective-permute-done.2.refs_4_
  32.4 0.0 collective-permute-done.3.refs_5_
  32.4 0.0 copy-done.3
  32.4 0.0 copy-done.1
  32.4 0.0 copy-done.2
  32.4 3.1 %shard_map.155 = bf16[8,8,768]{2,1,0:T(8,128)(2,1)S(1)} custom-call(f32[8,128]{1,0:T(8,128)S(1)} %get-tuple-element.24.slot_ref, bf16[8,8,768]{2,1,0:T(8,128)(2,1)S(1)} %all_to_all.16.pieces, f32[8,768]{1,0:T(8,128)S(1)} %get-tuple-element.26.gains, bf16[168,6144]{1,0:T(8,128)(2,1)S(1)} %bitcast.7, bf16[168,6144]{1,0:T(8,128)(2,1)S(1)} %bitcast.9, ...), custom_call_target="tpu_custom_call" | custom-call | flops 99090432 | bytes 12386304 | tf_op jit(solution)/shard_map/pallas_call | solution.py:461
  35.5 9.5 %all_to_all.17.pieces = bf16[8,8,768]{2,1,0:T(8,128)(2,1)S(1)} all-to-all(bf16[8,8,768]{2,1,0:T(8,128)(2,1)S(1)} %shard_map.155), channel_id=1, replica_groups=mesh['group'=2,'attn'=8,'expert'=2] {'attn'}, dimensions={0} | all-to-all | bytes 196608 | tf_op jit(solution)/shard_map/all_to_all | solution.py:510
  45.0 0.2 shard_map.156.mine_ref
  45.2 0.0 collective-permute-start.4
  45.2 1.3 %collective-permute-done.4.other_ref = f32[32,768]{1,0:T(8,128)S(1)} collective-permute-done((f32[32,768]{1,0:T(8,128)S(1)}, f32[32,768]{1,0:T(8,128)S(1)}, u32[]{:S(2)}, u32[]{:S(2)}) %collective-permute-start.4) | collective-permute-done | bytes 98336 | tf_op jit(solution)/shard_map/ppermute | solution.py:514
  46.5 0.6 %shard_map.157 = (bf16[32,768]{1,0:T(8,128)(2,1)}, bf16[32,768]{1,0:T(8,128)(2,1)}) custom-call(bf16[32,768]{1,0:T(8,128)(2,1)S(1)} %get-tuple-element.23.stream_ref, f32[32,768]{1,0:T(8,128)S(1)} %shard_map.156.mine_ref, f32[32,768]{1,0:T(8,128)S(1)} %collective-permute-done.4.other_ref), custom_call_target="tpu_custom_call" | custom-call | flops 24576 | bytes 344064 | tf_op jit(solution)/shard_map/pallas_call | solution.py:500
  (5 shorter events, 0.0 us)
Async XLA Ops:
  0.6 1.1 %copy-start.5 = (bf16[4,3072]{1,0:T(4,128)(2,1)S(1)}, bf16[4,3072]{1,0:T(4,128)(2,1)}, u32[]{:S(2)}) copy-start(bf16[4,3072]{1,0:T(4,128)(2,1)} %query_ref.1) | copy-start | bytes 73732
  0.6 1.1 %copy-start.6 = (bf16[4,512]{1,0:T(4,128)(2,1)S(1)}, bf16[4,512]{1,0:T(4,128)(2,1)}, u32[]{:S(2)}) copy-start(bf16[4,512]{1,0:T(4,128)(2,1)} %own_key_ref.1) | copy-start | bytes 12292
  0.7 1.1 %copy-start.7 = (s32[32,4]{0,1:T(4,128)S(1)}, s32[32,4]{0,1:T(4,128)}, u32[]{:S(2)}) copy-start(s32[32,4]{0,1:T(4,128)} %param.26) | copy-start | bytes 1540
  0.7 1.1 %copy-start.8 = (f32[32,4]{0,1:T(4,128)S(1)}, f32[32,4]{0,1:T(4,128)}, u32[]{:S(2)}) copy-start(f32[32,4]{0,1:T(4,128)} %param.27) | copy-start | bytes 1540
  0.7 1.1 %copy-start.9 = (s32[4]{0:T(128)S(1)}, s32[4]{0:T(128)}, u32[]{:S(2)}) copy-start(s32[4]{0:T(128)} %length_ref.1) | copy-start | bytes 52
  0.7 1.6 %copy-start = (bf16[4,512,512]{2,1,0:T(8,128)(2,1)S(1)}, bf16[4,512,512]{2,1,0:T(8,128)(2,1)}, u32[]{:S(2)}) copy-start(bf16[4,512,512]{2,1,0:T(8,128)(2,1)} %key_ref.1) | copy-start | bytes 6291460
  0.7 31.7 %collective-permute-start.1 = (bf16[168,6144]{1,0:T(8,128)(2,1)}, bf16[168,6144]{1,0:T(8,128)(2,1)S(1)}, u32[]{:S(2)}, u32[]{:S(2)}) collective-permute-start(bf16[168,6144]{1,0:T(8,128)(2,1)} %bitcast.6), channel_id=1, source_target_pairs={{0,1},{1,0},{2,3},{3,2},{4,5},{5,4},{6,7},{7,6},{8,9},{9,8},{10,11... | collective-permute-start | bytes 6193160 | tf_op jit(solution)/shard_map/ppermute | solution.py:514
  1.2 31.2 %collective-permute-start.2 = (bf16[168,6144]{1,0:T(8,128)(2,1)}, bf16[168,6144]{1,0:T(8,128)(2,1)S(1)}, u32[]{:S(2)}, u32[]{:S(2)}) collective-permute-start(bf16[168,6144]{1,0:T(8,128)(2,1)} %bitcast.8), channel_id=1, source_target_pairs={{0,1},{1,0},{2,3},{3,2},{4,5},{5,4},{6,7},{7,6},{8,9},{9,8},{10,11... | collective-permute-start | bytes 6193160 | tf_op jit(solution)/shard_map/ppermute | solution.py:514
  1.3 31.1 %collective-permute-start.3 = (bf16[168,6144]{1,0:T(8,128)(2,1)}, bf16[168,6144]{1,0:T(8,128)(2,1)S(1)}, u32[]{:S(2)}, u32[]{:S(2)}) collective-permute-start(bf16[168,6144]{1,0:T(8,128)(2,1)} %refs_2_.1), channel_id=1, source_target_pairs={{0,1},{1,0},{2,3},{3,2},{4,5},{5,4},{6,7},{7,6},{8,9},{9,8},{10,11... | collective-permute-start | bytes 6193160 | tf_op jit(solution)/shard_map/ppermute | solution.py:514
  1.7 1.7 %copy-start.10 = (bf16[4,512,512]{2,1,0:T(8,128)(2,1)S(1)}, bf16[4,512,512]{2,1,0:T(8,128)(2,1)}, u32[]{:S(2)}) copy-start(bf16[4,512,512]{2,1,0:T(8,128)(2,1)} %value_ref.1) | copy-start | bytes 6291460
  1.7 1.7 %copy-start.11 = (bf16[4,512]{1,0:T(4,128)(2,1)S(1)}, bf16[4,512]{1,0:T(4,128)(2,1)}, u32[]{:S(2)}) copy-start(bf16[4,512]{1,0:T(4,128)(2,1)} %own_value_ref.1) | copy-start | bytes 12292
  1.7 1.7 %copy-start.12 = (f32[768]{0:T(1024)S(1)}, f32[768]{0:T(1024)}, u32[]{:S(2)}) copy-start(f32[768]{0:T(1024)} %gain_ref.1) | copy-start | bytes 9220
  2.3 17.4 %slice-start = ((s8[4718592]{0:T(1024)(128)(4,1)}), s8[4194304]{0:T(1024)(128)(4,1)S(1)}, s32[]{:S(2)}) async-start(s8[4718592]{0:T(1024)(128)(4,1)} %bitcast.4), calls=%async_computation.3 | async-start | bytes 8388608
  3.5 16.2 %slice-start.1 = ((s8[4718592]{0:T(1024)(128)(4,1)}), s8[524288]{0:T(1024)(128)(4,1)S(1)}, s32[]{:S(2)}) async-start(s8[4718592]{0:T(1024)(128)(4,1)} %bitcast.4), calls=%async_computation.4 | async-start | bytes 1048576
  3.5 28.9 %copy-start.3 = (bf16[168,6144]{1,0:T(8,128)(2,1)S(1)}, bf16[168,6144]{1,0:T(8,128)(2,1)}, u32[]{:S(2)}) copy-start(bf16[168,6144]{1,0:T(8,128)(2,1)} %refs_2_.1) | copy-start | bytes 6193156
  19.7 2.3 %copy-start.4 = (bf16[32,768]{1,0:T(8,128)(2,1)S(1)}, bf16[32,768]{1,0:T(8,128)(2,1)}, u32[]{:S(2)}) copy-start(bf16[32,768]{1,0:T(8,128)(2,1)} %residual_ref.1) | copy-start | bytes 147460
  19.7 12.7 %copy-start.1 = (bf16[6144,168]{0,1:T(8,128)(2,1)S(1)}, bf16[6144,168]{0,1:T(8,128)(2,1)}, u32[]{:S(2)}) copy-start(bf16[6144,168]{0,1:T(8,128)(2,1)} %param.23) | copy-start | bytes 6193156
  19.7 12.7 %copy-start.2 = (bf16[6144,168]{0,1:T(8,128)(2,1)S(1)}, bf16[6144,168]{0,1:T(8,128)(2,1)}, u32[]{:S(2)}) copy-start(bf16[6144,168]{0,1:T(8,128)(2,1)} %param.24) | copy-start | bytes 6193156
  20.6 1.4 %collective-permute-start = (f32[32,768]{1,0:T(8,128)S(1)}, f32[32,768]{1,0:T(8,128)S(1)}, u32[]{:S(2)}, u32[]{:S(2)}) collective-permute-start(f32[32,768]{1,0:T(8,128)S(1)} %get-tuple-element.21.mine_ref), channel_id=1, source_target_pairs={{0,1},{1,0},{2,3},{3,2},{4,5},{5,4},{6,7},{7,6},{8,9},{9,8},{10,11... | collective-permute-start | bytes 294920 | tf_op jit(solution)/shard_map/ppermute | solution.py:514
  45.2 1.3 %collective-permute-start.4 = (f32[32,768]{1,0:T(8,128)S(1)}, f32[32,768]{1,0:T(8,128)S(1)}, u32[]{:S(2)}, u32[]{:S(2)}) collective-permute-start(f32[32,768]{1,0:T(8,128)S(1)} %shard_map.156.mine_ref), channel_id=1, source_target_pairs={{0,1},{1,0},{2,3},{3,2},{4,5},{5,4},{6,7},{7,6},{8,9},{9,8},{10,11... | collective-permute-start | bytes 294920 | tf_op jit(solution)/shard_map/ppermute | solution.py:514

commit v22 on v21

--- a/solution.py
+++ b/solution.py
@@ -377,7 +377,7 @@
             weight_ref[part, :],
             preferred_element_type=jnp.float32,
         )
-    out_ref[...] = total
+    out_ref[...] = total.astype(jnp.bfloat16)
 
 
 def project(pieces, out_weight):
@@ -386,7 +386,7 @@
     return call(
         project_kernel,
         [
-            jax.ShapeDtypeStruct((rows * count, cols), jnp.float32),
+            jax.ShapeDtypeStruct((rows * count, cols), jnp.bfloat16),
             jax.ShapeDtypeStruct((count, cols), jnp.float32),
         ],
         [VMEM_SPEC, VMEM_SPEC],
@@ -397,7 +397,8 @@
 
 def pick_kernel(sharers, mine_ref, other_ref, residual_ref, taken_ref, stream_ref, out_ref):
     stream = (
-        residual_ref[...].astype(jnp.float32) + (mine_ref[...] + other_ref[...])
+        residual_ref[...].astype(jnp.float32)
+        + (mine_ref[...].astype(jnp.float32) + other_ref[...].astype(jnp.float32))
     ).astype(jnp.bfloat16)
     stream_ref[...] = stream
     chosen = [
@@ -476,7 +477,7 @@
         jnp.concatenate(rows, axis=0).astype(jnp.bfloat16),
         (((0,), (0,)), ((), ())),
         preferred_element_type=jnp.float32,
-    )
+    ).astype(jnp.bfloat16)
 
 
 def combine(sharers, taken, pieces):
@@ -484,7 +485,7 @@
     rows = taken.shape[2]
     return call(
         functools.partial(combine_kernel, sharers),
-        jax.ShapeDtypeStruct((rows, cols), jnp.float32),
+        jax.ShapeDtypeStruct((rows, cols), jnp.bfloat16),
         [VMEM_SPEC] * 2,
         [],
         2 * rows * capacity * count * cols, (count * capacity * 2 + rows * 4) * cols, 4,
@@ -493,7 +494,9 @@
 
 def finish_kernel(stream_ref, mine_ref, other_ref, stream_out_ref, out_ref):
     stream_out_ref[...] = stream_ref[...]
-    out_ref[...] = (mine_ref[...] + other_ref[...]).astype(jnp.bfloat16)
+    out_ref[...] = (
+        mine_ref[...].astype(jnp.float32) + other_ref[...].astype(jnp.float32)
+    ).astype(jnp.bfloat16)
 
 
 def finish(stream, mine, other):

time: 47.4 us -> 47.3 us (level)
  no operation moved by 1% of the time
where the time goes in v22:
time: 47.3 us; the launch traced here: 47 us
  blocking collectives  35.4 us (75%)
  Pallas kernels  6.71 us (14%)
  waiting for transfers between devices  2.44 us (5%)
  starting transfers between devices  1.14 us (2%)
  between operations  0.83 us (2%)
  local copies, waits for them, and re-layouts  0.48 us (1%)
    all_to_all x3, blocking collectives, exchange(): lax.all_to_all(blocks, 'attn', split_axis=0, concat_axis=0, tiled=True)  35.4 us
    pallas_call x1, Pallas kernels, run_experts(): call(expert_kernel, jax.ShapeDtypeStruct(pieces.shape, jnp.bfloat16), [VM...  3.08 us
    ppermute x5, waiting for transfers between devices, swap(): return lax.ppermute(block, 'expert', [(0, 1), (1, 0)])  2.44 us
    ppermute x5, starting transfers between devices, swap(): return lax.ppermute(block, 'expert', [(0, 1), (1, 0)])  1.14 us
    pallas_call x1, Pallas kernels, attend(): call(score_kernel, [jax.ShapeDtypeStruct((row_count, heads, length_max),...  1.03 us
  transfers between devices with their start and end apart: 5, of which 2 were waited for; matrix products, arithmetic and copies ran while one was open for 0% of the time, Pallas kernels for 6%

profile of v22, /device:TPU:0, one launch (start us, length us, event | category | flops | bytes accessed | tf_op | source)
XLA Modules:
  0.0 47.0 jit_solution(2038618207845479828)
XLA Ops:
  0.6 0.0 copy-start.5
  0.6 0.0 copy-start.6
  0.7 0.0 copy-start.7
  0.7 0.0 copy-start.8
  0.7 0.0 copy-start.9
  0.7 0.0 copy-start
  0.7 0.5 %collective-permute-start.1 = (bf16[168,6144]{1,0:T(8,128)(2,1)}, bf16[168,6144]{1,0:T(8,128)(2,1)S(1)}, u32[]{:S(2)}, u32[]{:S(2)}) collective-permute-start(bf16[168,6144]{1,0:T(8,128)(2,1)} %bitcast.6), channel_id=1, source_target_pairs={{0,1},{1,0},{2,3},{3,2},{4,5},{5,4},{6,7},{7,6},{8,9},{9,8},{10,11... | collective-permute-start | bytes 6193160 | tf_op jit(solution)/shard_map/ppermute | solution.py:517
  1.2 0.1 collective-permute-start.2
  1.3 0.4 collective-permute-start.3
  1.7 0.0 copy-start.10
  1.7 0.0 copy-start.11
  1.7 0.0 copy-start.12
  1.7 0.0 copy-done.5
  1.8 0.0 copy-done.6
  1.8 0.0 copy-done.7
  1.8 0.0 copy-done.8
  1.8 0.0 copy-done.9
  1.8 0.2 shard_map.150
  2.0 0.3 copy-done
  2.3 0.0 slice-start
  2.3 1.0 %shard_map.151 = (bf16[4,24,512]{2,1,0:T(8,128)(2,1)S(1)}, f32[4,24,128]{2,1,0:T(8,128)S(1)}) custom-call(bf16[4,24,512]{2,1,0:T(8,128)(2,1)S(1)} %get-tuple-element.16.spread_ref, f32[4,24,128]{2,1,0:T(8,128)S(1)} %get-tuple-element.17.own_ref, s32[4,24,128]{2,1,0:T(8,128)S(1)} %get-tuple-element.18.limit_ref, bf16[4,512,512]{2,1,0:T(8,128)(2,1)S(1)} %copy-done), custom_call_target="tpu_custom_call" | custom-call | flops 50331648 | bytes 2097152 | tf_op jit(solution)/shard_map/pallas_call | solution.py:341
  3.3 0.1 copy-done.10
  3.5 0.0 copy-done.11
  3.5 0.0 copy-done.12
  3.5 0.5 %shard_map.152 = bf16[8,4,3456]{2,1,0:T(4,128)(2,1)S(1)} custom-call(bf16[4,24,512]{2,1,0:T(8,128)(2,1)S(1)} %get-tuple-element.19.probs_ref, f32[4,24,128]{2,1,0:T(8,128)S(1)} %get-tuple-element.20.own_ref, bf16[4,512,512]{2,1,0:T(8,128)(2,1)S(1)} %copy-done.10, bf16[4,512]{1,0:T(4,128)(2,1)S(1)} %copy-done.11, f32[768]{0:T(1024)S(1)} %copy-done.12), custom_call_target="tpu_custom_call" | custom-call | flops 10000000000 | bytes 2097152 | tf_op jit(solution)/shard_map/pallas_call | solution.py:352
  4.0 15.7 %all_to_all.15.pieces = bf16[8,4,3456]{2,1,0:T(4,128)(2,1)S(1)} all-to-all(bf16[8,4,3456]{2,1,0:T(4,128)(2,1)S(1)} %shard_map.152), channel_id=1, replica_groups=mesh['group'=2,'attn'=8,'expert'=2] {'attn'}, dimensions={0} | all-to-all | bytes 442368 | tf_op jit(solution)/shard_map/all_to_all | solution.py:513
  19.7 0.0 slice-done
  19.7 0.0 slice-done.1
  19.7 0.0 copy-start.1
  19.7 0.0 copy-start.2
  19.7 0.9 %shard_map.153 = (bf16[32,768]{1,0:T(8,128)(2,1)S(1)}, f32[8,768]{1,0:T(8,128)S(1)}) custom-call(bf16[8,4,3456]{2,1,0:T(4,128)(2,1)S(1)} %all_to_all.15.pieces, bf16[3072,768]{1,0:T(8,128)(2,1)S(1)} %bitcast.5), custom_call_target="tpu_custom_call" | custom-call | flops 150994944 | bytes 4718592 | tf_op jit(solution)/shard_map/pallas_call | solution.py:386
  20.6 0.0 collective-permute-start
  20.7 1.2 %collective-permute-done.other_ref = bf16[32,768]{1,0:T(8,128)(2,1)S(1)} collective-permute-done((bf16[32,768]{1,0:T(8,128)(2,1)S(1)}, bf16[32,768]{1,0:T(8,128)(2,1)S(1)}, u32[]{:S(2)}, u32[]{:S(2)}) %collective-permute-start) | collective-permute-done | bytes 49184 | tf_op jit(solution)/shard_map/ppermute | solution.py:517
  21.9 0.0 copy-done.4
  21.9 0.1 shard_map.154
  22.1 10.2 %all_to_all.16.pieces = bf16[8,8,768]{2,1,0:T(8,128)(2,1)S(1)} all-to-all(bf16[8,8,768]{2,1,0:T(8,128)(2,1)S(1)} %get-tuple-element.25), channel_id=1, replica_groups=mesh['group'=2,'attn'=8,'expert'=2] {'attn'}, dimensions={0} | all-to-all | bytes 196608 | tf_op jit(solution)/shard_map/all_to_all | solution.py:513
  32.3 0.0 collective-permute-done.1.refs_3_
  32.3 0.0 collective-permute-done.2.refs_4_
  32.3 0.0 collective-permute-done.3.refs_5_
  32.3 0.0 copy-done.3
  32.3 0.0 copy-done.1
  32.3 0.0 copy-done.2
  32.3 3.1 %shard_map.155 = bf16[8,8,768]{2,1,0:T(8,128)(2,1)S(1)} custom-call(f32[8,128]{1,0:T(8,128)S(1)} %get-tuple-element.24.slot_ref, bf16[8,8,768]{2,1,0:T(8,128)(2,1)S(1)} %all_to_all.16.pieces, f32[8,768]{1,0:T(8,128)S(1)} %get-tuple-element.26.gains, bf16[168,6144]{1,0:T(8,128)(2,1)S(1)} %bitcast.7, bf16[168,6144]{1,0:T(8,128)(2,1)S(1)} %bitcast.9, ...), custom_call_target="tpu_custom_call" | custom-call | flops 99090432 | bytes 12386304 | tf_op jit(solution)/shard_map/pallas_call | solution.py:462
  35.4 9.5 %all_to_all.17.pieces = bf16[8,8,768]{2,1,0:T(8,128)(2,1)S(1)} all-to-all(bf16[8,8,768]{2,1,0:T(8,128)(2,1)S(1)} %shard_map.155), channel_id=1, replica_groups=mesh['group'=2,'attn'=8,'expert'=2] {'attn'}, dimensions={0} | all-to-all | bytes 196608 | tf_op jit(solution)/shard_map/all_to_all | solution.py:513
  44.9 0.2 shard_map.156.mine_ref
  45.1 0.1 collective-permute-start.4
  45.2 1.2 %collective-permute-done.4.other_ref = bf16[32,768]{1,0:T(8,128)(2,1)S(1)} collective-permute-done((bf16[32,768]{1,0:T(8,128)(2,1)S(1)}, bf16[32,768]{1,0:T(8,128)(2,1)S(1)}, u32[]{:S(2)}, u32[]{:S(2)}) %collective-permute-start.4) | collective-permute-done | bytes 49184 | tf_op jit(solution)/shard_map/ppermute | solution.py:517
  46.4 0.6 %shard_map.157 = (bf16[32,768]{1,0:T(8,128)(2,1)}, bf16[32,768]{1,0:T(8,128)(2,1)}) custom-call(bf16[32,768]{1,0:T(8,128)(2,1)S(1)} %get-tuple-element.23.stream_ref, bf16[32,768]{1,0:T(8,128)(2,1)S(1)} %shard_map.156.mine_ref, bf16[32,768]{1,0:T(8,128)(2,1)S(1)} %collective-permute-done.4.other_ref), custom_call_target="tpu_custom_call" | custom-call | flops 24576 | bytes 344064 | tf_op jit(solution)/shard_map/pallas_call | solution.py:503
  (5 shorter events, 0.0 us)
Async XLA Ops:
  0.6 1.1 %copy-start.5 = (bf16[4,3072]{1,0:T(4,128)(2,1)S(1)}, bf16[4,3072]{1,0:T(4,128)(2,1)}, u32[]{:S(2)}) copy-start(bf16[4,3072]{1,0:T(4,128)(2,1)} %query_ref.1) | copy-start | bytes 73732
  0.6 1.1 %copy-start.6 = (bf16[4,512]{1,0:T(4,128)(2,1)S(1)}, bf16[4,512]{1,0:T(4,128)(2,1)}, u32[]{:S(2)}) copy-start(bf16[4,512]{1,0:T(4,128)(2,1)} %own_key_ref.1) | copy-start | bytes 12292
  0.7 1.1 %copy-start.7 = (s32[32,4]{0,1:T(4,128)S(1)}, s32[32,4]{0,1:T(4,128)}, u32[]{:S(2)}) copy-start(s32[32,4]{0,1:T(4,128)} %param.26) | copy-start | bytes 1540
  0.7 1.1 %copy-start.8 = (f32[32,4]{0,1:T(4,128)S(1)}, f32[32,4]{0,1:T(4,128)}, u32[]{:S(2)}) copy-start(f32[32,4]{0,1:T(4,128)} %param.27) | copy-start | bytes 1540
  0.7 1.1 %copy-start.9 = (s32[4]{0:T(128)S(1)}, s32[4]{0:T(128)}, u32[]{:S(2)}) copy-start(s32[4]{0:T(128)} %length_ref.1) | copy-start | bytes 52
  0.7 1.6 %copy-start = (bf16[4,512,512]{2,1,0:T(8,128)(2,1)S(1)}, bf16[4,512,512]{2,1,0:T(8,128)(2,1)}, u32[]{:S(2)}) copy-start(bf16[4,512,512]{2,1,0:T(8,128)(2,1)} %key_ref.1) | copy-start | bytes 6291460
  0.7 31.6 %collective-permute-start.1 = (bf16[168,6144]{1,0:T(8,128)(2,1)}, bf16[168,6144]{1,0:T(8,128)(2,1)S(1)}, u32[]{:S(2)}, u32[]{:S(2)}) collective-permute-start(bf16[168,6144]{1,0:T(8,128)(2,1)} %bitcast.6), channel_id=1, source_target_pairs={{0,1},{1,0},{2,3},{3,2},{4,5},{5,4},{6,7},{7,6},{8,9},{9,8},{10,11... | collective-permute-start | bytes 6193160 | tf_op jit(solution)/shard_map/ppermute | solution.py:517
  1.2 31.1 %collective-permute-start.2 = (bf16[168,6144]{1,0:T(8,128)(2,1)}, bf16[168,6144]{1,0:T(8,128)(2,1)S(1)}, u32[]{:S(2)}, u32[]{:S(2)}) collective-permute-start(bf16[168,6144]{1,0:T(8,128)(2,1)} %bitcast.8), channel_id=1, source_target_pairs={{0,1},{1,0},{2,3},{3,2},{4,5},{5,4},{6,7},{7,6},{8,9},{9,8},{10,11... | collective-permute-start | bytes 6193160 | tf_op jit(solution)/shard_map/ppermute | solution.py:517
  1.3 31.0 %collective-permute-start.3 = (bf16[168,6144]{1,0:T(8,128)(2,1)}, bf16[168,6144]{1,0:T(8,128)(2,1)S(1)}, u32[]{:S(2)}, u32[]{:S(2)}) collective-permute-start(bf16[168,6144]{1,0:T(8,128)(2,1)} %refs_2_.1), channel_id=1, source_target_pairs={{0,1},{1,0},{2,3},{3,2},{4,5},{5,4},{6,7},{7,6},{8,9},{9,8},{10,11... | collective-permute-start | bytes 6193160 | tf_op jit(solution)/shard_map/ppermute | solution.py:517
  1.7 1.7 %copy-start.10 = (bf16[4,512,512]{2,1,0:T(8,128)(2,1)S(1)}, bf16[4,512,512]{2,1,0:T(8,128)(2,1)}, u32[]{:S(2)}) copy-start(bf16[4,512,512]{2,1,0:T(8,128)(2,1)} %value_ref.1) | copy-start | bytes 6291460
  1.7 1.7 %copy-start.11 = (bf16[4,512]{1,0:T(4,128)(2,1)S(1)}, bf16[4,512]{1,0:T(4,128)(2,1)}, u32[]{:S(2)}) copy-start(bf16[4,512]{1,0:T(4,128)(2,1)} %own_value_ref.1) | copy-start | bytes 12292
  1.7 1.7 %copy-start.12 = (f32[768]{0:T(1024)S(1)}, f32[768]{0:T(1024)}, u32[]{:S(2)}) copy-start(f32[768]{0:T(1024)} %gain_ref.1) | copy-start | bytes 9220
  2.3 17.4 %slice-start = ((s8[4718592]{0:T(1024)(128)(4,1)}), s8[4194304]{0:T(1024)(128)(4,1)S(1)}, s32[]{:S(2)}) async-start(s8[4718592]{0:T(1024)(128)(4,1)} %bitcast.4), calls=%async_computation.3 | async-start | bytes 8388608
  3.5 16.2 %slice-start.1 = ((s8[4718592]{0:T(1024)(128)(4,1)}), s8[524288]{0:T(1024)(128)(4,1)S(1)}, s32[]{:S(2)}) async-start(s8[4718592]{0:T(1024)(128)(4,1)} %bitcast.4), calls=%async_computation.4 | async-start | bytes 1048576
  3.5 28.8 %copy-start.3 = (bf16[168,6144]{1,0:T(8,128)(2,1)S(1)}, bf16[168,6144]{1,0:T(8,128)(2,1)}, u32[]{:S(2)}) copy-start(bf16[168,6144]{1,0:T(8,128)(2,1)} %refs_2_.1) | copy-start | bytes 6193156
  19.7 2.2 %copy-start.4 = (bf16[32,768]{1,0:T(8,128)(2,1)S(1)}, bf16[32,768]{1,0:T(8,128)(2,1)}, u32[]{:S(2)}) copy-start(bf16[32,768]{1,0:T(8,128)(2,1)} %residual_ref.1) | copy-start | bytes 147460
  19.7 12.6 %copy-start.1 = (bf16[6144,168]{0,1:T(8,128)(2,1)S(1)}, bf16[6144,168]{0,1:T(8,128)(2,1)}, u32[]{:S(2)}) copy-start(bf16[6144,168]{0,1:T(8,128)(2,1)} %param.23) | copy-start | bytes 6193156
  19.7 12.6 %copy-start.2 = (bf16[6144,168]{0,1:T(8,128)(2,1)S(1)}, bf16[6144,168]{0,1:T(8,128)(2,1)}, u32[]{:S(2)}) copy-start(bf16[6144,168]{0,1:T(8,128)(2,1)} %param.24) | copy-start | bytes 6193156
  20.6 1.3 %collective-permute-start = (bf16[32,768]{1,0:T(8,128)(2,1)S(1)}, bf16[32,768]{1,0:T(8,128)(2,1)S(1)}, u32[]{:S(2)}, u32[]{:S(2)}) collective-permute-start(bf16[32,768]{1,0:T(8,128)(2,1)S(1)} %get-tuple-element.21.mine_ref), channel_id=1, source_target_pairs={{0,1},{1,0},{2,3},{3,2},{4,5},{5,4},{6,7},{7,6},{8,9},{9,8},{10,11... | collective-permute-start | bytes 147464 | tf_op jit(solution)/shard_map/ppermute | solution.py:517
  45.1 1.3 %collective-permute-start.4 = (bf16[32,768]{1,0:T(8,128)(2,1)S(1)}, bf16[32,768]{1,0:T(8,128)(2,1)S(1)}, u32[]{:S(2)}, u32[]{:S(2)}) collective-permute-start(bf16[32,768]{1,0:T(8,128)(2,1)S(1)} %shard_map.156.mine_ref), channel_id=1, source_target_pairs={{0,1},{1,0},{2,3},{3,2},{4,5},{5,4},{6,7},{7,6},{8,9},{9,8},{10,11... | collective-permute-start | bytes 147464 | tf_op jit(solution)/shard_map/ppermute | solution.py:517

commit v23 on v21

--- a/solution.py
+++ b/solution.py
@@ -205,8 +205,8 @@
 
 
 def prepare_kernel(sharers, length_ref, earlier_ref, routes_ref, weight_ref, query_ref,
-                   own_key_ref, spread_ref, own_ref, limit_ref, taken_ref, slot_ref, query_rows,
-                   key_rows):
+                   own_key_ref, own_value_ref, gain_ref, spread_ref, own_ref, limit_ref, taken_ref,
+                   slot_ref, value_rows, part_ref, query_rows, key_rows):
     row_count = query_ref.shape[0]
     kv_local = own_key_ref.shape[1] // HEAD_DIM
     group = HEADS // KV_HEADS
@@ -220,6 +220,17 @@
                 :, index * HEAD_DIM : (index + 1) * HEAD_DIM
             ].astype(jnp.float32)
             key_rows[rows, :] = own_key
+            value_rows[rows, :] = own_value_ref[
+                :, g * HEAD_DIM : (g + 1) * HEAD_DIM
+            ].astype(jnp.float32)
+    gain_row = gain_ref[...].reshape(1, -1)
+    half = gain_row.shape[1] // 2
+    row = lax.broadcasted_iota(jnp.int32, (row_count, half), 0)
+    left = jnp.broadcast_to(gain_row[:, :half], (row_count, half))
+    right = jnp.broadcast_to(gain_row[:, half:], (row_count, half))
+    gain = jnp.where(row % 2 == 0, left, right)
+    upper = gain.astype(jnp.bfloat16).astype(jnp.float32)
+    part_ref[...] = jnp.where(row < 2, upper, gain - upper).astype(jnp.bfloat16)
     scale = 1.0 / math.sqrt(HEAD_DIM)
     lengths = length_ref[...].reshape(1, -1)
     head = lax.broadcasted_iota(jnp.int32, (heads, 1), 0) // group
@@ -252,7 +263,8 @@
 
 
 def prepare(
-    sharers, capacity, cache_length, earlier, routes, route_weight, queries, new_key
+    sharers, capacity, cache_length, earlier, routes, route_weight, queries, new_key, new_value,
+    gain,
 ):
     row_count, width = queries.shape
     heads = width // HEAD_DIM
@@ -265,11 +277,13 @@
             jax.ShapeDtypeStruct((row_count, heads, HEAD_DIM), jnp.int32),
             jax.ShapeDtypeStruct((HELD, capacity, routes.shape[1]), jnp.float32),
             jax.ShapeDtypeStruct((capacity, HEAD_DIM), jnp.float32),
+            jax.ShapeDtypeStruct((heads * row_count, HEAD_DIM), jnp.float32),
+            jax.ShapeDtypeStruct((row_count, gain.shape[0] // 2), jnp.bfloat16),
         ],
-        [VMEM_SPEC] * 6,
+        [VMEM_SPEC] * 8,
         [table, table],
         queries.size * 8, queries.size * 16, 4,
-    )(cache_length, earlier, routes, route_weight, queries, new_key)
+    )(cache_length, earlier, routes, route_weight, queries, new_key, new_value, gain)
 
 
 def score_kernel(spread_ref, own_ref, limit_ref, key_ref, probs_ref, own_probs_ref):
@@ -299,16 +313,11 @@
             own_probs_ref[r] = jnp.broadcast_to(own_prob[rows], own_probs_ref.shape[1:])
 
 
-def value_kernel(probs_ref, own_ref, value_ref, own_value_ref, gain_ref, out_ref, value_rows,
-                 result_rows):
+def value_kernel(probs_ref, own_ref, value_ref, value_rows, part_ref, out_ref, result_rows):
     row_count, length_max, width = value_ref.shape
     kv_local = width // HEAD_DIM
     group = HEADS // KV_HEADS
     heads = kv_local * group
-    for g in range(kv_local):
-        own_value = own_value_ref[:, g * HEAD_DIM : (g + 1) * HEAD_DIM].astype(jnp.float32)
-        for i in range(group):
-            value_rows[pl.ds((g * group + i) * row_count, row_count), :] = own_value
     head = lax.broadcasted_iota(jnp.int32, (heads, 1), 0) // group
     for r in range(row_count):
         strided = pl.ds(r, heads, stride=row_count)
@@ -322,19 +331,12 @@
         rows = result_rows[pl.ds(index * row_count, row_count), :].astype(jnp.bfloat16)
         for copy in range(out_ref.shape[0]):
             out_ref[copy, :, index * HEAD_DIM : (index + 1) * HEAD_DIM] = rows
-    gain_row = gain_ref[...].reshape(1, -1)
-    half = gain_row.shape[1] // 2
-    row = lax.broadcasted_iota(jnp.int32, (row_count, half), 0)
-    left = jnp.broadcast_to(gain_row[:, :half], (row_count, half))
-    right = jnp.broadcast_to(gain_row[:, half:], (row_count, half))
-    gain = jnp.where(row % 2 == 0, left, right)
-    upper = gain.astype(jnp.bfloat16).astype(jnp.float32)
-    parts = jnp.where(row < 2, upper, gain - upper).astype(jnp.bfloat16)
+    parts = part_ref[...]
     for copy in range(out_ref.shape[0]):
         out_ref[copy, :, heads * HEAD_DIM :] = parts
 
 
-def attend(count, spread, own, limit, key_cache, value_cache, new_value, gain):
+def attend(count, spread, own, limit, key_cache, value_cache, value_rows, parts):
     row_count, heads, _ = spread.shape
     length_max = key_cache.shape[1]
     table = pltpu.VMEM((heads * row_count, HEAD_DIM), jnp.float32)
@@ -348,14 +350,14 @@
         [],
         2 * key_cache.size * heads, key_cache.size * 2, 8,
     )(spread, own, limit, key_cache)
-    width = heads * HEAD_DIM + gain.shape[0] // 2
+    width = heads * HEAD_DIM + parts.shape[1]
     return call(
         value_kernel,
         jax.ShapeDtypeStruct((count, row_count, width), jnp.bfloat16),
         [VMEM_SPEC] * 5,
-        [table, table],
+        [table],
         EXCHANGE_FLOPS, value_cache.size * 2, 8,
-    )(probs, own_probs, value_cache, new_value, gain)
+    )(probs, own_probs, value_cache, value_rows, parts)
 
 
 def project_kernel(pieces, weight_ref, out_ref, gain_ref, stack):
@@ -536,12 +538,13 @@
 
     earlier = order(routes.shape[0])
     weights = (gate_weight.T, up_weight.T, down_weight)
-    spread, own, limit, taken, slots = prepare(
-        sharers, capacity, cache_length, earlier, routes.T, route_weight.T, queries, new_key
+    spread, own, limit, taken, slots, value_rows, parts = prepare(
+        sharers, capacity, cache_length, earlier, routes.T, route_weight.T, queries, new_key,
+        new_value, ln_gain,
     )
     other_weights = [swap(block) for block in lax.optimization_barrier(weights)]
     attended = exchange(
-        attend(count, spread, own, limit, key_cache, value_cache, new_value, ln_gain)
+        attend(count, spread, own, limit, key_cache, value_cache, value_rows, parts)
     )
     mine, gains = project(attended, out_weight)
     stream, chosen = pick(sharers, count, mine, swap(mine), residual, taken)

time: 47.4 us -> 47.4 us (level)
  no operation moved by 1% of the time
where the time goes in v23:
time: 47.4 us; the launch traced here: 47.1 us
  blocking collectives  35.4 us (75%)
  Pallas kernels  6.71 us (14%)
  waiting for transfers between devices  2.59 us (5%)
  starting transfers between devices  1.09 us (2%)
  between operations  0.83 us (2%)
  local copies, waits for them, and re-layouts  0.48 us (1%)
    all_to_all x3, blocking collectives, exchange(): lax.all_to_all(blocks, 'attn', split_axis=0, concat_axis=0, tiled=True)  35.4 us
    pallas_call x1, Pallas kernels, run_experts(): call(expert_kernel, jax.ShapeDtypeStruct(pieces.shape, jnp.bfloat16), [VM...  3.08 us
    ppermute x5, waiting for transfers between devices, swap(): return lax.ppermute(block, 'expert', [(0, 1), (1, 0)])  2.59 us
    ppermute x5, starting transfers between devices, swap(): return lax.ppermute(block, 'expert', [(0, 1), (1, 0)])  1.09 us
    pallas_call x1, Pallas kernels, attend(): call(score_kernel, [jax.ShapeDtypeStruct((row_count, heads, length_max),...  1.03 us
  transfers between devices with their start and end apart: 5, of which 2 were waited for; matrix products, arithmetic and copies ran while one was open for 0% of the time, Pallas kernels for 6%

profile of v23, /device:TPU:0, one launch (start us, length us, event | category | flops | bytes accessed | tf_op | source)
XLA Modules:
  0.0 47.1 jit_solution(6355106404477979120)
XLA Ops:
  0.6 0.0 copy-start.5
  0.6 0.0 copy-start.6
  0.7 0.0 copy-start.7
  0.7 0.0 copy-start.8
  0.7 0.0 copy-start.9
  0.7 0.0 copy-start.10
  0.7 0.0 copy-start.11
  0.7 0.0 copy-start
  0.7 0.5 %collective-permute-start.1 = (bf16[168,6144]{1,0:T(8,128)(2,1)}, bf16[168,6144]{1,0:T(8,128)(2,1)S(1)}, u32[]{:S(2)}, u32[]{:S(2)}) collective-permute-start(bf16[168,6144]{1,0:T(8,128)(2,1)} %bitcast.6), channel_id=1, source_target_pairs={{0,1},{1,0},{2,3},{3,2},{4,5},{5,4},{6,7},{7,6},{8,9},{9,8},{10,11... | collective-permute-start | bytes 6193160 | tf_op jit(solution)/shard_map/ppermute | solution.py:516
  1.2 0.1 collective-permute-start.2
  1.3 0.4 collective-permute-start.3
  1.7 0.0 copy-start.12
  1.8 0.0 copy-done.5
  1.8 0.0 copy-done.6
  1.8 0.0 copy-done.7
  1.8 0.0 copy-done.8
  1.8 0.0 copy-done.9
  1.8 0.0 copy-done.10
  1.8 0.0 copy-done.11
  1.8 0.2 shard_map.150
  2.0 0.3 copy-done
  2.3 0.0 slice-start
  2.3 1.0 %shard_map.151 = (bf16[4,24,512]{2,1,0:T(8,128)(2,1)S(1)}, f32[4,24,128]{2,1,0:T(8,128)S(1)}) custom-call(bf16[4,24,512]{2,1,0:T(8,128)(2,1)S(1)} %get-tuple-element.18.spread_ref, f32[4,24,128]{2,1,0:T(8,128)S(1)} %get-tuple-element.19.own_ref, s32[4,24,128]{2,1,0:T(8,128)S(1)} %get-tuple-element.20.limit_ref, bf16[4,512,512]{2,1,0:T(8,128)(2,1)S(1)} %copy-done), custom_call_target="tpu_custom_call" | custom-call | flops 50331648 | bytes 2097152 | tf_op jit(solution)/shard_map/pallas_call | solution.py:343
  3.4 0.1 copy-done.12
  3.5 0.5 %shard_map.152 = bf16[8,4,3456]{2,1,0:T(4,128)(2,1)S(1)} custom-call(bf16[4,24,512]{2,1,0:T(8,128)(2,1)S(1)} %get-tuple-element.21.probs_ref, f32[4,24,128]{2,1,0:T(8,128)S(1)} %get-tuple-element.22.own_ref, bf16[4,512,512]{2,1,0:T(8,128)(2,1)S(1)} %copy-done.12, f32[96,128]{1,0:T(8,128)S(1)} %get-tuple-element.23.value_rows, ...), custom_call_target="tpu_custom_call" | custom-call | flops 10000000000 | bytes 2097152 | tf_op jit(solution)/shard_map/pallas_call | solution.py:354
  4.0 15.7 %all_to_all.15.pieces = bf16[8,4,3456]{2,1,0:T(4,128)(2,1)S(1)} all-to-all(bf16[8,4,3456]{2,1,0:T(4,128)(2,1)S(1)} %shard_map.152), channel_id=1, replica_groups=mesh['group'=2,'attn'=8,'expert'=2] {'attn'}, dimensions={0} | all-to-all | bytes 442368 | tf_op jit(solution)/shard_map/all_to_all | solution.py:512
  19.7 0.0 slice-done
  19.7 0.0 slice-done.1
  19.7 0.0 copy-start.1
  19.7 0.0 copy-start.2
  19.7 0.9 %shard_map.153 = (f32[32,768]{1,0:T(8,128)S(1)}, f32[8,768]{1,0:T(8,128)S(1)}) custom-call(bf16[8,4,3456]{2,1,0:T(4,128)(2,1)S(1)} %all_to_all.15.pieces, bf16[3072,768]{1,0:T(8,128)(2,1)S(1)} %bitcast.5), custom_call_target="tpu_custom_call" | custom-call | flops 150994944 | bytes 4718592 | tf_op jit(solution)/shard_map/pallas_call | solution.py:388
  20.6 0.1 collective-permute-start
  20.7 1.3 %collective-permute-done.other_ref = f32[32,768]{1,0:T(8,128)S(1)} collective-permute-done((f32[32,768]{1,0:T(8,128)S(1)}, f32[32,768]{1,0:T(8,128)S(1)}, u32[]{:S(2)}, u32[]{:S(2)}) %collective-permute-start) | collective-permute-done | bytes 98336 | tf_op jit(solution)/shard_map/ppermute | solution.py:516
  22.0 0.0 copy-done.4
  22.0 0.1 shard_map.154
  22.1 10.2 %all_to_all.16.pieces = bf16[8,8,768]{2,1,0:T(8,128)(2,1)S(1)} all-to-all(bf16[8,8,768]{2,1,0:T(8,128)(2,1)S(1)} %get-tuple-element.29), channel_id=1, replica_groups=mesh['group'=2,'attn'=8,'expert'=2] {'attn'}, dimensions={0} | all-to-all | bytes 196608 | tf_op jit(solution)/shard_map/all_to_all | solution.py:512
  32.4 0.0 collective-permute-done.1.refs_3_
  32.4 0.0 collective-permute-done.2.refs_4_
  32.4 0.0 collective-permute-done.3.refs_5_
  32.4 0.0 copy-done.3
  32.4 0.0 copy-done.1
  32.4 0.0 copy-done.2
  32.4 3.1 %shard_map.155 = bf16[8,8,768]{2,1,0:T(8,128)(2,1)S(1)} custom-call(f32[8,128]{1,0:T(8,128)S(1)} %get-tuple-element.28.slot_ref, bf16[8,8,768]{2,1,0:T(8,128)(2,1)S(1)} %all_to_all.16.pieces, f32[8,768]{1,0:T(8,128)S(1)} %get-tuple-element.30.gains, bf16[168,6144]{1,0:T(8,128)(2,1)S(1)} %bitcast.7, bf16[168,6144]{1,0:T(8,128)(2,1)S(1)} %bitcast.9, ...), custom_call_target="tpu_custom_call" | custom-call | flops 99090432 | bytes 12386304 | tf_op jit(solution)/shard_map/pallas_call | solution.py:463
  35.5 9.5 %all_to_all.17.pieces = bf16[8,8,768]{2,1,0:T(8,128)(2,1)S(1)} all-to-all(bf16[8,8,768]{2,1,0:T(8,128)(2,1)S(1)} %shard_map.155), channel_id=1, replica_groups=mesh['group'=2,'attn'=8,'expert'=2] {'attn'}, dimensions={0} | all-to-all | bytes 196608 | tf_op jit(solution)/shard_map/all_to_all | solution.py:512
  45.0 0.2 shard_map.156.mine_ref
  45.2 0.0 collective-permute-start.4
  45.2 1.3 %collective-permute-done.4.other_ref = f32[32,768]{1,0:T(8,128)S(1)} collective-permute-done((f32[32,768]{1,0:T(8,128)S(1)}, f32[32,768]{1,0:T(8,128)S(1)}, u32[]{:S(2)}, u32[]{:S(2)}) %collective-permute-start.4) | collective-permute-done | bytes 98336 | tf_op jit(solution)/shard_map/ppermute | solution.py:516
  46.5 0.6 %shard_map.157 = (bf16[32,768]{1,0:T(8,128)(2,1)}, bf16[32,768]{1,0:T(8,128)(2,1)}) custom-call(bf16[32,768]{1,0:T(8,128)(2,1)S(1)} %get-tuple-element.27.stream_ref, f32[32,768]{1,0:T(8,128)S(1)} %shard_map.156.mine_ref, f32[32,768]{1,0:T(8,128)S(1)} %collective-permute-done.4.other_ref), custom_call_target="tpu_custom_call" | custom-call | flops 24576 | bytes 344064 | tf_op jit(solution)/shard_map/pallas_call | solution.py:502
  (5 shorter events, 0.0 us)
Async XLA Ops:
  0.6 1.1 %copy-start.5 = (bf16[4,3072]{1,0:T(4,128)(2,1)S(1)}, bf16[4,3072]{1,0:T(4,128)(2,1)}, u32[]{:S(2)}) copy-start(bf16[4,3072]{1,0:T(4,128)(2,1)} %query_ref.1) | copy-start | bytes 73732
  0.6 1.1 %copy-start.6 = (bf16[4,512]{1,0:T(4,128)(2,1)S(1)}, bf16[4,512]{1,0:T(4,128)(2,1)}, u32[]{:S(2)}) copy-start(bf16[4,512]{1,0:T(4,128)(2,1)} %own_key_ref.1) | copy-start | bytes 12292
  0.7 1.1 %copy-start.7 = (bf16[4,512]{1,0:T(4,128)(2,1)S(1)}, bf16[4,512]{1,0:T(4,128)(2,1)}, u32[]{:S(2)}) copy-start(bf16[4,512]{1,0:T(4,128)(2,1)} %own_value_ref.1) | copy-start | bytes 12292
  0.7 1.1 %copy-start.8 = (f32[768]{0:T(1024)S(1)}, f32[768]{0:T(1024)}, u32[]{:S(2)}) copy-start(f32[768]{0:T(1024)} %gain_ref.1) | copy-start | bytes 9220
  0.7 1.1 %copy-start.9 = (s32[32,4]{0,1:T(4,128)S(1)}, s32[32,4]{0,1:T(4,128)}, u32[]{:S(2)}) copy-start(s32[32,4]{0,1:T(4,128)} %param.26) | copy-start | bytes 1540
  0.7 1.1 %copy-start.10 = (f32[32,4]{0,1:T(4,128)S(1)}, f32[32,4]{0,1:T(4,128)}, u32[]{:S(2)}) copy-start(f32[32,4]{0,1:T(4,128)} %param.27) | copy-start | bytes 1540
  0.7 1.1 %copy-start.11 = (s32[4]{0:T(128)S(1)}, s32[4]{0:T(128)}, u32[]{:S(2)}) copy-start(s32[4]{0:T(128)} %length_ref.1) | copy-start | bytes 52
  0.7 1.6 %copy-start = (bf16[4,512,512]{2,1,0:T(8,128)(2,1)S(1)}, bf16[4,512,512]{2,1,0:T(8,128)(2,1)}, u32[]{:S(2)}) copy-start(bf16[4,512,512]{2,1,0:T(8,128)(2,1)} %key_ref.1) | copy-start | bytes 6291460
  0.7 31.7 %collective-permute-start.1 = (bf16[168,6144]{1,0:T(8,128)(2,1)}, bf16[168,6144]{1,0:T(8,128)(2,1)S(1)}, u32[]{:S(2)}, u32[]{:S(2)}) collective-permute-start(bf16[168,6144]{1,0:T(8,128)(2,1)} %bitcast.6), channel_id=1, source_target_pairs={{0,1},{1,0},{2,3},{3,2},{4,5},{5,4},{6,7},{7,6},{8,9},{9,8},{10,11... | collective-permute-start | bytes 6193160 | tf_op jit(solution)/shard_map/ppermute | solution.py:516
  1.2 31.2 %collective-permute-start.2 = (bf16[168,6144]{1,0:T(8,128)(2,1)}, bf16[168,6144]{1,0:T(8,128)(2,1)S(1)}, u32[]{:S(2)}, u32[]{:S(2)}) collective-permute-start(bf16[168,6144]{1,0:T(8,128)(2,1)} %bitcast.8), channel_id=1, source_target_pairs={{0,1},{1,0},{2,3},{3,2},{4,5},{5,4},{6,7},{7,6},{8,9},{9,8},{10,11... | collective-permute-start | bytes 6193160 | tf_op jit(solution)/shard_map/ppermute | solution.py:516
  1.3 31.1 %collective-permute-start.3 = (bf16[168,6144]{1,0:T(8,128)(2,1)}, bf16[168,6144]{1,0:T(8,128)(2,1)S(1)}, u32[]{:S(2)}, u32[]{:S(2)}) collective-permute-start(bf16[168,6144]{1,0:T(8,128)(2,1)} %refs_2_.1), channel_id=1, source_target_pairs={{0,1},{1,0},{2,3},{3,2},{4,5},{5,4},{6,7},{7,6},{8,9},{9,8},{10,11... | collective-permute-start | bytes 6193160 | tf_op jit(solution)/shard_map/ppermute | solution.py:516
  1.7 1.7 %copy-start.12 = (bf16[4,512,512]{2,1,0:T(8,128)(2,1)S(1)}, bf16[4,512,512]{2,1,0:T(8,128)(2,1)}, u32[]{:S(2)}) copy-start(bf16[4,512,512]{2,1,0:T(8,128)(2,1)} %value_ref.1) | copy-start | bytes 6291460
  2.3 17.4 %slice-start = ((s8[4718592]{0:T(1024)(128)(4,1)}), s8[4194304]{0:T(1024)(128)(4,1)S(1)}, s32[]{:S(2)}) async-start(s8[4718592]{0:T(1024)(128)(4,1)} %bitcast.4), calls=%async_computation.3 | async-start | bytes 8388608
  3.5 16.2 %slice-start.1 = ((s8[4718592]{0:T(1024)(128)(4,1)}), s8[524288]{0:T(1024)(128)(4,1)S(1)}, s32[]{:S(2)}) async-start(s8[4718592]{0:T(1024)(128)(4,1)} %bitcast.4), calls=%async_computation.4 | async-start | bytes 1048576
  3.5 28.9 %copy-start.3 = (bf16[168,6144]{1,0:T(8,128)(2,1)S(1)}, bf16[168,6144]{1,0:T(8,128)(2,1)}, u32[]{:S(2)}) copy-start(bf16[168,6144]{1,0:T(8,128)(2,1)} %refs_2_.1) | copy-start | bytes 6193156
  19.7 2.3 %copy-start.4 = (bf16[32,768]{1,0:T(8,128)(2,1)S(1)}, bf16[32,768]{1,0:T(8,128)(2,1)}, u32[]{:S(2)}) copy-start(bf16[32,768]{1,0:T(8,128)(2,1)} %residual_ref.1) | copy-start | bytes 147460
  19.7 12.7 %copy-start.1 = (bf16[6144,168]{0,1:T(8,128)(2,1)S(1)}, bf16[6144,168]{0,1:T(8,128)(2,1)}, u32[]{:S(2)}) copy-start(bf16[6144,168]{0,1:T(8,128)(2,1)} %param.23) | copy-start | bytes 6193156
  19.7 12.7 %copy-start.2 = (bf16[6144,168]{0,1:T(8,128)(2,1)S(1)}, bf16[6144,168]{0,1:T(8,128)(2,1)}, u32[]{:S(2)}) copy-start(bf16[6144,168]{0,1:T(8,128)(2,1)} %param.24) | copy-start | bytes 6193156
  20.6 1.4 %collective-permute-start = (f32[32,768]{1,0:T(8,128)S(1)}, f32[32,768]{1,0:T(8,128)S(1)}, u32[]{:S(2)}, u32[]{:S(2)}) collective-permute-start(f32[32,768]{1,0:T(8,128)S(1)} %get-tuple-element.25.mine_ref), channel_id=1, source_target_pairs={{0,1},{1,0},{2,3},{3,2},{4,5},{5,4},{6,7},{7,6},{8,9},{9,8},{10,11... | collective-permute-start | bytes 294920 | tf_op jit(solution)/shard_map/ppermute | solution.py:516
  45.2 1.3 %collective-permute-start.4 = (f32[32,768]{1,0:T(8,128)S(1)}, f32[32,768]{1,0:T(8,128)S(1)}, u32[]{:S(2)}, u32[]{:S(2)}) collective-permute-start(f32[32,768]{1,0:T(8,128)S(1)} %shard_map.156.mine_ref), channel_id=1, source_target_pairs={{0,1},{1,0},{2,3},{3,2},{4,5},{5,4},{6,7},{7,6},{8,9},{9,8},{10,11... | collective-permute-start | bytes 294920 | tf_op jit(solution)/shard_map/ppermute | solution.py:516

commit v24 on v23

--- a/solution.py
+++ b/solution.py
@@ -542,12 +542,14 @@
         sharers, capacity, cache_length, earlier, routes.T, route_weight.T, queries, new_key,
         new_value, ln_gain,
     )
-    other_weights = [swap(block) for block in lax.optimization_barrier(weights)]
+    other_weights = [swap(block) for block in lax.optimization_barrier(weights[:2])]
     attended = exchange(
         attend(count, spread, own, limit, key_cache, value_cache, value_rows, parts)
     )
     mine, gains = project(attended, out_weight)
     stream, chosen = pick(sharers, count, mine, swap(mine), residual, taken)
+    late_down, chosen = lax.optimization_barrier((weights[2], chosen))
+    other_weights.append(swap(late_down))
     outgoing = run_experts(slots, exchange(chosen), gains, weights, other_weights)
     combined = combine(sharers, taken, exchange(outgoing))
     attn_stream, expert_out = finish(stream, combined, swap(combined))

time: 47.4 us -> 47.6 us (level)
  local copies, waits for them, and re-layouts: 0.48 us -> 2.64 us
  waiting for transfers between devices: 2.59 us -> 1.38 us
  starting transfers between devices: 1.09 us -> 0.57 us
    unnamed x30, local copies, waits for them, and re-layouts: 0.48 us -> 2.64 us
    ppermute x5, waiting for transfers between devices: 2.59 us -> 1.38 us  [swap(): return lax.ppermute(block, 'expert', [(0, 1), (1, 0)])]
    ppermute x5, starting transfers between devices: 1.09 us -> 0.57 us  [swap(): return lax.ppermute(block, 'expert', [(0, 1), (1, 0)])]
  transfers between devices with their start and end apart: 5 -> 5, of which waited for: 2 -> 2; matrix products, arithmetic and copies ran while one was open for 0% -> 0% of each run, Pallas kernels for 6% -> 0%
where the time goes in v24:
time: 47.6 us; the launch traced here: 47.4 us
  blocking collectives  35.3 us (74%)
  Pallas kernels  6.72 us (14%)
  local copies, waits for them, and re-layouts  2.64 us (6%)
  waiting for transfers between devices  1.38 us (3%)
  between operations  0.81 us (2%)
  starting transfers between devices  0.57 us (1%)
    all_to_all x3, blocking collectives, exchange(): lax.all_to_all(blocks, 'attn', split_axis=0, concat_axis=0, tiled=True)  35.3 us
    pallas_call x1, Pallas kernels, run_experts(): call(expert_kernel, jax.ShapeDtypeStruct(pieces.shape, jnp.bfloat16), [VM...  3.08 us
    unnamed x30, local copies, waits for them, and re-layouts  2.64 us
    ppermute x5, waiting for transfers between devices, swap(): return lax.ppermute(block, 'expert', [(0, 1), (1, 0)])  1.38 us
    pallas_call x1, Pallas kernels, attend(): call(score_kernel, [jax.ShapeDtypeStruct((row_count, heads, length_max),...  1.03 us
  transfers between devices with their start and end apart: 5, of which 2 were waited for; matrix products, arithmetic and copies ran while one was open for 0% of the time, Pallas kernels for 0%

profile of v24, /device:TPU:0, one launch (start us, length us, event | category | flops | bytes accessed | tf_op | source)
XLA Modules:
  0.0 47.4 jit_solution(139183468813654502)
XLA Ops:
  0.6 0.0 copy-start.10
  0.6 0.0 copy-start.9
  0.7 0.0 copy-start.8
  0.7 0.0 copy-start.11
  0.7 0.0 copy-start.7
  0.7 0.0 copy-start.6
  0.7 0.0 copy-start.5
  0.7 0.0 copy-start
  0.7 0.0 copy-start.12
  0.7 0.6 %copy-done.10 = f32[32,4]{0,1:T(4,128)S(1)} copy-done((f32[32,4]{0,1:T(4,128)S(1)}, f32[32,4]{0,1:T(4,128)}, u32[]{:S(2)}) %copy-start.10) | copy-done | bytes 536
  1.3 0.0 copy-done.9
  1.3 0.0 copy-done.8
  1.4 0.0 copy-done.11
  1.4 0.0 copy-done.7
  1.4 0.0 copy-done.6
  1.4 0.1 copy-done.5
  1.5 0.2 shard_map.150
  1.7 0.7 %copy-done = bf16[4,512,512]{2,1,0:T(8,128)(2,1)S(1)} copy-done((bf16[4,512,512]{2,1,0:T(8,128)(2,1)S(1)}, bf16[4,512,512]{2,1,0:T(8,128)(2,1)}, u32[]{:S(2)}) %copy-start) | copy-done | bytes 2097176
  2.3 1.0 %shard_map.151 = (bf16[4,24,512]{2,1,0:T(8,128)(2,1)S(1)}, f32[4,24,128]{2,1,0:T(8,128)S(1)}) custom-call(bf16[4,24,512]{2,1,0:T(8,128)(2,1)S(1)} %get-tuple-element.19.spread_ref, f32[4,24,128]{2,1,0:T(8,128)S(1)} %get-tuple-element.20.own_ref, s32[4,24,128]{2,1,0:T(8,128)S(1)} %get-tuple-element.21.limit_ref, bf16[4,512,512]{2,1,0:T(8,128)(2,1)S(1)} %copy-done), custom_call_target="tpu_custom_call" | custom-call | flops 50331648 | bytes 2097152 | tf_op jit(solution)/shard_map/pallas_call | solution.py:343
  3.4 0.0 copy-done.12
  3.4 0.0 slice-start.1
  3.4 0.0 copy-start.3
  3.4 0.5 %shard_map.152 = bf16[8,4,3456]{2,1,0:T(4,128)(2,1)S(1)} custom-call(bf16[4,24,512]{2,1,0:T(8,128)(2,1)S(1)} %get-tuple-element.22.probs_ref, f32[4,24,128]{2,1,0:T(8,128)S(1)} %get-tuple-element.23.own_ref, bf16[4,512,512]{2,1,0:T(8,128)(2,1)S(1)} %copy-done.12, f32[96,128]{1,0:T(8,128)S(1)} %get-tuple-element.24.value_rows, ...), custom_call_target="tpu_custom_call" | custom-call | flops 10000000000 | bytes 2097152 | tf_op jit(solution)/shard_map/pallas_call | solution.py:354
  3.9 15.5 %all_to_all.15.pieces = bf16[8,4,3456]{2,1,0:T(4,128)(2,1)S(1)} all-to-all(bf16[8,4,3456]{2,1,0:T(4,128)(2,1)S(1)} %shard_map.152), channel_id=1, replica_groups=mesh['group'=2,'attn'=8,'expert'=2] {'attn'}, dimensions={0} | all-to-all | bytes 442368 | tf_op jit(solution)/shard_map/all_to_all | solution.py:512
  19.5 0.0 slice-done
  19.5 0.0 copy-start.2
  19.5 0.0 copy-start.4
  19.5 0.9 %shard_map.153 = (f32[32,768]{1,0:T(8,128)S(1)}, f32[8,768]{1,0:T(8,128)S(1)}) custom-call(bf16[8,4,3456]{2,1,0:T(4,128)(2,1)S(1)} %all_to_all.15.pieces, bf16[3072,768]{1,0:T(8,128)(2,1)S(1)} %bitcast.5), custom_call_target="tpu_custom_call" | custom-call | flops 150994944 | bytes 4718592 | tf_op jit(solution)/shard_map/pallas_call | solution.py:388
  20.4 0.1 collective-permute-start
  20.5 0.6 %copy-done.1 = bf16[6144,168]{0,1:T(8,128)(2,1)S(1)} copy-done((bf16[6144,168]{0,1:T(8,128)(2,1)S(1)}, bf16[6144,168]{0,1:T(8,128)(2,1)}, u32[]{:S(2)}) %copy-start.1) | copy-done | bytes 2064408
  21.0 0.0 collective-permute-start.1
  21.1 0.6 %copy-done.2 = bf16[6144,168]{0,1:T(8,128)(2,1)S(1)} copy-done((bf16[6144,168]{0,1:T(8,128)(2,1)S(1)}, bf16[6144,168]{0,1:T(8,128)(2,1)}, u32[]{:S(2)}) %copy-start.2) | copy-done | bytes 2064408
  21.7 0.0 collective-permute-start.2
  21.7 0.1 collective-permute-done.other_ref
  21.8 0.0 copy-done.4
  21.8 0.1 shard_map.154
  21.9 0.0 copy-done.3
  21.9 0.5 %collective-permute-start.3 = (bf16[168,6144]{1,0:T(8,128)(2,1)S(1)}, bf16[168,6144]{1,0:T(8,128)(2,1)S(1)}, u32[]{:S(2)}, u32[]{:S(2)}) collective-permute-start(bf16[168,6144]{1,0:T(8,128)(2,1)S(1)} %copy-done.3), channel_id=1, source_target_pairs={{0,1},{1,0},{2,3},{3,2},{4,5},{5,4},{6,7},{7,6},{8,9},{9,8},{10,11... | collective-permute-start | bytes 6193160 | tf_op jit(solution)/shard_map/ppermute | solution.py:516
  22.4 10.2 %all_to_all.16.pieces = bf16[8,8,768]{2,1,0:T(8,128)(2,1)S(1)} all-to-all(bf16[8,8,768]{2,1,0:T(8,128)(2,1)S(1)} %get-tuple-element.31), channel_id=1, replica_groups=mesh['group'=2,'attn'=8,'expert'=2] {'attn'}, dimensions={0} | all-to-all | bytes 196608 | tf_op jit(solution)/shard_map/all_to_all | solution.py:512
  32.6 0.0 collective-permute-done.1.refs_3_
  32.6 0.0 collective-permute-done.2.refs_4_
  32.6 0.0 collective-permute-done.3.refs_5_
  32.6 3.1 %shard_map.155 = bf16[8,8,768]{2,1,0:T(8,128)(2,1)S(1)} custom-call(f32[8,128]{1,0:T(8,128)S(1)} %get-tuple-element.29.slot_ref, bf16[8,8,768]{2,1,0:T(8,128)(2,1)S(1)} %all_to_all.16.pieces, f32[8,768]{1,0:T(8,128)S(1)} %get-tuple-element.32.gains, bf16[168,6144]{1,0:T(8,128)(2,1)S(1)} %bitcast.7, bf16[168,6144]{1,0:T(8,128)(2,1)S(1)} %bitcast.9, ...), custom_call_target="tpu_custom_call" | custom-call | flops 99090432 | bytes 12386304 | tf_op jit(solution)/shard_map/pallas_call | solution.py:463
  35.7 9.5 %all_to_all.17.pieces = bf16[8,8,768]{2,1,0:T(8,128)(2,1)S(1)} all-to-all(bf16[8,8,768]{2,1,0:T(8,128)(2,1)S(1)} %shard_map.155), channel_id=1, replica_groups=mesh['group'=2,'attn'=8,'expert'=2] {'attn'}, dimensions={0} | all-to-all | bytes 196608 | tf_op jit(solution)/shard_map/all_to_all | solution.py:512
  45.2 0.2 shard_map.156.mine_ref
  45.4 0.0 collective-permute-start.4
  45.4 1.3 %collective-permute-done.4.other_ref = f32[32,768]{1,0:T(8,128)S(1)} collective-permute-done((f32[32,768]{1,0:T(8,128)S(1)}, f32[32,768]{1,0:T(8,128)S(1)}, u32[]{:S(2)}, u32[]{:S(2)}) %collective-permute-start.4) | collective-permute-done | bytes 98336 | tf_op jit(solution)/shard_map/ppermute | solution.py:516
  46.7 0.6 %shard_map.157 = (bf16[32,768]{1,0:T(8,128)(2,1)}, bf16[32,768]{1,0:T(8,128)(2,1)}) custom-call(bf16[32,768]{1,0:T(8,128)(2,1)S(1)} %get-tuple-element.28.stream_ref, f32[32,768]{1,0:T(8,128)S(1)} %shard_map.156.mine_ref, f32[32,768]{1,0:T(8,128)S(1)} %collective-permute-done.4.other_ref), custom_call_target="tpu_custom_call" | custom-call | flops 24576 | bytes 344064 | tf_op jit(solution)/shard_map/pallas_call | solution.py:502
  (5 shorter events, 0.0 us)
Async XLA Ops:
  0.6 0.7 %copy-start.10 = (f32[32,4]{0,1:T(4,128)S(1)}, f32[32,4]{0,1:T(4,128)}, u32[]{:S(2)}) copy-start(f32[32,4]{0,1:T(4,128)} %param.27) | copy-start | bytes 1540
  0.6 0.7 %copy-start.9 = (s32[32,4]{0,1:T(4,128)S(1)}, s32[32,4]{0,1:T(4,128)}, u32[]{:S(2)}) copy-start(s32[32,4]{0,1:T(4,128)} %param.26) | copy-start | bytes 1540
  0.7 0.7 %copy-start.8 = (f32[768]{0:T(1024)S(1)}, f32[768]{0:T(1024)}, u32[]{:S(2)}) copy-start(f32[768]{0:T(1024)} %gain_ref.1) | copy-start | bytes 9220
  0.7 0.7 %copy-start.11 = (s32[4]{0:T(128)S(1)}, s32[4]{0:T(128)}, u32[]{:S(2)}) copy-start(s32[4]{0:T(128)} %length_ref.1) | copy-start | bytes 52
  0.7 0.7 %copy-start.7 = (bf16[4,512]{1,0:T(4,128)(2,1)S(1)}, bf16[4,512]{1,0:T(4,128)(2,1)}, u32[]{:S(2)}) copy-start(bf16[4,512]{1,0:T(4,128)(2,1)} %own_value_ref.1) | copy-start | bytes 12292
  0.7 0.7 %copy-start.6 = (bf16[4,512]{1,0:T(4,128)(2,1)S(1)}, bf16[4,512]{1,0:T(4,128)(2,1)}, u32[]{:S(2)}) copy-start(bf16[4,512]{1,0:T(4,128)(2,1)} %own_key_ref.1) | copy-start | bytes 12292
  0.7 0.8 %copy-start.5 = (bf16[4,3072]{1,0:T(4,128)(2,1)S(1)}, bf16[4,3072]{1,0:T(4,128)(2,1)}, u32[]{:S(2)}) copy-start(bf16[4,3072]{1,0:T(4,128)(2,1)} %query_ref.1) | copy-start | bytes 73732
  0.7 1.6 %copy-start = (bf16[4,512,512]{2,1,0:T(8,128)(2,1)S(1)}, bf16[4,512,512]{2,1,0:T(8,128)(2,1)}, u32[]{:S(2)}) copy-start(bf16[4,512,512]{2,1,0:T(8,128)(2,1)} %key_ref.1) | copy-start | bytes 6291460
  0.7 2.6 %copy-start.12 = (bf16[4,512,512]{2,1,0:T(8,128)(2,1)S(1)}, bf16[4,512,512]{2,1,0:T(8,128)(2,1)}, u32[]{:S(2)}) copy-start(bf16[4,512,512]{2,1,0:T(8,128)(2,1)} %value_ref.1) | copy-start | bytes 6291460
  2.3 17.1 %slice-start = ((s8[4718592]{0:T(1024)(128)(4,1)}), s8[4194304]{0:T(1024)(128)(4,1)S(1)}, s32[]{:S(2)}) async-start(s8[4718592]{0:T(1024)(128)(4,1)} %bitcast.4), calls=%async_computation.3 | async-start | bytes 8388608
  3.4 16.1 %slice-start.1 = ((s8[4718592]{0:T(1024)(128)(4,1)}), s8[524288]{0:T(1024)(128)(4,1)S(1)}, s32[]{:S(2)}) async-start(s8[4718592]{0:T(1024)(128)(4,1)} %bitcast.4), calls=%async_computation.4 | async-start | bytes 1048576
  3.4 18.5 %copy-start.3 = (bf16[168,6144]{1,0:T(8,128)(2,1)S(1)}, bf16[168,6144]{1,0:T(8,128)(2,1)}, u32[]{:S(2)}) copy-start(bf16[168,6144]{1,0:T(8,128)(2,1)} %refs_2_.1) | copy-start | bytes 6193156
  19.5 1.6 %copy-start.1 = (bf16[6144,168]{0,1:T(8,128)(2,1)S(1)}, bf16[6144,168]{0,1:T(8,128)(2,1)}, u32[]{:S(2)}) copy-start(bf16[6144,168]{0,1:T(8,128)(2,1)} %param.23) | copy-start | bytes 6193156
  19.5 2.2 %copy-start.2 = (bf16[6144,168]{0,1:T(8,128)(2,1)S(1)}, bf16[6144,168]{0,1:T(8,128)(2,1)}, u32[]{:S(2)}) copy-start(bf16[6144,168]{0,1:T(8,128)(2,1)} %param.24) | copy-start | bytes 6193156
  19.5 2.3 %copy-start.4 = (bf16[32,768]{1,0:T(8,128)(2,1)S(1)}, bf16[32,768]{1,0:T(8,128)(2,1)}, u32[]{:S(2)}) copy-start(bf16[32,768]{1,0:T(8,128)(2,1)} %residual_ref.1) | copy-start | bytes 147460
  20.4 1.4 %collective-permute-start = (f32[32,768]{1,0:T(8,128)S(1)}, f32[32,768]{1,0:T(8,128)S(1)}, u32[]{:S(2)}, u32[]{:S(2)}) collective-permute-start(f32[32,768]{1,0:T(8,128)S(1)} %get-tuple-element.26.mine_ref), channel_id=1, source_target_pairs={{0,1},{1,0},{2,3},{3,2},{4,5},{5,4},{6,7},{7,6},{8,9},{9,8},{10,11... | collective-permute-start | bytes 294920 | tf_op jit(solution)/shard_map/ppermute | solution.py:516
  21.0 11.6 %collective-permute-start.1 = (bf16[168,6144]{1,0:T(8,128)(2,1)S(1)}, bf16[168,6144]{1,0:T(8,128)(2,1)S(1)}, u32[]{:S(2)}, u32[]{:S(2)}) collective-permute-start(bf16[168,6144]{1,0:T(8,128)(2,1)S(1)} %bitcast.6), channel_id=1, source_target_pairs={{0,1},{1,0},{2,3},{3,2},{4,5},{5,4},{6,7},{7,6},{8,9},{9,8},{10,11... | collective-permute-start | bytes 6193160 | tf_op jit(solution)/shard_map/ppermute | solution.py:516
  21.7 11.0 %collective-permute-start.2 = (bf16[168,6144]{1,0:T(8,128)(2,1)S(1)}, bf16[168,6144]{1,0:T(8,128)(2,1)S(1)}, u32[]{:S(2)}, u32[]{:S(2)}) collective-permute-start(bf16[168,6144]{1,0:T(8,128)(2,1)S(1)} %bitcast.8), channel_id=1, source_target_pairs={{0,1},{1,0},{2,3},{3,2},{4,5},{5,4},{6,7},{7,6},{8,9},{9,8},{10,11... | collective-permute-start | bytes 6193160 | tf_op jit(solution)/shard_map/ppermute | solution.py:516
  21.9 10.7 %collective-permute-start.3 = (bf16[168,6144]{1,0:T(8,128)(2,1)S(1)}, bf16[168,6144]{1,0:T(8,128)(2,1)S(1)}, u32[]{:S(2)}, u32[]{:S(2)}) collective-permute-start(bf16[168,6144]{1,0:T(8,128)(2,1)S(1)} %copy-done.3), channel_id=1, source_target_pairs={{0,1},{1,0},{2,3},{3,2},{4,5},{5,4},{6,7},{7,6},{8,9},{9,8},{10,11... | collective-permute-start | bytes 6193160 | tf_op jit(solution)/shard_map/ppermute | solution.py:516
  45.4 1.3 %collective-permute-start.4 = (f32[32,768]{1,0:T(8,128)S(1)}, f32[32,768]{1,0:T(8,128)S(1)}, u32[]{:S(2)}, u32[]{:S(2)}) collective-permute-start(f32[32,768]{1,0:T(8,128)S(1)} %shard_map.156.mine_ref), channel_id=1, source_target_pairs={{0,1},{1,0},{2,3},{3,2},{4,5},{5,4},{6,7},{7,6},{8,9},{9,8},{10,11... | collective-permute-start | bytes 294920 | tf_op jit(solution)/shard_map/ppermute | solution.py:516

commit v25 on v24

--- a/solution.py
+++ b/solution.py
@@ -547,9 +547,9 @@
         attend(count, spread, own, limit, key_cache, value_cache, value_rows, parts)
     )
     mine, gains = project(attended, out_weight)
+    late_down, mine = lax.optimization_barrier((weights[2], mine))
+    other_weights.append(swap(late_down))
     stream, chosen = pick(sharers, count, mine, swap(mine), residual, taken)
-    late_down, chosen = lax.optimization_barrier((weights[2], chosen))
-    other_weights.append(swap(late_down))
     outgoing = run_experts(slots, exchange(chosen), gains, weights, other_weights)
     combined = combine(sharers, taken, exchange(outgoing))
     attn_stream, expert_out = finish(stream, combined, swap(combined))

time: 47.6 us -> 56 us (1.18)
  blocking collectives: 35.3 us -> 19.7 us
  waiting for transfers between devices: 1.38 us -> 12.8 us
  starting transfers between devices: 0.57 us -> 8.36 us
  Pallas kernels: 6.72 us -> 9.61 us
  local copies, waits for them, and re-layouts: 2.64 us -> 4.43 us
    all_to_all x3 -> x2, blocking collectives: 35.3 us -> 19.7 us  [exchange(): lax.all_to_all(blocks, 'attn', split_axis=0, concat_axis=0, tiled=True)]
    all_to_all x0 -> x1, waiting for transfers between devices: none -> 7.73 us  [exchange(): lax.all_to_all(blocks, 'attn', split_axis=0, concat_axis=0, tiled=True)]
    all_to_all x0 -> x1, starting transfers between devices: none -> 7.28 us  [exchange(): lax.all_to_all(blocks, 'attn', split_axis=0, concat_axis=0, tiled=True)]
    ppermute x5, waiting for transfers between devices: 1.38 us -> 5.05 us  [swap(): return lax.ppermute(block, 'expert', [(0, 1), (1, 0)])]
    pallas_call x1, Pallas kernels: 3.08 us -> 5.29 us  [run_experts(): call(expert_kernel, jax.ShapeDtypeStruct(pieces.shape, jnp.bfloat16), [VM...]
    unnamed x30 -> x28, local copies, waits for them, and re-layouts: 2.64 us -> 4.43 us
    pallas_call x1, Pallas kernels: 0.52 us -> 1.22 us  [attend(): call(value_kernel, jax.ShapeDtypeStruct((count, row_count, width), jnp.bf...]
  transfers between devices with their start and end apart: 5 -> 6, of which waited for: 2 -> 3; matrix products, arithmetic and copies ran while one was open for 0% -> 0% of each run, Pallas kernels for 0% -> 2%
where the time goes in v25:
time: 56 us; the launch traced here: 55.7 us
  blocking collectives  19.7 us (35%)
  waiting for transfers between devices  12.8 us (23%)
  Pallas kernels  9.61 us (17%)
  starting transfers between devices  8.36 us (15%)
  local copies, waits for them, and re-layouts  4.43 us (8%)
  between operations  0.78 us (1%)
    all_to_all x2, blocking collectives, exchange(): lax.all_to_all(blocks, 'attn', split_axis=0, concat_axis=0, tiled=True)  19.7 us
    all_to_all x1, waiting for transfers between devices, exchange(): lax.all_to_all(blocks, 'attn', split_axis=0, concat_axis=0, tiled=True)  7.73 us
    all_to_all x1, starting transfers between devices, exchange(): lax.all_to_all(blocks, 'attn', split_axis=0, concat_axis=0, tiled=True)  7.28 us
    pallas_call x1, Pallas kernels, run_experts(): call(expert_kernel, jax.ShapeDtypeStruct(pieces.shape, jnp.bfloat16), [VM...  5.29 us
    ppermute x5, waiting for transfers between devices, swap(): return lax.ppermute(block, 'expert', [(0, 1), (1, 0)])  5.05 us
    unnamed x28, local copies, waits for them, and re-layouts  4.43 us
    pallas_call x1, Pallas kernels, attend(): call(value_kernel, jax.ShapeDtypeStruct((count, row_count, width), jnp.bf...  1.22 us
  transfers between devices with their start and end apart: 6, of which 3 were waited for; matrix products, arithmetic and copies ran while one was open for 0% of the time, Pallas kernels for 2%

profile of v25, /device:TPU:0, one launch (start us, length us, event | category | flops | bytes accessed | tf_op | source)
XLA Modules:
  0.0 55.7 jit_solution(5963810444103152733)
XLA Ops:
  0.6 0.0 copy-start.11
  0.6 0.0 copy-start.10
  0.7 0.0 copy-start.9
  0.7 0.0 copy-start.12
  0.7 0.0 copy-start.8
  0.7 0.0 copy-start.7
  0.7 0.0 copy-start.6
  0.7 0.0 copy-start.1
  0.7 0.0 copy-start.13
  0.7 0.6 %copy-done.11 = f32[32,4]{0,1:T(4,128)S(1)} copy-done((f32[32,4]{0,1:T(4,128)S(1)}, f32[32,4]{0,1:T(4,128)}, u32[]{:S(2)}) %copy-start.11) | copy-done | bytes 536
  1.3 0.0 copy-done.10
  1.3 0.0 copy-done.9
  1.4 0.0 copy-done.12
  1.4 0.0 copy-done.8
  1.4 0.0 copy-done.7
  1.4 0.1 copy-done.6
  1.5 0.2 shard_map.150
  1.7 0.7 %copy-done.1 = bf16[4,512,512]{2,1,0:T(8,128)(2,1)S(1)} copy-done((bf16[4,512,512]{2,1,0:T(8,128)(2,1)S(1)}, bf16[4,512,512]{2,1,0:T(8,128)(2,1)}, u32[]{:S(2)}) %copy-start.1) | copy-done | bytes 2097176
  2.3 1.0 %shard_map.151 = (bf16[4,24,512]{2,1,0:T(8,128)(2,1)S(1)}, f32[4,24,128]{2,1,0:T(8,128)S(1)}) custom-call(bf16[4,24,512]{2,1,0:T(8,128)(2,1)S(1)} %get-tuple-element.19.spread_ref, f32[4,24,128]{2,1,0:T(8,128)S(1)} %get-tuple-element.20.own_ref, s32[4,24,128]{2,1,0:T(8,128)S(1)} %get-tuple-element.21.limit_ref, bf16[4,512,512]{2,1,0:T(8,128)(2,1)S(1)} %copy-done.1), custom_call_target="tpu_custom_call" | custom-call | flops 50331648 | bytes 2097152 | tf_op jit(solution)/shard_map/pallas_call | solution.py:343
  3.4 0.0 copy-done.13
  3.4 0.0 copy-start.2
  3.4 1.2 %shard_map.152 = bf16[8,4,3456]{2,1,0:T(4,128)(2,1)} custom-call(bf16[4,24,512]{2,1,0:T(8,128)(2,1)S(1)} %get-tuple-element.22.probs_ref, f32[4,24,128]{2,1,0:T(8,128)S(1)} %get-tuple-element.23.own_ref, bf16[4,512,512]{2,1,0:T(8,128)(2,1)S(1)} %copy-done.13, f32[96,128]{1,0:T(8,128)S(1)} %get-tuple-element.24.value_rows, ...), custom_call_target="tpu_custom_call" | custom-call | flops 10000000000 | bytes 2097152 | tf_op jit(solution)/shard_map/pallas_call | solution.py:354
  4.6 7.3 %all-to-all-start = ((bf16[8,4,3456]{2,1,0:T(4,128)(2,1)}), bf16[8,4,3456]{2,1,0:T(4,128)(2,1)S(1)}, u32[]{:S(2)}, u32[]{:S(2)}) async-start(bf16[8,4,3456]{2,1,0:T(4,128)(2,1)} %shard_map.152), calls=%async_computation | async-start | bytes 442368 | tf_op jit(solution)/shard_map/all_to_all | solution.py:512
  11.9 0.0 copy-done.2
  11.9 0.1 collective-permute-start.1
  12.0 0.5 collective-permute-start.2
  12.5 7.7 %all-to-all-done.pieces = bf16[8,4,3456]{2,1,0:T(4,128)(2,1)S(1)} async-done(((bf16[8,4,3456]{2,1,0:T(4,128)(2,1)}), bf16[8,4,3456]{2,1,0:T(4,128)(2,1)S(1)}, u32[]{:S(2)}, u32[]{:S(2)}) %all-to-all-start) | async-done | bytes 221216 | tf_op jit(solution)/shard_map/all_to_all | solution.py:512
  20.2 0.0 copy-start
  20.2 2.3 %copy-done = bf16[3072,768]{1,0:T(8,128)(2,1)S(1)} copy-done((bf16[3072,768]{1,0:T(8,128)(2,1)S(1)}, bf16[3072,768]{1,0:T(8,128)(2,1)}, u32[]{:S(2)}) %copy-start) | copy-done | bytes 4718616
  22.5 0.0 copy-start.5
  22.6 0.9 %shard_map.153 = (f32[32,768]{1,0:T(8,128)S(1)}, f32[8,768]{1,0:T(8,128)S(1)}) custom-call(bf16[8,4,3456]{2,1,0:T(4,128)(2,1)S(1)} %all-to-all-done.pieces, bf16[3072,768]{1,0:T(8,128)(2,1)S(1)} %copy-done), custom_call_target="tpu_custom_call" | custom-call | flops 150994944 | bytes 4718592 | tf_op jit(solution)/shard_map/pallas_call | solution.py:388
  23.4 0.7 %copy-done.4 = bf16[168,6144]{1,0:T(8,128)(2,1)S(1)} copy-done((bf16[168,6144]{1,0:T(8,128)(2,1)S(1)}, bf16[168,6144]{1,0:T(8,128)(2,1)}, u32[]{:S(2)}) %copy-start.4) | copy-done | bytes 2064408
  24.1 0.0 collective-permute-start.3
  24.1 0.5 collective-permute-start
  24.6 3.7 %collective-permute-done.other_ref = f32[32,768]{1,0:T(8,128)S(1)} collective-permute-done((f32[32,768]{1,0:T(8,128)S(1)}, f32[32,768]{1,0:T(8,128)S(1)}, u32[]{:S(2)}, u32[]{:S(2)}) %collective-permute-start) | collective-permute-done | bytes 98336 | tf_op jit(solution)/shard_map/ppermute | solution.py:516
  28.4 0.0 copy-done.5
  28.4 0.1 shard_map.154
  28.5 10.2 %all_to_all.15.pieces = bf16[8,8,768]{2,1,0:T(8,128)(2,1)S(1)} all-to-all(bf16[8,8,768]{2,1,0:T(8,128)(2,1)S(1)} %get-tuple-element.31), channel_id=1, replica_groups=mesh['group'=2,'attn'=8,'expert'=2] {'attn'}, dimensions={0} | all-to-all | bytes 196608 | tf_op jit(solution)/shard_map/all_to_all | solution.py:512
  38.8 0.0 collective-permute-done.1.refs_3_
  38.8 0.0 collective-permute-done.2.refs_4_
  38.8 0.0 collective-permute-done.3.refs_5_
  38.8 0.0 copy-done.3
  38.8 5.3 %shard_map.155 = bf16[8,8,768]{2,1,0:T(8,128)(2,1)S(1)} custom-call(f32[8,128]{1,0:T(8,128)S(1)} %get-tuple-element.30.slot_ref, bf16[8,8,768]{2,1,0:T(8,128)(2,1)S(1)} %all_to_all.15.pieces, f32[8,768]{1,0:T(8,128)S(1)} %get-tuple-element.32.gains, bf16[168,6144]{1,0:T(8,128)(2,1)S(1)} %bitcast.5, bf16[168,6144]{1,0:T(8,128)(2,1)S(1)} %bitcast.7, ...), custom_call_target="tpu_custom_call" | custom-call | flops 99090432 | bytes 12386304 | tf_op jit(solution)/shard_map/pallas_call | solution.py:463
  44.1 9.5 %all_to_all.16.pieces = bf16[8,8,768]{2,1,0:T(8,128)(2,1)S(1)} all-to-all(bf16[8,8,768]{2,1,0:T(8,128)(2,1)S(1)} %shard_map.155), channel_id=1, replica_groups=mesh['group'=2,'attn'=8,'expert'=2] {'attn'}, dimensions={0} | all-to-all | bytes 196608 | tf_op jit(solution)/shard_map/all_to_all | solution.py:512
  53.6 0.2 shard_map.156.mine_ref
  53.8 0.0 collective-permute-start.4
  53.8 1.3 %collective-permute-done.4.other_ref = f32[32,768]{1,0:T(8,128)S(1)} collective-permute-done((f32[32,768]{1,0:T(8,128)S(1)}, f32[32,768]{1,0:T(8,128)S(1)}, u32[]{:S(2)}, u32[]{:S(2)}) %collective-permute-start.4) | collective-permute-done | bytes 98336 | tf_op jit(solution)/shard_map/ppermute | solution.py:516
  55.1 0.6 %shard_map.157 = (bf16[32,768]{1,0:T(8,128)(2,1)}, bf16[32,768]{1,0:T(8,128)(2,1)}) custom-call(bf16[32,768]{1,0:T(8,128)(2,1)S(1)} %get-tuple-element.29.stream_ref, f32[32,768]{1,0:T(8,128)S(1)} %shard_map.156.mine_ref, f32[32,768]{1,0:T(8,128)S(1)} %collective-permute-done.4.other_ref), custom_call_target="tpu_custom_call" | custom-call | flops 24576 | bytes 344064 | tf_op jit(solution)/shard_map/pallas_call | solution.py:502
  (3 shorter events, 0.0 us)
Async XLA Ops:
  0.6 0.7 %copy-start.11 = (f32[32,4]{0,1:T(4,128)S(1)}, f32[32,4]{0,1:T(4,128)}, u32[]{:S(2)}) copy-start(f32[32,4]{0,1:T(4,128)} %param.27) | copy-start | bytes 1540
  0.6 0.7 %copy-start.10 = (s32[32,4]{0,1:T(4,128)S(1)}, s32[32,4]{0,1:T(4,128)}, u32[]{:S(2)}) copy-start(s32[32,4]{0,1:T(4,128)} %param.26) | copy-start | bytes 1540
  0.7 0.7 %copy-start.9 = (f32[768]{0:T(1024)S(1)}, f32[768]{0:T(1024)}, u32[]{:S(2)}) copy-start(f32[768]{0:T(1024)} %gain_ref.1) | copy-start | bytes 9220
  0.7 0.7 %copy-start.12 = (s32[4]{0:T(128)S(1)}, s32[4]{0:T(128)}, u32[]{:S(2)}) copy-start(s32[4]{0:T(128)} %length_ref.1) | copy-start | bytes 52
  0.7 0.7 %copy-start.8 = (bf16[4,512]{1,0:T(4,128)(2,1)S(1)}, bf16[4,512]{1,0:T(4,128)(2,1)}, u32[]{:S(2)}) copy-start(bf16[4,512]{1,0:T(4,128)(2,1)} %own_value_ref.1) | copy-start | bytes 12292
  0.7 0.7 %copy-start.7 = (bf16[4,512]{1,0:T(4,128)(2,1)S(1)}, bf16[4,512]{1,0:T(4,128)(2,1)}, u32[]{:S(2)}) copy-start(bf16[4,512]{1,0:T(4,128)(2,1)} %own_key_ref.1) | copy-start | bytes 12292
  0.7 0.8 %copy-start.6 = (bf16[4,3072]{1,0:T(4,128)(2,1)S(1)}, bf16[4,3072]{1,0:T(4,128)(2,1)}, u32[]{:S(2)}) copy-start(bf16[4,3072]{1,0:T(4,128)(2,1)} %query_ref.1) | copy-start | bytes 73732
  0.7 1.6 %copy-start.1 = (bf16[4,512,512]{2,1,0:T(8,128)(2,1)S(1)}, bf16[4,512,512]{2,1,0:T(8,128)(2,1)}, u32[]{:S(2)}) copy-start(bf16[4,512,512]{2,1,0:T(8,128)(2,1)} %key_ref.1) | copy-start | bytes 6291460
  0.7 2.6 %copy-start.13 = (bf16[4,512,512]{2,1,0:T(8,128)(2,1)S(1)}, bf16[4,512,512]{2,1,0:T(8,128)(2,1)}, u32[]{:S(2)}) copy-start(bf16[4,512,512]{2,1,0:T(8,128)(2,1)} %value_ref.1) | copy-start | bytes 6291460
  3.4 8.5 %copy-start.2 = (bf16[6144,168]{0,1:T(8,128)(2,1)S(1)}, bf16[6144,168]{0,1:T(8,128)(2,1)}, u32[]{:S(2)}) copy-start(bf16[6144,168]{0,1:T(8,128)(2,1)} %param.23) | copy-start | bytes 6193156
  4.6 15.6 %all-to-all-start = ((bf16[8,4,3456]{2,1,0:T(4,128)(2,1)}), bf16[8,4,3456]{2,1,0:T(4,128)(2,1)S(1)}, u32[]{:S(2)}, u32[]{:S(2)}) async-start(bf16[8,4,3456]{2,1,0:T(4,128)(2,1)} %shard_map.152), calls=%async_computation | async-start | bytes 442368 | tf_op jit(solution)/shard_map/all_to_all | solution.py:512
  11.9 26.9 %collective-permute-start.1 = (bf16[168,6144]{1,0:T(8,128)(2,1)S(1)}, bf16[168,6144]{1,0:T(8,128)(2,1)}, u32[]{:S(2)}, u32[]{:S(2)}) collective-permute-start(bf16[168,6144]{1,0:T(8,128)(2,1)S(1)} %bitcast.4), channel_id=1, source_target_pairs={{0,1},{1,0},{2,3},{3,2},{4,5},{5,4},{6,7},{7,6},{8,9},{9,8},{10,11... | collective-permute-start | bytes 6193160 | tf_op jit(solution)/shard_map/ppermute | solution.py:516
  12.0 26.8 %collective-permute-start.2 = (bf16[168,6144]{1,0:T(8,128)(2,1)}, bf16[168,6144]{1,0:T(8,128)(2,1)}, u32[]{:S(2)}, u32[]{:S(2)}) collective-permute-start(bf16[168,6144]{1,0:T(8,128)(2,1)} %bitcast.6), channel_id=1, source_target_pairs={{0,1},{1,0},{2,3},{3,2},{4,5},{5,4},{6,7},{7,6},{8,9},{9,8},{10,11... | collective-permute-start | bytes 6193160 | tf_op jit(solution)/shard_map/ppermute | solution.py:516
  20.2 2.3 %copy-start = (bf16[3072,768]{1,0:T(8,128)(2,1)S(1)}, bf16[3072,768]{1,0:T(8,128)(2,1)}, u32[]{:S(2)}) copy-start(bf16[3072,768]{1,0:T(8,128)(2,1)} %weight_ref.1) | copy-start | bytes 14155780
  22.5 1.6 %copy-start.4 = (bf16[168,6144]{1,0:T(8,128)(2,1)S(1)}, bf16[168,6144]{1,0:T(8,128)(2,1)}, u32[]{:S(2)}) copy-start(bf16[168,6144]{1,0:T(8,128)(2,1)} %refs_2_.1) | copy-start | bytes 6193156
  22.5 5.8 %copy-start.5 = (bf16[32,768]{1,0:T(8,128)(2,1)S(1)}, bf16[32,768]{1,0:T(8,128)(2,1)}, u32[]{:S(2)}) copy-start(bf16[32,768]{1,0:T(8,128)(2,1)} %residual_ref.1) | copy-start | bytes 147460
  22.5 16.2 %copy-start.3 = (bf16[6144,168]{0,1:T(8,128)(2,1)S(1)}, bf16[6144,168]{0,1:T(8,128)(2,1)}, u32[]{:S(2)}) copy-start(bf16[6144,168]{0,1:T(8,128)(2,1)} %param.24) | copy-start | bytes 6193156
  24.1 14.6 %collective-permute-start.3 = (bf16[168,6144]{1,0:T(8,128)(2,1)S(1)}, bf16[168,6144]{1,0:T(8,128)(2,1)S(1)}, u32[]{:S(2)}, u32[]{:S(2)}) collective-permute-start(bf16[168,6144]{1,0:T(8,128)(2,1)S(1)} %copy-done.4), channel_id=1, source_target_pairs={{0,1},{1,0},{2,3},{3,2},{4,5},{5,4},{6,7},{7,6},{8,9},{9,8},{10,11... | collective-permute-start | bytes 6193160 | tf_op jit(solution)/shard_map/ppermute | solution.py:516
  24.1 4.3 %collective-permute-start = (f32[32,768]{1,0:T(8,128)S(1)}, f32[32,768]{1,0:T(8,128)S(1)}, u32[]{:S(2)}, u32[]{:S(2)}) collective-permute-start(f32[32,768]{1,0:T(8,128)S(1)} %get-tuple-element.27.mine_ref), channel_id=1, source_target_pairs={{0,1},{1,0},{2,3},{3,2},{4,5},{5,4},{6,7},{7,6},{8,9},{9,8},{10,11... | collective-permute-start | bytes 294920 | tf_op jit(solution)/shard_map/ppermute | solution.py:516
  53.8 1.3 %collective-permute-start.4 = (f32[32,768]{1,0:T(8,128)S(1)}, f32[32,768]{1,0:T(8,128)S(1)}, u32[]{:S(2)}, u32[]{:S(2)}) collective-permute-start(f32[32,768]{1,0:T(8,128)S(1)} %shard_map.156.mine_ref), channel_id=1, source_target_pairs={{0,1},{1,0},{2,3},{3,2},{4,5},{5,4},{6,7},{7,6},{8,9},{9,8},{10,11... | collective-permute-start | bytes 294920 | tf_op jit(solution)/shard_map/ppermute | solution.py:516
